TPU v7x, 32 devices: a whole 2x2x4 slice. The times are simulated.
32 devices in a mesh: ctx: 8 (over y, x, core), fsdp: 4 (over z).
Axes of the slice: x: 2, y: 2, z: 4, core: 2. Of those that a mesh axis runs over, the one named last changes fastest.
Arguments:
- inputs: bfloat16 [4, 1024, 768], P('fsdp', 'ctx'), may hold values from -6 to 6
- cotangent: bfloat16 [4, 1024, 768], P('fsdp', 'ctx'), may hold values from -6 to 6
- first_gain: bfloat16 [768], P('fsdp'), may hold values from 0.5 to 1.5
- first_shift: bfloat16 [768], P('fsdp'), may hold values from -1.75 to 1.75
- input_weight: bfloat16 [768, 2304], P('fsdp'), may hold values from -0.3125 to 0.3125
- query_bias: bfloat16 [768], P('fsdp'), may hold values from -1.75 to 1.75
- value_bias: bfloat16 [768], P('fsdp'), may hold values from -1.75 to 1.75
- output_weight: bfloat16 [768, 768], P('fsdp'), may hold values from -0.625 to 0.625
- output_bias: bfloat16 [768], P('fsdp'), may hold values from -1.75 to 1.75
- second_gain: bfloat16 [768], P('fsdp'), may hold values from 0.5 to 1.5
- second_shift: bfloat16 [768], P('fsdp'), may hold values from -1.75 to 1.75
- expand_weight: bfloat16 [768, 3072], P('fsdp'), may hold values from -0.21875 to 0.21875
- expand_bias: bfloat16 [3072], P('fsdp'), may hold values from -1.75 to 1.75
- contract_weight: bfloat16 [3072, 768], P('fsdp'), may hold values from -0.21875 to 0.21875
- contract_bias: bfloat16 [768], P('fsdp'), may hold values from -1.75 to 1.75
Outputs:
- outputs: bfloat16 [4, 1024, 768], P('fsdp', 'ctx')
- delta_inputs: bfloat16 [4, 1024, 768], P('fsdp', 'ctx')
- delta_first_gain: float32 [768], P('fsdp')
- delta_first_shift: float32 [768], P('fsdp')
- delta_input_weight: float32 [768, 2304], P('fsdp')
- delta_query_bias: float32 [768], P('fsdp')
- delta_value_bias: float32 [768], P('fsdp')
- delta_output_weight: float32 [768, 768], P('fsdp')
- delta_output_bias: float32 [768], P('fsdp')
- delta_second_gain: float32 [768], P('fsdp')
- delta_second_shift: float32 [768], P('fsdp')
- delta_expand_weight: float32 [768, 3072], P('fsdp')
- delta_expand_bias: float32 [3072], P('fsdp')
- delta_contract_weight: float32 [3072, 768], P('fsdp')
- delta_contract_bias: float32 [768], P('fsdp')
All inputs are finite; a program needn't handle non-finite values.
Results may differ from a plain program's by a relative error of at most 0.022.
Values may be sent and summed in bfloat16 or wider, within the bound.
No kernel may reach another device: no remote copies, remote signals or barrier semaphores. Data moves between devices by JAX's collectives and lax.ppermute only.
A program may use at most 128 MiB of HBM per device.

v0:
```python
import functools

import jax
import jax.numpy as jnp
from jax import lax
from jax.experimental import pallas as pl
from jax.experimental.pallas import tpu as pltpu
from jax.sharding import Mesh, PartitionSpec as P

HEADS = 12
GROUPS = 4

NORM_EPS = 1e-05
MASK_FILL = -1e30
GELU_COEF = 0.7978845608028654
GELU_CUBE = 0.044715

BF = jnp.bfloat16
F32 = jnp.float32


def mm(left, right):
    return jnp.dot(left, right, preferred_element_type=F32)


def mm_lt(left, right):
    return lax.dot_general(left, right, (((0,), (0,)), ((), ())), preferred_element_type=F32)


def mm_rt(left, right):
    return lax.dot_general(left, right, (((1,), (1,)), ((), ())), preferred_element_type=F32)


def send(value, axis, flip):
    count = lax.axis_size(axis)
    return lax.ppermute(value, axis, [(s, s ^ flip) for s in range(count)])


def gather_flips(value, axis):
    return [value] + [send(value, axis, i) for i in range(1, lax.axis_size(axis))]


def swap_flips(pieces, axis):
    return [pieces[0]] + [send(p, axis, i) for i, p in enumerate(pieces) if i]


def pick(stacked, place):
    return lax.dynamic_index_in_dim(stacked, place, axis=0, keepdims=False)


def in_order(pieces, me):
    stacked = jnp.stack(pieces)
    return jnp.stack([pick(stacked, me ^ j) for j in range(len(pieces))])


def norm_stats(values):
    center = values - jnp.mean(values, axis=-1, keepdims=True)
    spread = jnp.mean(center * center, axis=-1, keepdims=True)
    rate = lax.rsqrt(spread + NORM_EPS)
    return center * rate, rate


def norm_back(slope, gain, hat, rate):
    scaled = slope * gain
    return rate * (
        scaled
        - jnp.mean(scaled, axis=-1, keepdims=True)
        - hat * jnp.mean(scaled * hat, axis=-1, keepdims=True)
    )


def total(parts):
    out = parts[0].astype(F32)
    for part in parts[1:]:
        out = out + part.astype(F32)
    return out


def cut_columns(source, cut, parts, i):
    wide = cut.shape[1] // parts
    for part in range(parts):
        low = (part * GROUPS + i) * wide
        cut[:, part * wide : (part + 1) * wide] = source[:, low : low + wide]


def cut_kernel(parts, place, in_ref, exp_ref, con_ref, out_ref, in_cut, exp_cut, con_cut, out_cut):
    con_cut[...] = con_ref[...]
    out_cut[...] = out_ref[...]
    for i in range(GROUPS):

        @pl.when(place[0] == i)
        def _():
            cut_columns(in_ref, in_cut, 3, i)
            cut_columns(exp_ref, exp_cut, parts, i)


def cut_weights(g, k, ks, zs, in_w, exp_w, con_w, out_w):
    rows = in_w.shape[0] // ks
    ff_rows = con_w.shape[0] // (GROUPS * ks)
    in_cols, exp_cols = in_w.shape[1] // GROUPS, exp_w.shape[1] // GROUPS
    width = out_w.shape[1]
    if rows % 16 == 0 and ff_rows % 16 == 0:
        by_k = lambda i, place: (place[1], 0)
        by_g = lambda i, place: (place[0] * ks + place[1], 0)
        whole = lambda i, place: (0, 0)
        shapes = [(rows, in_cols), (rows, exp_cols), (ff_rows, width), (rows, width)]
        return pl.pallas_call(
            functools.partial(cut_kernel, zs),
            grid_spec=pltpu.PrefetchScalarGridSpec(
                num_scalar_prefetch=1,
                grid=(1,),
                in_specs=[
                    pl.BlockSpec((rows, in_w.shape[1]), by_k),
                    pl.BlockSpec((rows, exp_w.shape[1]), by_k),
                    pl.BlockSpec((ff_rows, width), by_g),
                    pl.BlockSpec((rows, width), by_k),
                ],
                out_specs=[pl.BlockSpec(s, whole) for s in shapes],
            ),
            out_shape=[jax.ShapeDtypeStruct(s, BF) for s in shapes],
            compiler_params=pltpu.CompilerParams(vmem_limit_bytes=16 * 2**20),
        )(jnp.stack([g, k]).astype(jnp.int32), in_w, exp_w, con_w, out_w)

    def cut(weight, parts):
        half = pick(weight.reshape(ks, rows, -1), k)
        wide = weight.shape[1] // (parts * GROUPS)
        return lax.dynamic_index_in_dim(
            half.reshape(rows, parts, GROUPS, wide), g, axis=2, keepdims=False
        ).reshape(rows, parts * wide)

    return (
        cut(in_w, 3),
        cut(exp_w, zs),
        pick(con_w.reshape(GROUPS * ks, ff_rows, width), g * ks + k),
        pick(out_w.reshape(ks, rows, width), k),
    )


def weave_kernel(parts, pieces, out):
    wide = pieces.shape[2] // parts
    for i in range(GROUPS):
        for part in range(parts):
            low = (part * GROUPS + i) * wide
            out[:, low : low + wide] = pieces[i, :, part * wide : (part + 1) * wide].astype(F32)


def weave(pieces, parts):
    rows, cols = pieces.shape[1], pieces.shape[2]
    step = 32
    return pl.pallas_call(
        functools.partial(weave_kernel, parts),
        grid=(rows // step,),
        in_specs=[pl.BlockSpec((GROUPS, step, cols), lambda i: (0, i, 0))],
        out_specs=pl.BlockSpec((step, GROUPS * cols), lambda i: (i, 0)),
        out_shape=jax.ShapeDtypeStruct((rows, GROUPS * cols), F32),
        compiler_params=pltpu.CompilerParams(vmem_limit_bytes=16 * 2**20),
    )(pieces)


def shards(
    inputs,
    cotangent,
    first_gain,
    first_shift,
    input_weight,
    query_bias,
    value_bias,
    output_weight,
    output_bias,
    second_gain,
    second_shift,
    expand_weight,
    expand_bias,
    contract_weight,
    contract_bias,
):
    tok, width = inputs.shape[1:]
    ks, zs = lax.axis_size("core"), lax.axis_size("fsdp")
    g, k, z = lax.axis_index("grp"), lax.axis_index("core"), lax.axis_index("fsdp")
    rows_z = width // zs
    heads_here = HEADS // GROUPS
    head = width // HEADS
    cols = width // GROUPS
    ff = expand_weight.shape[1]
    ff_z = ff // zs
    ff_g = ff_z // GROUPS
    mine = GROUPS * tok
    scale = head ** (-0.5)

    x_own = inputs[0]
    slope_own = cotangent[0]

    x_rows = gather_flips(x_own, "grp")
    x_more = [[send(b, "core", j) for b in x_rows] for j in range(1, ks)]

    smalls = jnp.concatenate(
        [
            first_gain,
            first_shift,
            query_bias,
            value_bias,
            output_bias,
            second_gain,
            second_shift,
            contract_bias,
            expand_bias,
        ]
    )
    smalls_all = in_order(gather_flips(smalls, "fsdp"), z).astype(F32)

    def small(i):
        return smalls_all[:, i * rows_z : (i + 1) * rows_z].reshape(width)

    gain_one, shift_one, q_bias, v_bias, o_bias, gain_two, shift_two, c_bias = [
        small(i) for i in range(8)
    ]
    e_bias = pick(
        smalls_all[:, 8 * rows_z :].reshape(zs, GROUPS, ff_g).transpose(1, 0, 2), g
    ).reshape(zs * ff_g)
    q_bias = pick(q_bias.reshape(GROUPS, cols), g)
    v_bias = pick(v_bias.reshape(GROUPS, cols), g)

    in_cut, exp_cut, con_cut, out_cut = cut_weights(
        g, k, ks, zs, input_weight, expand_weight, contract_weight, output_weight
    )
    in_half = in_order(gather_flips(in_cut, "fsdp"), z)
    in_w = jnp.stack(in_order(gather_flips(in_half, "core"), k), axis=1).reshape(width, 3 * cols)

    slope_rows = jnp.concatenate(gather_flips(slope_own, "grp"))

    def whole(cut):
        return lax.all_gather(cut, ("fsdp", "core"), axis=0, tiled=True)

    out_w = whole(out_cut)
    con_w = whole(con_cut)
    exp_w = whole(exp_cut)
    out_w = out_w.reshape(GROUPS, cols, width)
    out_w = jnp.concatenate([pick(out_w, g ^ i) for i in range(GROUPS)])

    x_mine = jnp.concatenate(x_rows).astype(F32)
    hat_one, _ = norm_stats(x_mine)
    h1 = (hat_one * gain_one + shift_one).astype(BF)
    more = [jnp.concatenate(bs).astype(F32) for bs in x_more]
    h1_all = jnp.concatenate(
        [h1] + [(norm_stats(v)[0] * gain_one + shift_one).astype(BF) for v in more]
    )
    queries = (mm(h1, in_w[:, :cols]) + q_bias).astype(BF)
    kv = mm(h1_all, in_w[:, cols:])
    keys = kv[:, :cols].astype(BF)
    values = (kv[:, cols:] + v_bias).astype(BF)

    def to_heads(flat):
        return flat.reshape(flat.shape[0], heads_here, head).transpose(1, 0, 2)

    def from_heads(split):
        return split.transpose(1, 0, 2).reshape(split.shape[1], cols)

    qh, kh, vh = to_heads(queries), to_heads(keys), to_heads(values)
    steps = jnp.arange(tok, dtype=jnp.int32)
    q_place = jnp.concatenate([((g ^ i) * ks + k) * tok + steps for i in range(GROUPS)])
    k_place = jnp.concatenate(
        [((g ^ i) * ks + (k ^ j)) * tok + steps for j in range(ks) for i in range(GROUPS)]
    )
    scores = jnp.einsum("hqd,hkd->hqk", qh, kh, preferred_element_type=F32) * scale
    scores = jnp.where((k_place[None, :] <= q_place[:, None])[None], scores, MASK_FILL)
    peak = jnp.max(scores, axis=-1, keepdims=True)
    weights = jnp.exp(scores - peak)
    mass = jnp.sum(weights, axis=-1, keepdims=True)
    chances = weights / mass
    chances_low = chances.astype(BF)
    att_full = jnp.einsum("hqk,hkd->hqd", chances_low, vh, preferred_element_type=F32)
    att_rows = from_heads(att_full).astype(BF)

    att = jnp.concatenate(
        swap_flips([att_rows[i * tok : (i + 1) * tok] for i in range(GROUPS)], "grp"), axis=1
    )
    x_f = x_own.astype(F32)
    middle = x_f + mm(att, out_w) + o_bias
    hat_two, rate_two = norm_stats(middle)
    h2 = (hat_two * gain_two + shift_two).astype(BF)
    h2_rows = jnp.concatenate(gather_flips(h2, "grp"))

    slope_act = mm_rt(slope_rows, con_w)
    inner = mm(h2_rows, exp_w) + e_bias
    cube = GELU_COEF * (inner + GELU_CUBE * inner * inner * inner)
    tanh = jnp.tanh(cube)
    act = (0.5 * inner * (1.0 + tanh)).astype(BF)
    gelu_slope = 0.5 * (1.0 + tanh) + 0.5 * inner * (1.0 - tanh * tanh) * GELU_COEF * (
        1.0 + 3.0 * GELU_CUBE * inner * inner
    )
    slope_inner = (slope_act * gelu_slope).astype(BF)
    sh2_part = mm_rt(slope_inner, exp_w).astype(BF)
    sh2 = total(
        swap_flips([sh2_part[i * tok : (i + 1) * tok] for i in range(GROUPS)], "grp")
    )
    out_part = mm(act, con_w).astype(BF)
    out_sum = total(
        swap_flips([out_part[i * tok : (i + 1) * tok] for i in range(GROUPS)], "grp")
    )
    outputs = (middle + out_sum + c_bias).astype(BF)[None]

    slope_f = slope_own.astype(F32)
    d_gain_two = jnp.sum(sh2 * hat_two, axis=0)
    d_shift_two = jnp.sum(sh2, axis=0)
    slope_middle = slope_f + norm_back(sh2, gain_two, hat_two, rate_two)
    slope_branch = slope_middle.astype(BF)
    slope_att = mm_rt(slope_branch, out_w).astype(BF)
    datt = jnp.concatenate(
        swap_flips([slope_att[:, i * cols : (i + 1) * cols] for i in range(GROUPS)], "grp")
    )

    def reduced(grad, axes):
        return lax.psum_scatter(grad.astype(BF), axes, scatter_dimension=0, tiled=True)

    def spread(grad):
        return lax.all_gather(grad, ("grp", "core"), axis=0, tiled=True)

    d_con = reduced(mm_lt(act, slope_rows), ("fsdp", "core"))
    d_exp = reduced(mm_lt(h2_rows, slope_inner), ("fsdp", "core"))
    d_con_w = spread(d_con).astype(F32)
    d_exp_w = weave(spread(d_exp).reshape(GROUPS, rows_z, zs * ff_g), zs)

    d_out = mm_lt(att, slope_branch).reshape(GROUPS, cols, width)
    d_out = in_order([d_out[i] for i in range(GROUPS)], g).reshape(width, width)
    d_out_w = spread(reduced(d_out, ("fsdp", "grp", "core"))).astype(F32)

    dh = to_heads(datt)
    diag = jnp.sum(dh.astype(F32) * att_full, axis=-1, keepdims=True)
    slope_chances = jnp.einsum("hqd,hkd->hqk", dh, vh, preferred_element_type=F32)
    slope_scores = (chances * (slope_chances - diag)).astype(BF)
    dq = jnp.einsum("hqk,hkd->hqd", slope_scores, kh, preferred_element_type=F32) * scale
    dk = jnp.einsum("hqk,hqd->hkd", slope_scores, qh, preferred_element_type=F32) * scale
    dv = jnp.einsum("hqk,hqd->hkd", chances_low, dh, preferred_element_type=F32)
    dkv = jnp.concatenate([from_heads(dk), from_heads(dv)], axis=1)
    dkv = total(
        swap_flips([dkv[j * mine : (j + 1) * mine].astype(BF) for j in range(ks)], "core")
    )
    slope_project = jnp.concatenate([from_heads(dq), dkv], axis=1).astype(BF)
    sh1_part = mm_rt(slope_project, in_w)
    sh1_low = sh1_part.astype(BF)
    sh1 = total(swap_flips([sh1_low[i * tok : (i + 1) * tok] for i in range(GROUPS)], "grp"))
    hat_own, rate_own = norm_stats(x_f)
    delta_inputs = (slope_middle + norm_back(sh1, gain_one, hat_own, rate_own)).astype(BF)[None]

    def at_group(vec, lead):
        parts = vec.reshape(lead, 1, -1)
        spot = (jnp.arange(GROUPS) == g).astype(F32)[None, :, None]
        return (parts * spot).reshape(-1)

    sums = jnp.sum(slope_project.astype(F32), axis=0)
    vectors = [
        jnp.sum(sh1_part * hat_one, axis=0),
        jnp.sum(sh1_part, axis=0),
        at_group(sums[:cols], 1),
        at_group(sums[2 * cols :], 1),
        jnp.sum(slope_branch.astype(F32), axis=0),
        d_gain_two,
        d_shift_two,
        jnp.sum(slope_f, axis=0),
    ]
    packed = jnp.concatenate(
        [v.reshape(zs, rows_z) for v in vectors]
        + [at_group(jnp.sum(slope_inner.astype(F32), axis=0), zs).reshape(zs, ff_z)],
        axis=1,
    )
    count = packed.shape[1]
    extra = -(-count // (3 * cols * ks))
    packed = jnp.pad(packed, ((0, 0), (0, extra * ks * 3 * cols - count)))
    d_in = mm_lt(h1, slope_project).astype(BF).reshape(zs, ks, rows_z // ks, 3 * cols)
    d_in = jnp.concatenate([d_in, packed.astype(BF).reshape(zs, ks, extra, 3 * cols)], axis=2)
    pieces = [lax.dynamic_index_in_dim(d_in, k ^ j, axis=1, keepdims=False) for j in range(ks)]
    d_in = total(swap_flips(pieces, "core")).astype(BF)
    d_in = total(swap_flips([pick(d_in, z ^ i) for i in range(zs)], "fsdp")).astype(BF)
    d_in = in_order(gather_flips(d_in, "grp"), g)
    d_in = in_order(gather_flips(d_in, "core"), k)
    packed = jnp.sum(d_in[:, :, rows_z // ks :].astype(F32), axis=1).reshape(-1)
    d_in = d_in[:, :, : rows_z // ks].transpose(1, 0, 2, 3).reshape(GROUPS, rows_z, 3 * cols)
    d_in_w = weave(d_in, 3)

    def vec(i):
        return packed[i * rows_z : (i + 1) * rows_z]

    return (
        outputs,
        delta_inputs,
        vec(0),
        vec(1),
        d_in_w,
        vec(2),
        vec(3),
        d_out_w,
        vec(4),
        vec(5),
        vec(6),
        d_exp_w,
        packed[8 * rows_z : 8 * rows_z + ff_z],
        d_con_w,
        vec(7),
    )


def solution(mesh):
    ctx, zs = mesh.shape["ctx"], mesh.shape["fsdp"]
    axes = ("grp", "core", "fsdp")
    split = Mesh(mesh.devices.reshape(GROUPS, ctx // GROUPS, zs), axes)
    row, vec, mat = P("fsdp", ("grp", "core"), None), P("fsdp"), P("fsdp", None)
    placed = (row, row, vec, vec, mat, vec, vec, mat, vec, vec, vec, mat, vec, mat, vec)
    return jax.shard_map(
        shards,
        mesh=split,
        in_specs=placed,
        out_specs=placed,
        check_vma=False,
    )
```

profile of v0, /device:TPU:0, one launch (start us, length us, event | category | flops | bytes accessed | tf_op | source)
XLA Modules:
  0.0 330.6 jit_solution(14090225827038721640)
XLA Ops:
  14.5 5.0 %collective-permute-start.5 = (bf16[2304]{0:T(1024)(128)(2,1)S(1)}, bf16[2304]{0:T(1024)(128)(2,1)S(1)}, u32[]{:S(2)}, u32[]{:S(2)}) collective-permute-start(bf16[2304]{0:T(1024)(128)(2,1)S(1)} %concatenate.50), channel_id=1, source_target_pairs={{0,3},{1,2},{2,1},{3,0},{4,7},{5,6},{6,5},{7,4},{8,11},{9,10},{10,... | collective-permute-start | bytes 13832 | tf_op jit(solution)/shard_map/ppermute | solution.py:36
  24.1 3.7 %collective-permute-start.8 = (bf16[96,576]{1,0:T(8,128)(2,1)S(1)}, bf16[96,576]{1,0:T(8,128)(2,1)S(1)}, u32[]{:S(2)}, u32[]{:S(2)}) collective-permute-start(bf16[96,576]{1,0:T(8,128)(2,1)S(1)} %get-tuple-element.19), channel_id=1, source_target_pairs={{0,3},{1,2},{2,1},{3,0},{4,7},{5,6},{6,5},{7,4},{8,11},{9,10},{10,... | collective-permute-start | bytes 331784 | tf_op jit(solution)/shard_map/ppermute | solution.py:36
  31.1 3.2 collective-permute-done.8
  35.2 11.0 %collective-permute-done.7 = bf16[96,576]{1,0:T(8,128)(2,1)S(1)} collective-permute-done((bf16[96,576]{1,0:T(8,128)(2,1)S(1)}, bf16[96,576]{1,0:T(8,128)(2,1)S(1)}, u32[]{:S(2)}, u32[]{:S(2)}) %collective-permute-start.7) | collective-permute-done | bytes 110624 | tf_op jit(solution)/shard_map/ppermute | solution.py:36
  54.9 4.9 %fusion.92 = (f32[3,512]{1,0:T(4,128)S(1)}, f32[3,512,1024]{2,1,0:T(8,128)}) fusion(pred[512,1024]{1,0:T(8,128)(4,1)S(1)} %broadcast_compare_fusion, bf16[3,512,64]{1,2,0:T(8,128)(2,1)S(1)} %bitcast.156, bf16[3,1024,64]{1,2,0:T(8,128)(2,1)S(1)} %bitcast.149), kind=kOutput, calls=%fused_computation.230 | convolution fusion | flops 207619072 | bytes 7411712 | tf_op jit(solution)/shard_map/sub | solution.py:267
  59.8 3.6 %fusion.5 = bf16[3,512,1024]{2,1,0:T(8,128)(2,1)S(1)} fusion(f32[3,512,1024]{2,1,0:T(8,128)} %get-tuple-element.112, f32[3,512]{1,0:T(4,128)S(1)} %get-tuple-element.111), kind=kLoop, calls=%fused_computation.9 | loop fusion | flops 3145728 | bytes 9443328 | tf_op jit(solution)/shard_map/convert_element_type | solution.py:270
  86.4 2.9 collective-permute-done.18
  89.3 3.6 %convolution_add_fusion = f32[512,768]{1,0:T(8,128)} fusion(bf16[768,768]{1,0:T(8,128)(2,1)} %all-gather.8.cloned.1.call-done, f32[768]{0:T(1024)S(1)} %add.382, bf16[128,768]{1,0:T(8,128)(2,1)} %collective-permute-done.19, bf16[128,768]{1,0:T(8,128)(2,1)} %collective-permute-done.18, bf16[128,768]{1,0:T(8,128)(2,1)} %collective-permute-done.17, ...), kind=kOutput, calls=%fused_computation.47 | convolution fusion | flops 607518720 | bytes 3542016 | tf_op jit(solution)/shard_map/dot_general | solution.py:23
  93.5 3.1 collective-permute-done.24
  96.5 3.5 %convert_reduce_fusion.2 = (f32[768]{0:T(1024)S(1)}, bf16[512,768]{1,0:T(8,128)(2,1)S(1)}) fusion(f32[512,768]{1,0:T(8,128)} %convolution_add_fusion, bf16[768,768]{1,0:T(8,128)(2,1)} %all-gather.10.cloned.1.call-done, bf16[128,768]{1,0:T(8,128)(2,1)} %collective-permute-done.25, bf16[128,768]{1,0:T(8,128)(2,1)} %collective-permute-done.24, ...), kind=kOutput, calls=%fused_computation.43 | convolution fusion | flops 615382272 | bytes 4328448 | tf_op jit(solution)/shard_map/dot_general | solution.py:31
  100.9 3.0 convolution_convert_fusion.1
  121.8 3.1 convolution_convert_fusion
  128.9 4.2 %collective-permute-done.22 = bf16[128,768]{1,0:T(8,128)(2,1)} collective-permute-done((bf16[128,768]{1,0:T(8,128)(2,1)}, bf16[128,768]{1,0:T(8,128)(2,1)}, u32[]{:S(2)}, u32[]{:S(2)}) %collective-permute-start.22) | collective-permute-done | bytes 196640 | tf_op jit(solution)/shard_map/ppermute | solution.py:36
  134.5 3.2 multiply_reduce_fusion
  151.0 3.7 %multiply_convert_fusion = bf16[3,512,1024]{2,1,0:T(8,128)(2,1)S(1)} fusion(f32[3,512]{1,0:T(4,128)S(1)} %multiply_reduce_fusion.1, bf16[3,512,64]{1,2,0:T(8,128)(2,1)S(1)} %bitcast.147, bf16[3,1024,64]{1,2,0:T(8,128)(2,1)} %bitcast.153, f32[3,512,1024]{2,1,0:T(8,128)} %get-tuple-element.112, f32[3,512]{1,0:T(4,128)} %copy-done.65), kind=kOutput, calls=%fused_computation.1 | convolution fusion | flops 207618048 | bytes 10039296 | tf_op jit(solution)/shard_map/hqd,hkd->hqk/dot_general | solution.py:329
  159.2 3.1 fusion.32
  183.2 4.2 %collective-permute-done.38 = bf16[98,576]{1,0:T(8,128)(2,1)S(1)} collective-permute-done((bf16[98,576]{1,0:T(8,128)(2,1)S(1)}, bf16[98,576]{1,0:T(8,128)(2,1)S(1)}, u32[]{:S(2)}, u32[]{:S(2)}) %collective-permute-start.38) | collective-permute-done | bytes 112928 | tf_op jit(solution)/shard_map/ppermute | solution.py:36
  191.1 3.5 %collective-permute-done.42 = bf16[98,576]{1,0:T(8,128)(2,1)S(1)} collective-permute-done((bf16[98,576]{1,0:T(8,128)(2,1)S(1)}, bf16[98,576]{1,0:T(8,128)(2,1)S(1)}, u32[]{:S(2)}, u32[]{:S(2)}) %collective-permute-start.42) | collective-permute-done | bytes 112928 | tf_op jit(solution)/shard_map/ppermute | solution.py:36
  202.5 67.4 %reduce-scatter.4.cloned.1.call-done = bf16[24,768]{1,0:T(8,128)(2,1)} async-done(((bf16[768,768]{1,0:T(8,128)(2,1)}), bf16[24,768]{1,0:T(8,128)(2,1)}) %reduce-scatter.4.cloned.1.call-update) | async-done | bytes 36880 | tf_op jit(solution)/shard_map/reduce_scatter | solution.py:313
  269.9 9.5 %all_gather.21 = bf16[192,768]{1,0:T(8,128)(2,1)S(1)} all-gather(bf16[24,768]{1,0:T(8,128)(2,1)} %reduce-scatter.4.cloned.1.call-done), channel_id=1, replica_groups=mesh['grp'=4,'core'=2,'fsdp'=4] {'grp','core'}, dimensions={0}, use_global_device_ids=true | all-gather | bytes 331776 | tf_op jit(solution)/shard_map/all_gather | solution.py:316
  280.3 14.7 %all-gather.12.cloned.1.call-done = bf16[768,768]{1,0:T(8,128)(2,1)} async-done(((bf16[96,768]{1,0:T(8,128)(2,1)}), bf16[768,768]{1,0:T(8,128)(2,1)}) %all-gather.12.cloned.1.call-update) | async-done | bytes 1179664 | tf_op jit(solution)/shard_map/all_gather | solution.py:316
  296.3 2.8 shard_map.264
  299.0 21.9 %all-gather.14.cloned.1.call-done = bf16[768,768]{1,0:T(8,128)(2,1)} async-done(((bf16[96,768]{1,0:T(8,128)(2,1)}), bf16[768,768]{1,0:T(8,128)(2,1)}) %all-gather.14.cloned.1.call-update) | async-done | bytes 1179664 | tf_op jit(solution)/shard_map/all_gather | solution.py:316
  321.0 2.8 convert_element_type.251
  (406 shorter events, 123.2 us)
Async XLA Ops:
  7.2 62.4 %all-gather.6.cloned.1.call-start = ((), (), s32[]{:S(2)}) async-start(), calls=%async_computation.3 | async-start | bytes 1327104 | tf_op jit(solution)/shard_map/all_gather | solution.py:232
  13.5 72.8 %all-gather.8.cloned.1.call-start = ((), (), s32[]{:S(2)}) async-start(), calls=%async_computation.4 | async-start | bytes 1327104 | tf_op jit(solution)/shard_map/all_gather | solution.py:232
  14.3 82.2 %all-gather.10.cloned.1.call-start = ((), (), s32[]{:S(2)}) async-start(), calls=%async_computation.5 | async-start | bytes 1327104 | tf_op jit(solution)/shard_map/all_gather | solution.py:232
  20.2 26.8 %collective-permute-start.2 = (bf16[128,768]{1,0:T(8,128)(2,1)S(1)}, bf16[128,768]{1,0:T(8,128)(2,1)S(1)}, u32[]{:S(2)}, u32[]{:S(2)}) collective-permute-start(bf16[128,768]{1,0:T(8,128)(2,1)S(1)} %bitcast.131), channel_id=1, source_target_pairs={{0,24},{8,16},{16,8},{24,0},{1,25},{9,17},{17,9},{25,1},{2,26},{10... | collective-permute-start | bytes 589832 | tf_op jit(solution)/shard_map/ppermute | solution.py:36
  22.8 24.2 %collective-permute-start.1 = (bf16[128,768]{1,0:T(8,128)(2,1)S(1)}, bf16[128,768]{1,0:T(8,128)(2,1)S(1)}, u32[]{:S(2)}, u32[]{:S(2)}) collective-permute-start(bf16[128,768]{1,0:T(8,128)(2,1)S(1)} %bitcast.132), channel_id=1, source_target_pairs={{0,16},{8,24},{16,0},{24,8},{1,17},{9,25},{17,1},{25,9},{2,18},{10... | collective-permute-start | bytes 589832 | tf_op jit(solution)/shard_map/ppermute | solution.py:36
  23.4 138.9 %reduce-scatter.6.cloned.1.call-start = ((), (), s32[]{:S(2)}) async-start(), calls=%async_computation.7 | async-start | bytes 1327104 | tf_op jit(solution)/shard_map/reduce_scatter | solution.py:313
  27.8 18.4 %collective-permute-start.7 = (bf16[96,576]{1,0:T(8,128)(2,1)S(1)}, bf16[96,576]{1,0:T(8,128)(2,1)S(1)}, u32[]{:S(2)}, u32[]{:S(2)}) collective-permute-start(bf16[96,576]{1,0:T(8,128)(2,1)S(1)} %get-tuple-element.19), channel_id=1, source_target_pairs={{0,2},{1,3},{2,0},{3,1},{4,6},{5,7},{6,4},{7,5},{8,10},{9,11},{10,... | collective-permute-start | bytes 331784 | tf_op jit(solution)/shard_map/ppermute | solution.py:36
  27.9 18.3 %collective-permute-start.6 = (bf16[96,576]{1,0:T(8,128)(2,1)S(1)}, bf16[96,576]{1,0:T(8,128)(2,1)S(1)}, u32[]{:S(2)}, u32[]{:S(2)}) collective-permute-start(bf16[96,576]{1,0:T(8,128)(2,1)S(1)} %get-tuple-element.19), channel_id=1, source_target_pairs={{0,1},{1,0},{2,3},{3,2},{4,5},{5,4},{6,7},{7,6},{8,9},{9,8},{10,11... | collective-permute-start | bytes 331784 | tf_op jit(solution)/shard_map/ppermute | solution.py:36
  34.4 12.7 %collective-permute-start = (bf16[128,768]{1,0:T(8,128)(2,1)S(1)}, bf16[128,768]{1,0:T(8,128)(2,1)S(1)}, u32[]{:S(2)}, u32[]{:S(2)}) collective-permute-start(bf16[128,768]{1,0:T(8,128)(2,1)S(1)} %bitcast.133), channel_id=1, source_target_pairs={{0,8},{8,0},{16,24},{24,16},{1,9},{9,1},{17,25},{25,17},{2,10},{10... | collective-permute-start | bytes 589832 | tf_op jit(solution)/shard_map/ppermute | solution.py:36
  78.2 11.1 %collective-permute-start.18 = (bf16[128,768]{1,0:T(8,128)(2,1)}, bf16[128,768]{1,0:T(8,128)(2,1)}, u32[]{:S(2)}, u32[]{:S(2)}) collective-permute-start(bf16[128,768]{1,0:T(8,128)(2,1)} %add_convert_fusion.2), channel_id=1, source_target_pairs={{0,16},{8,24},{16,0},{24,8},{1,17},{9,25},{17,1},{25,9},{2,18},{10... | collective-permute-start | bytes 589832 | tf_op jit(solution)/shard_map/ppermute | solution.py:36
  79.4 14.0 %collective-permute-start.25 = (bf16[128,768]{1,0:T(8,128)(2,1)S(1)}, bf16[128,768]{1,0:T(8,128)(2,1)}, u32[]{:S(2)}, u32[]{:S(2)}) collective-permute-start(bf16[128,768]{1,0:T(8,128)(2,1)S(1)} %bitcast.161), channel_id=1, source_target_pairs={{0,24},{8,16},{16,8},{24,0},{1,25},{9,17},{17,9},{25,1},{2,26},{10... | collective-permute-start | bytes 589832 | tf_op jit(solution)/shard_map/ppermute | solution.py:36
  81.7 14.9 %collective-permute-start.24 = (bf16[128,768]{1,0:T(8,128)(2,1)S(1)}, bf16[128,768]{1,0:T(8,128)(2,1)}, u32[]{:S(2)}, u32[]{:S(2)}) collective-permute-start(bf16[128,768]{1,0:T(8,128)(2,1)S(1)} %bitcast.162), channel_id=1, source_target_pairs={{0,16},{8,24},{16,0},{24,8},{1,17},{9,25},{17,1},{25,9},{2,18},{10... | collective-permute-start | bytes 589832 | tf_op jit(solution)/shard_map/ppermute | solution.py:36
  85.0 11.6 %collective-permute-start.23 = (bf16[128,768]{1,0:T(8,128)(2,1)S(1)}, bf16[128,768]{1,0:T(8,128)(2,1)}, u32[]{:S(2)}, u32[]{:S(2)}) collective-permute-start(bf16[128,768]{1,0:T(8,128)(2,1)S(1)} %bitcast.163), channel_id=1, source_target_pairs={{0,8},{8,0},{16,24},{24,16},{1,9},{9,1},{17,25},{25,17},{2,10},{10... | collective-permute-start | bytes 589832 | tf_op jit(solution)/shard_map/ppermute | solution.py:36
  104.0 72.0 %reduce-scatter.8.cloned.1.call-start = ((), (), s32[]{:S(2)}) async-start(), calls=%async_computation.9 | async-start | bytes 1327104 | tf_op jit(solution)/shard_map/reduce_scatter | solution.py:313
  113.6 11.5 %collective-permute-start.28 = (bf16[128,768]{1,0:T(8,128)(2,1)}, bf16[128,768]{1,0:T(8,128)(2,1)}, u32[]{:S(2)}, u32[]{:S(2)}) collective-permute-start(bf16[128,768]{1,0:T(8,128)(2,1)} %get-tuple-element.56), channel_id=1, source_target_pairs={{0,24},{8,16},{16,8},{24,0},{1,25},{9,17},{17,9},{25,1},{2,26},{10... | collective-permute-start | bytes 589832 | tf_op jit(solution)/shard_map/ppermute | solution.py:36
  115.1 12.3 %collective-permute-start.27 = (bf16[128,768]{1,0:T(8,128)(2,1)}, bf16[128,768]{1,0:T(8,128)(2,1)}, u32[]{:S(2)}, u32[]{:S(2)}) collective-permute-start(bf16[128,768]{1,0:T(8,128)(2,1)} %get-tuple-element.57), channel_id=1, source_target_pairs={{0,16},{8,24},{16,0},{24,8},{1,17},{9,25},{17,1},{25,9},{2,18},{10... | collective-permute-start | bytes 589832 | tf_op jit(solution)/shard_map/ppermute | solution.py:36
  119.4 13.6 %collective-permute-start.22 = (bf16[128,768]{1,0:T(8,128)(2,1)}, bf16[128,768]{1,0:T(8,128)(2,1)}, u32[]{:S(2)}, u32[]{:S(2)}) collective-permute-start(bf16[128,768]{1,0:T(8,128)(2,1)} %get-tuple-element.59), channel_id=1, source_target_pairs={{0,24},{8,16},{16,8},{24,0},{1,25},{9,17},{17,9},{25,1},{2,26},{10... | collective-permute-start | bytes 589832 | tf_op jit(solution)/shard_map/ppermute | solution.py:36
  120.9 13.6 %collective-permute-start.21 = (bf16[128,768]{1,0:T(8,128)(2,1)}, bf16[128,768]{1,0:T(8,128)(2,1)}, u32[]{:S(2)}, u32[]{:S(2)}) collective-permute-start(bf16[128,768]{1,0:T(8,128)(2,1)} %get-tuple-element.60), channel_id=1, source_target_pairs={{0,16},{8,24},{16,0},{24,8},{1,17},{9,25},{17,1},{25,9},{2,18},{10... | collective-permute-start | bytes 589832 | tf_op jit(solution)/shard_map/ppermute | solution.py:36
  124.9 145.0 %reduce-scatter.4.cloned.1.call-start = ((), (), s32[]{:S(2)}) async-start(), calls=%async_computation.6 | async-start | bytes 1216512 | tf_op jit(solution)/shard_map/reduce_scatter | solution.py:313
  145.4 149.6 %all-gather.12.cloned.1.call-start = ((), (), s32[]{:S(2)}) async-start(), calls=%async_computation.8 | async-start | bytes 1327104 | tf_op jit(solution)/shard_map/all_gather | solution.py:316
  162.3 158.7 %all-gather.14.cloned.1.call-start = ((), (), s32[]{:S(2)}) async-start(), calls=%async_computation.10 | async-start | bytes 1327104 | tf_op jit(solution)/shard_map/all_gather | solution.py:316
  169.5 10.6 %collective-permute-start.35 = (bf16[128,768]{1,0:T(8,128)(2,1)S(1)}, bf16[128,768]{1,0:T(8,128)(2,1)S(1)}, u32[]{:S(2)}, u32[]{:S(2)}) collective-permute-start(bf16[128,768]{1,0:T(8,128)(2,1)S(1)} %get-tuple-element.53), channel_id=1, source_target_pairs={{0,24},{8,16},{16,8},{24,0},{1,25},{9,17},{17,9},{25,1},{2,26},{10... | collective-permute-start | bytes 589832 | tf_op jit(solution)/shard_map/ppermute | solution.py:36
  170.9 10.6 %collective-permute-start.34 = (bf16[128,768]{1,0:T(8,128)(2,1)S(1)}, bf16[128,768]{1,0:T(8,128)(2,1)}, u32[]{:S(2)}, u32[]{:S(2)}) collective-permute-start(bf16[128,768]{1,0:T(8,128)(2,1)S(1)} %get-tuple-element.54), channel_id=1, source_target_pairs={{0,16},{8,24},{16,0},{24,8},{1,17},{9,25},{17,1},{25,9},{2,18},{10... | collective-permute-start | bytes 589832 | tf_op jit(solution)/shard_map/ppermute | solution.py:36
  176.7 10.8 %collective-permute-start.38 = (bf16[98,576]{1,0:T(8,128)(2,1)S(1)}, bf16[98,576]{1,0:T(8,128)(2,1)S(1)}, u32[]{:S(2)}, u32[]{:S(2)}) collective-permute-start(bf16[98,576]{1,0:T(8,128)(2,1)S(1)} %get-tuple-element.69), channel_id=1, source_target_pairs={{0,2},{1,3},{2,0},{3,1},{4,6},{5,7},{6,4},{7,5},{8,10},{9,11},{10,... | collective-permute-start | bytes 338696 | tf_op jit(solution)/shard_map/ppermute | solution.py:36
  (114 other events, 554.2 us)
Sparse Core Ops, SparseCore 0:
  13.7 33.8 all-gather.5
  49.7 21.6 all-gather.7
  73.7 22.4 all-gather.9
  104.1 32.1 reduce-scatter.5
  139.0 31.0 reduce-scatter.7
  175.6 94.2 reduce-scatter.3
  271.8 23.1 all-gather.11
  296.9 24.0 all-gather.13
where the time goes:
time: 332 us; the launch traced here: 331 us
  waiting for transfers between devices  154 us (46%)
  starting transfers between devices  50.4 us (15%)
  matrix products  37 us (11%)
  local copies, waits for them, and re-layouts  29.8 us (9%)
  other arithmetic  27.7 us (8%)
  between operations  15.7 us (5%)
  blocking collectives  9.5 us (3%)
  Pallas kernels  6.82 us (2%)
    reduce_scatter x3, waiting for transfers between devices, reduced(): lax.psum_scatter(grad.astype(BF), axes, scatter_dimension=0, tiled=True)  67.4 us
    ppermute x44, starting transfers between devices, send(): return lax.ppermute(value, axis, [(s, s ^ flip) for s in range(count)])  49.6 us
    ppermute x44, waiting for transfers between devices, send(): return lax.ppermute(value, axis, [(s, s ^ flip) for s in range(count)])  48.8 us
    all_gather x2, waiting for transfers between devices, spread(): return lax.all_gather(grad, ('grp', 'core'), axis=0, tiled=True)  36.7 us
    unnamed x170, local copies, waits for them, and re-layouts  12.5 us
    all_gather x1, blocking collectives, spread(): return lax.all_gather(grad, ('grp', 'core'), axis=0, tiled=True)  9.5 us
    dot_general x4, matrix products, mm_rt(): lax.dot_general(left, right, (((1,), (1,)), ((), ())), preferred_element_...  8.29 us
    dot_general x5, matrix products, mm(): return jnp.dot(left, right, preferred_element_type=F32)  7.39 us
  transfers between devices with their start and end apart: 52, of which 30 were waited for; matrix products, arithmetic and copies ran while one was open for 22% of the time, Pallas kernels for 2%

commit v1 on v0

--- a/solution.py
+++ b/solution.py
@@ -83,57 +83,33 @@
         cut[:, part * wide : (part + 1) * wide] = source[:, low : low + wide]
 
 
-def cut_kernel(parts, place, in_ref, exp_ref, con_ref, out_ref, in_cut, exp_cut, con_cut, out_cut):
-    con_cut[...] = con_ref[...]
-    out_cut[...] = out_ref[...]
+def cut_kernel(parts, place, source, cut):
     for i in range(GROUPS):
 
         @pl.when(place[0] == i)
         def _():
-            cut_columns(in_ref, in_cut, 3, i)
-            cut_columns(exp_ref, exp_cut, parts, i)
-
-
-def cut_weights(g, k, ks, zs, in_w, exp_w, con_w, out_w):
-    rows = in_w.shape[0] // ks
-    ff_rows = con_w.shape[0] // (GROUPS * ks)
-    in_cols, exp_cols = in_w.shape[1] // GROUPS, exp_w.shape[1] // GROUPS
-    width = out_w.shape[1]
-    if rows % 16 == 0 and ff_rows % 16 == 0:
-        by_k = lambda i, place: (place[1], 0)
-        by_g = lambda i, place: (place[0] * ks + place[1], 0)
-        whole = lambda i, place: (0, 0)
-        shapes = [(rows, in_cols), (rows, exp_cols), (ff_rows, width), (rows, width)]
+            cut_columns(source, cut, parts, i)
+
+
+def cut_weight(weight, parts, g, k, ks):
+    rows = weight.shape[0] // ks
+    cols = weight.shape[1] // GROUPS
+    if rows % 16 == 0:
         return pl.pallas_call(
-            functools.partial(cut_kernel, zs),
+            functools.partial(cut_kernel, parts),
             grid_spec=pltpu.PrefetchScalarGridSpec(
                 num_scalar_prefetch=1,
                 grid=(1,),
-                in_specs=[
-                    pl.BlockSpec((rows, in_w.shape[1]), by_k),
-                    pl.BlockSpec((rows, exp_w.shape[1]), by_k),
-                    pl.BlockSpec((ff_rows, width), by_g),
-                    pl.BlockSpec((rows, width), by_k),
-                ],
-                out_specs=[pl.BlockSpec(s, whole) for s in shapes],
+                in_specs=[pl.BlockSpec((rows, weight.shape[1]), lambda i, place: (place[1], 0))],
+                out_specs=pl.BlockSpec((rows, cols), lambda i, place: (0, 0)),
             ),
-            out_shape=[jax.ShapeDtypeStruct(s, BF) for s in shapes],
-            compiler_params=pltpu.CompilerParams(vmem_limit_bytes=16 * 2**20),
-        )(jnp.stack([g, k]).astype(jnp.int32), in_w, exp_w, con_w, out_w)
-
-    def cut(weight, parts):
-        half = pick(weight.reshape(ks, rows, -1), k)
-        wide = weight.shape[1] // (parts * GROUPS)
-        return lax.dynamic_index_in_dim(
-            half.reshape(rows, parts, GROUPS, wide), g, axis=2, keepdims=False
-        ).reshape(rows, parts * wide)
-
-    return (
-        cut(in_w, 3),
-        cut(exp_w, zs),
-        pick(con_w.reshape(GROUPS * ks, ff_rows, width), g * ks + k),
-        pick(out_w.reshape(ks, rows, width), k),
-    )
+            out_shape=jax.ShapeDtypeStruct((rows, cols), BF),
+            compiler_params=pltpu.CompilerParams(vmem_limit_bytes=8 * 2**20),
+        )(jnp.stack([g, k]).astype(jnp.int32), weight)
+    half = pick(weight.reshape(ks, rows, -1), k)
+    return lax.dynamic_index_in_dim(
+        half.reshape(rows, parts, GROUPS, cols // parts), g, axis=2, keepdims=False
+    ).reshape(rows, cols)
 
 
 def weave_kernel(parts, pieces, out):
@@ -155,6 +131,154 @@
         out_shape=jax.ShapeDtypeStruct((rows, GROUPS * cols), F32),
         compiler_params=pltpu.CompilerParams(vmem_limit_bytes=16 * 2**20),
     )(pieces)
+
+
+def unfold_kernel(parts, pieces, exp_out, con_out):
+    wide = con_out.shape[2]
+    part_wide = wide // parts
+    for i in range(GROUPS):
+        con_out[i] = pieces[i, :, wide:].astype(F32)
+        for part in range(parts):
+            low = (part * GROUPS + i) * part_wide
+            exp_out[:, low : low + part_wide] = pieces[
+                i, :, part * part_wide : (part + 1) * part_wide
+            ].astype(F32)
+
+
+def unfold(pieces, parts):
+    rows, wide = pieces.shape[1], pieces.shape[2] // 2
+    step = 32
+    return pl.pallas_call(
+        functools.partial(unfold_kernel, parts),
+        grid=(rows // step,),
+        in_specs=[pl.BlockSpec((GROUPS, step, 2 * wide), lambda i: (0, i, 0))],
+        out_specs=[
+            pl.BlockSpec((step, GROUPS * wide), lambda i: (i, 0)),
+            pl.BlockSpec((GROUPS, step, wide), lambda i: (0, i, 0)),
+        ],
+        out_shape=[
+            jax.ShapeDtypeStruct((rows, GROUPS * wide), F32),
+            jax.ShapeDtypeStruct((GROUPS, rows, wide), F32),
+        ],
+        compiler_params=pltpu.CompilerParams(vmem_limit_bytes=16 * 2**20),
+    )(pieces)
+
+
+def hidden_kernel(
+    h_a, h_b, h_c, h_d, s_a, s_b, s_c, s_d, exp_w, con_w, bias,
+    act_ref, inner_ref, back_ref, out_ref, bias_ref, h_ref, s_ref, back_sum, out_sum,
+):
+    step = pl.program_id(0)
+    tok = h_a.shape[0]
+
+    @pl.when(step == 0)
+    def _():
+        for i, (h, s) in enumerate(((h_a, s_a), (h_b, s_b), (h_c, s_c), (h_d, s_d))):
+            h_ref[i * tok : (i + 1) * tok, :] = h[...]
+            s_ref[i * tok : (i + 1) * tok, :] = s[...]
+
+    inner = mm(h_ref[...], exp_w[...]) + bias[...]
+    square = inner * inner
+    tanh = jnp.tanh(GELU_COEF * (inner + GELU_CUBE * square * inner))
+    half = 0.5 + 0.5 * tanh
+    act = (inner * half).astype(BF)
+    gelu_slope = half + (0.5 * GELU_COEF) * inner * (1.0 - tanh * tanh) * (
+        1.0 + (3.0 * GELU_CUBE) * square
+    )
+    slope = (mm_rt(s_ref[...], con_w[...]) * gelu_slope).astype(BF)
+    act_ref[...] = act
+    inner_ref[...] = slope
+    bias_ref[...] = jnp.sum(slope.astype(F32), axis=0, keepdims=True)
+    back = mm_rt(slope, exp_w[...])
+    out = mm(act, con_w[...])
+
+    @pl.when(step == 0)
+    def _():
+        back_sum[...] = back
+        out_sum[...] = out
+
+    @pl.when(step > 0)
+    def _():
+        back_sum[...] += back
+        out_sum[...] += out
+
+    @pl.when(step == pl.num_programs(0) - 1)
+    def _():
+        for i in range(GROUPS):
+            back_ref[i] = back_sum[i * tok : (i + 1) * tok, :].astype(BF)
+            out_ref[i] = out_sum[i * tok : (i + 1) * tok, :].astype(BF)
+
+
+def hidden_part(h_rows, s_rows, exp_w, con_w, bias):
+    tok, width = h_rows[0].shape
+    hidden = exp_w.shape[1]
+    rows = GROUPS * tok
+    step = 256
+    fixed = lambda i: (0, 0)
+    cols = lambda i: (0, i)
+    return pl.pallas_call(
+        hidden_kernel,
+        grid=(hidden // step,),
+        in_specs=[pl.BlockSpec((tok, width), fixed)] * (2 * GROUPS)
+        + [
+            pl.BlockSpec((width, step), cols),
+            pl.BlockSpec((step, width), lambda i: (i, 0)),
+            pl.BlockSpec((1, step), cols),
+        ],
+        out_specs=[
+            pl.BlockSpec((rows, step), cols),
+            pl.BlockSpec((rows, step), cols),
+            pl.BlockSpec((GROUPS, tok, width), lambda i: (0, 0, 0)),
+            pl.BlockSpec((GROUPS, tok, width), lambda i: (0, 0, 0)),
+            pl.BlockSpec((1, step), cols),
+            pl.BlockSpec((rows, width), fixed),
+            pl.BlockSpec((rows, width), fixed),
+        ],
+        out_shape=[
+            jax.ShapeDtypeStruct((rows, hidden), BF),
+            jax.ShapeDtypeStruct((rows, hidden), BF),
+            jax.ShapeDtypeStruct((GROUPS, tok, width), BF),
+            jax.ShapeDtypeStruct((GROUPS, tok, width), BF),
+            jax.ShapeDtypeStruct((1, hidden), F32),
+            jax.ShapeDtypeStruct((rows, width), BF),
+            jax.ShapeDtypeStruct((rows, width), BF),
+        ],
+        scratch_shapes=[pltpu.VMEM((rows, width), F32), pltpu.VMEM((rows, width), F32)],
+        compiler_params=pltpu.CompilerParams(vmem_limit_bytes=40 * 2**20),
+        cost_estimate=pl.CostEstimate(
+            flops=8 * rows * width * hidden, bytes_accessed=12 * rows * width, transcendentals=0
+        ),
+    )(*h_rows, *s_rows, exp_w, con_w, bias)
+
+
+def hidden_grad_kernel(h_ref, inner_ref, act_ref, s_ref, out_ref):
+    wide = inner_ref.shape[1]
+    out_ref[:, :wide] = mm_lt(h_ref[...], inner_ref[...]).astype(BF)
+    out_ref[:, wide:] = mm_lt(act_ref[...], s_ref[...]).astype(BF)
+
+
+def hidden_grads(h_rows, slope_inner, act, s_rows):
+    rows, width = h_rows.shape
+    hidden = act.shape[1]
+    step = 256
+    cols = lambda i: (0, i)
+    fixed = lambda i: (0, 0)
+    return pl.pallas_call(
+        hidden_grad_kernel,
+        grid=(width // step,),
+        in_specs=[
+            pl.BlockSpec((rows, step), cols),
+            pl.BlockSpec((rows, hidden), fixed),
+            pl.BlockSpec((rows, step), cols),
+            pl.BlockSpec((rows, width), fixed),
+        ],
+        out_specs=pl.BlockSpec((step, hidden + width), lambda i: (i, 0)),
+        out_shape=jax.ShapeDtypeStruct((width, hidden + width), BF),
+        compiler_params=pltpu.CompilerParams(vmem_limit_bytes=40 * 2**20),
+        cost_estimate=pl.CostEstimate(
+            flops=4 * rows * width * hidden, bytes_accessed=12 * rows * width, transcendentals=0
+        ),
+    )(h_rows, slope_inner, act, s_rows)
 
 
 def shards(
@@ -191,6 +315,8 @@
     slope_own = cotangent[0]
 
     x_rows = gather_flips(x_own, "grp")
+    in_cut = cut_weight(input_weight, 3, g, k, ks)
+    in_pieces = gather_flips(in_cut, "fsdp")
     x_more = [[send(b, "core", j) for b in x_rows] for j in range(1, ks)]
 
     smalls = jnp.concatenate(
@@ -220,22 +346,19 @@
     q_bias = pick(q_bias.reshape(GROUPS, cols), g)
     v_bias = pick(v_bias.reshape(GROUPS, cols), g)
 
-    in_cut, exp_cut, con_cut, out_cut = cut_weights(
-        g, k, ks, zs, input_weight, expand_weight, contract_weight, output_weight
-    )
-    in_half = in_order(gather_flips(in_cut, "fsdp"), z)
+    in_half = in_order(in_pieces, z)
     in_w = jnp.stack(in_order(gather_flips(in_half, "core"), k), axis=1).reshape(width, 3 * cols)
-
-    slope_rows = jnp.concatenate(gather_flips(slope_own, "grp"))
 
     def whole(cut):
         return lax.all_gather(cut, ("fsdp", "core"), axis=0, tiled=True)
 
-    out_w = whole(out_cut)
-    con_w = whole(con_cut)
-    exp_w = whole(exp_cut)
+    out_w = whole(pick(output_weight.reshape(ks, rows_z // ks, width), k))
+    con_w = whole(pick(contract_weight.reshape(GROUPS * ks, ff_g // ks, width), g * ks + k))
+    exp_w = whole(cut_weight(expand_weight, zs, g, k, ks))
     out_w = out_w.reshape(GROUPS, cols, width)
     out_w = jnp.concatenate([pick(out_w, g ^ i) for i in range(GROUPS)])
+    slope_late, _ = lax.optimization_barrier((slope_own, x_rows[-1]))
+    slope_rows = gather_flips(slope_late, "grp")
 
     x_mine = jnp.concatenate(x_rows).astype(F32)
     hat_one, _ = norm_stats(x_mine)
@@ -278,26 +401,24 @@
     middle = x_f + mm(att, out_w) + o_bias
     hat_two, rate_two = norm_stats(middle)
     h2 = (hat_two * gain_two + shift_two).astype(BF)
-    h2_rows = jnp.concatenate(gather_flips(h2, "grp"))
-
-    slope_act = mm_rt(slope_rows, con_w)
-    inner = mm(h2_rows, exp_w) + e_bias
-    cube = GELU_COEF * (inner + GELU_CUBE * inner * inner * inner)
-    tanh = jnp.tanh(cube)
-    act = (0.5 * inner * (1.0 + tanh)).astype(BF)
-    gelu_slope = 0.5 * (1.0 + tanh) + 0.5 * inner * (1.0 - tanh * tanh) * GELU_COEF * (
-        1.0 + 3.0 * GELU_CUBE * inner * inner
-    )
-    slope_inner = (slope_act * gelu_slope).astype(BF)
-    sh2_part = mm_rt(slope_inner, exp_w).astype(BF)
-    sh2 = total(
-        swap_flips([sh2_part[i * tok : (i + 1) * tok] for i in range(GROUPS)], "grp")
-    )
-    out_part = mm(act, con_w).astype(BF)
-    out_sum = total(
-        swap_flips([out_part[i * tok : (i + 1) * tok] for i in range(GROUPS)], "grp")
-    )
-    outputs = (middle + out_sum + c_bias).astype(BF)[None]
+    h2_rows = gather_flips(h2, "grp")
+
+    act, slope_inner, sh2_part, out_part, d_exp_b, h2_all, slope_all = hidden_part(
+        h2_rows, slope_rows, exp_w, con_w, e_bias[None]
+    )
+    sh2 = total(swap_flips([sh2_part[i] for i in range(GROUPS)], "grp"))
+
+    def spread(grad):
+        return lax.all_gather(grad, ("grp", "core"), axis=0, tiled=True)
+
+    d_hidden = lax.psum_scatter(
+        hidden_grads(h2_all, slope_inner, act, slope_all),
+        ("fsdp", "core"),
+        scatter_dimension=0,
+        tiled=True,
+    )
+    d_exp_w, d_con_w = unfold(spread(d_hidden).reshape(GROUPS, rows_z, -1), zs)
+    d_con_w = d_con_w.reshape(ff_z, width)
 
     slope_f = slope_own.astype(F32)
     d_gain_two = jnp.sum(sh2 * hat_two, axis=0)
@@ -309,20 +430,22 @@
         swap_flips([slope_att[:, i * cols : (i + 1) * cols] for i in range(GROUPS)], "grp")
     )
 
-    def reduced(grad, axes):
-        return lax.psum_scatter(grad.astype(BF), axes, scatter_dimension=0, tiled=True)
-
-    def spread(grad):
-        return lax.all_gather(grad, ("grp", "core"), axis=0, tiled=True)
-
-    d_con = reduced(mm_lt(act, slope_rows), ("fsdp", "core"))
-    d_exp = reduced(mm_lt(h2_rows, slope_inner), ("fsdp", "core"))
-    d_con_w = spread(d_con).astype(F32)
-    d_exp_w = weave(spread(d_exp).reshape(GROUPS, rows_z, zs * ff_g), zs)
-
-    d_out = mm_lt(att, slope_branch).reshape(GROUPS, cols, width)
-    d_out = in_order([d_out[i] for i in range(GROUPS)], g).reshape(width, width)
-    d_out_w = spread(reduced(d_out, ("fsdp", "grp", "core"))).astype(F32)
+    d_out = mm_lt(att, slope_branch).astype(BF).reshape(GROUPS, cols, width)
+    d_out = in_order([d_out[i] for i in range(GROUPS)], g)
+    d_out = d_out.reshape(zs, GROUPS, ks, rows_z // GROUPS // ks, width)
+    pieces = [lax.dynamic_index_in_dim(d_out, k ^ j, axis=2, keepdims=False) for j in range(ks)]
+    d_out = total(swap_flips(pieces, "core")).astype(BF)
+    pieces = [lax.dynamic_index_in_dim(d_out, g ^ i, axis=1, keepdims=False) for i in range(GROUPS)]
+    d_out = total(swap_flips(pieces, "grp")).astype(BF)
+    third = d_out.shape[1] // 3
+    tail = d_out[:, :, 3 * cols :]
+    d_out = jnp.concatenate(
+        [
+            d_out[:, :, : 3 * cols],
+            jnp.concatenate([tail[:, i * third : (i + 1) * third] for i in range(3)], axis=2),
+        ],
+        axis=1,
+    )
 
     dh = to_heads(datt)
     diag = jnp.sum(dh.astype(F32) * att_full, axis=-1, keepdims=True)
@@ -360,7 +483,7 @@
     ]
     packed = jnp.concatenate(
         [v.reshape(zs, rows_z) for v in vectors]
-        + [at_group(jnp.sum(slope_inner.astype(F32), axis=0), zs).reshape(zs, ff_z)],
+        + [at_group(d_exp_b, zs).reshape(zs, ff_z)],
         axis=1,
     )
     count = packed.shape[1]
@@ -370,11 +493,29 @@
     d_in = jnp.concatenate([d_in, packed.astype(BF).reshape(zs, ks, extra, 3 * cols)], axis=2)
     pieces = [lax.dynamic_index_in_dim(d_in, k ^ j, axis=1, keepdims=False) for j in range(ks)]
     d_in = total(swap_flips(pieces, "core")).astype(BF)
+    d_in = jnp.concatenate([d_in, d_out], axis=1)
+    out_late, _ = lax.optimization_barrier((out_part, d_in))
+    out_sum = total(swap_flips([out_late[i] for i in range(GROUPS)], "grp"))
+    outputs = (middle + out_sum + c_bias).astype(BF)[None]
     d_in = total(swap_flips([pick(d_in, z ^ i) for i in range(zs)], "fsdp")).astype(BF)
     d_in = in_order(gather_flips(d_in, "grp"), g)
     d_in = in_order(gather_flips(d_in, "core"), k)
-    packed = jnp.sum(d_in[:, :, rows_z // ks :].astype(F32), axis=1).reshape(-1)
-    d_in = d_in[:, :, : rows_z // ks].transpose(1, 0, 2, 3).reshape(GROUPS, rows_z, 3 * cols)
+    own = rows_z // ks
+    packed = jnp.sum(d_in[:, :, own : own + extra].astype(F32), axis=1).reshape(-1)
+    d_out = d_in[:, :, own + extra :].transpose(1, 0, 2, 3)
+    tail = d_out[:, :, 3 * third :].reshape(GROUPS, ks, third, 3, width - 3 * cols)
+    d_out_w = (
+        jnp.concatenate(
+            [
+                d_out[:, :, : 3 * third],
+                jnp.concatenate([tail[:, :, :, i] for i in range(3)], axis=2),
+            ],
+            axis=3,
+        )
+        .reshape(rows_z, width)
+        .astype(F32)
+    )
+    d_in = d_in[:, :, :own].transpose(1, 0, 2, 3).reshape(GROUPS, rows_z, 3 * cols)
     d_in_w = weave(d_in, 3)
 
     def vec(i):

time: 332 us -> 252 us (0.76)
  waiting for transfers between devices: 154 us -> 76.1 us
  local copies, waits for them, and re-layouts: 29.8 us -> 44.5 us
  matrix products: 37 us -> 24.1 us
  blocking collectives: 9.5 us -> 0 us
  Pallas kernels: 6.82 us -> 16 us
  other arithmetic: 27.7 us -> 23.4 us
    reduce_scatter x3 -> x1, waiting for transfers between devices: 67.4 us -> 0.02 us  [shards(): lax.psum_scatter(hidden_grads(h2_all, slope_inner, act, slope_all), ('fsd...]
    all_gather x2 -> x1, waiting for transfers between devices: 36.7 us -> 0.01 us  [spread(): return lax.all_gather(grad, ('grp', 'core'), axis=0, tiled=True)]
    all_gather x3, waiting for transfers between devices: 0.01 us -> 14 us  [whole(): return lax.all_gather(cut, ('fsdp', 'core'), axis=0, tiled=True)]
    ppermute x44 -> x48, waiting for transfers between devices: 48.8 us -> 62 us  [send(): return lax.ppermute(value, axis, [(s, s ^ flip) for s in range(count)])]
    pallas_call x1 -> x5, Pallas kernels: 1.45 us -> 13.4 us  [the longest x1 4.98 us: hidden_part(): pl.pallas_call(hidden_kernel, grid=(hidden // step,), in_specs=[pl.BlockS...]
    all_gather x1 -> x0, blocking collectives: 9.5 us -> none  [spread(): return lax.all_gather(grad, ('grp', 'core'), axis=0, tiled=True)]
    unnamed x170 -> x195, local copies, waits for them, and re-layouts: 12.5 us -> 21.1 us
    dot_general x5 -> x3, matrix products: 7.39 us -> 1.86 us  [mm(): return jnp.dot(left, right, preferred_element_type=F32)]
  transfers between devices with their start and end apart: 52 -> 53, of which waited for: 30 -> 21; matrix products, arithmetic and copies ran while one was open for 22% -> 27% of each run, Pallas kernels for 2% -> 3%
where the time goes in v1:
time: 252 us; the launch traced here: 251 us
  waiting for transfers between devices  76.1 us (30%)
  starting transfers between devices  51.2 us (20%)
  local copies, waits for them, and re-layouts  44.5 us (18%)
  matrix products  24.1 us (10%)
  other arithmetic  23.4 us (9%)
  Pallas kernels  16 us (6%)
  between operations  15.4 us (6%)
    ppermute x48, waiting for transfers between devices, send(): return lax.ppermute(value, axis, [(s, s ^ flip) for s in range(count)])  62 us
    ppermute x48, starting transfers between devices, send(): return lax.ppermute(value, axis, [(s, s ^ flip) for s in range(count)])  50.8 us
    unnamed x195, local copies, waits for them, and re-layouts  21.1 us
    all_gather x3, waiting for transfers between devices, whole(): return lax.all_gather(cut, ('fsdp', 'core'), axis=0, tiled=True)  14 us
  transfers between devices with their start and end apart: 53, of which 21 were waited for; matrix products, arithmetic and copies ran while one was open for 27% of the time, Pallas kernels for 3%

profile of v1, /device:TPU:0, one launch (start us, length us, event | category | flops | bytes accessed | tf_op | source)
XLA Modules:
  0.0 250.7 jit_solution(6498742082127370034)
XLA Ops:
  12.1 5.0 %collective-permute-start.5 = (bf16[2304]{0:T(1024)(128)(2,1)S(1)}, bf16[2304]{0:T(1024)(128)(2,1)S(1)}, u32[]{:S(2)}, u32[]{:S(2)}) collective-permute-start(bf16[2304]{0:T(1024)(128)(2,1)S(1)} %concatenate.56), channel_id=1, source_target_pairs={{0,3},{1,2},{2,1},{3,0},{4,7},{5,6},{6,5},{7,4},{8,11},{9,10},{10,... | collective-permute-start | bytes 13832 | tf_op jit(solution)/shard_map/ppermute | solution.py:36
  25.0 3.6 %collective-permute-start.8 = (bf16[96,576]{1,0:T(8,128)(2,1)S(1)}, bf16[96,576]{1,0:T(8,128)(2,1)S(1)}, u32[]{:S(2)}, u32[]{:S(2)}) collective-permute-start(bf16[96,576]{1,0:T(8,128)(2,1)S(1)} %shard_map.262), channel_id=1, source_target_pairs={{0,3},{1,2},{2,1},{3,0},{4,7},{5,6},{6,5},{7,4},{8,11},{9,10},{10,... | collective-permute-start | bytes 331784 | tf_op jit(solution)/shard_map/ppermute | solution.py:36
  30.2 5.4 %collective-permute-done.8 = bf16[96,576]{1,0:T(8,128)(2,1)S(1)} collective-permute-done((bf16[96,576]{1,0:T(8,128)(2,1)S(1)}, bf16[96,576]{1,0:T(8,128)(2,1)S(1)}, u32[]{:S(2)}, u32[]{:S(2)}) %collective-permute-start.8) | collective-permute-done | bytes 110624 | tf_op jit(solution)/shard_map/ppermute | solution.py:36
  36.0 8.4 %collective-permute-done.7 = bf16[96,576]{1,0:T(8,128)(2,1)S(1)} collective-permute-done((bf16[96,576]{1,0:T(8,128)(2,1)S(1)}, bf16[96,576]{1,0:T(8,128)(2,1)S(1)}, u32[]{:S(2)}, u32[]{:S(2)}) %collective-permute-start.7) | collective-permute-done | bytes 110624 | tf_op jit(solution)/shard_map/ppermute | solution.py:36
  54.2 4.9 %fusion.94 = (f32[3,512]{1,0:T(4,128)S(1)}, f32[3,512,1024]{2,1,0:T(8,128)}) fusion(pred[512,1024]{1,0:T(8,128)(4,1)S(1)} %broadcast_compare_fusion, bf16[3,512,64]{1,2,0:T(8,128)(2,1)S(1)} %bitcast.212, bf16[3,1024,64]{1,2,0:T(8,128)(2,1)S(1)} %bitcast.205), kind=kOutput, calls=%fused_computation.245 | convolution fusion | flops 207619072 | bytes 7411712 | tf_op jit(solution)/shard_map/sub | solution.py:390
  59.1 3.5 %fusion.5 = bf16[3,512,1024]{2,1,0:T(8,128)(2,1)S(1)} fusion(f32[3,512,1024]{2,1,0:T(8,128)} %get-tuple-element.136, f32[3,512]{1,0:T(4,128)S(1)} %get-tuple-element.135), kind=kLoop, calls=%fused_computation.9 | loop fusion | flops 3145728 | bytes 9443328 | tf_op jit(solution)/shard_map/convert_element_type | solution.py:393
  78.8 14.0 %all-gather.13.cloned.1.call-done = bf16[1,768,768]{2,1,0:T(8,128)(2,1)} async-done(((bf16[1,96,768]{2,1,0:T(8,128)(2,1)}), bf16[1,768,768]{2,1,0:T(8,128)(2,1)}) %all-gather.13.cloned.1.call-update) | async-done | bytes 1179664 | tf_op jit(solution)/shard_map/all_gather | solution.py:353
  100.1 5.0 %shard_map.264 = (bf16[512,768]{1,0:T(8,128)(2,1)S(1)}, bf16[512,768]{1,0:T(8,128)(2,1)S(1)}, bf16[4,128,768]{2,1,0:T(8,128)(2,1)S(1)}, bf16[4,128,768]{2,1,0:T(...) custom-call(bf16[128,768]{1,0:T(8,128)(2,1)S(1)} %add_convert_fusion.1.h_a, ...), custom_call_target="tpu_custom_call" | custom-call | flops 2415919104 | bytes 4718592 | tf_op jit(solution)/shard_map/pallas_call | solution.py:219
  116.3 3.1 %shard_map.266 = bf16[768,1536]{1,0:T(8,128)(2,1)} custom-call(bf16[512,768]{1,0:T(8,128)(2,1)S(1)} %copy-done.9, bf16[512,768]{1,0:T(8,128)(2,1)S(1)} %copy-done.7, bf16[512,768]{1,0:T(8,128)(2,1)S(1)} %get-tuple-element.33.act_ref, bf16[512,768]{1,0:T(8,128)(2,1)S(1)} %copy-done.11), custom_call_target="tpu_custom_call" | custom-call | flops 1207959552 | bytes 4718592 | tf_op jit(solution)/shard_map/pallas_call | solution.py:266
  134.5 2.6 %fusion.97 = bf16[3,1024,64]{1,2,0:T(8,128)(2,1)S(1)} fusion(bf16[3,512,64]{1,2,0:T(8,128)(2,1)S(1)} %bitcast.203, bf16[3,512,1024]{2,1,0:T(8,128)(2,1)} %copy-done.20), kind=kOutput, calls=%fused_computation.248 | convolution fusion | flops 201326592 | bytes 3735552 | tf_op jit(solution)/shard_map/hqk,hqd->hkd/dot_general | solution.py:456
  137.2 3.6 %multiply_convert_fusion = bf16[3,512,1024]{2,1,0:T(8,128)(2,1)S(1)} fusion(f32[3,512]{1,0:T(4,128)S(1)} %multiply_reduce_fusion.1, bf16[3,512,64]{1,2,0:T(8,128)(2,1)S(1)} %bitcast.204, bf16[3,1024,64]{1,2,0:T(8,128)(2,1)S(1)} %bitcast.210, f32[3,512,1024]{2,1,0:T(8,128)} %get-tuple-element.136, f32[3,512]{1,0:T(4,128)S(1)} %copy-done.80), kind=kOutput, calls=%fused_computation.1 | convolution fusion | flops 207618048 | bytes 10039296 | tf_op jit(solution)/shard_map/hqd,hkd->hqk/dot_general | solution.py:452
  147.8 3.1 %fusion.26 = bf16[3,512,64]{1,2,0:T(8,128)(2,1)S(1)} fusion(bf16[3,512,1024]{2,1,0:T(8,128)(2,1)} %copy-done.21, bf16[3,1024,64]{1,2,0:T(8,128)(2,1)S(1)} %bitcast.206), kind=kOutput, calls=%fused_computation.54 | convolution fusion | flops 201523200 | bytes 3735552 | tf_op jit(solution)/shard_map/hqk,hkd->hqd/dot_general | solution.py:454
  156.1 3.7 %fusion.83 = (bf16[768]{0:T(1024)(128)(2,1)}, bf16[768]{0:T(1024)(128)(2,1)}, bf16[512,768]{1,0:T(8,128)(2,1)}) fusion(f32[512]{0:T(512)} %copy-done.75, f32[512]{0:T(512)S(1)} %copy-done.70, bf16[128,768]{1,0:T(8,128)(2,1)S(1)} %copy-done.34, bf16[128,768]{1,0:T(8,128)(2,1)S(1)} %copy-done.36, bf16[128,768]{1,0:T(8,128)(2,1)S(1)} %copy-done.38, ...), kind=kOutput, calls=%fused_computation.235 | convolution fusion | flops 459667968 | bytes 3054592 | tf_op jit(solution)/shard_map/dot_general | solution.py:31
  172.4 2.7 %collective-permute-done.40 = bf16[128,768]{1,0:T(8,128)(2,1)} collective-permute-done((bf16[128,768]{1,0:T(8,128)(2,1)}, bf16[128,768]{1,0:T(8,128)(2,1)}, u32[]{:S(2)}, u32[]{:S(2)}) %collective-permute-start.40) | collective-permute-done | bytes 196640 | tf_op jit(solution)/shard_map/ppermute | solution.py:36
  175.8 3.5 %collective-permute-done.39 = bf16[128,768]{1,0:T(8,128)(2,1)} collective-permute-done((bf16[128,768]{1,0:T(8,128)(2,1)}, bf16[128,768]{1,0:T(8,128)(2,1)}, u32[]{:S(2)}, u32[]{:S(2)}) %collective-permute-start.39) | collective-permute-done | bytes 196640 | tf_op jit(solution)/shard_map/ppermute | solution.py:36
  181.3 2.6 %collective-permute-done.34 = bf16[4,24,768]{2,1,0:T(8,128)(2,1)S(1)} collective-permute-done((bf16[4,24,768]{2,1,0:T(8,128)(2,1)S(1)}, bf16[4,24,768]{2,1,0:T(8,128)(2,1)S(1)}, u32[]{:S(2)}, u32[]{:S(2)}) %collective-permute-start.34) | collective-permute-done | bytes 147488 | tf_op jit(solution)/shard_map/ppermute | solution.py:36
  183.9 4.0 %collective-permute-done.33 = bf16[4,24,768]{2,1,0:T(8,128)(2,1)S(1)} collective-permute-done((bf16[4,24,768]{2,1,0:T(8,128)(2,1)S(1)}, bf16[4,24,768]{2,1,0:T(8,128)(2,1)S(1)}, u32[]{:S(2)}, u32[]{:S(2)}) %collective-permute-start.33) | collective-permute-done | bytes 147488 | tf_op jit(solution)/shard_map/ppermute | solution.py:36
  194.0 4.8 %collective-permute-done.43 = bf16[130,576]{1,0:T(8,128)(2,1)S(1)} collective-permute-done((bf16[130,576]{1,0:T(8,128)(2,1)S(1)}, bf16[130,576]{1,0:T(8,128)(2,1)S(1)}, u32[]{:S(2)}, u32[]{:S(2)}) %collective-permute-start.43) | collective-permute-done | bytes 149792 | tf_op jit(solution)/shard_map/ppermute | solution.py:36
  198.8 9.1 %collective-permute-done.42 = bf16[130,576]{1,0:T(8,128)(2,1)S(1)} collective-permute-done((bf16[130,576]{1,0:T(8,128)(2,1)S(1)}, bf16[130,576]{1,0:T(8,128)(2,1)S(1)}, u32[]{:S(2)}, u32[]{:S(2)}) %collective-permute-start.42) | collective-permute-done | bytes 149792 | tf_op jit(solution)/shard_map/ppermute | solution.py:36
  211.6 4.8 %collective-permute-done.46 = bf16[130,576]{1,0:T(8,128)(2,1)S(1)} collective-permute-done((bf16[130,576]{1,0:T(8,128)(2,1)S(1)}, bf16[130,576]{1,0:T(8,128)(2,1)S(1)}, u32[]{:S(2)}, u32[]{:S(2)}) %collective-permute-start.46) | collective-permute-done | bytes 149792 | tf_op jit(solution)/shard_map/ppermute | solution.py:36
  223.4 4.3 %collective-permute-done.37 = bf16[128,768]{1,0:T(8,128)(2,1)S(1)} collective-permute-done((bf16[128,768]{1,0:T(8,128)(2,1)S(1)}, bf16[128,768]{1,0:T(8,128)(2,1)S(1)}, u32[]{:S(2)}, u32[]{:S(2)}) %collective-permute-start.37) | collective-permute-done | bytes 196640 | tf_op jit(solution)/shard_map/ppermute | solution.py:36
  227.7 3.8 %collective-permute-done.36 = bf16[128,768]{1,0:T(8,128)(2,1)S(1)} collective-permute-done((bf16[128,768]{1,0:T(8,128)(2,1)S(1)}, bf16[128,768]{1,0:T(8,128)(2,1)S(1)}, u32[]{:S(2)}, u32[]{:S(2)}) %collective-permute-start.36) | collective-permute-done | bytes 196640 | tf_op jit(solution)/shard_map/ppermute | solution.py:36
  234.0 2.6 %shard_map.265 = f32[192,2304]{1,0:T(8,128)} custom-call(bf16[4,192,576]{2,1,0:T(8,128)(2,1)S(1)} %bitcast.179), custom_call_target="tpu_custom_call" | custom-call | tf_op jit(solution)/shard_map/pallas_call | solution.py:126
  240.8 3.4 %shard_map.267 = (f32[192,3072]{1,0:T(8,128)}, f32[4,192,768]{2,1,0:T(8,128)}) custom-call(bf16[4,192,1536]{2,1,0:T(8,128)(2,1)S(1)} %bitcast.180), custom_call_target="tpu_custom_call" | custom-call | tf_op jit(solution)/shard_map/pallas_call | solution.py:151
  (444 shorter events, 123.8 us)
Async XLA Ops:
  7.3 60.7 %all-gather.11.cloned.1.call-start = ((), (), s32[]{:S(2)}) async-start(), calls=%async_computation.4 | async-start | bytes 1327104 | tf_op jit(solution)/shard_map/all_gather | solution.py:353
  9.1 69.7 %all-gather.7.cloned.1.call-start = ((), (), s32[]{:S(2)}) async-start(), calls=%async_computation.1 | async-start | bytes 1327104 | tf_op jit(solution)/shard_map/all_gather | solution.py:353
  11.9 80.9 %all-gather.13.cloned.1.call-start = ((), (), s32[]{:S(2)}) async-start(), calls=%async_computation.5 | async-start | bytes 1327104 | tf_op jit(solution)/shard_map/all_gather | solution.py:353
  12.1 12.9 %collective-permute-start.5 = (bf16[2304]{0:T(1024)(128)(2,1)S(1)}, bf16[2304]{0:T(1024)(128)(2,1)S(1)}, u32[]{:S(2)}, u32[]{:S(2)}) collective-permute-start(bf16[2304]{0:T(1024)(128)(2,1)S(1)} %concatenate.56), channel_id=1, source_target_pairs={{0,3},{1,2},{2,1},{3,0},{4,7},{5,6},{6,5},{7,4},{8,11},{9,10},{10,... | collective-permute-start | bytes 13832 | tf_op jit(solution)/shard_map/ppermute | solution.py:36
  17.8 27.4 %collective-permute-start.2 = (bf16[128,768]{1,0:T(8,128)(2,1)S(1)}, bf16[128,768]{1,0:T(8,128)(2,1)S(1)}, u32[]{:S(2)}, u32[]{:S(2)}) collective-permute-start(bf16[128,768]{1,0:T(8,128)(2,1)S(1)} %bitcast.187), channel_id=1, source_target_pairs={{0,24},{8,16},{16,8},{24,0},{1,25},{9,17},{17,9},{25,1},{2,26},{10... | collective-permute-start | bytes 589832 | tf_op jit(solution)/shard_map/ppermute | solution.py:36
  20.4 24.8 %collective-permute-start.1 = (bf16[128,768]{1,0:T(8,128)(2,1)S(1)}, bf16[128,768]{1,0:T(8,128)(2,1)S(1)}, u32[]{:S(2)}, u32[]{:S(2)}) collective-permute-start(bf16[128,768]{1,0:T(8,128)(2,1)S(1)} %bitcast.188), channel_id=1, source_target_pairs={{0,16},{8,24},{16,0},{24,8},{1,17},{9,25},{17,1},{25,9},{2,18},{10... | collective-permute-start | bytes 589832 | tf_op jit(solution)/shard_map/ppermute | solution.py:36
  21.6 149.2 %reduce-scatter.2.cloned.1.call-start = ((), (), s32[]{:S(2)}) async-start(), calls=%async_computation.2 | async-start | bytes 2654208 | tf_op jit(solution)/shard_map/reduce_scatter | solution.py:414
  28.6 15.8 %collective-permute-start.7 = (bf16[96,576]{1,0:T(8,128)(2,1)S(1)}, bf16[96,576]{1,0:T(8,128)(2,1)S(1)}, u32[]{:S(2)}, u32[]{:S(2)}) collective-permute-start(bf16[96,576]{1,0:T(8,128)(2,1)S(1)} %shard_map.262), channel_id=1, source_target_pairs={{0,2},{1,3},{2,0},{3,1},{4,6},{5,7},{6,4},{7,5},{8,10},{9,11},{10,... | collective-permute-start | bytes 331784 | tf_op jit(solution)/shard_map/ppermute | solution.py:36
  28.7 15.7 %collective-permute-start.6 = (bf16[96,576]{1,0:T(8,128)(2,1)S(1)}, bf16[96,576]{1,0:T(8,128)(2,1)S(1)}, u32[]{:S(2)}, u32[]{:S(2)}) collective-permute-start(bf16[96,576]{1,0:T(8,128)(2,1)S(1)} %shard_map.262), channel_id=1, source_target_pairs={{0,1},{1,0},{2,3},{3,2},{4,5},{5,4},{6,7},{7,6},{8,9},{9,8},{10,11... | collective-permute-start | bytes 331784 | tf_op jit(solution)/shard_map/ppermute | solution.py:36
  46.5 28.5 %collective-permute-start.20 = (bf16[128,768]{1,0:T(8,128)(2,1)S(1)}, bf16[128,768]{1,0:T(8,128)(2,1)S(1)}, u32[]{:S(2)}, u32[]{:S(2)}) collective-permute-start(bf16[128,768]{1,0:T(8,128)(2,1)S(1)} %bitcast.181), channel_id=1, source_target_pairs={{0,8},{8,0},{16,24},{24,16},{1,9},{9,1},{17,25},{25,17},{2,10},{10... | collective-permute-start | bytes 589832 | tf_op jit(solution)/shard_map/ppermute | solution.py:36
  47.9 29.4 %collective-permute-start.21 = (bf16[128,768]{1,0:T(8,128)(2,1)S(1)}, bf16[128,768]{1,0:T(8,128)(2,1)S(1)}, u32[]{:S(2)}, u32[]{:S(2)}) collective-permute-start(bf16[128,768]{1,0:T(8,128)(2,1)S(1)} %bitcast.182), channel_id=1, source_target_pairs={{0,16},{8,24},{16,0},{24,8},{1,17},{9,25},{17,1},{25,9},{2,18},{10... | collective-permute-start | bytes 589832 | tf_op jit(solution)/shard_map/ppermute | solution.py:36
  72.4 20.4 %collective-permute-start.17 = (bf16[128,768]{1,0:T(8,128)(2,1)S(1)}, bf16[128,768]{1,0:T(8,128)(2,1)S(1)}, u32[]{:S(2)}, u32[]{:S(2)}) collective-permute-start(bf16[128,768]{1,0:T(8,128)(2,1)S(1)} %add_convert_fusion.1.h_a), channel_id=1, source_target_pairs={{0,8},{8,0},{16,24},{24,16},{1,9},{9,1},{17,25},{25,17},{2,10},{10... | collective-permute-start | bytes 589832 | tf_op jit(solution)/shard_map/ppermute | solution.py:36
  73.9 19.6 %collective-permute-start.18 = (bf16[128,768]{1,0:T(8,128)(2,1)S(1)}, bf16[128,768]{1,0:T(8,128)(2,1)S(1)}, u32[]{:S(2)}, u32[]{:S(2)}) collective-permute-start(bf16[128,768]{1,0:T(8,128)(2,1)S(1)} %add_convert_fusion.1.h_a), channel_id=1, source_target_pairs={{0,16},{8,24},{16,0},{24,8},{1,17},{9,25},{17,1},{25,9},{2,18},{10... | collective-permute-start | bytes 589832 | tf_op jit(solution)/shard_map/ppermute | solution.py:36
  75.0 19.1 %collective-permute-start.19 = (bf16[128,768]{1,0:T(8,128)(2,1)S(1)}, bf16[128,768]{1,0:T(8,128)(2,1)S(1)}, u32[]{:S(2)}, u32[]{:S(2)}) collective-permute-start(bf16[128,768]{1,0:T(8,128)(2,1)S(1)} %add_convert_fusion.1.h_a), channel_id=1, source_target_pairs={{0,24},{8,16},{16,8},{24,0},{1,25},{9,17},{17,9},{25,1},{2,26},{10... | collective-permute-start | bytes 589832 | tf_op jit(solution)/shard_map/ppermute | solution.py:36
  119.4 119.8 %all-gather.9.cloned.1.call-start = ((), (), s32[]{:S(2)}) async-start(), calls=%async_computation.3 | async-start | bytes 2654208 | tf_op jit(solution)/shard_map/all_gather | solution.py:412
  145.3 24.3 %collective-permute-start.31 = (bf16[4,4,24,768]{3,2,0,1:T(8,128)(2,1)}, bf16[4,4,24,768]{3,2,0,1:T(8,128)(2,1)}, u32[]{:S(2)}, u32[]{:S(2)}) collective-permute-start(bf16[4,4,24,768]{3,2,0,1:T(8,128)(2,1)} %bitcast.173), channel_id=1, source_target_pairs={{0,4},{4,0},{1,5},{5,1},{2,6},{6,2},{3,7},{7,3},{8,12},{12,8},{9,1... | collective-permute-start | bytes 1769480 | tf_op jit(solution)/shard_map/ppermute | solution.py:36
  165.2 22.9 %collective-permute-start.30 = (bf16[4,98,576]{2,0,1:T(4,128)(2,1)}, bf16[4,98,576]{2,0,1:T(4,128)(2,1)}, u32[]{:S(2)}, u32[]{:S(2)}) collective-permute-start(bf16[4,98,576]{2,0,1:T(4,128)(2,1)} %bitcast.174), channel_id=1, source_target_pairs={{0,4},{4,0},{1,5},{5,1},{2,6},{6,2},{3,7},{7,3},{8,12},{12,8},{9,1... | collective-permute-start | bytes 1354760 | tf_op jit(solution)/shard_map/ppermute | solution.py:36
  167.5 11.8 %collective-permute-start.39 = (bf16[128,768]{1,0:T(8,128)(2,1)}, bf16[128,768]{1,0:T(8,128)(2,1)}, u32[]{:S(2)}, u32[]{:S(2)}) collective-permute-start(bf16[128,768]{1,0:T(8,128)(2,1)} %get-tuple-element.70), channel_id=1, source_target_pairs={{0,16},{8,24},{16,0},{24,8},{1,17},{9,25},{17,1},{25,9},{2,18},{10... | collective-permute-start | bytes 589832 | tf_op jit(solution)/shard_map/ppermute | solution.py:36
  168.1 11.8 %collective-permute-start.38 = (bf16[128,768]{1,0:T(8,128)(2,1)S(1)}, bf16[128,768]{1,0:T(8,128)(2,1)}, u32[]{:S(2)}, u32[]{:S(2)}) collective-permute-start(bf16[128,768]{1,0:T(8,128)(2,1)S(1)} %get-tuple-element.68), channel_id=1, source_target_pairs={{0,8},{8,0},{16,24},{24,16},{1,9},{9,1},{17,25},{25,17},{2,10},{10... | collective-permute-start | bytes 589832 | tf_op jit(solution)/shard_map/ppermute | solution.py:36
  170.9 13.0 %collective-permute-start.34 = (bf16[4,24,768]{2,1,0:T(8,128)(2,1)S(1)}, bf16[4,24,768]{2,1,0:T(8,128)(2,1)S(1)}, u32[]{:S(2)}, u32[]{:S(2)}) collective-permute-start(bf16[4,24,768]{2,1,0:T(8,128)(2,1)S(1)} %get-tuple-element.87), channel_id=1, source_target_pairs={{0,24},{8,16},{16,8},{24,0},{1,25},{9,17},{17,9},{25,1},{2,26},{10... | collective-permute-start | bytes 442376 | tf_op jit(solution)/shard_map/ppermute | solution.py:36
  175.0 12.9 %collective-permute-start.33 = (bf16[4,24,768]{2,1,0:T(8,128)(2,1)S(1)}, bf16[4,24,768]{2,1,0:T(8,128)(2,1)S(1)}, u32[]{:S(2)}, u32[]{:S(2)}) collective-permute-start(bf16[4,24,768]{2,1,0:T(8,128)(2,1)S(1)} %get-tuple-element.88), channel_id=1, source_target_pairs={{0,16},{8,24},{16,0},{24,8},{1,17},{9,25},{17,1},{25,9},{2,18},{10... | collective-permute-start | bytes 442376 | tf_op jit(solution)/shard_map/ppermute | solution.py:36
  191.6 16.3 %collective-permute-start.42 = (bf16[130,576]{1,0:T(8,128)(2,1)S(1)}, bf16[130,576]{1,0:T(8,128)(2,1)S(1)}, u32[]{:S(2)}, u32[]{:S(2)}) collective-permute-start(bf16[130,576]{1,0:T(8,128)(2,1)S(1)} %get-tuple-element.85), channel_id=1, source_target_pairs={{0,2},{1,3},{2,0},{3,1},{4,6},{5,7},{6,4},{7,5},{8,10},{9,11},{10,... | collective-permute-start | bytes 449288 | tf_op jit(solution)/shard_map/ppermute | solution.py:36
  192.4 15.5 %collective-permute-start.41 = (bf16[130,576]{1,0:T(8,128)(2,1)S(1)}, bf16[130,576]{1,0:T(8,128)(2,1)S(1)}, u32[]{:S(2)}, u32[]{:S(2)}) collective-permute-start(bf16[130,576]{1,0:T(8,128)(2,1)S(1)} %get-tuple-element.83), channel_id=1, source_target_pairs={{0,1},{1,0},{2,3},{3,2},{4,5},{5,4},{6,7},{7,6},{8,9},{9,8},{10,11... | collective-permute-start | bytes 449288 | tf_op jit(solution)/shard_map/ppermute | solution.py:36
  218.9 13.4 %collective-permute-start.47 = (bf16[4,130,576]{2,0,1:T(4,128)(2,1)S(1)}, bf16[4,130,576]{2,0,1:T(4,128)(2,1)S(1)}, u32[]{:S(2)}, u32[]{:S(2)}) collective-permute-start(bf16[4,130,576]{2,0,1:T(4,128)(2,1)S(1)} %copy.80), channel_id=1, source_target_pairs={{0,4},{4,0},{1,5},{5,1},{2,6},{6,2},{3,7},{7,3},{8,12},{12,8},{9,1... | collective-permute-start | bytes 1797128 | tf_op jit(solution)/shard_map/ppermute | solution.py:36
  (127 other events, 622.1 us)
Sparse Core Ops, SparseCore 0:
  10.3 33.7 all-gather.10
  46.4 21.6 all-gather.6
  70.3 22.4 all-gather.12
  119.5 36.0 reduce-scatter.1
  171.0 31.3 all-gather.8

commit v2 on v1

--- a/solution.py
+++ b/solution.py
@@ -112,6 +112,49 @@
     ).reshape(rows, cols)
 
 
+def cut_rest_kernel(parts, place, con_ref, exp_ref, out_ref, cut):
+    width = con_ref.shape[1]
+    wide = exp_ref.shape[1] // GROUPS
+    cut[:, :width] = con_ref[...]
+    cut[:, width + wide :] = out_ref[...]
+    for i in range(GROUPS):
+
+        @pl.when(place[0] == i)
+        def _():
+            cut_columns(exp_ref, cut.at[:, width : width + wide], parts, i)
+
+
+def cut_rest(con_w, exp_w, out_w, parts, g, k, ks):
+    width = out_w.shape[1]
+    rows, ff_rows = out_w.shape[0] // ks, con_w.shape[0] // (GROUPS * ks)
+    wide = exp_w.shape[1] // GROUPS
+    if rows % 16 == 0 and rows == ff_rows:
+        by_k = lambda i, place: (place[1], 0)
+        return pl.pallas_call(
+            functools.partial(cut_rest_kernel, parts),
+            grid_spec=pltpu.PrefetchScalarGridSpec(
+                num_scalar_prefetch=1,
+                grid=(1,),
+                in_specs=[
+                    pl.BlockSpec((rows, width), lambda i, place: (place[0] * ks + place[1], 0)),
+                    pl.BlockSpec((rows, exp_w.shape[1]), by_k),
+                    pl.BlockSpec((rows, width), by_k),
+                ],
+                out_specs=pl.BlockSpec((rows, 2 * width + wide), lambda i, place: (0, 0)),
+            ),
+            out_shape=jax.ShapeDtypeStruct((rows, 2 * width + wide), BF),
+            compiler_params=pltpu.CompilerParams(vmem_limit_bytes=8 * 2**20),
+        )(jnp.stack([g, k]).astype(jnp.int32), con_w, exp_w, out_w)
+    return jnp.concatenate(
+        [
+            pick(con_w.reshape(GROUPS * ks, ff_rows, width), g * ks + k),
+            cut_weight(exp_w, parts, g, k, ks),
+            pick(out_w.reshape(ks, rows, width), k),
+        ],
+        axis=1,
+    )
+
+
 def weave_kernel(parts, pieces, out):
     wide = pieces.shape[2] // parts
     for i in range(GROUPS):
@@ -164,18 +207,23 @@
     )(pieces)
 
 
-def hidden_kernel(
-    h_a, h_b, h_c, h_d, s_a, s_b, s_c, s_d, exp_w, con_w, bias,
-    act_ref, inner_ref, back_ref, out_ref, bias_ref, h_ref, s_ref, back_sum, out_sum,
-):
+def join_rows(pieces, joined):
+    tok = pieces[0].shape[0]
+    for i, piece in enumerate(pieces):
+        joined[i * tok : (i + 1) * tok, :] = piece[...]
+
+
+def hidden_kernel(*refs):
+    h_rows, s_rows = refs[:GROUPS], refs[GROUPS : 2 * GROUPS]
+    (exp_w, con_w, bias, act_ref, inner_ref, back_ref, out_ref, bias_ref) = refs[2 * GROUPS : -4]
+    h_ref, s_ref, back_sum, out_sum = refs[-4:]
     step = pl.program_id(0)
-    tok = h_a.shape[0]
+    tok = h_rows[0].shape[0]
 
     @pl.when(step == 0)
     def _():
-        for i, (h, s) in enumerate(((h_a, s_a), (h_b, s_b), (h_c, s_c), (h_d, s_d))):
-            h_ref[i * tok : (i + 1) * tok, :] = h[...]
-            s_ref[i * tok : (i + 1) * tok, :] = s[...]
+        join_rows(h_rows, h_ref)
+        join_rows(s_rows, s_ref)
 
     inner = mm(h_ref[...], exp_w[...]) + bias[...]
     square = inner * inner
@@ -209,30 +257,29 @@
             out_ref[i] = out_sum[i * tok : (i + 1) * tok, :].astype(BF)
 
 
-def hidden_part(h_rows, s_rows, exp_w, con_w, bias):
+def hidden_part(h_rows, s_rows, weights, bias):
     tok, width = h_rows[0].shape
-    hidden = exp_w.shape[1]
+    hidden = bias.shape[1]
     rows = GROUPS * tok
     step = 256
     fixed = lambda i: (0, 0)
     cols = lambda i: (0, i)
+    slots = pl.BlockSpec((GROUPS, tok, width), lambda i: (0, 0, 0))
     return pl.pallas_call(
         hidden_kernel,
         grid=(hidden // step,),
         in_specs=[pl.BlockSpec((tok, width), fixed)] * (2 * GROUPS)
         + [
-            pl.BlockSpec((width, step), cols),
+            pl.BlockSpec((width, step), lambda i: (0, width // step + i)),
             pl.BlockSpec((step, width), lambda i: (i, 0)),
             pl.BlockSpec((1, step), cols),
         ],
         out_specs=[
             pl.BlockSpec((rows, step), cols),
             pl.BlockSpec((rows, step), cols),
-            pl.BlockSpec((GROUPS, tok, width), lambda i: (0, 0, 0)),
-            pl.BlockSpec((GROUPS, tok, width), lambda i: (0, 0, 0)),
+            slots,
+            slots,
             pl.BlockSpec((1, step), cols),
-            pl.BlockSpec((rows, width), fixed),
-            pl.BlockSpec((rows, width), fixed),
         ],
         out_shape=[
             jax.ShapeDtypeStruct((rows, hidden), BF),
@@ -240,45 +287,238 @@
             jax.ShapeDtypeStruct((GROUPS, tok, width), BF),
             jax.ShapeDtypeStruct((GROUPS, tok, width), BF),
             jax.ShapeDtypeStruct((1, hidden), F32),
-            jax.ShapeDtypeStruct((rows, width), BF),
-            jax.ShapeDtypeStruct((rows, width), BF),
-        ],
-        scratch_shapes=[pltpu.VMEM((rows, width), F32), pltpu.VMEM((rows, width), F32)],
-        compiler_params=pltpu.CompilerParams(vmem_limit_bytes=40 * 2**20),
+        ],
+        scratch_shapes=[pltpu.VMEM((rows, width), BF)] * 2 + [pltpu.VMEM((rows, width), F32)] * 2,
+        compiler_params=pltpu.CompilerParams(vmem_limit_bytes=24 * 2**20),
         cost_estimate=pl.CostEstimate(
             flops=8 * rows * width * hidden, bytes_accessed=12 * rows * width, transcendentals=0
         ),
-    )(*h_rows, *s_rows, exp_w, con_w, bias)
-
-
-def hidden_grad_kernel(h_ref, inner_ref, act_ref, s_ref, out_ref):
-    wide = inner_ref.shape[1]
+    )(*h_rows, *s_rows, weights, weights, bias)
+
+
+def hidden_grad_kernel(*refs):
+    h_rows, s_rows = refs[:GROUPS], refs[GROUPS : 2 * GROUPS]
+    inner_ref, act_ref, out_ref, h_ref, s_ref = refs[2 * GROUPS :]
+    wide, step = inner_ref.shape[1], act_ref.shape[1]
+
+    @pl.when(pl.program_id(0) == 0)
+    def _():
+        join_rows(s_rows, s_ref)
+
+    join_rows(h_rows, h_ref)
     out_ref[:, :wide] = mm_lt(h_ref[...], inner_ref[...]).astype(BF)
     out_ref[:, wide:] = mm_lt(act_ref[...], s_ref[...]).astype(BF)
 
 
-def hidden_grads(h_rows, slope_inner, act, s_rows):
-    rows, width = h_rows.shape
-    hidden = act.shape[1]
+def hidden_grads(h_rows, s_rows, slope_inner, act):
+    tok, width = h_rows[0].shape
+    rows, hidden = act.shape
     step = 256
     cols = lambda i: (0, i)
     fixed = lambda i: (0, 0)
     return pl.pallas_call(
         hidden_grad_kernel,
         grid=(width // step,),
-        in_specs=[
-            pl.BlockSpec((rows, step), cols),
-            pl.BlockSpec((rows, hidden), fixed),
-            pl.BlockSpec((rows, step), cols),
-            pl.BlockSpec((rows, width), fixed),
-        ],
+        in_specs=[pl.BlockSpec((tok, step), cols)] * GROUPS
+        + [pl.BlockSpec((tok, width), fixed)] * GROUPS
+        + [pl.BlockSpec((rows, hidden), fixed), pl.BlockSpec((rows, step), cols)],
         out_specs=pl.BlockSpec((step, hidden + width), lambda i: (i, 0)),
         out_shape=jax.ShapeDtypeStruct((width, hidden + width), BF),
-        compiler_params=pltpu.CompilerParams(vmem_limit_bytes=40 * 2**20),
+        scratch_shapes=[pltpu.VMEM((rows, step), BF), pltpu.VMEM((rows, width), BF)],
+        compiler_params=pltpu.CompilerParams(vmem_limit_bytes=16 * 2**20),
         cost_estimate=pl.CostEstimate(
             flops=4 * rows * width * hidden, bytes_accessed=12 * rows * width, transcendentals=0
         ),
-    )(h_rows, slope_inner, act, s_rows)
+    )(*h_rows, *s_rows, slope_inner, act)
+
+
+def visible(k, tok, keys):
+    row = lax.broadcasted_iota(jnp.int32, (tok, keys), 0)
+    col = lax.broadcasted_iota(jnp.int32, (tok, keys), 1)
+    return col <= k * tok + row
+
+
+def masked_scores(query, keys, seen):
+    scores = mm_rt(query, keys)
+    near = keys.shape[0] - seen.shape[1]
+    last = jnp.where(seen, scores[:, near:], MASK_FILL)
+    return last if near == 0 else jnp.concatenate([scores[:, :near], last], axis=1)
+
+
+def attend_kernel(ks, head, place, *refs):
+    pieces = refs[: GROUPS * ks]
+    in_w, gain, shift, q_bias, v_bias = refs[GROUPS * ks : GROUPS * ks + 5]
+    slots, q_out, k_out, v_out, att_out, lse_out, h_out, hat_out, h_all = refs[GROUPS * ks + 5 :]
+    g, k = place[0], place[1]
+    tok, width = pieces[0].shape
+    cols = q_out.shape[1]
+    for j in range(ks):
+        for i in range(GROUPS):
+            hat, _ = norm_stats(pieces[j * GROUPS + i][...].astype(F32))
+            normed = (hat * gain[...] + shift[...]).astype(BF)
+            spot = pl.multiple_of(((g ^ i) * ks + (k ^ j)) * tok, tok)
+            h_all[pl.ds(spot, tok), :] = normed
+            if j == 0:
+                spot = pl.multiple_of((g ^ i) * tok, tok)
+                h_out[pl.ds(spot, tok), :] = normed
+                hat_out[pl.ds(spot, tok), :] = hat.astype(BF)
+    q_out[...] = (mm(h_out[...], in_w[:, :cols]) + q_bias[...]).astype(BF)
+    kv = mm(h_all[...], in_w[:, cols:])
+    k_out[...] = kv[:, :cols].astype(BF)
+    v_out[...] = (kv[:, cols:] + v_bias[...]).astype(BF)
+    seen = visible(k, tok, ks * tok)
+    for h in range(cols // head):
+        low, high = h * head, (h + 1) * head
+        for i in range(GROUPS):
+            rows = slice(i * tok, (i + 1) * tok)
+            span = (i + 1) * ks * tok
+            query = (q_out[rows, low:high].astype(F32) * head**-0.5).astype(BF)
+            scores = masked_scores(query, k_out[:span, low:high], seen)
+            peak = jnp.max(scores, axis=-1, keepdims=True)
+            weights = jnp.exp(scores - peak)
+            mass = jnp.sum(weights, axis=-1, keepdims=True)
+            lse_out[rows, h : h + 1] = peak + jnp.log(mass)
+            att = mm(weights.astype(BF), v_out[:span, low:high]) / mass
+            att_out[rows, low:high] = att
+    for i in range(GROUPS):
+        slots[g ^ i] = att_out[i * tok : (i + 1) * tok, :].astype(BF)
+
+
+def attend(g, k, ks, head, pieces, in_w, gain, shift, q_bias, v_bias):
+    tok, width = pieces[0].shape
+    cols = in_w.shape[1] // 3
+    mine, rows = GROUPS * tok, GROUPS * ks * tok
+    vmem = pl.BlockSpec(memory_space=pltpu.VMEM)
+    shapes = [
+        ((GROUPS, tok, cols), BF),
+        ((mine, cols), BF),
+        ((rows, cols), BF),
+        ((rows, cols), BF),
+        ((mine, cols), F32),
+        ((mine, 8), F32),
+        ((mine, width), BF),
+        ((mine, width), BF),
+    ]
+    return pl.pallas_call(
+        functools.partial(attend_kernel, ks, head),
+        grid_spec=pltpu.PrefetchScalarGridSpec(
+            num_scalar_prefetch=1,
+            in_specs=[vmem] * (len(pieces) + 5),
+            out_specs=[vmem] * len(shapes),
+            scratch_shapes=[pltpu.VMEM((rows, width), BF)],
+        ),
+        out_shape=[jax.ShapeDtypeStruct(s, t) for s, t in shapes],
+        compiler_params=pltpu.CompilerParams(vmem_limit_bytes=(16 if ks == 2 else 48) * 2**20),
+        cost_estimate=pl.CostEstimate(
+            flops=6 * rows * width * cols, bytes_accessed=4 * rows * width, transcendentals=0
+        ),
+    )(jnp.stack([g, k]).astype(jnp.int32), *pieces, in_w, gain, shift, q_bias, v_bias)
+
+
+def attend_back_kernel(ks, head, place, *refs):
+    slopes = refs[:GROUPS]
+    q_ref, k_ref, v_ref, att_ref, lse_ref, dq_out, dkv_out, dk_sum, dv_sum = refs[GROUPS:]
+    g, k = place[0], place[1]
+    tok, cols = slopes[0].shape
+    d_rows = dq_out
+    for i in range(GROUPS):
+        d_rows[pl.ds(pl.multiple_of((g ^ i) * tok, tok), tok), :] = slopes[i][...]
+    seen = visible(k, tok, ks * tok)
+    for i in reversed(range(GROUPS)):
+        rows = slice(i * tok, (i + 1) * tok)
+        span = (i + 1) * ks * tok
+        slope_all = d_rows[rows, :]
+        parts = []
+        for h in range(cols // head):
+            low, high = h * head, (h + 1) * head
+            query = (q_ref[rows, low:high].astype(F32) * head**-0.5).astype(BF)
+            keys = k_ref[:span, low:high]
+            slope = slope_all[:, low:high]
+            scores = masked_scores(query, keys, seen)
+            chances = jnp.exp(scores - lse_ref[rows, h : h + 1])
+            diag = jnp.sum(slope.astype(F32) * att_ref[rows, low:high], axis=-1, keepdims=True)
+            slope_chances = mm_rt(slope, v_ref[:span, low:high])
+            slope_scores = (chances * (slope_chances - diag)).astype(BF)
+            parts.append(mm(slope_scores, keys) * head**-0.5)
+            dk = mm_lt(slope_scores, query)
+            dv = mm_lt(chances.astype(BF), slope)
+            if i == GROUPS - 1:
+                dk_sum[:, low:high] = dk
+                dv_sum[:, low:high] = dv
+            else:
+                dk_sum[:span, low:high] += dk
+                dv_sum[:span, low:high] += dv
+        dq_out[rows, :] = jnp.concatenate(parts, axis=1).astype(BF)
+    for i in range(GROUPS):
+        for j in range(ks):
+            spot = slice((i * ks + j) * tok, (i * ks + j + 1) * tok)
+            dkv_out[k ^ j, i * tok : (i + 1) * tok, :] = jnp.concatenate(
+                [dk_sum[spot, :], dv_sum[spot, :]], axis=1
+            ).astype(BF)
+
+
+def attend_back(g, k, ks, head, slopes, q, keys, values, att, lse):
+    tok, cols = slopes[0].shape
+    mine, rows = GROUPS * tok, GROUPS * ks * tok
+    vmem = pl.BlockSpec(memory_space=pltpu.VMEM)
+    return pl.pallas_call(
+        functools.partial(attend_back_kernel, ks, head),
+        grid_spec=pltpu.PrefetchScalarGridSpec(
+            num_scalar_prefetch=1,
+            in_specs=[vmem] * (len(slopes) + 5),
+            out_specs=[vmem] * 2,
+            scratch_shapes=[pltpu.VMEM((rows, cols), F32)] * 2,
+        ),
+        out_shape=[
+            jax.ShapeDtypeStruct((mine, cols), BF),
+            jax.ShapeDtypeStruct((ks, mine, 2 * cols), BF),
+        ],
+        compiler_params=pltpu.CompilerParams(vmem_limit_bytes=(16 if ks == 2 else 48) * 2**20),
+        cost_estimate=pl.CostEstimate(
+            flops=10 * mine * rows * cols, bytes_accessed=8 * rows * cols, transcendentals=0
+        ),
+    )(jnp.stack([g, k]).astype(jnp.int32), *slopes, q, keys, values, att, lse)
+
+
+def project_back_kernel(ks, place, *refs):
+    dq, dkv = refs[0], refs[1 : 1 + ks]
+    h_ref, hat_ref, in_w, slots, d_in, sums, project = refs[1 + ks :]
+    g = place[0]
+    tok = slots.shape[1]
+    cols = dq.shape[1]
+    project[:, :cols] = dq[...]
+    project[:, cols:] = total([part[...] for part in dkv]).astype(BF)
+    back = mm_rt(project[...], in_w[...])
+    for i in range(GROUPS):
+        slots[g ^ i] = back[i * tok : (i + 1) * tok, :].astype(BF)
+    sums[0:1, :] = jnp.sum(back * hat_ref[...].astype(F32), axis=0, keepdims=True)
+    sums[1:2, :] = jnp.sum(back, axis=0, keepdims=True)
+    sums[2:3, : 3 * cols] = jnp.sum(project[...].astype(F32), axis=0, keepdims=True)
+    d_in[...] = mm_lt(h_ref[...], project[...]).astype(BF)
+
+
+def project_back(g, k, dq, dkv, h, hat, in_w):
+    mine, width = h.shape
+    cols = dq.shape[1]
+    vmem = pl.BlockSpec(memory_space=pltpu.VMEM)
+    return pl.pallas_call(
+        functools.partial(project_back_kernel, len(dkv)),
+        grid_spec=pltpu.PrefetchScalarGridSpec(
+            num_scalar_prefetch=1,
+            in_specs=[vmem] * (len(dkv) + 4),
+            out_specs=[vmem] * 3,
+            scratch_shapes=[pltpu.VMEM((mine, 3 * cols), BF)],
+        ),
+        out_shape=[
+            jax.ShapeDtypeStruct((GROUPS, mine // GROUPS, width), BF),
+            jax.ShapeDtypeStruct((width, 3 * cols), BF),
+            jax.ShapeDtypeStruct((8, width), F32),
+        ],
+        compiler_params=pltpu.CompilerParams(vmem_limit_bytes=16 * 2**20),
+        cost_estimate=pl.CostEstimate(
+            flops=12 * mine * width * cols, bytes_accessed=4 * mine * width, transcendentals=0
+        ),
+    )(jnp.stack([g, k]).astype(jnp.int32), dq, *dkv, h, hat, in_w)
 
 
 def shards(
@@ -349,76 +589,42 @@
     in_half = in_order(in_pieces, z)
     in_w = jnp.stack(in_order(gather_flips(in_half, "core"), k), axis=1).reshape(width, 3 * cols)
 
-    def whole(cut):
-        return lax.all_gather(cut, ("fsdp", "core"), axis=0, tiled=True)
-
-    out_w = whole(pick(output_weight.reshape(ks, rows_z // ks, width), k))
-    con_w = whole(pick(contract_weight.reshape(GROUPS * ks, ff_g // ks, width), g * ks + k))
-    exp_w = whole(cut_weight(expand_weight, zs, g, k, ks))
-    out_w = out_w.reshape(GROUPS, cols, width)
+    rest = cut_rest(contract_weight, expand_weight, output_weight, zs, g, k, ks)
+    rest = lax.all_gather(rest, ("fsdp", "core"), axis=0, tiled=True)
+    out_w = rest[:, width + zs * ff_g :].reshape(GROUPS, cols, width)
     out_w = jnp.concatenate([pick(out_w, g ^ i) for i in range(GROUPS)])
     slope_late, _ = lax.optimization_barrier((slope_own, x_rows[-1]))
     slope_rows = gather_flips(slope_late, "grp")
 
-    x_mine = jnp.concatenate(x_rows).astype(F32)
-    hat_one, _ = norm_stats(x_mine)
-    h1 = (hat_one * gain_one + shift_one).astype(BF)
-    more = [jnp.concatenate(bs).astype(F32) for bs in x_more]
-    h1_all = jnp.concatenate(
-        [h1] + [(norm_stats(v)[0] * gain_one + shift_one).astype(BF) for v in more]
-    )
-    queries = (mm(h1, in_w[:, :cols]) + q_bias).astype(BF)
-    kv = mm(h1_all, in_w[:, cols:])
-    keys = kv[:, :cols].astype(BF)
-    values = (kv[:, cols:] + v_bias).astype(BF)
-
-    def to_heads(flat):
-        return flat.reshape(flat.shape[0], heads_here, head).transpose(1, 0, 2)
-
-    def from_heads(split):
-        return split.transpose(1, 0, 2).reshape(split.shape[1], cols)
-
-    qh, kh, vh = to_heads(queries), to_heads(keys), to_heads(values)
-    steps = jnp.arange(tok, dtype=jnp.int32)
-    q_place = jnp.concatenate([((g ^ i) * ks + k) * tok + steps for i in range(GROUPS)])
-    k_place = jnp.concatenate(
-        [((g ^ i) * ks + (k ^ j)) * tok + steps for j in range(ks) for i in range(GROUPS)]
-    )
-    scores = jnp.einsum("hqd,hkd->hqk", qh, kh, preferred_element_type=F32) * scale
-    scores = jnp.where((k_place[None, :] <= q_place[:, None])[None], scores, MASK_FILL)
-    peak = jnp.max(scores, axis=-1, keepdims=True)
-    weights = jnp.exp(scores - peak)
-    mass = jnp.sum(weights, axis=-1, keepdims=True)
-    chances = weights / mass
-    chances_low = chances.astype(BF)
-    att_full = jnp.einsum("hqk,hkd->hqd", chances_low, vh, preferred_element_type=F32)
-    att_rows = from_heads(att_full).astype(BF)
-
-    att = jnp.concatenate(
-        swap_flips([att_rows[i * tok : (i + 1) * tok] for i in range(GROUPS)], "grp"), axis=1
-    )
+    slots, qs, keys, values, att_full, lse, h1, hat_one = attend(
+        g,
+        k,
+        ks,
+        head,
+        x_rows + [b for bs in x_more for b in bs],
+        in_w,
+        gain_one[None],
+        shift_one[None],
+        q_bias[None],
+        v_bias[None],
+    )
+    att = jnp.concatenate(swap_flips([slots[i] for i in range(GROUPS)], "grp"), axis=1)
     x_f = x_own.astype(F32)
     middle = x_f + mm(att, out_w) + o_bias
     hat_two, rate_two = norm_stats(middle)
     h2 = (hat_two * gain_two + shift_two).astype(BF)
     h2_rows = gather_flips(h2, "grp")
 
-    act, slope_inner, sh2_part, out_part, d_exp_b, h2_all, slope_all = hidden_part(
-        h2_rows, slope_rows, exp_w, con_w, e_bias[None]
+    act, slope_inner, sh2_part, out_part, d_exp_b = hidden_part(
+        h2_rows, slope_rows, rest, e_bias[None]
     )
     sh2 = total(swap_flips([sh2_part[i] for i in range(GROUPS)], "grp"))
-
-    def spread(grad):
-        return lax.all_gather(grad, ("grp", "core"), axis=0, tiled=True)
-
     d_hidden = lax.psum_scatter(
-        hidden_grads(h2_all, slope_inner, act, slope_all),
+        hidden_grads(h2_rows, slope_rows, slope_inner, act),
         ("fsdp", "core"),
         scatter_dimension=0,
         tiled=True,
     )
-    d_exp_w, d_con_w = unfold(spread(d_hidden).reshape(GROUPS, rows_z, -1), zs)
-    d_con_w = d_con_w.reshape(ff_z, width)
 
     slope_f = slope_own.astype(F32)
     d_gain_two = jnp.sum(sh2 * hat_two, axis=0)
@@ -426,9 +632,7 @@
     slope_middle = slope_f + norm_back(sh2, gain_two, hat_two, rate_two)
     slope_branch = slope_middle.astype(BF)
     slope_att = mm_rt(slope_branch, out_w).astype(BF)
-    datt = jnp.concatenate(
-        swap_flips([slope_att[:, i * cols : (i + 1) * cols] for i in range(GROUPS)], "grp")
-    )
+    datt = swap_flips([slope_att[:, i * cols : (i + 1) * cols] for i in range(GROUPS)], "grp")
 
     d_out = mm_lt(att, slope_branch).astype(BF).reshape(GROUPS, cols, width)
     d_out = in_order([d_out[i] for i in range(GROUPS)], g)
@@ -447,21 +651,11 @@
         axis=1,
     )
 
-    dh = to_heads(datt)
-    diag = jnp.sum(dh.astype(F32) * att_full, axis=-1, keepdims=True)
-    slope_chances = jnp.einsum("hqd,hkd->hqk", dh, vh, preferred_element_type=F32)
-    slope_scores = (chances * (slope_chances - diag)).astype(BF)
-    dq = jnp.einsum("hqk,hkd->hqd", slope_scores, kh, preferred_element_type=F32) * scale
-    dk = jnp.einsum("hqk,hqd->hkd", slope_scores, qh, preferred_element_type=F32) * scale
-    dv = jnp.einsum("hqk,hqd->hkd", chances_low, dh, preferred_element_type=F32)
-    dkv = jnp.concatenate([from_heads(dk), from_heads(dv)], axis=1)
-    dkv = total(
-        swap_flips([dkv[j * mine : (j + 1) * mine].astype(BF) for j in range(ks)], "core")
-    )
-    slope_project = jnp.concatenate([from_heads(dq), dkv], axis=1).astype(BF)
-    sh1_part = mm_rt(slope_project, in_w)
-    sh1_low = sh1_part.astype(BF)
-    sh1 = total(swap_flips([sh1_low[i * tok : (i + 1) * tok] for i in range(GROUPS)], "grp"))
+    datt, d_out = lax.optimization_barrier((datt, d_out))
+    dq, dkv = attend_back(g, k, ks, head, datt, qs, keys, values, att_full, lse)
+    dkv = swap_flips([dkv[j] for j in range(ks)], "core")
+    sh1_part, d_in, sums = project_back(g, k, dq, dkv, h1, hat_one, in_w)
+    sh1 = total(swap_flips([sh1_part[i] for i in range(GROUPS)], "grp"))
     hat_own, rate_own = norm_stats(x_f)
     delta_inputs = (slope_middle + norm_back(sh1, gain_one, hat_own, rate_own)).astype(BF)[None]
 
@@ -470,12 +664,11 @@
         spot = (jnp.arange(GROUPS) == g).astype(F32)[None, :, None]
         return (parts * spot).reshape(-1)
 
-    sums = jnp.sum(slope_project.astype(F32), axis=0)
     vectors = [
-        jnp.sum(sh1_part * hat_one, axis=0),
-        jnp.sum(sh1_part, axis=0),
-        at_group(sums[:cols], 1),
-        at_group(sums[2 * cols :], 1),
+        sums[0],
+        sums[1],
+        at_group(sums[2, :cols], 1),
+        at_group(sums[2, 2 * cols : 3 * cols], 1),
         jnp.sum(slope_branch.astype(F32), axis=0),
         d_gain_two,
         d_shift_two,
@@ -489,7 +682,7 @@
     count = packed.shape[1]
     extra = -(-count // (3 * cols * ks))
     packed = jnp.pad(packed, ((0, 0), (0, extra * ks * 3 * cols - count)))
-    d_in = mm_lt(h1, slope_project).astype(BF).reshape(zs, ks, rows_z // ks, 3 * cols)
+    d_in = d_in.reshape(zs, ks, rows_z // ks, 3 * cols)
     d_in = jnp.concatenate([d_in, packed.astype(BF).reshape(zs, ks, extra, 3 * cols)], axis=2)
     pieces = [lax.dynamic_index_in_dim(d_in, k ^ j, axis=1, keepdims=False) for j in range(ks)]
     d_in = total(swap_flips(pieces, "core")).astype(BF)
@@ -517,6 +710,10 @@
     )
     d_in = d_in[:, :, :own].transpose(1, 0, 2, 3).reshape(GROUPS, rows_z, 3 * cols)
     d_in_w = weave(d_in, 3)
+    d_hidden = in_order(gather_flips(d_hidden, "grp"), g)
+    d_hidden = jnp.stack(in_order(gather_flips(d_hidden, "core"), k), axis=1)
+    d_exp_w, d_con_w = unfold(d_hidden.reshape(GROUPS, rows_z, -1), zs)
+    d_con_w = d_con_w.reshape(ff_z, width)
 
     def vec(i):
         return packed[i * rows_z : (i + 1) * rows_z]

time: 252 us -> 242 us (0.960)
  matrix products: 24.1 us -> 2.58 us
  Pallas kernels: 16 us -> 32.1 us
  starting transfers between devices: 51.2 us -> 57.6 us
  other arithmetic: 23.4 us -> 17.7 us
  local copies, waits for them, and re-layouts: 44.5 us -> 41.1 us
    pallas_call x0 -> x4, Pallas kernels: none -> 17.3 us  [the longest x1 6.9 us: attend(): pl.pallas_call(functools.partial(attend_kernel, ks, head), grid_spec=pltp...]
    all_gather x4 -> x1, waiting for transfers between devices: 14 us -> 0.01 us  [shards(): rest = lax.all_gather(rest, ('fsdp', 'core'), axis=0, tiled=True)]
    ppermute x48 -> x52, waiting for transfers between devices: 62 us -> 74.5 us  [send(): return lax.ppermute(value, axis, [(s, s ^ flip) for s in range(count)])]
    dot_general x5 -> x0, matrix products: 11.1 us -> none  [the longest x1 3.64 us: shards(): jnp.einsum('hqd,hkd->hqk', dh, vh, preferred_element_type=F32)]
    ppermute x48 -> x52, starting transfers between devices: 50.8 us -> 57.5 us  [send(): return lax.ppermute(value, axis, [(s, s ^ flip) for s in range(count)])]
    convert_element_type x4 -> x0, other arithmetic: 5.47 us -> none  [the longest x1 3.52 us: shards(): chances_low = chances.astype(BF)]
    unnamed x195 -> x186, local copies, waits for them, and re-layouts: 21.1 us -> 26.5 us
    sub x1 -> x0, matrix products: 4.9 us -> none  [shards(): weights = jnp.exp(scores - peak)]
  transfers between devices with their start and end apart: 53 -> 54, of which waited for: 21 -> 23; matrix products, arithmetic and copies ran while one was open for 27% -> 10% of each run, Pallas kernels for 3% -> 9%
where the time goes in v2:
time: 242 us; the launch traced here: 241 us
  waiting for transfers between devices  74.6 us (31%)
  starting transfers between devices  57.6 us (24%)
  local copies, waits for them, and re-layouts  41.1 us (17%)
  Pallas kernels  32.1 us (13%)
  other arithmetic  17.7 us (7%)
  between operations  15.3 us (6%)
  matrix products  2.58 us (1%)
    ppermute x52, waiting for transfers between devices, send(): return lax.ppermute(value, axis, [(s, s ^ flip) for s in range(count)])  74.5 us
    ppermute x52, starting transfers between devices, send(): return lax.ppermute(value, axis, [(s, s ^ flip) for s in range(count)])  57.5 us
    unnamed x186, local copies, waits for them, and re-layouts  26.5 us
    pallas_call x1, Pallas kernels, attend(): pl.pallas_call(functools.partial(attend_kernel, ks, head), grid_spec=pltp...  6.9 us
    pallas_call x1, Pallas kernels, attend_back(): pl.pallas_call(functools.partial(attend_back_kernel, ks, head), grid_spec...  6.86 us
    pallas_call x1, Pallas kernels, hidden_part(): pl.pallas_call(hidden_kernel, grid=(hidden // step,), in_specs=[pl.BlockS...  5.06 us
  transfers between devices with their start and end apart: 54, of which 23 were waited for; matrix products, arithmetic and copies ran while one was open for 10% of the time, Pallas kernels for 9%

profile of v2, /device:TPU:0, one launch (start us, length us, event | category | flops | bytes accessed | tf_op | source)
XLA Modules:
  0.0 241.0 jit_solution(14968286750248317991)
XLA Ops:
  12.6 5.0 %collective-permute-start.13 = (bf16[2304]{0:T(1024)(128)(2,1)S(1)}, bf16[2304]{0:T(1024)(128)(2,1)S(1)}, u32[]{:S(2)}, u32[]{:S(2)}) collective-permute-start(bf16[2304]{0:T(1024)(128)(2,1)S(1)} %concatenate.31), channel_id=1, source_target_pairs={{0,3},{1,2},{2,1},{3,0},{4,7},{5,6},{6,5},{7,4},{8,11},{9,10},{10,... | collective-permute-start | bytes 13832 | tf_op jit(solution)/shard_map/ppermute | solution.py:36
  22.2 3.7 %collective-permute-start.9 = (bf16[96,576]{1,0:T(8,128)(2,1)S(1)}, bf16[96,576]{1,0:T(8,128)(2,1)S(1)}, u32[]{:S(2)}, u32[]{:S(2)}) collective-permute-start(bf16[96,576]{1,0:T(8,128)(2,1)S(1)} %shard_map.262), channel_id=1, source_target_pairs={{0,3},{1,2},{2,1},{3,0},{4,7},{5,6},{6,5},{7,4},{8,11},{9,10},{10,... | collective-permute-start | bytes 331784 | tf_op jit(solution)/shard_map/ppermute | solution.py:36
  26.9 5.9 %collective-permute-done.9 = bf16[96,576]{1,0:T(8,128)(2,1)S(1)} collective-permute-done((bf16[96,576]{1,0:T(8,128)(2,1)S(1)}, bf16[96,576]{1,0:T(8,128)(2,1)S(1)}, u32[]{:S(2)}, u32[]{:S(2)}) %collective-permute-start.9) | collective-permute-done | bytes 110624 | tf_op jit(solution)/shard_map/ppermute | solution.py:36
  32.8 14.5 %collective-permute-done.8 = bf16[96,576]{1,0:T(8,128)(2,1)S(1)} collective-permute-done((bf16[96,576]{1,0:T(8,128)(2,1)S(1)}, bf16[96,576]{1,0:T(8,128)(2,1)S(1)}, u32[]{:S(2)}, u32[]{:S(2)}) %collective-permute-start.8) | collective-permute-done | bytes 110624 | tf_op jit(solution)/shard_map/ppermute | solution.py:36
  52.4 6.9 %shard_map.263 = (bf16[4,128,192]{2,1,0:T(8,128)(2,1)S(1)}, bf16[512,192]{1,0:T(8,128)(2,1)S(1)}, bf16[1024,192]{1,0:T(8,128)(2,1)S(1)}, bf16[1024,192]{1,0:T(8,...) custom-call(s32[2]{0:T(128)S(1)} %pad_add_fusion.place, ...), custom_call_target="tpu_custom_call" | custom-call | flops 905969664 | bytes 3145728 | tf_op jit(solution)/shard_map/pallas_call | solution.py:402
  70.1 2.9 %collective-permute-start.22 = (bf16[128,768]{1,0:T(8,128)(2,1)S(1)}, bf16[128,768]{1,0:T(8,128)(2,1)S(1)}, u32[]{:S(2)}, u32[]{:S(2)}) collective-permute-start(bf16[128,768]{1,0:T(8,128)(2,1)S(1)} %bitcast.181), channel_id=1, source_target_pairs={{0,24},{8,16},{16,8},{24,0},{1,25},{9,17},{17,9},{25,1},{2,26},{10... | collective-permute-start | bytes 589832 | tf_op jit(solution)/shard_map/ppermute | solution.py:36
  75.7 2.4 %collective-permute-start.19 = (bf16[128,768]{1,0:T(8,128)(2,1)S(1)}, bf16[128,768]{1,0:T(8,128)(2,1)S(1)}, u32[]{:S(2)}, u32[]{:S(2)}) collective-permute-start(bf16[128,768]{1,0:T(8,128)(2,1)S(1)} %add_convert_fusion.refs_0_), channel_id=1, source_target_pairs={{0,24},{8,16},{16,8},{24,0},{1,25},{9,17},{17,9},{25,1},{2,26},{10... | collective-permute-start | bytes 589832 | tf_op jit(solution)/shard_map/ppermute | solution.py:36
  79.0 3.4 %collective-permute-done.17.refs_1_ = bf16[128,768]{1,0:T(8,128)(2,1)S(1)} collective-permute-done((bf16[128,768]{1,0:T(8,128)(2,1)S(1)}, bf16[128,768]{1,0:T(8,128)(2,1)S(1)}, u32[]{:S(2)}, u32[]{:S(2)}) %collective-permute-start.17) | collective-permute-done | bytes 196640 | tf_op jit(solution)/shard_map/ppermute | solution.py:36
  83.1 2.7 %collective-permute-done.18.refs_2_ = bf16[128,768]{1,0:T(8,128)(2,1)S(1)} collective-permute-done((bf16[128,768]{1,0:T(8,128)(2,1)S(1)}, bf16[128,768]{1,0:T(8,128)(2,1)S(1)}, u32[]{:S(2)}, u32[]{:S(2)}) %collective-permute-start.18) | collective-permute-done | bytes 196640 | tf_op jit(solution)/shard_map/ppermute | solution.py:36
  92.9 5.1 %shard_map.265 = (bf16[512,768]{1,0:T(8,128)(2,1)S(1)}, bf16[512,768]{1,0:T(8,128)(2,1)S(1)}, bf16[4,128,768]{2,1,0:T(8,128)(2,1)S(1)}, bf16[4,128,768]{2,1,0:T(8,128)(2,1)S(1)}, f32[1,768]{1,0:T(1,128)S(1)}) custom-call(bf16[128,768]{1,0:T(8,128)(2,1)S(1)} %add_convert_fusion.refs_0_, bf16[128,768]{1,0:T(8,128)(2,1)S(1)} %copy-done.23, ...), custom_call_target="tpu_custom_call" | custom-call | flops 2415919104 | bytes 4718592 | tf_op jit(solution)/shard_map/pallas_call | solution.py:268
  110.1 2.7 %collective-permute-done.24 = bf16[128,768]{1,0:T(8,128)(2,1)} collective-permute-done((bf16[128,768]{1,0:T(8,128)(2,1)}, bf16[128,768]{1,0:T(8,128)(2,1)}, u32[]{:S(2)}, u32[]{:S(2)}) %collective-permute-start.24) | collective-permute-done | bytes 196640 | tf_op jit(solution)/shard_map/ppermute | solution.py:36
  112.7 2.8 %collective-permute-done.37 = bf16[128,768]{1,0:T(8,128)(2,1)} collective-permute-done((bf16[128,768]{1,0:T(8,128)(2,1)}, bf16[128,768]{1,0:T(8,128)(2,1)}, u32[]{:S(2)}, u32[]{:S(2)}) %collective-permute-start.37) | collective-permute-done | bytes 196640 | tf_op jit(solution)/shard_map/ppermute | solution.py:36
  117.3 3.1 %multiply_reduce_fusion = (bf16[768]{0:T(1024)(128)(2,1)}, f32[128]{0:T(128)S(1)}, f32[128]{0:T(128)S(1)}, bf16[768]{0:T(1024)(128)(2,1)}, f32[128,768]{1,0:T(8,128)S(1)}, /*index=5*/bf16[1,128,768]{2,1,0:T(8,128)(2,1)}) fusion(f32[128,768]{1,0:T(8,128)} %copy-done.41, f32[128]{0:T(128)} %copy-done.79, f32[128]{0:T(128)} %copy-done.69, f32[768]{0:T(1024)S(1)} %mul.138, ...), kind=kLoop, calls=%fused_computation.87 | loop fusion | flops 2554112 | bytes 2567168 | tf_op jit(solution)/shard_map/reduce_sum | solution.py:630
  124.9 3.1 %shard_map.269 = bf16[768,1536]{1,0:T(8,128)(2,1)} custom-call(bf16[128,768]{1,0:T(8,128)(2,1)S(1)} %add_convert_fusion.refs_0_, bf16[128,768]{1,0:T(8,128)(2,1)S(1)} %copy-done.24, bf16[128,768]{1,0:T(8,128)(2,1)S(1)} %copy-done.27, bf16[128,768]{1,0:T(8,128)(2,1)S(1)} %copy-done.30, bf16[128,768]{1,0:T(8,128)(2,1)S(1)} %bitcast.183, ...), custom_call_target="tpu_custom_call" | custom-call | flops 1207959552 | bytes 4718592 | tf_op jit(solution)/shard_map/pallas_call | solution.py:319
  145.5 6.9 %shard_map.266 = (bf16[512,192]{1,0:T(8,128)(2,1)S(1)}, bf16[2,512,384]{2,1,0:T(8,128)(2,1)S(1)}) custom-call(s32[2]{0:T(128)S(1)} %pad_add_fusion.place, bf16[128,192]{1,0:T(8,128)(2,1)S(1)} %get-tuple-element.46.refs_0_, bf16[128,192]{1,0:T(8,128)(2,1)S(1)} %collective-permute-done.26.refs_1_, bf16[128,192]{1,0:T(8,128)(2,1)S(1)} %collective-permute-done.27.refs_2_, ...), custom_call_target="tpu_custom_call" | custom-call | flops 1006632960 | bytes 1572864 | tf_op jit(solution)/shard_map/pallas_call | solution.py:464
  168.3 3.9 %collective-permute-done.40 = bf16[128,768]{1,0:T(8,128)(2,1)S(1)} collective-permute-done((bf16[128,768]{1,0:T(8,128)(2,1)S(1)}, bf16[128,768]{1,0:T(8,128)(2,1)S(1)}, u32[]{:S(2)}, u32[]{:S(2)}) %collective-permute-start.40) | collective-permute-done | bytes 196640 | tf_op jit(solution)/shard_map/ppermute | solution.py:36
  172.1 3.9 %collective-permute-done.39 = bf16[128,768]{1,0:T(8,128)(2,1)} collective-permute-done((bf16[128,768]{1,0:T(8,128)(2,1)S(1)}, bf16[128,768]{1,0:T(8,128)(2,1)}, u32[]{:S(2)}, u32[]{:S(2)}) %collective-permute-start.39) | collective-permute-done | bytes 196640 | tf_op jit(solution)/shard_map/ppermute | solution.py:36
  183.2 4.8 %collective-permute-done.43 = bf16[130,576]{1,0:T(8,128)(2,1)S(1)} collective-permute-done((bf16[130,576]{1,0:T(8,128)(2,1)S(1)}, bf16[130,576]{1,0:T(8,128)(2,1)S(1)}, u32[]{:S(2)}, u32[]{:S(2)}) %collective-permute-start.43) | collective-permute-done | bytes 149792 | tf_op jit(solution)/shard_map/ppermute | solution.py:36
  188.0 6.6 %collective-permute-done.42 = bf16[130,576]{1,0:T(8,128)(2,1)S(1)} collective-permute-done((bf16[130,576]{1,0:T(8,128)(2,1)S(1)}, bf16[130,576]{1,0:T(8,128)(2,1)S(1)}, u32[]{:S(2)}, u32[]{:S(2)}) %collective-permute-start.42) | collective-permute-done | bytes 149792 | tf_op jit(solution)/shard_map/ppermute | solution.py:36
  204.1 2.6 %collective-permute-done.45 = bf16[130,576]{1,0:T(8,128)(2,1)S(1)} collective-permute-done((bf16[130,576]{1,0:T(8,128)(2,1)S(1)}, bf16[130,576]{1,0:T(8,128)(2,1)S(1)}, u32[]{:S(2)}, u32[]{:S(2)}) %collective-permute-start.45) | collective-permute-done | bytes 149792 | tf_op jit(solution)/shard_map/ppermute | solution.py:36
  207.5 5.5 %collective-permute-done.50 = bf16[96,1536]{1,0:T(8,128)(2,1)S(1)} collective-permute-done((bf16[96,1536]{1,0:T(8,128)(2,1)}, bf16[96,1536]{1,0:T(8,128)(2,1)S(1)}, u32[]{:S(2)}, u32[]{:S(2)}) %collective-permute-start.50) | collective-permute-done | bytes 294944 | tf_op jit(solution)/shard_map/ppermute | solution.py:36
  213.1 5.4 %collective-permute-done.49 = bf16[96,1536]{1,0:T(8,128)(2,1)S(1)} collective-permute-done((bf16[96,1536]{1,0:T(8,128)(2,1)}, bf16[96,1536]{1,0:T(8,128)(2,1)S(1)}, u32[]{:S(2)}, u32[]{:S(2)}) %collective-permute-start.49) | collective-permute-done | bytes 294944 | tf_op jit(solution)/shard_map/ppermute | solution.py:36
  222.5 2.6 %shard_map.268 = f32[192,2304]{1,0:T(8,128)} custom-call(bf16[4,192,576]{2,1,0:T(8,128)(2,1)S(1)} %bitcast.173), custom_call_target="tpu_custom_call" | custom-call | tf_op jit(solution)/shard_map/pallas_call | solution.py:169
  230.8 3.4 %shard_map.270 = (f32[192,3072]{1,0:T(8,128)}, f32[4,192,768]{2,1,0:T(8,128)}) custom-call(bf16[4,192,1536]{2,1,0:T(8,128)(2,1)S(1)} %bitcast.168), custom_call_target="tpu_custom_call" | custom-call | tf_op jit(solution)/shard_map/pallas_call | solution.py:194
  (407 shorter events, 116.0 us)
Async XLA Ops:
  7.2 61.2 %all-gather.2.cloned.1.call-start = ((), (), s32[]{:S(2)}) async-start(), calls=%async_computation.1 | async-start | bytes 3981312 | tf_op jit(solution)/shard_map/all_gather | solution.py:593
  12.4 185.9 %reduce-scatter.2.cloned.1.call-start = ((), (), s32[]{:S(2)}) async-start(), calls=%async_computation.2 | async-start | bytes 2654208 | tf_op jit(solution)/shard_map/reduce_scatter | solution.py:622
  18.3 32.1 %collective-permute-start = (bf16[128,768]{1,0:T(8,128)(2,1)S(1)}, bf16[128,768]{1,0:T(8,128)(2,1)S(1)}, u32[]{:S(2)}, u32[]{:S(2)}) collective-permute-start(bf16[128,768]{1,0:T(8,128)(2,1)S(1)} %bitcast.174), channel_id=1, source_target_pairs={{0,8},{8,0},{16,24},{24,16},{1,9},{9,1},{17,25},{25,17},{2,10},{10... | collective-permute-start | bytes 589832 | tf_op jit(solution)/shard_map/ppermute | solution.py:36
  19.9 30.5 %collective-permute-start.1 = (bf16[128,768]{1,0:T(8,128)(2,1)S(1)}, bf16[128,768]{1,0:T(8,128)(2,1)S(1)}, u32[]{:S(2)}, u32[]{:S(2)}) collective-permute-start(bf16[128,768]{1,0:T(8,128)(2,1)S(1)} %bitcast.175), channel_id=1, source_target_pairs={{0,16},{8,24},{16,0},{24,8},{1,17},{9,25},{17,1},{25,9},{2,18},{10... | collective-permute-start | bytes 589832 | tf_op jit(solution)/shard_map/ppermute | solution.py:36
  22.2 10.6 %collective-permute-start.9 = (bf16[96,576]{1,0:T(8,128)(2,1)S(1)}, bf16[96,576]{1,0:T(8,128)(2,1)S(1)}, u32[]{:S(2)}, u32[]{:S(2)}) collective-permute-start(bf16[96,576]{1,0:T(8,128)(2,1)S(1)} %shard_map.262), channel_id=1, source_target_pairs={{0,3},{1,2},{2,1},{3,0},{4,7},{5,6},{6,5},{7,4},{8,11},{9,10},{10,... | collective-permute-start | bytes 331784 | tf_op jit(solution)/shard_map/ppermute | solution.py:36
  25.8 21.4 %collective-permute-start.8 = (bf16[96,576]{1,0:T(8,128)(2,1)S(1)}, bf16[96,576]{1,0:T(8,128)(2,1)S(1)}, u32[]{:S(2)}, u32[]{:S(2)}) collective-permute-start(bf16[96,576]{1,0:T(8,128)(2,1)S(1)} %shard_map.262), channel_id=1, source_target_pairs={{0,2},{1,3},{2,0},{3,1},{4,6},{5,7},{6,4},{7,5},{8,10},{9,11},{10,... | collective-permute-start | bytes 331784 | tf_op jit(solution)/shard_map/ppermute | solution.py:36
  25.9 21.3 %collective-permute-start.7 = (bf16[96,576]{1,0:T(8,128)(2,1)S(1)}, bf16[96,576]{1,0:T(8,128)(2,1)S(1)}, u32[]{:S(2)}, u32[]{:S(2)}) collective-permute-start(bf16[96,576]{1,0:T(8,128)(2,1)S(1)} %shard_map.262), channel_id=1, source_target_pairs={{0,1},{1,0},{2,3},{3,2},{4,5},{5,4},{6,7},{7,6},{8,9},{9,8},{10,11... | collective-permute-start | bytes 331784 | tf_op jit(solution)/shard_map/ppermute | solution.py:36
  32.8 16.9 %collective-permute-start.2 = (bf16[128,768]{1,0:T(8,128)(2,1)S(1)}, bf16[128,768]{1,0:T(8,128)(2,1)S(1)}, u32[]{:S(2)}, u32[]{:S(2)}) collective-permute-start(bf16[128,768]{1,0:T(8,128)(2,1)S(1)} %bitcast.176), channel_id=1, source_target_pairs={{0,24},{8,16},{16,8},{24,0},{1,25},{9,17},{17,9},{25,1},{2,26},{10... | collective-permute-start | bytes 589832 | tf_op jit(solution)/shard_map/ppermute | solution.py:36
  49.7 26.0 %collective-permute-start.20 = (bf16[128,768]{1,0:T(8,128)(2,1)S(1)}, bf16[128,768]{1,0:T(8,128)(2,1)S(1)}, u32[]{:S(2)}, u32[]{:S(2)}) collective-permute-start(bf16[128,768]{1,0:T(8,128)(2,1)S(1)} %bitcast.179), channel_id=1, source_target_pairs={{0,8},{8,0},{16,24},{24,16},{1,9},{9,1},{17,25},{25,17},{2,10},{10... | collective-permute-start | bytes 589832 | tf_op jit(solution)/shard_map/ppermute | solution.py:36
  51.7 26.6 %collective-permute-start.21 = (bf16[128,768]{1,0:T(8,128)(2,1)S(1)}, bf16[128,768]{1,0:T(8,128)(2,1)S(1)}, u32[]{:S(2)}, u32[]{:S(2)}) collective-permute-start(bf16[128,768]{1,0:T(8,128)(2,1)S(1)} %bitcast.180), channel_id=1, source_target_pairs={{0,16},{8,24},{16,0},{24,8},{1,17},{9,25},{17,1},{25,9},{2,18},{10... | collective-permute-start | bytes 589832 | tf_op jit(solution)/shard_map/ppermute | solution.py:36
  74.6 11.2 %collective-permute-start.18 = (bf16[128,768]{1,0:T(8,128)(2,1)S(1)}, bf16[128,768]{1,0:T(8,128)(2,1)S(1)}, u32[]{:S(2)}, u32[]{:S(2)}) collective-permute-start(bf16[128,768]{1,0:T(8,128)(2,1)S(1)} %add_convert_fusion.refs_0_), channel_id=1, source_target_pairs={{0,16},{8,24},{16,0},{24,8},{1,17},{9,25},{17,1},{25,9},{2,18},{10... | collective-permute-start | bytes 589832 | tf_op jit(solution)/shard_map/ppermute | solution.py:36
  75.7 10.8 %collective-permute-start.19 = (bf16[128,768]{1,0:T(8,128)(2,1)S(1)}, bf16[128,768]{1,0:T(8,128)(2,1)S(1)}, u32[]{:S(2)}, u32[]{:S(2)}) collective-permute-start(bf16[128,768]{1,0:T(8,128)(2,1)S(1)} %add_convert_fusion.refs_0_), channel_id=1, source_target_pairs={{0,24},{8,16},{16,8},{24,0},{1,25},{9,17},{17,9},{25,1},{2,26},{10... | collective-permute-start | bytes 589832 | tf_op jit(solution)/shard_map/ppermute | solution.py:36
  100.3 12.4 %collective-permute-start.24 = (bf16[128,768]{1,0:T(8,128)(2,1)}, bf16[128,768]{1,0:T(8,128)(2,1)}, u32[]{:S(2)}, u32[]{:S(2)}) collective-permute-start(bf16[128,768]{1,0:T(8,128)(2,1)} %get-tuple-element.114), channel_id=1, source_target_pairs={{0,16},{8,24},{16,0},{24,8},{1,17},{9,25},{17,1},{25,9},{2,18},{10... | collective-permute-start | bytes 589832 | tf_op jit(solution)/shard_map/ppermute | solution.py:36
  101.8 10.9 %collective-permute-start.23 = (bf16[128,768]{1,0:T(8,128)(2,1)}, bf16[128,768]{1,0:T(8,128)(2,1)}, u32[]{:S(2)}, u32[]{:S(2)}) collective-permute-start(bf16[128,768]{1,0:T(8,128)(2,1)} %get-tuple-element.112), channel_id=1, source_target_pairs={{0,8},{8,0},{16,24},{24,16},{1,9},{9,1},{17,25},{25,17},{2,10},{10... | collective-permute-start | bytes 589832 | tf_op jit(solution)/shard_map/ppermute | solution.py:36
  103.2 12.4 %collective-permute-start.37 = (bf16[128,768]{1,0:T(8,128)(2,1)}, bf16[128,768]{1,0:T(8,128)(2,1)}, u32[]{:S(2)}, u32[]{:S(2)}) collective-permute-start(bf16[128,768]{1,0:T(8,128)(2,1)} %get-tuple-element.116), channel_id=1, source_target_pairs={{0,24},{8,16},{16,8},{24,0},{1,25},{9,17},{17,9},{25,1},{2,26},{10... | collective-permute-start | bytes 589832 | tf_op jit(solution)/shard_map/ppermute | solution.py:36
  104.6 12.7 %collective-permute-start.36 = (bf16[128,768]{1,0:T(8,128)(2,1)}, bf16[128,768]{1,0:T(8,128)(2,1)}, u32[]{:S(2)}, u32[]{:S(2)}) collective-permute-start(bf16[128,768]{1,0:T(8,128)(2,1)} %get-tuple-element.117), channel_id=1, source_target_pairs={{0,16},{8,24},{16,0},{24,8},{1,17},{9,25},{17,1},{25,9},{2,18},{10... | collective-permute-start | bytes 589832 | tf_op jit(solution)/shard_map/ppermute | solution.py:36
  165.4 10.6 %collective-permute-start.39 = (bf16[128,768]{1,0:T(8,128)(2,1)S(1)}, bf16[128,768]{1,0:T(8,128)(2,1)}, u32[]{:S(2)}, u32[]{:S(2)}) collective-permute-start(bf16[128,768]{1,0:T(8,128)(2,1)S(1)} %get-tuple-element.109), channel_id=1, source_target_pairs={{0,16},{8,24},{16,0},{24,8},{1,17},{9,25},{17,1},{25,9},{2,18},{10... | collective-permute-start | bytes 589832 | tf_op jit(solution)/shard_map/ppermute | solution.py:36
  180.9 13.7 %collective-permute-start.42 = (bf16[130,576]{1,0:T(8,128)(2,1)S(1)}, bf16[130,576]{1,0:T(8,128)(2,1)S(1)}, u32[]{:S(2)}, u32[]{:S(2)}) collective-permute-start(bf16[130,576]{1,0:T(8,128)(2,1)S(1)} %get-tuple-element.125), channel_id=1, source_target_pairs={{0,2},{1,3},{2,0},{3,1},{4,6},{5,7},{6,4},{7,5},{8,10},{9,11},{10,... | collective-permute-start | bytes 449288 | tf_op jit(solution)/shard_map/ppermute | solution.py:36
  180.9 13.7 %collective-permute-start.41 = (bf16[130,576]{1,0:T(8,128)(2,1)S(1)}, bf16[130,576]{1,0:T(8,128)(2,1)S(1)}, u32[]{:S(2)}, u32[]{:S(2)}) collective-permute-start(bf16[130,576]{1,0:T(8,128)(2,1)S(1)} %get-tuple-element.124), channel_id=1, source_target_pairs={{0,1},{1,0},{2,3},{3,2},{4,5},{5,4},{6,7},{7,6},{8,9},{9,8},{10,11... | collective-permute-start | bytes 449288 | tf_op jit(solution)/shard_map/ppermute | solution.py:36
  196.2 10.6 %collective-permute-start.45 = (bf16[130,576]{1,0:T(8,128)(2,1)S(1)}, bf16[130,576]{1,0:T(8,128)(2,1)S(1)}, u32[]{:S(2)}, u32[]{:S(2)}) collective-permute-start(bf16[130,576]{1,0:T(8,128)(2,1)S(1)} %fusion.37), channel_id=1, source_target_pairs={{0,16},{8,24},{16,0},{24,8},{1,17},{9,25},{17,1},{25,9},{2,18},{10... | collective-permute-start | bytes 449288 | tf_op jit(solution)/shard_map/ppermute | solution.py:36
  198.3 14.8 %collective-permute-start.50 = (bf16[96,1536]{1,0:T(8,128)(2,1)}, bf16[96,1536]{1,0:T(8,128)(2,1)S(1)}, u32[]{:S(2)}, u32[]{:S(2)}) collective-permute-start(bf16[96,1536]{1,0:T(8,128)(2,1)} %reduce-scatter.2.cloned.1.call-done), channel_id=1, source_target_pairs={{0,24},{8,16},{16,8},{24,0},{1,25},{9,17},{17,9},{25,1},{2,26},{10... | collective-permute-start | bytes 884744 | tf_op jit(solution)/shard_map/ppermute | solution.py:36
  199.6 18.8 %collective-permute-start.49 = (bf16[96,1536]{1,0:T(8,128)(2,1)}, bf16[96,1536]{1,0:T(8,128)(2,1)S(1)}, u32[]{:S(2)}, u32[]{:S(2)}) collective-permute-start(bf16[96,1536]{1,0:T(8,128)(2,1)} %reduce-scatter.2.cloned.1.call-done), channel_id=1, source_target_pairs={{0,16},{8,24},{16,0},{24,8},{1,17},{9,25},{17,1},{25,9},{2,18},{10... | collective-permute-start | bytes 884744 | tf_op jit(solution)/shard_map/ppermute | solution.py:36
  203.0 15.5 %collective-permute-start.48 = (bf16[96,1536]{1,0:T(8,128)(2,1)}, bf16[96,1536]{1,0:T(8,128)(2,1)S(1)}, u32[]{:S(2)}, u32[]{:S(2)}) collective-permute-start(bf16[96,1536]{1,0:T(8,128)(2,1)} %reduce-scatter.2.cloned.1.call-done), channel_id=1, source_target_pairs={{0,8},{8,0},{16,24},{24,16},{1,9},{9,1},{17,25},{25,17},{2,10},{10... | collective-permute-start | bytes 884744 | tf_op jit(solution)/shard_map/ppermute | solution.py:36
  207.5 13.4 %collective-permute-start.47 = (bf16[4,130,576]{2,0,1:T(4,128)(2,1)S(1)}, bf16[4,130,576]{2,0,1:T(4,128)(2,1)S(1)}, u32[]{:S(2)}, u32[]{:S(2)}) collective-permute-start(bf16[4,130,576]{2,0,1:T(4,128)(2,1)S(1)} %copy.111), channel_id=1, source_target_pairs={{0,4},{4,0},{1,5},{5,1},{2,6},{6,2},{3,7},{7,3},{8,12},{12,8},{9,1... | collective-permute-start | bytes 1797128 | tf_op jit(solution)/shard_map/ppermute | solution.py:36
  (127 other events, 510.0 us)
Sparse Core Ops, SparseCore 0:
  12.5 52.4 all-gather.1
  128.2 35.1 reduce-scatter.1

commit v3 on v2

--- a/solution.py
+++ b/solution.py
@@ -17,6 +17,10 @@
 
 BF = jnp.bfloat16
 F32 = jnp.float32
+
+
+def in_hbm(*values):
+    return [pltpu.with_memory_space_constraint(v, pltpu.HBM) for v in values]
 
 
 def mm(left, right):
@@ -285,7 +289,7 @@
             jax.ShapeDtypeStruct((rows, hidden), BF),
             jax.ShapeDtypeStruct((rows, hidden), BF),
             jax.ShapeDtypeStruct((GROUPS, tok, width), BF),
-            jax.ShapeDtypeStruct((GROUPS, tok, width), BF),
+            pltpu.HBM((GROUPS, tok, width), BF),
             jax.ShapeDtypeStruct((1, hidden), F32),
         ],
         scratch_shapes=[pltpu.VMEM((rows, width), BF)] * 2 + [pltpu.VMEM((rows, width), F32)] * 2,
@@ -293,7 +297,7 @@
         cost_estimate=pl.CostEstimate(
             flops=8 * rows * width * hidden, bytes_accessed=12 * rows * width, transcendentals=0
         ),
-    )(*h_rows, *s_rows, weights, weights, bias)
+    )(*h_rows, *in_hbm(*s_rows, weights, weights), bias)
 
 
 def hidden_grad_kernel(*refs):
@@ -329,7 +333,7 @@
         cost_estimate=pl.CostEstimate(
             flops=4 * rows * width * hidden, bytes_accessed=12 * rows * width, transcendentals=0
         ),
-    )(*h_rows, *s_rows, slope_inner, act)
+    )(*h_rows, *in_hbm(*s_rows), slope_inner, act)
 
 
 def visible(k, tok, keys):
@@ -407,7 +411,7 @@
             out_specs=[vmem] * len(shapes),
             scratch_shapes=[pltpu.VMEM((rows, width), BF)],
         ),
-        out_shape=[jax.ShapeDtypeStruct(s, t) for s, t in shapes],
+        out_shape=[jax.ShapeDtypeStruct(*shapes[0])] + [pltpu.HBM(s, t) for s, t in shapes[1:]],
         compiler_params=pltpu.CompilerParams(vmem_limit_bytes=(16 if ks == 2 else 48) * 2**20),
         cost_estimate=pl.CostEstimate(
             flops=6 * rows * width * cols, bytes_accessed=4 * rows * width, transcendentals=0
@@ -477,7 +481,7 @@
         cost_estimate=pl.CostEstimate(
             flops=10 * mine * rows * cols, bytes_accessed=8 * rows * cols, transcendentals=0
         ),
-    )(jnp.stack([g, k]).astype(jnp.int32), *slopes, q, keys, values, att, lse)
+    )(jnp.stack([g, k]).astype(jnp.int32), *slopes, *in_hbm(q, keys, values, att, lse))
 
 
 def project_back_kernel(ks, place, *refs):
@@ -518,7 +522,7 @@
         cost_estimate=pl.CostEstimate(
             flops=12 * mine * width * cols, bytes_accessed=4 * mine * width, transcendentals=0
         ),
-    )(jnp.stack([g, k]).astype(jnp.int32), dq, *dkv, h, hat, in_w)
+    )(jnp.stack([g, k]).astype(jnp.int32), dq, *dkv, *in_hbm(h, hat), in_w)
 
 
 def shards(
@@ -586,16 +590,19 @@
     q_bias = pick(q_bias.reshape(GROUPS, cols), g)
     v_bias = pick(v_bias.reshape(GROUPS, cols), g)
 
+    rest = cut_rest(contract_weight, expand_weight, output_weight, zs, g, k, ks)
+    rest, in_pieces = lax.optimization_barrier((rest, in_pieces))
+
     in_half = in_order(in_pieces, z)
     in_w = jnp.stack(in_order(gather_flips(in_half, "core"), k), axis=1).reshape(width, 3 * cols)
 
-    rest = cut_rest(contract_weight, expand_weight, output_weight, zs, g, k, ks)
-    rest = lax.all_gather(rest, ("fsdp", "core"), axis=0, tiled=True)
-    out_w = rest[:, width + zs * ff_g :].reshape(GROUPS, cols, width)
-    out_w = jnp.concatenate([pick(out_w, g ^ i) for i in range(GROUPS)])
-    slope_late, _ = lax.optimization_barrier((slope_own, x_rows[-1]))
+    split = width + zs * ff_g
+    out_pieces = gather_flips(rest[:, split:], "fsdp")
+    rest_pieces = gather_flips(rest[:, :split], "fsdp")
+    slope_late, x_rows = lax.optimization_barrier((slope_own, x_rows))
     slope_rows = gather_flips(slope_late, "grp")
 
+    in_w, slope_rows = lax.optimization_barrier((in_w, slope_rows))
     slots, qs, keys, values, att_full, lse, h1, hat_one = attend(
         g,
         k,
@@ -608,23 +615,31 @@
         q_bias[None],
         v_bias[None],
     )
+    out_pieces, lse = lax.optimization_barrier((out_pieces, lse))
+
+    def whole(pieces):
+        half = in_order(pieces, z)
+        return jnp.stack(in_order(gather_flips(half, "core"), k), axis=1).reshape(width, -1)
+
+    out_w = whole(out_pieces).reshape(GROUPS, cols, width)
+    out_w = jnp.concatenate([pick(out_w, g ^ i) for i in range(GROUPS)])
     att = jnp.concatenate(swap_flips([slots[i] for i in range(GROUPS)], "grp"), axis=1)
     x_f = x_own.astype(F32)
     middle = x_f + mm(att, out_w) + o_bias
     hat_two, rate_two = norm_stats(middle)
     h2 = (hat_two * gain_two + shift_two).astype(BF)
     h2_rows = gather_flips(h2, "grp")
+    middle, rest_pieces = lax.optimization_barrier((middle, rest_pieces))
+    rest = whole(rest_pieces)
 
     act, slope_inner, sh2_part, out_part, d_exp_b = hidden_part(
         h2_rows, slope_rows, rest, e_bias[None]
     )
-    sh2 = total(swap_flips([sh2_part[i] for i in range(GROUPS)], "grp"))
-    d_hidden = lax.psum_scatter(
-        hidden_grads(h2_rows, slope_rows, slope_inner, act),
-        ("fsdp", "core"),
-        scatter_dimension=0,
-        tiled=True,
-    )
+    sh2 = swap_flips([sh2_part[i] for i in range(GROUPS)], "grp")
+    d_hidden = hidden_grads(h2_rows, slope_rows, slope_inner, act)
+    sh2, d_hidden = lax.optimization_barrier((sh2, d_hidden))
+    sh2 = total(sh2)
+    d_hidden = lax.psum_scatter(d_hidden, ("fsdp", "core"), scatter_dimension=0, tiled=True)
 
     slope_f = slope_own.astype(F32)
     d_gain_two = jnp.sum(sh2 * hat_two, axis=0)
@@ -634,24 +649,14 @@
     slope_att = mm_rt(slope_branch, out_w).astype(BF)
     datt = swap_flips([slope_att[:, i * cols : (i + 1) * cols] for i in range(GROUPS)], "grp")
 
-    d_out = mm_lt(att, slope_branch).astype(BF).reshape(GROUPS, cols, width)
+    datt, slope_late = lax.optimization_barrier((datt, slope_branch))
+    d_out = mm_lt(att, slope_late).astype(BF).reshape(GROUPS, cols, width)
     d_out = in_order([d_out[i] for i in range(GROUPS)], g)
-    d_out = d_out.reshape(zs, GROUPS, ks, rows_z // GROUPS // ks, width)
-    pieces = [lax.dynamic_index_in_dim(d_out, k ^ j, axis=2, keepdims=False) for j in range(ks)]
-    d_out = total(swap_flips(pieces, "core")).astype(BF)
+    d_out = d_out.reshape(zs, GROUPS, rows_z // GROUPS, width)
     pieces = [lax.dynamic_index_in_dim(d_out, g ^ i, axis=1, keepdims=False) for i in range(GROUPS)]
-    d_out = total(swap_flips(pieces, "grp")).astype(BF)
-    third = d_out.shape[1] // 3
-    tail = d_out[:, :, 3 * cols :]
-    d_out = jnp.concatenate(
-        [
-            d_out[:, :, : 3 * cols],
-            jnp.concatenate([tail[:, i * third : (i + 1) * third] for i in range(3)], axis=2),
-        ],
-        axis=1,
-    )
-
-    datt, d_out = lax.optimization_barrier((datt, d_out))
+    datt, pieces = lax.optimization_barrier((datt, pieces))
+    d_out = swap_flips(pieces, "grp")
+
     dq, dkv = attend_back(g, k, ks, head, datt, qs, keys, values, att_full, lse)
     dkv = swap_flips([dkv[j] for j in range(ks)], "core")
     sh1_part, d_in, sums = project_back(g, k, dq, dkv, h1, hat_one, in_w)
@@ -679,15 +684,20 @@
         + [at_group(d_exp_b, zs).reshape(zs, ff_z)],
         axis=1,
     )
+    d_out = total(d_out).astype(BF).reshape(zs, ks, -1, width)
+    third = d_out.shape[2] // 3
+    tail = d_out[..., 3 * cols :]
+    tail = [tail[:, :, i * third : (i + 1) * third] for i in range(3)]
+    d_out = jnp.concatenate([d_out[..., : 3 * cols], jnp.concatenate(tail, axis=3)], axis=2)
     count = packed.shape[1]
     extra = -(-count // (3 * cols * ks))
     packed = jnp.pad(packed, ((0, 0), (0, extra * ks * 3 * cols - count)))
     d_in = d_in.reshape(zs, ks, rows_z // ks, 3 * cols)
-    d_in = jnp.concatenate([d_in, packed.astype(BF).reshape(zs, ks, extra, 3 * cols)], axis=2)
+    packed = packed.astype(BF).reshape(zs, ks, extra, 3 * cols)
+    d_in = jnp.concatenate([d_in, packed, d_out], axis=2)
     pieces = [lax.dynamic_index_in_dim(d_in, k ^ j, axis=1, keepdims=False) for j in range(ks)]
     d_in = total(swap_flips(pieces, "core")).astype(BF)
-    d_in = jnp.concatenate([d_in, d_out], axis=1)
-    out_late, _ = lax.optimization_barrier((out_part, d_in))
+    out_late, d_in = lax.optimization_barrier((out_part, d_in))
     out_sum = total(swap_flips([out_late[i] for i in range(GROUPS)], "grp"))
     outputs = (middle + out_sum + c_bias).astype(BF)[None]
     d_in = total(swap_flips([pick(d_in, z ^ i) for i in range(zs)], "fsdp")).astype(BF)

time: 242 us -> 247 us (1.021)
  local copies, waits for them, and re-layouts: 41.1 us -> 29.1 us
  starting transfers between devices: 57.6 us -> 69.3 us
  Pallas kernels: 32.1 us -> 38.8 us
  waiting for transfers between devices: 74.6 us -> 69.5 us
  other arithmetic: 17.7 us -> 22.6 us
    unnamed x186 -> x98, local copies, waits for them, and re-layouts: 26.5 us -> 5.56 us
    ppermute x52 -> x59, starting transfers between devices: 57.5 us -> 69.3 us  [send(): return lax.ppermute(value, axis, [(s, s ^ flip) for s in range(count)])]
    concatenate x1, local copies, waits for them, and re-layouts: 0.09 us -> 6.1 us  [shards(): jnp.concatenate([first_gain, first_shift, query_bias, value_bias, output_...]
    ppermute x52 -> x59, waiting for transfers between devices: 74.5 us -> 69.5 us  [send(): return lax.ppermute(value, axis, [(s, s ^ flip) for s in range(count)])]
    another operation x8 -> x12, other arithmetic: 3.82 us -> 8.82 us  [in_order(): stacked = jnp.stack(pieces)]
    mul x5, local copies, waits for them, and re-layouts: 0.32 us -> 4.77 us  [at_group(): return (parts * spot).reshape(-1)]
    another operation x4 -> x6, other arithmetic: 1.63 us -> 4.53 us  [in_order(): return jnp.stack([pick(stacked, me ^ j) for j in range(len(pieces))])]
  transfers between devices with their start and end apart: 54 -> 60, of which waited for: 23 -> 20; matrix products, arithmetic and copies ran while one was open for 10% -> 13% of each run, Pallas kernels for 9% -> 12%
where the time goes in v3:
time: 247 us; the launch traced here: 246 us
  waiting for transfers between devices  69.5 us (28%)
  starting transfers between devices  69.3 us (28%)
  Pallas kernels  38.8 us (16%)
  local copies, waits for them, and re-layouts  29.1 us (12%)
  other arithmetic  22.6 us (9%)
  between operations  15.1 us (6%)
    ppermute x59, waiting for transfers between devices, send(): return lax.ppermute(value, axis, [(s, s ^ flip) for s in range(count)])  69.5 us
    ppermute x59, starting transfers between devices, send(): return lax.ppermute(value, axis, [(s, s ^ flip) for s in range(count)])  69.3 us
    another operation x12, other arithmetic, in_order(): stacked = jnp.stack(pieces)  8.82 us
    pallas_call x1, Pallas kernels, attend_back(): pl.pallas_call(functools.partial(attend_back_kernel, ks, head), grid_spec...  8.5 us
    pallas_call x1, Pallas kernels, attend(): pl.pallas_call(functools.partial(attend_kernel, ks, head), grid_spec=pltp...  8.04 us
    pallas_call x1, Pallas kernels, hidden_part(): pl.pallas_call(hidden_kernel, grid=(hidden // step,), in_specs=[pl.BlockS...  7.12 us
    concatenate x1, local copies, waits for them, and re-layouts, shards(): jnp.concatenate([first_gain, first_shift, query_bias, value_bias, output_...  6.1 us
    unnamed x98, local copies, waits for them, and re-layouts  5.56 us
  transfers between devices with their start and end apart: 60, of which 20 were waited for; matrix products, arithmetic and copies ran while one was open for 13% of the time, Pallas kernels for 12%

profile of v3, /device:TPU:0, one launch (start us, length us, event | category | flops | bytes accessed | tf_op | source)
XLA Modules:
  0.0 245.9 jit_solution(10117126762703613605)
XLA Ops:
  7.2 6.1 %concatenate.25 = bf16[2304]{0:T(1024)(128)(2,1)S(1)} concatenate(bf16[192]{0:T(256)(128)(2,1)} %param.17, bf16[192]{0:T(256)(128)(2,1)} %param.18, bf16[192]{0:T(256)(128)(2,1)} %param.20, bf16[192]{0:T(256)(128)(2,1)} %param.21, bf16[192]{0:T(256)(128)(2,1)} %param.23, bf16[192]{0:T(256)(128)(2,1)} %param.24, bf16[192]{0:T(256)(128)(2,1)} %param.25, bf16[192]{0:T(256)(128)(2,1)} %param.29, ...), dimensions={0} | concatenate | bytes 9216 | tf_op jit(solution)/shard_map/concatenate | solution.py:566
  13.3 5.1 %collective-permute-start.16 = (bf16[2304]{0:T(1024)(128)(2,1)S(1)}, bf16[2304]{0:T(1024)(128)(2,1)S(1)}, u32[]{:S(2)}, u32[]{:S(2)}) collective-permute-start(bf16[2304]{0:T(1024)(128)(2,1)S(1)} %concatenate.25), channel_id=1, source_target_pairs={{0,3},{1,2},{2,1},{3,0},{4,7},{5,6},{6,5},{7,4},{8,11},{9,10},{10,... | collective-permute-start | bytes 13832 | tf_op jit(solution)/shard_map/ppermute | solution.py:40
  22.4 2.9 %collective-permute-start.8 = (bf16[96,576]{1,0:T(8,128)(2,1)S(1)}, bf16[96,576]{1,0:T(8,128)(2,1)S(1)}, u32[]{:S(2)}, u32[]{:S(2)}) collective-permute-start(bf16[96,576]{1,0:T(8,128)(2,1)S(1)} %shard_map.263), channel_id=1, source_target_pairs={{0,2},{1,3},{2,0},{3,1},{4,6},{5,7},{6,4},{7,5},{8,10},{9,11},{10,... | collective-permute-start | bytes 331784 | tf_op jit(solution)/shard_map/ppermute | solution.py:40
  32.5 2.8 %collective-permute-done.9 = bf16[96,576]{1,0:T(8,128)(2,1)S(1)} collective-permute-done((bf16[96,576]{1,0:T(8,128)(2,1)S(1)}, bf16[96,576]{1,0:T(8,128)(2,1)S(1)}, u32[]{:S(2)}, u32[]{:S(2)}) %collective-permute-start.9) | collective-permute-done | bytes 110624 | tf_op jit(solution)/shard_map/ppermute | solution.py:40
  48.2 2.4 collective-permute-done.12.refs_6_
  54.2 8.0 %shard_map.264 = (bf16[4,128,192]{2,1,0:T(8,128)(2,1)S(1)}, bf16[512,192]{1,0:T(8,128)(2,1)}, bf16[1024,192]{1,0:T(8,128)(2,1)}, bf16[1024,192]{1,0:T(8,128)(2,1...) custom-call(s32[2]{0:T(128)S(1)} %pad_add_fusion.place, ...), custom_call_target="tpu_custom_call" | custom-call | flops 905969664 | bytes 3145728 | tf_op jit(solution)/shard_map/pallas_call | solution.py:406
  75.1 2.8 %collective-permute-done.17 = bf16[128,192]{1,0:T(8,128)(2,1)S(1)} collective-permute-done((bf16[128,192]{1,0:T(8,128)(2,1)S(1)}, bf16[128,192]{1,0:T(8,128)(2,1)S(1)}, u32[]{:S(2)}, u32[]{:S(2)}) %collective-permute-start.17) | collective-permute-done | bytes 49184 | tf_op jit(solution)/shard_map/ppermute | solution.py:40
  79.4 9.8 %collective-permute-done.25 = bf16[96,1536]{1,0:T(8,128)(2,1)S(1)} collective-permute-done((bf16[96,1536]{1,0:T(8,128)(2,1)S(1)}, bf16[96,1536]{1,0:T(8,128)(2,1)S(1)}, u32[]{:S(2)}, u32[]{:S(2)}) %collective-permute-start.25) | collective-permute-done | bytes 294944 | tf_op jit(solution)/shard_map/ppermute | solution.py:40
  96.4 2.3 fusion.5
  100.7 4.3 %collective-permute-done.29.refs_3_ = bf16[128,768]{1,0:T(8,128)(2,1)S(1)} collective-permute-done((bf16[128,768]{1,0:T(8,128)(2,1)S(1)}, bf16[128,768]{1,0:T(8,128)(2,1)S(1)}, u32[]{:S(2)}, u32[]{:S(2)}) %collective-permute-start.29) | collective-permute-done | bytes 196640 | tf_op jit(solution)/shard_map/ppermute | solution.py:40
  105.0 7.1 %shard_map.265 = (bf16[512,768]{1,0:T(8,128)(2,1)S(1)}, bf16[512,768]{1,0:T(8,128)(2,1)S(1)}, bf16[4,128,768]{2,1,0:T(8,128)(2,1)S(1)}, bf16[4,128,768]{2,1,0:T(8,128)(2,1)}, f32[1,768]{1,0:T(1,128)S(1)}) custom-call(bf16[128,768]{1,0:T(8,128)(2,1)S(1)} %add_convert_fusion.1.refs_0_, bf16[128,768]{1,0:T(8,128)(2,1)S(1)} %collective-permute-done.27.refs_1_, ...), custom_call_target="tpu_custom_call" | custom-call | flops 2415919104 | bytes 4718592 | tf_op jit(solution)/shard_map/pallas_call | solution.py:272
  123.8 4.3 %shard_map.266 = bf16[768,1536]{1,0:T(8,128)(2,1)} custom-call(bf16[128,768]{1,0:T(8,128)(2,1)S(1)} %add_convert_fusion.1.refs_0_, bf16[128,768]{1,0:T(8,128)(2,1)S(1)} %collective-permute-done.27.refs_1_, bf16[128,768]{1,0:T(8,128)(2,1)S(1)} %collective-permute-done.28.refs_2_, bf16[128,768]{1,0:T(8,128)(2,1)S(1)} %collective-permute-done.29.refs_3_, ...), custom_call_target="tpu_custom_call" | custom-call | flops 1207959552 | bytes 4718592 | tf_op jit(solution)/shard_map/pallas_call | solution.py:323
  144.2 8.5 %shard_map.267 = (bf16[512,192]{1,0:T(8,128)(2,1)S(1)}, bf16[2,512,384]{2,1,0:T(8,128)(2,1)S(1)}) custom-call(s32[2]{0:T(128)S(1)} %pad_add_fusion.place, bf16[128,192]{1,0:T(8,128)(2,1)S(1)} %get-tuple-element.119.refs_0_, bf16[128,192]{1,0:T(8,128)(2,1)S(1)} %collective-permute-done.34.refs_1_, bf16[128,192]{1,0:T(8,128)(2,1)S(1)} %collective-permute-done.35.refs_2_, ...), custom_call_target="tpu_custom_call" | custom-call | flops 1006632960 | bytes 1572864 | tf_op jit(solution)/shard_map/pallas_call | solution.py:468
  155.3 3.5 %shard_map.268 = (bf16[4,128,768]{2,1,0:T(8,128)(2,1)S(1)}, bf16[768,576]{1,0:T(8,128)(2,1)S(1)}, f32[8,768]{1,0:T(8,128)S(1)}) custom-call(s32[2]{0:T(128)S(1)} %pad_add_fusion.place, bf16[512,192]{1,0:T(8,128)(2,1)S(1)} %get-tuple-element.128.refs_0_, bf16[512,384]{1,0:T(8,128)(2,1)S(1)} %get-tuple-element.203.refs_1_, ...), custom_call_target="tpu_custom_call" | custom-call | flops 905969664 | bytes 1572864 | tf_op jit(solution)/shard_map/pallas_call | solution.py:508
  163.6 4.5 %collective-permute-done.47 = bf16[128,768]{1,0:T(8,128)(2,1)S(1)} collective-permute-done((bf16[128,768]{1,0:T(8,128)(2,1)S(1)}, bf16[128,768]{1,0:T(8,128)(2,1)S(1)}, u32[]{:S(2)}, u32[]{:S(2)}) %collective-permute-start.47) | collective-permute-done | bytes 196640 | tf_op jit(solution)/shard_map/ppermute | solution.py:40
  168.1 2.7 %collective-permute-done.46 = bf16[128,768]{1,0:T(8,128)(2,1)S(1)} collective-permute-done((bf16[128,768]{1,0:T(8,128)(2,1)S(1)}, bf16[128,768]{1,0:T(8,128)(2,1)S(1)}, u32[]{:S(2)}, u32[]{:S(2)}) %collective-permute-start.46) | collective-permute-done | bytes 196640 | tf_op jit(solution)/shard_map/ppermute | solution.py:40
  171.4 2.7 %collective-permute-start.50 = (bf16[130,576]{1,0:T(8,128)(2,1)S(1)}, bf16[130,576]{1,0:T(8,128)(2,1)S(1)}, u32[]{:S(2)}, u32[]{:S(2)}) collective-permute-start(bf16[130,576]{1,0:T(8,128)(2,1)S(1)} %get-tuple-element.215), channel_id=1, source_target_pairs={{0,3},{1,2},{2,1},{3,0},{4,7},{5,6},{6,5},{7,4},{8,11},{9,10},{10,... | collective-permute-start | bytes 449288 | tf_op jit(solution)/shard_map/ppermute | solution.py:40
  174.1 5.0 %collective-permute-start.49 = (bf16[130,576]{1,0:T(8,128)(2,1)S(1)}, bf16[130,576]{1,0:T(8,128)(2,1)S(1)}, u32[]{:S(2)}, u32[]{:S(2)}) collective-permute-start(bf16[130,576]{1,0:T(8,128)(2,1)S(1)} %get-tuple-element.216), channel_id=1, source_target_pairs={{0,2},{1,3},{2,0},{3,1},{4,6},{5,7},{6,4},{7,5},{8,10},{9,11},{10,... | collective-permute-start | bytes 449288 | tf_op jit(solution)/shard_map/ppermute | solution.py:40
  180.2 10.5 %collective-permute-done.49 = bf16[130,576]{1,0:T(8,128)(2,1)S(1)} collective-permute-done((bf16[130,576]{1,0:T(8,128)(2,1)S(1)}, bf16[130,576]{1,0:T(8,128)(2,1)S(1)}, u32[]{:S(2)}, u32[]{:S(2)}) %collective-permute-start.49) | collective-permute-done | bytes 149792 | tf_op jit(solution)/shard_map/ppermute | solution.py:40
  200.9 9.5 %collective-permute-done.52 = bf16[130,576]{1,0:T(8,128)(2,1)S(1)} collective-permute-done((bf16[130,576]{1,0:T(8,128)(2,1)S(1)}, bf16[130,576]{1,0:T(8,128)(2,1)S(1)}, u32[]{:S(2)}, u32[]{:S(2)}) %collective-permute-start.52) | collective-permute-done | bytes 149792 | tf_op jit(solution)/shard_map/ppermute | solution.py:40
  210.4 2.7 %collective-permute-start.55 = (bf16[96,1536]{1,0:T(8,128)(2,1)}, bf16[96,1536]{1,0:T(8,128)(2,1)S(1)}, u32[]{:S(2)}, u32[]{:S(2)}) collective-permute-start(bf16[96,1536]{1,0:T(8,128)(2,1)} %reduce-scatter.2.cloned.1.call-done), channel_id=1, source_target_pairs={{0,8},{8,0},{16,24},{24,16},{1,9},{9,1},{17,25},{25,17},{2,10},{10... | collective-permute-start | bytes 884744 | tf_op jit(solution)/shard_map/ppermute | solution.py:40
  214.5 7.5 %collective-permute-done.56 = bf16[96,1536]{1,0:T(8,128)(2,1)S(1)} collective-permute-done((bf16[96,1536]{1,0:T(8,128)(2,1)}, bf16[96,1536]{1,0:T(8,128)(2,1)S(1)}, u32[]{:S(2)}, u32[]{:S(2)}) %collective-permute-start.56) | collective-permute-done | bytes 294944 | tf_op jit(solution)/shard_map/ppermute | solution.py:40
  227.4 2.6 %shard_map.269 = f32[192,2304]{1,0:T(8,128)} custom-call(bf16[4,192,576]{2,1,0:T(8,128)(2,1)S(1)} %bitcast.181), custom_call_target="tpu_custom_call" | custom-call | tf_op jit(solution)/shard_map/pallas_call | solution.py:173
  235.7 3.4 %shard_map.270 = (f32[192,3072]{1,0:T(8,128)}, f32[4,192,768]{2,1,0:T(8,128)}) custom-call(bf16[4,192,1536]{2,1,0:T(8,128)(2,1)S(1)} %bitcast.178), custom_call_target="tpu_custom_call" | custom-call | tf_op jit(solution)/shard_map/pallas_call | solution.py:198
  (339 shorter events, 109.6 us)
Async XLA Ops:
  7.2 191.6 %reduce-scatter.2.cloned.1.call-start = ((), (), s32[]{:S(2)}) async-start(), calls=%async_computation.1 | async-start | bytes 2654208 | tf_op jit(solution)/shard_map/reduce_scatter | solution.py:642
  13.3 15.2 %collective-permute-start.16 = (bf16[2304]{0:T(1024)(128)(2,1)S(1)}, bf16[2304]{0:T(1024)(128)(2,1)S(1)}, u32[]{:S(2)}, u32[]{:S(2)}) collective-permute-start(bf16[2304]{0:T(1024)(128)(2,1)S(1)} %concatenate.25), channel_id=1, source_target_pairs={{0,3},{1,2},{2,1},{3,0},{4,7},{5,6},{6,5},{7,4},{8,11},{9,10},{10,... | collective-permute-start | bytes 13832 | tf_op jit(solution)/shard_map/ppermute | solution.py:40
  18.4 12.1 %collective-permute-start.14 = (bf16[2304]{0:T(1024)(128)(2,1)S(1)}, bf16[2304]{0:T(1024)(128)(2,1)S(1)}, u32[]{:S(2)}, u32[]{:S(2)}) collective-permute-start(bf16[2304]{0:T(1024)(128)(2,1)S(1)} %concatenate.25), channel_id=1, source_target_pairs={{0,1},{1,0},{2,3},{3,2},{4,5},{5,4},{6,7},{7,6},{8,9},{9,8},{10,11... | collective-permute-start | bytes 13832 | tf_op jit(solution)/shard_map/ppermute | solution.py:40
  20.9 11.3 %collective-permute-start.7 = (bf16[96,576]{1,0:T(8,128)(2,1)S(1)}, bf16[96,576]{1,0:T(8,128)(2,1)S(1)}, u32[]{:S(2)}, u32[]{:S(2)}) collective-permute-start(bf16[96,576]{1,0:T(8,128)(2,1)S(1)} %shard_map.263), channel_id=1, source_target_pairs={{0,1},{1,0},{2,3},{3,2},{4,5},{5,4},{6,7},{7,6},{8,9},{9,8},{10,11... | collective-permute-start | bytes 331784 | tf_op jit(solution)/shard_map/ppermute | solution.py:40
  47.6 14.7 %collective-permute-start.20 = (bf16[96,768]{1,0:T(8,128)(2,1)S(1)}, bf16[96,768]{1,0:T(8,128)(2,1)S(1)}, u32[]{:S(2)}, u32[]{:S(2)}) collective-permute-start(bf16[96,768]{1,0:T(8,128)(2,1)S(1)} %slice.216), channel_id=1, source_target_pairs={{0,1},{1,0},{2,3},{3,2},{4,5},{5,4},{6,7},{7,6},{8,9},{9,8},{10,11... | collective-permute-start | bytes 442376 | tf_op jit(solution)/shard_map/ppermute | solution.py:40
  50.6 11.7 %collective-permute-start.21 = (bf16[96,768]{1,0:T(8,128)(2,1)S(1)}, bf16[96,768]{1,0:T(8,128)(2,1)S(1)}, u32[]{:S(2)}, u32[]{:S(2)}) collective-permute-start(bf16[96,768]{1,0:T(8,128)(2,1)S(1)} %slice.216), channel_id=1, source_target_pairs={{0,2},{1,3},{2,0},{3,1},{4,6},{5,7},{6,4},{7,5},{8,10},{9,11},{10,... | collective-permute-start | bytes 442376 | tf_op jit(solution)/shard_map/ppermute | solution.py:40
  63.6 15.8 %collective-permute-start.24 = (bf16[96,1536]{1,0:T(8,128)(2,1)S(1)}, bf16[96,1536]{1,0:T(8,128)(2,1)S(1)}, u32[]{:S(2)}, u32[]{:S(2)}) collective-permute-start(bf16[96,1536]{1,0:T(8,128)(2,1)S(1)} %slice.218), channel_id=1, source_target_pairs={{0,1},{1,0},{2,3},{3,2},{4,5},{5,4},{6,7},{7,6},{8,9},{9,8},{10,11... | collective-permute-start | bytes 884744 | tf_op jit(solution)/shard_map/ppermute | solution.py:40
  65.8 23.4 %collective-permute-start.25 = (bf16[96,1536]{1,0:T(8,128)(2,1)S(1)}, bf16[96,1536]{1,0:T(8,128)(2,1)S(1)}, u32[]{:S(2)}, u32[]{:S(2)}) collective-permute-start(bf16[96,1536]{1,0:T(8,128)(2,1)S(1)} %slice.218), channel_id=1, source_target_pairs={{0,2},{1,3},{2,0},{3,1},{4,6},{5,7},{6,4},{7,5},{8,10},{9,11},{10,... | collective-permute-start | bytes 884744 | tf_op jit(solution)/shard_map/ppermute | solution.py:40
  66.9 22.3 %collective-permute-start.26 = (bf16[96,1536]{1,0:T(8,128)(2,1)S(1)}, bf16[96,1536]{1,0:T(8,128)(2,1)S(1)}, u32[]{:S(2)}, u32[]{:S(2)}) collective-permute-start(bf16[96,1536]{1,0:T(8,128)(2,1)S(1)} %slice.218), channel_id=1, source_target_pairs={{0,3},{1,2},{2,1},{3,0},{4,7},{5,6},{6,5},{7,4},{8,11},{9,10},{10,... | collective-permute-start | bytes 884744 | tf_op jit(solution)/shard_map/ppermute | solution.py:40
  113.0 15.1 %collective-permute-start.31 = (bf16[128,768]{1,0:T(8,128)(2,1)}, bf16[128,768]{1,0:T(8,128)(2,1)}, u32[]{:S(2)}, u32[]{:S(2)}) collective-permute-start(bf16[128,768]{1,0:T(8,128)(2,1)} %get-tuple-element.206), channel_id=1, source_target_pairs={{0,8},{8,0},{16,24},{24,16},{1,9},{9,1},{17,25},{25,17},{2,10},{10... | collective-permute-start | bytes 589832 | tf_op jit(solution)/shard_map/ppermute | solution.py:40
  114.3 13.9 %collective-permute-start.32 = (bf16[128,768]{1,0:T(8,128)(2,1)}, bf16[128,768]{1,0:T(8,128)(2,1)}, u32[]{:S(2)}, u32[]{:S(2)}) collective-permute-start(bf16[128,768]{1,0:T(8,128)(2,1)} %get-tuple-element.205), channel_id=1, source_target_pairs={{0,16},{8,24},{16,0},{24,8},{1,17},{9,25},{17,1},{25,9},{2,18},{10... | collective-permute-start | bytes 589832 | tf_op jit(solution)/shard_map/ppermute | solution.py:40
  115.4 12.8 %collective-permute-start.33 = (bf16[128,768]{1,0:T(8,128)(2,1)}, bf16[128,768]{1,0:T(8,128)(2,1)}, u32[]{:S(2)}, u32[]{:S(2)}) collective-permute-start(bf16[128,768]{1,0:T(8,128)(2,1)} %get-tuple-element.204), channel_id=1, source_target_pairs={{0,24},{8,16},{16,8},{24,0},{1,25},{9,17},{17,9},{25,1},{2,26},{10... | collective-permute-start | bytes 589832 | tf_op jit(solution)/shard_map/ppermute | solution.py:40
  140.6 12.2 %collective-permute-start.40 = (bf16[4,48,768]{2,1,0:T(8,128)(2,1)S(1)}, bf16[4,48,768]{2,1,0:T(8,128)(2,1)S(1)}, u32[]{:S(2)}, u32[]{:S(2)}) collective-permute-start(bf16[4,48,768]{2,1,0:T(8,128)(2,1)S(1)} %get-tuple-element.138), channel_id=1, source_target_pairs={{0,24},{8,16},{16,8},{24,0},{1,25},{9,17},{17,9},{25,1},{2,26},{10... | collective-permute-start | bytes 884744 | tf_op jit(solution)/shard_map/ppermute | solution.py:40
  141.8 12.4 %collective-permute-start.39 = (bf16[4,48,768]{2,1,0:T(8,128)(2,1)S(1)}, bf16[4,48,768]{2,1,0:T(8,128)(2,1)S(1)}, u32[]{:S(2)}, u32[]{:S(2)}) collective-permute-start(bf16[4,48,768]{2,1,0:T(8,128)(2,1)S(1)} %get-tuple-element.137), channel_id=1, source_target_pairs={{0,16},{8,24},{16,0},{24,8},{1,17},{9,25},{17,1},{25,9},{2,18},{10... | collective-permute-start | bytes 884744 | tf_op jit(solution)/shard_map/ppermute | solution.py:40
  142.8 11.5 %collective-permute-start.38 = (bf16[4,48,768]{2,1,0:T(8,128)(2,1)S(1)}, bf16[4,48,768]{2,1,0:T(8,128)(2,1)S(1)}, u32[]{:S(2)}, u32[]{:S(2)}) collective-permute-start(bf16[4,48,768]{2,1,0:T(8,128)(2,1)S(1)} %get-tuple-element.136), channel_id=1, source_target_pairs={{0,8},{8,0},{16,24},{24,16},{1,9},{9,1},{17,25},{25,17},{2,10},{10... | collective-permute-start | bytes 884744 | tf_op jit(solution)/shard_map/ppermute | solution.py:40
  174.1 16.7 %collective-permute-start.49 = (bf16[130,576]{1,0:T(8,128)(2,1)S(1)}, bf16[130,576]{1,0:T(8,128)(2,1)S(1)}, u32[]{:S(2)}, u32[]{:S(2)}) collective-permute-start(bf16[130,576]{1,0:T(8,128)(2,1)S(1)} %get-tuple-element.216), channel_id=1, source_target_pairs={{0,2},{1,3},{2,0},{3,1},{4,6},{5,7},{6,4},{7,5},{8,10},{9,11},{10,... | collective-permute-start | bytes 449288 | tf_op jit(solution)/shard_map/ppermute | solution.py:40
  179.1 11.7 %collective-permute-start.48 = (bf16[130,576]{1,0:T(8,128)(2,1)S(1)}, bf16[130,576]{1,0:T(8,128)(2,1)S(1)}, u32[]{:S(2)}, u32[]{:S(2)}) collective-permute-start(bf16[130,576]{1,0:T(8,128)(2,1)S(1)} %get-tuple-element.214), channel_id=1, source_target_pairs={{0,1},{1,0},{2,3},{3,2},{4,5},{5,4},{6,7},{7,6},{8,9},{9,8},{10,11... | collective-permute-start | bytes 449288 | tf_op jit(solution)/shard_map/ppermute | solution.py:40
  192.6 17.8 %collective-permute-start.52 = (bf16[130,576]{1,0:T(8,128)(2,1)S(1)}, bf16[130,576]{1,0:T(8,128)(2,1)S(1)}, u32[]{:S(2)}, u32[]{:S(2)}) collective-permute-start(bf16[130,576]{1,0:T(8,128)(2,1)S(1)} %fusion.34), channel_id=1, source_target_pairs={{0,16},{8,24},{16,0},{24,8},{1,17},{9,25},{17,1},{25,9},{2,18},{10... | collective-permute-start | bytes 449288 | tf_op jit(solution)/shard_map/ppermute | solution.py:40
  193.4 17.1 %collective-permute-start.51 = (bf16[130,576]{1,0:T(8,128)(2,1)S(1)}, bf16[130,576]{1,0:T(8,128)(2,1)S(1)}, u32[]{:S(2)}, u32[]{:S(2)}) collective-permute-start(bf16[130,576]{1,0:T(8,128)(2,1)S(1)} %fusion.34), channel_id=1, source_target_pairs={{0,8},{8,0},{16,24},{24,16},{1,9},{9,1},{17,25},{25,17},{2,10},{10... | collective-permute-start | bytes 449288 | tf_op jit(solution)/shard_map/ppermute | solution.py:40
  194.5 29.5 %collective-permute-start.44 = (bf16[128,768]{1,0:T(8,128)(2,1)S(1)}, bf16[128,768]{1,0:T(8,128)(2,1)S(1)}, u32[]{:S(2)}, u32[]{:S(2)}) collective-permute-start(bf16[128,768]{1,0:T(8,128)(2,1)S(1)} %get-tuple-element.200), channel_id=1, source_target_pairs={{0,24},{8,16},{16,8},{24,0},{1,25},{9,17},{17,9},{25,1},{2,26},{10... | collective-permute-start | bytes 589832 | tf_op jit(solution)/shard_map/ppermute | solution.py:40
  196.5 27.5 %collective-permute-start.43 = (bf16[128,768]{1,0:T(8,128)(2,1)S(1)}, bf16[128,768]{1,0:T(8,128)(2,1)S(1)}, u32[]{:S(2)}, u32[]{:S(2)}) collective-permute-start(bf16[128,768]{1,0:T(8,128)(2,1)S(1)} %get-tuple-element.201), channel_id=1, source_target_pairs={{0,16},{8,24},{16,0},{24,8},{1,17},{9,25},{17,1},{25,9},{2,18},{10... | collective-permute-start | bytes 589832 | tf_op jit(solution)/shard_map/ppermute | solution.py:40
  198.8 15.0 %collective-permute-start.57 = (bf16[96,1536]{1,0:T(8,128)(2,1)}, bf16[96,1536]{1,0:T(8,128)(2,1)S(1)}, u32[]{:S(2)}, u32[]{:S(2)}) collective-permute-start(bf16[96,1536]{1,0:T(8,128)(2,1)} %reduce-scatter.2.cloned.1.call-done), channel_id=1, source_target_pairs={{0,24},{8,16},{16,8},{24,0},{1,25},{9,17},{17,9},{25,1},{2,26},{10... | collective-permute-start | bytes 884744 | tf_op jit(solution)/shard_map/ppermute | solution.py:40
  210.4 11.6 %collective-permute-start.56 = (bf16[96,1536]{1,0:T(8,128)(2,1)}, bf16[96,1536]{1,0:T(8,128)(2,1)S(1)}, u32[]{:S(2)}, u32[]{:S(2)}) collective-permute-start(bf16[96,1536]{1,0:T(8,128)(2,1)} %reduce-scatter.2.cloned.1.call-done), channel_id=1, source_target_pairs={{0,16},{8,24},{16,0},{24,8},{1,17},{9,25},{17,1},{25,9},{2,18},{10... | collective-permute-start | bytes 884744 | tf_op jit(solution)/shard_map/ppermute | solution.py:40
  210.4 11.6 %collective-permute-start.55 = (bf16[96,1536]{1,0:T(8,128)(2,1)}, bf16[96,1536]{1,0:T(8,128)(2,1)S(1)}, u32[]{:S(2)}, u32[]{:S(2)}) collective-permute-start(bf16[96,1536]{1,0:T(8,128)(2,1)} %reduce-scatter.2.cloned.1.call-done), channel_id=1, source_target_pairs={{0,8},{8,0},{16,24},{24,16},{1,9},{9,1},{17,25},{25,17},{2,10},{10... | collective-permute-start | bytes 884744 | tf_op jit(solution)/shard_map/ppermute | solution.py:40
  (87 other events, 482.4 us)
Sparse Core Ops, SparseCore 0:
  135.8 40.5 reduce-scatter.1

commit v4 on v3

--- a/solution.py
+++ b/solution.py
@@ -14,6 +14,8 @@
 MASK_FILL = -1e30
 GELU_COEF = 0.7978845608028654
 GELU_CUBE = 0.044715
+
+SHORT = pl.CostEstimate(flops=1, bytes_accessed=1, transcendentals=0)
 
 BF = jnp.bfloat16
 F32 = jnp.float32
@@ -114,6 +116,127 @@
     return lax.dynamic_index_in_dim(
         half.reshape(rows, parts, GROUPS, cols // parts), g, axis=2, keepdims=False
     ).reshape(rows, cols)
+
+
+def cut_first_kernel(place, *refs):
+    source, vectors, cut, held = refs[0], refs[1:-2], refs[-2], refs[-1]
+    rows, wide = source.shape
+    unit = vectors[0].shape[0]
+    per = cut.shape[1] // unit
+    held[...] = jnp.zeros_like(held)
+    spot = 0
+    for vector in vectors:
+        row = vector[...].astype(F32).reshape(1, vector.shape[0])
+        for part in range(vector.shape[0] // unit):
+            col = spot % per * unit
+            held[spot // per : spot // per + 1, col : col + unit] = row[
+                :, part * unit : (part + 1) * unit
+            ]
+            spot += 1
+    cut[rows:, :] = held[...].astype(BF)
+    for i in range(GROUPS):
+
+        @pl.when(place[0] == i)
+        def _():
+            cut_columns(source, cut.at[:rows, :], 3, i)
+
+
+def cut_first(weight, vectors, g, k, ks):
+    rows, cols = weight.shape[0] // ks, weight.shape[1] // GROUPS
+    return pl.pallas_call(
+        cut_first_kernel,
+        grid_spec=pltpu.PrefetchScalarGridSpec(
+            num_scalar_prefetch=1,
+            grid=(1,),
+            in_specs=[pl.BlockSpec((rows, weight.shape[1]), lambda i, place: (place[1], 0))]
+            + [pl.BlockSpec(v.shape, lambda i, place: (0,)) for v in vectors],
+            out_specs=pl.BlockSpec((rows + 16, cols), lambda i, place: (0, 0)),
+            scratch_shapes=[pltpu.VMEM((16, cols), F32)],
+        ),
+        out_shape=jax.ShapeDtypeStruct((rows + 16, cols), BF),
+        compiler_params=pltpu.CompilerParams(vmem_limit_bytes=8 * 2**20),
+    )(jnp.stack([g, k]).astype(jnp.int32), weight, *vectors)
+
+
+def table_kernel(unit, place, *refs):
+    pieces, out, held = refs[:-2], refs[-2], refs[-1]
+    zs = len(pieces)
+    per = held.shape[2] // unit
+    cols = out.shape[1] // GROUPS
+    for i, piece in enumerate(pieces):
+        held[place[1] ^ i] = piece[...].astype(F32)
+
+    def unpack(row, slot):
+        for zz in range(zs):
+            col = slot % per * unit
+            out[row : row + 1, zz * unit : (zz + 1) * unit] = held[
+                zz, slot // per : slot // per + 1, col : col + unit
+            ]
+
+    out[...] = jnp.zeros_like(out)
+    for slot in range(8):
+        unpack(slot + 8 if slot in (2, 3) else slot, slot)
+    for i in range(GROUPS):
+
+        @pl.when(place[0] == i)
+        def _():
+            unpack(8, 8 + i)
+            out[2:4, :cols] = out[10:12, i * cols : (i + 1) * cols]
+
+
+def vector_table(pieces, unit, width, g, z):
+    rows, cols = pieces[0].shape
+    return pl.pallas_call(
+        functools.partial(table_kernel, unit),
+        grid_spec=pltpu.PrefetchScalarGridSpec(
+            num_scalar_prefetch=1,
+            grid=(1,),
+            in_specs=[pl.BlockSpec((16, cols), lambda i, place: (rows // 16 - 1, 0))] * len(pieces),
+            out_specs=pl.BlockSpec((16, width), lambda i, place: (0, 0)),
+            scratch_shapes=[pltpu.VMEM((len(pieces), 16, cols), F32)],
+        ),
+        out_shape=jax.ShapeDtypeStruct((16, width), F32),
+        compiler_params=pltpu.CompilerParams(vmem_limit_bytes=8 * 2**20),
+    )(jnp.stack([g, z]).astype(jnp.int32), *pieces)
+
+
+def pack_kernel(zs, stride, unit, place, sums, out_bias, gain, shift, con_bias, exp_bias, out):
+    per = out.shape[1] // unit
+    cols = out.shape[1] // 3
+
+    def put(zz, slot, value):
+        row, col = zz * stride + slot // per, slot % per * unit
+        out[row : row + 1, col : col + unit] = value
+
+    out[...] = jnp.zeros_like(out)
+    whole = [(0, sums, 0), (1, sums, 1), (4, out_bias, 0), (5, gain, 0), (6, shift, 0), (7, con_bias, 0)]
+    for slot, source, row in whole:
+        for zz in range(zs):
+            put(zz, slot, source[row : row + 1, zz * unit : (zz + 1) * unit])
+    for i in range(GROUPS):
+
+        @pl.when(place[0] == i)
+        def _():
+            for zz in range(zs):
+                put(zz, 8 + i, exp_bias[:, zz * unit : (zz + 1) * unit])
+            for part in range(cols // unit):
+                zz = i * cols // unit + part
+                low = part * unit
+                put(zz, 2, sums[2:3, low : low + unit])
+                put(zz, 3, sums[2:3, 2 * cols + low : 2 * cols + low + unit])
+
+
+def pack_vectors(g, zs, stride, unit, sums, *vectors):
+    wide = 3 * (vectors[0].shape[1] // GROUPS)
+    vmem = pl.BlockSpec(memory_space=pltpu.VMEM)
+    return pl.pallas_call(
+        functools.partial(pack_kernel, zs, stride, unit),
+        grid_spec=pltpu.PrefetchScalarGridSpec(
+            num_scalar_prefetch=1, in_specs=[vmem] * (1 + len(vectors)), out_specs=vmem
+        ),
+        out_shape=jax.ShapeDtypeStruct((zs * stride, wide), F32),
+        compiler_params=pltpu.CompilerParams(vmem_limit_bytes=8 * 2**20),
+    )(jnp.stack([g]).astype(jnp.int32), sums, *vectors)
 
 
 def cut_rest_kernel(parts, place, con_ref, exp_ref, out_ref, cut):
@@ -229,7 +352,7 @@
         join_rows(h_rows, h_ref)
         join_rows(s_rows, s_ref)
 
-    inner = mm(h_ref[...], exp_w[...]) + bias[...]
+    inner = mm(h_ref[...], exp_w[...]) + bias[8:9, :]
     square = inner * inner
     tanh = jnp.tanh(GELU_COEF * (inner + GELU_CUBE * square * inner))
     half = 0.5 + 0.5 * tanh
@@ -261,9 +384,9 @@
             out_ref[i] = out_sum[i * tok : (i + 1) * tok, :].astype(BF)
 
 
-def hidden_part(h_rows, s_rows, weights, bias):
+def hidden_part(h_rows, s_rows, weights, table):
     tok, width = h_rows[0].shape
-    hidden = bias.shape[1]
+    hidden = weights.shape[1] - width
     rows = GROUPS * tok
     step = 256
     fixed = lambda i: (0, 0)
@@ -276,7 +399,7 @@
         + [
             pl.BlockSpec((width, step), lambda i: (0, width // step + i)),
             pl.BlockSpec((step, width), lambda i: (i, 0)),
-            pl.BlockSpec((1, step), cols),
+            pl.BlockSpec((16, step), cols),
         ],
         out_specs=[
             pl.BlockSpec((rows, step), cols),
@@ -294,10 +417,8 @@
         ],
         scratch_shapes=[pltpu.VMEM((rows, width), BF)] * 2 + [pltpu.VMEM((rows, width), F32)] * 2,
         compiler_params=pltpu.CompilerParams(vmem_limit_bytes=24 * 2**20),
-        cost_estimate=pl.CostEstimate(
-            flops=8 * rows * width * hidden, bytes_accessed=12 * rows * width, transcendentals=0
-        ),
-    )(*h_rows, *in_hbm(*s_rows, weights, weights), bias)
+        cost_estimate=SHORT,
+    )(*h_rows, *in_hbm(*s_rows, weights, weights), table)
 
 
 def hidden_grad_kernel(*refs):
@@ -330,9 +451,7 @@
         out_shape=jax.ShapeDtypeStruct((width, hidden + width), BF),
         scratch_shapes=[pltpu.VMEM((rows, step), BF), pltpu.VMEM((rows, width), BF)],
         compiler_params=pltpu.CompilerParams(vmem_limit_bytes=16 * 2**20),
-        cost_estimate=pl.CostEstimate(
-            flops=4 * rows * width * hidden, bytes_accessed=12 * rows * width, transcendentals=0
-        ),
+        cost_estimate=SHORT,
     )(*h_rows, *in_hbm(*s_rows), slope_inner, act)
 
 
@@ -351,25 +470,26 @@
 
 def attend_kernel(ks, head, place, *refs):
     pieces = refs[: GROUPS * ks]
-    in_w, gain, shift, q_bias, v_bias = refs[GROUPS * ks : GROUPS * ks + 5]
-    slots, q_out, k_out, v_out, att_out, lse_out, h_out, hat_out, h_all = refs[GROUPS * ks + 5 :]
+    in_w, table = refs[GROUPS * ks : GROUPS * ks + 2]
+    slots, q_out, k_out, v_out, att_out, lse_out, h_out, hat_out, h_all = refs[GROUPS * ks + 2 :]
     g, k = place[0], place[1]
     tok, width = pieces[0].shape
     cols = q_out.shape[1]
+    gain, shift = table[0:1, :], table[1:2, :]
     for j in range(ks):
         for i in range(GROUPS):
             hat, _ = norm_stats(pieces[j * GROUPS + i][...].astype(F32))
-            normed = (hat * gain[...] + shift[...]).astype(BF)
+            normed = (hat * gain + shift).astype(BF)
             spot = pl.multiple_of(((g ^ i) * ks + (k ^ j)) * tok, tok)
             h_all[pl.ds(spot, tok), :] = normed
             if j == 0:
                 spot = pl.multiple_of((g ^ i) * tok, tok)
                 h_out[pl.ds(spot, tok), :] = normed
                 hat_out[pl.ds(spot, tok), :] = hat.astype(BF)
-    q_out[...] = (mm(h_out[...], in_w[:, :cols]) + q_bias[...]).astype(BF)
+    q_out[...] = (mm(h_out[...], in_w[:, :cols]) + table[2:3, :cols]).astype(BF)
     kv = mm(h_all[...], in_w[:, cols:])
     k_out[...] = kv[:, :cols].astype(BF)
-    v_out[...] = (kv[:, cols:] + v_bias[...]).astype(BF)
+    v_out[...] = (kv[:, cols:] + table[3:4, :cols]).astype(BF)
     seen = visible(k, tok, ks * tok)
     for h in range(cols // head):
         low, high = h * head, (h + 1) * head
@@ -388,7 +508,7 @@
         slots[g ^ i] = att_out[i * tok : (i + 1) * tok, :].astype(BF)
 
 
-def attend(g, k, ks, head, pieces, in_w, gain, shift, q_bias, v_bias):
+def attend(g, k, ks, head, pieces, in_w, table):
     tok, width = pieces[0].shape
     cols = in_w.shape[1] // 3
     mine, rows = GROUPS * tok, GROUPS * ks * tok
@@ -407,16 +527,14 @@
         functools.partial(attend_kernel, ks, head),
         grid_spec=pltpu.PrefetchScalarGridSpec(
             num_scalar_prefetch=1,
-            in_specs=[vmem] * (len(pieces) + 5),
+            in_specs=[vmem] * (len(pieces) + 2),
             out_specs=[vmem] * len(shapes),
             scratch_shapes=[pltpu.VMEM((rows, width), BF)],
         ),
         out_shape=[jax.ShapeDtypeStruct(*shapes[0])] + [pltpu.HBM(s, t) for s, t in shapes[1:]],
         compiler_params=pltpu.CompilerParams(vmem_limit_bytes=(16 if ks == 2 else 48) * 2**20),
-        cost_estimate=pl.CostEstimate(
-            flops=6 * rows * width * cols, bytes_accessed=4 * rows * width, transcendentals=0
-        ),
-    )(jnp.stack([g, k]).astype(jnp.int32), *pieces, in_w, gain, shift, q_bias, v_bias)
+        cost_estimate=SHORT,
+    )(jnp.stack([g, k]).astype(jnp.int32), *pieces, in_w, table)
 
 
 def attend_back_kernel(ks, head, place, *refs):
@@ -478,9 +596,7 @@
             jax.ShapeDtypeStruct((ks, mine, 2 * cols), BF),
         ],
         compiler_params=pltpu.CompilerParams(vmem_limit_bytes=(16 if ks == 2 else 48) * 2**20),
-        cost_estimate=pl.CostEstimate(
-            flops=10 * mine * rows * cols, bytes_accessed=8 * rows * cols, transcendentals=0
-        ),
+        cost_estimate=SHORT,
     )(jnp.stack([g, k]).astype(jnp.int32), *slopes, *in_hbm(q, keys, values, att, lse))
 
 
@@ -519,9 +635,7 @@
             jax.ShapeDtypeStruct((8, width), F32),
         ],
         compiler_params=pltpu.CompilerParams(vmem_limit_bytes=16 * 2**20),
-        cost_estimate=pl.CostEstimate(
-            flops=12 * mine * width * cols, bytes_accessed=4 * mine * width, transcendentals=0
-        ),
+        cost_estimate=SHORT,
     )(jnp.stack([g, k]).astype(jnp.int32), dq, *dkv, *in_hbm(h, hat), in_w)
 
 
@@ -559,81 +673,58 @@
     slope_own = cotangent[0]
 
     x_rows = gather_flips(x_own, "grp")
-    in_cut = cut_weight(input_weight, 3, g, k, ks)
-    in_pieces = gather_flips(in_cut, "fsdp")
+
+    smalls = [first_gain, first_shift, query_bias, value_bias, output_bias]
+    smalls += [second_gain, second_shift, contract_bias, expand_bias]
+    own = rows_z // ks
+    aligned = own % 16 == 0
+    if aligned:
+        in_pieces = gather_flips(cut_first(input_weight, smalls, g, k, ks), "fsdp")
+    else:
+        in_pieces = gather_flips(cut_weight(input_weight, 3, g, k, ks), "fsdp")
+    in_pieces, x_rows = lax.optimization_barrier((in_pieces, x_rows))
     x_more = [[send(b, "core", j) for b in x_rows] for j in range(1, ks)]
-
-    smalls = jnp.concatenate(
-        [
-            first_gain,
-            first_shift,
-            query_bias,
-            value_bias,
-            output_bias,
-            second_gain,
-            second_shift,
-            contract_bias,
-            expand_bias,
-        ]
-    )
-    smalls_all = in_order(gather_flips(smalls, "fsdp"), z).astype(F32)
-
-    def small(i):
-        return smalls_all[:, i * rows_z : (i + 1) * rows_z].reshape(width)
-
-    gain_one, shift_one, q_bias, v_bias, o_bias, gain_two, shift_two, c_bias = [
-        small(i) for i in range(8)
-    ]
-    e_bias = pick(
-        smalls_all[:, 8 * rows_z :].reshape(zs, GROUPS, ff_g).transpose(1, 0, 2), g
-    ).reshape(zs * ff_g)
-    q_bias = pick(q_bias.reshape(GROUPS, cols), g)
-    v_bias = pick(v_bias.reshape(GROUPS, cols), g)
-
-    rest = cut_rest(contract_weight, expand_weight, output_weight, zs, g, k, ks)
-    rest, in_pieces = lax.optimization_barrier((rest, in_pieces))
-
-    in_half = in_order(in_pieces, z)
+    if aligned:
+        table = vector_table(in_pieces, rows_z, width, g, z)
+    else:
+        got = in_order(gather_flips(jnp.concatenate(smalls), "fsdp"), z).astype(F32)
+        vectors = [got[:, i * rows_z : (i + 1) * rows_z].reshape(width) for i in range(8)]
+        for i in (2, 3):
+            vectors[i] = jnp.tile(pick(vectors[i].reshape(GROUPS, cols), g), GROUPS)
+        got = got[:, 8 * rows_z :].reshape(zs, GROUPS, ff_g)
+        vectors.append(lax.dynamic_index_in_dim(got, g, axis=1, keepdims=False).reshape(width))
+        table = jnp.pad(jnp.stack(vectors), ((0, 7), (0, 0)))
+    o_bias, gain_two, shift_two, c_bias = [table[i : i + 1] for i in range(4, 8)]
+
+    con_raw, exp_raw, out_raw, slope_late, in_pieces = lax.optimization_barrier(
+        (contract_weight, expand_weight, output_weight, slope_own, in_pieces)
+    )
+    in_half = in_order([p[:own] for p in in_pieces], z)
     in_w = jnp.stack(in_order(gather_flips(in_half, "core"), k), axis=1).reshape(width, 3 * cols)
-
+    rest = cut_rest(con_raw, exp_raw, out_raw, zs, g, k, ks)
     split = width + zs * ff_g
     out_pieces = gather_flips(rest[:, split:], "fsdp")
-    rest_pieces = gather_flips(rest[:, :split], "fsdp")
-    slope_late, x_rows = lax.optimization_barrier((slope_own, x_rows))
+    rest = lax.all_gather(rest[:, :split], ("fsdp", "core"), axis=0, tiled=True)
+
     slope_rows = gather_flips(slope_late, "grp")
-
-    in_w, slope_rows = lax.optimization_barrier((in_w, slope_rows))
+    out_pieces, slope_rows, x_more = lax.optimization_barrier((out_pieces, slope_rows, x_more))
+    half = in_order(out_pieces, z)
+    out_w = jnp.stack(in_order(gather_flips(half, "core"), k), axis=1)
+    out_w = out_w.reshape(GROUPS, cols, width)
+    out_w = jnp.concatenate([pick(out_w, g ^ i) for i in range(GROUPS)])
+    in_w, out_w = lax.optimization_barrier((in_w, out_w))
     slots, qs, keys, values, att_full, lse, h1, hat_one = attend(
-        g,
-        k,
-        ks,
-        head,
-        x_rows + [b for bs in x_more for b in bs],
-        in_w,
-        gain_one[None],
-        shift_one[None],
-        q_bias[None],
-        v_bias[None],
-    )
-    out_pieces, lse = lax.optimization_barrier((out_pieces, lse))
-
-    def whole(pieces):
-        half = in_order(pieces, z)
-        return jnp.stack(in_order(gather_flips(half, "core"), k), axis=1).reshape(width, -1)
-
-    out_w = whole(out_pieces).reshape(GROUPS, cols, width)
-    out_w = jnp.concatenate([pick(out_w, g ^ i) for i in range(GROUPS)])
+        g, k, ks, head, x_rows + [b for bs in x_more for b in bs], in_w, table
+    )
     att = jnp.concatenate(swap_flips([slots[i] for i in range(GROUPS)], "grp"), axis=1)
     x_f = x_own.astype(F32)
     middle = x_f + mm(att, out_w) + o_bias
     hat_two, rate_two = norm_stats(middle)
     h2 = (hat_two * gain_two + shift_two).astype(BF)
     h2_rows = gather_flips(h2, "grp")
-    middle, rest_pieces = lax.optimization_barrier((middle, rest_pieces))
-    rest = whole(rest_pieces)
 
     act, slope_inner, sh2_part, out_part, d_exp_b = hidden_part(
-        h2_rows, slope_rows, rest, e_bias[None]
+        h2_rows, slope_rows, rest, table
     )
     sh2 = swap_flips([sh2_part[i] for i in range(GROUPS)], "grp")
     d_hidden = hidden_grads(h2_rows, slope_rows, slope_inner, act)
@@ -642,8 +733,8 @@
     d_hidden = lax.psum_scatter(d_hidden, ("fsdp", "core"), scatter_dimension=0, tiled=True)
 
     slope_f = slope_own.astype(F32)
-    d_gain_two = jnp.sum(sh2 * hat_two, axis=0)
-    d_shift_two = jnp.sum(sh2, axis=0)
+    d_gain_two = jnp.sum(sh2 * hat_two, axis=0, keepdims=True)
+    d_shift_two = jnp.sum(sh2, axis=0, keepdims=True)
     slope_middle = slope_f + norm_back(sh2, gain_two, hat_two, rate_two)
     slope_branch = slope_middle.astype(BF)
     slope_att = mm_rt(slope_branch, out_w).astype(BF)
@@ -660,50 +751,51 @@
     dq, dkv = attend_back(g, k, ks, head, datt, qs, keys, values, att_full, lse)
     dkv = swap_flips([dkv[j] for j in range(ks)], "core")
     sh1_part, d_in, sums = project_back(g, k, dq, dkv, h1, hat_one, in_w)
-    sh1 = total(swap_flips([sh1_part[i] for i in range(GROUPS)], "grp"))
+    sh1 = swap_flips([sh1_part[i] for i in range(GROUPS)], "grp")
+    sh1, out_late = lax.optimization_barrier((sh1, out_part))
+    sh1 = total(sh1)
+    out_sum = swap_flips([out_late[i] for i in range(GROUPS)], "grp")
     hat_own, rate_own = norm_stats(x_f)
-    delta_inputs = (slope_middle + norm_back(sh1, gain_one, hat_own, rate_own)).astype(BF)[None]
-
-    def at_group(vec, lead):
-        parts = vec.reshape(lead, 1, -1)
-        spot = (jnp.arange(GROUPS) == g).astype(F32)[None, :, None]
-        return (parts * spot).reshape(-1)
-
-    vectors = [
-        sums[0],
-        sums[1],
-        at_group(sums[2, :cols], 1),
-        at_group(sums[2, 2 * cols : 3 * cols], 1),
-        jnp.sum(slope_branch.astype(F32), axis=0),
+    delta_inputs = (slope_middle + norm_back(sh1, table[0:1], hat_own, rate_own)).astype(BF)[None]
+
+    extra = -(-(12 * rows_z) // (3 * cols * ks))
+    packed = pack_vectors(
+        g,
+        zs,
+        extra * ks,
+        rows_z,
+        sums,
+        jnp.sum(slope_branch.astype(F32), axis=0, keepdims=True),
         d_gain_two,
         d_shift_two,
-        jnp.sum(slope_f, axis=0),
-    ]
-    packed = jnp.concatenate(
-        [v.reshape(zs, rows_z) for v in vectors]
-        + [at_group(d_exp_b, zs).reshape(zs, ff_z)],
-        axis=1,
+        jnp.sum(slope_f, axis=0, keepdims=True),
+        d_exp_b,
     )
     d_out = total(d_out).astype(BF).reshape(zs, ks, -1, width)
     third = d_out.shape[2] // 3
     tail = d_out[..., 3 * cols :]
     tail = [tail[:, :, i * third : (i + 1) * third] for i in range(3)]
     d_out = jnp.concatenate([d_out[..., : 3 * cols], jnp.concatenate(tail, axis=3)], axis=2)
-    count = packed.shape[1]
-    extra = -(-count // (3 * cols * ks))
-    packed = jnp.pad(packed, ((0, 0), (0, extra * ks * 3 * cols - count)))
-    d_in = d_in.reshape(zs, ks, rows_z // ks, 3 * cols)
-    packed = packed.astype(BF).reshape(zs, ks, extra, 3 * cols)
-    d_in = jnp.concatenate([d_in, packed, d_out], axis=2)
+    d_in = jnp.concatenate(
+        [
+            d_in.reshape(zs, ks, own, 3 * cols),
+            packed.astype(BF).reshape(zs, ks, extra, 3 * cols),
+            d_out,
+        ],
+        axis=2,
+    )
     pieces = [lax.dynamic_index_in_dim(d_in, k ^ j, axis=1, keepdims=False) for j in range(ks)]
     d_in = total(swap_flips(pieces, "core")).astype(BF)
-    out_late, d_in = lax.optimization_barrier((out_part, d_in))
-    out_sum = total(swap_flips([out_late[i] for i in range(GROUPS)], "grp"))
-    outputs = (middle + out_sum + c_bias).astype(BF)[None]
-    d_in = total(swap_flips([pick(d_in, z ^ i) for i in range(zs)], "fsdp")).astype(BF)
-    d_in = in_order(gather_flips(d_in, "grp"), g)
+    d_in = swap_flips([pick(d_in, z ^ i) for i in range(zs)], "fsdp")
+    d_hidden = gather_flips(d_hidden, "grp")
+    d_in, d_hidden, out_sum = lax.optimization_barrier((d_in, d_hidden, out_sum))
+    d_in = in_order(gather_flips(total(d_in).astype(BF), "grp"), g)
     d_in = in_order(gather_flips(d_in, "core"), k)
-    own = rows_z // ks
+    outputs = (middle + total(out_sum) + c_bias).astype(BF)[None]
+    d_hidden = in_order(d_hidden, g)
+    d_hidden = jnp.stack(in_order(gather_flips(d_hidden, "core"), k), axis=1)
+    d_exp_w, d_con_w = unfold(d_hidden.reshape(GROUPS, rows_z, -1), zs)
+    d_con_w = d_con_w.reshape(ff_z, width)
     packed = jnp.sum(d_in[:, :, own : own + extra].astype(F32), axis=1).reshape(-1)
     d_out = d_in[:, :, own + extra :].transpose(1, 0, 2, 3)
     tail = d_out[:, :, 3 * third :].reshape(GROUPS, ks, third, 3, width - 3 * cols)
@@ -718,12 +810,9 @@
         .reshape(rows_z, width)
         .astype(F32)
     )
-    d_in = d_in[:, :, :own].transpose(1, 0, 2, 3).reshape(GROUPS, rows_z, 3 * cols)
-    d_in_w = weave(d_in, 3)
-    d_hidden = in_order(gather_flips(d_hidden, "grp"), g)
-    d_hidden = jnp.stack(in_order(gather_flips(d_hidden, "core"), k), axis=1)
-    d_exp_w, d_con_w = unfold(d_hidden.reshape(GROUPS, rows_z, -1), zs)
-    d_con_w = d_con_w.reshape(ff_z, width)
+    d_in_w = weave(
+        d_in[:, :, :own].transpose(1, 0, 2, 3).reshape(GROUPS, rows_z, 3 * cols), 3
+    )
 
     def vec(i):
         return packed[i * rows_z : (i + 1) * rows_z]

time: 247 us -> 221 us (0.89)
  local copies, waits for them, and re-layouts: 29.1 us -> 18.1 us
  waiting for transfers between devices: 69.5 us -> 60.3 us
  other arithmetic: 22.6 us -> 17.2 us
  starting transfers between devices: 69.3 us -> 66.6 us
    ppermute x59 -> x52, waiting for transfers between devices: 69.5 us -> 60.3 us  [send(): return lax.ppermute(value, axis, [(s, s ^ flip) for s in range(count)])]
    concatenate x2 -> x0, local copies, waits for them, and re-layouts: 6.2 us -> none  [the longest x1 6.1 us: shards(): jnp.concatenate([first_gain, first_shift, query_bias, value_bias, output_...]
    mul x7 -> x0, local copies, waits for them, and re-layouts: 5.5 us -> none  [the longest x5 4.77 us: at_group(): return (parts * spot).reshape(-1)]
    unnamed x98 -> x50, local copies, waits for them, and re-layouts: 5.56 us -> 11.1 us
    ppermute x59 -> x52, starting transfers between devices: 69.3 us -> 66.5 us  [send(): return lax.ppermute(value, axis, [(s, s ^ flip) for s in range(count)])]
    reshape x7 -> x2, local copies, waits for them, and re-layouts: 2.64 us -> 0.09 us  [the longest x1 0.08 us: shards(): out_w = jnp.stack(in_order(gather_flips(half, 'core'), k), axis=1)]
    another operation x12 -> x9, other arithmetic: 8.82 us -> 6.45 us  [in_order(): stacked = jnp.stack(pieces)]
  transfers between devices with their start and end apart: 60 -> 54, of which waited for: 20 -> 19; matrix products, arithmetic and copies ran while one was open for 13% -> 9% of each run, Pallas kernels for 12% -> 13%
where the time goes in v4:
time: 221 us; the launch traced here: 219 us
  starting transfers between devices  66.6 us (30%)
  waiting for transfers between devices  60.3 us (27%)
  Pallas kernels  40 us (18%)
  local copies, waits for them, and re-layouts  18.1 us (8%)
  other arithmetic  17.2 us (8%)
  between operations  14.9 us (7%)
    ppermute x52, starting transfers between devices, send(): return lax.ppermute(value, axis, [(s, s ^ flip) for s in range(count)])  66.5 us
    ppermute x52, waiting for transfers between devices, send(): return lax.ppermute(value, axis, [(s, s ^ flip) for s in range(count)])  60.3 us
    unnamed x50, local copies, waits for them, and re-layouts  11.1 us
    pallas_call x1, Pallas kernels, attend_back(): pl.pallas_call(functools.partial(attend_back_kernel, ks, head), grid_spec...  8.38 us
    pallas_call x1, Pallas kernels, attend(): pl.pallas_call(functools.partial(attend_kernel, ks, head), grid_spec=pltp...  8.11 us
    pallas_call x1, Pallas kernels, hidden_part(): pl.pallas_call(hidden_kernel, grid=(hidden // step,), in_specs=[pl.BlockS...  7.16 us
    another operation x9, other arithmetic, in_order(): stacked = jnp.stack(pieces)  6.45 us
  transfers between devices with their start and end apart: 54, of which 19 were waited for; matrix products, arithmetic and copies ran while one was open for 9% of the time, Pallas kernels for 13%

profile of v4, /device:TPU:0, one launch (start us, length us, event | category | flops | bytes accessed | tf_op | source)
XLA Modules:
  0.0 218.7 jit_solution(8197979402934512336)
XLA Ops:
  15.1 3.1 %collective-permute-start = (bf16[112,576]{1,0:T(8,128)(2,1)S(1)}, bf16[112,576]{1,0:T(8,128)(2,1)S(1)}, u32[]{:S(2)}, u32[]{:S(2)}) collective-permute-start(bf16[112,576]{1,0:T(8,128)(2,1)S(1)} %shard_map.262.refs_0_), channel_id=1, source_target_pairs={{0,1},{1,0},{2,3},{3,2},{4,5},{5,4},{6,7},{7,6},{8,9},{9,8},{10,11... | collective-permute-start | bytes 387080 | tf_op jit(solution)/shard_map/ppermute | solution.py:42
  21.7 2.6 %collective-permute-start.1 = (bf16[112,576]{1,0:T(8,128)(2,1)S(1)}, bf16[112,576]{1,0:T(8,128)(2,1)S(1)}, u32[]{:S(2)}, u32[]{:S(2)}) collective-permute-start(bf16[112,576]{1,0:T(8,128)(2,1)S(1)} %shard_map.262.refs_0_), channel_id=1, source_target_pairs={{0,2},{1,3},{2,0},{3,1},{4,6},{5,7},{6,4},{7,5},{8,10},{9,11},{10,... | collective-permute-start | bytes 387080 | tf_op jit(solution)/shard_map/ppermute | solution.py:42
  25.7 7.8 %collective-permute-done.1.refs_2_ = bf16[112,576]{1,0:T(8,128)(2,1)S(1)} collective-permute-done((bf16[112,576]{1,0:T(8,128)(2,1)S(1)}, bf16[112,576]{1,0:T(8,128)(2,1)S(1)}, u32[]{:S(2)}, u32[]{:S(2)}) %collective-permute-start.1) | collective-permute-done | bytes 129056 | tf_op jit(solution)/shard_map/ppermute | solution.py:42
  37.6 3.2 %collective-permute-start.6 = (bf16[96,768]{1,0:T(8,128)(2,1)S(1)}, bf16[96,768]{1,0:T(8,128)(2,1)S(1)}, u32[]{:S(2)}, u32[]{:S(2)}) collective-permute-start(bf16[96,768]{1,0:T(8,128)(2,1)S(1)} %slice.252), channel_id=1, source_target_pairs={{0,1},{1,0},{2,3},{3,2},{4,5},{5,4},{6,7},{7,6},{8,9},{9,8},{10,11... | collective-permute-start | bytes 442376 | tf_op jit(solution)/shard_map/ppermute | solution.py:42
  47.1 12.8 %collective-permute-done.7 = bf16[96,768]{1,0:T(8,128)(2,1)S(1)} collective-permute-done((bf16[96,768]{1,0:T(8,128)(2,1)S(1)}, bf16[96,768]{1,0:T(8,128)(2,1)S(1)}, u32[]{:S(2)}, u32[]{:S(2)}) %collective-permute-start.7) | collective-permute-done | bytes 147488 | tf_op jit(solution)/shard_map/ppermute | solution.py:42
  69.5 8.1 %shard_map.265 = (bf16[4,128,192]{2,1,0:T(8,128)(2,1)S(1)}, bf16[512,192]{1,0:T(8,128)(2,1)}, bf16[1024,192]{1,0:T(8,128)(2,1)}, bf16[1024,192]{1,0:T(8,128)(2,1...) custom-call(s32[2]{0:T(128)S(1)} %pad_add_fusion.place, ...), custom_call_target="tpu_custom_call" | custom-call | flops 1 | bytes 1 | tf_op jit(solution)/shard_map/pallas_call | solution.py:526
  83.5 2.4 %collective-permute-done.20 = bf16[128,192]{1,0:T(8,128)(2,1)S(1)} collective-permute-done((bf16[128,192]{1,0:T(8,128)(2,1)S(1)}, bf16[128,192]{1,0:T(8,128)(2,1)S(1)}, u32[]{:S(2)}, u32[]{:S(2)}) %collective-permute-start.20) | collective-permute-done | bytes 49184 | tf_op jit(solution)/shard_map/ppermute | solution.py:42
  87.9 2.4 %collective-permute-start.23 = (bf16[128,768]{1,0:T(8,128)(2,1)S(1)}, bf16[128,768]{1,0:T(8,128)(2,1)S(1)}, u32[]{:S(2)}, u32[]{:S(2)}) collective-permute-start(bf16[128,768]{1,0:T(8,128)(2,1)S(1)} %add_convert_fusion.2.refs_0_), channel_id=1, source_target_pairs={{0,24},{8,16},{16,8},{24,0},{1,25},{9,17},{17,9},{25,1},{2,26},{10... | collective-permute-start | bytes 589832 | tf_op jit(solution)/shard_map/ppermute | solution.py:42
  90.5 4.0 %collective-permute-done.21.refs_1_ = bf16[128,768]{1,0:T(8,128)(2,1)S(1)} collective-permute-done((bf16[128,768]{1,0:T(8,128)(2,1)S(1)}, bf16[128,768]{1,0:T(8,128)(2,1)S(1)}, u32[]{:S(2)}, u32[]{:S(2)}) %collective-permute-start.21) | collective-permute-done | bytes 196640 | tf_op jit(solution)/shard_map/ppermute | solution.py:42
  94.5 2.4 %collective-permute-done.22.refs_2_ = bf16[128,768]{1,0:T(8,128)(2,1)S(1)} collective-permute-done((bf16[128,768]{1,0:T(8,128)(2,1)S(1)}, bf16[128,768]{1,0:T(8,128)(2,1)S(1)}, u32[]{:S(2)}, u32[]{:S(2)}) %collective-permute-start.22) | collective-permute-done | bytes 196640 | tf_op jit(solution)/shard_map/ppermute | solution.py:42
  96.9 7.2 %shard_map.266 = (bf16[512,768]{1,0:T(8,128)(2,1)S(1)}, bf16[512,768]{1,0:T(8,128)(2,1)S(1)}, bf16[4,128,768]{2,1,0:T(8,128)(2,1)S(1)}, bf16[4,128,768]{2,1,0:T(8,128)(2,1)}, f32[1,768]{1,0:T(1,128)S(1)}) custom-call(bf16[128,768]{1,0:T(8,128)(2,1)S(1)} %add_convert_fusion.2.refs_0_, bf16[128,768]{1,0:T(8,128)(2,1)S(1)} %collective-permute-done.21.refs_1_, ...), custom_call_target="tpu_custom_call" | custom-call | flops 1 | bytes 1 | tf_op jit(solution)/shard_map/pallas_call | solution.py:395
  108.4 4.3 %shard_map.267 = bf16[768,1536]{1,0:T(8,128)(2,1)} custom-call(bf16[128,768]{1,0:T(8,128)(2,1)S(1)} %add_convert_fusion.2.refs_0_, bf16[128,768]{1,0:T(8,128)(2,1)S(1)} %collective-permute-done.21.refs_1_, bf16[128,768]{1,0:T(8,128)(2,1)S(1)} %collective-permute-done.22.refs_2_, bf16[128,768]{1,0:T(8,128)(2,1)S(1)} %collective-permute-done.23.refs_3_, ...), custom_call_target="tpu_custom_call" | custom-call | flops 1 | bytes 1 | tf_op jit(solution)/shard_map/pallas_call | solution.py:444
  122.4 2.4 %collective-permute-done.29.refs_3_ = bf16[128,192]{1,0:T(8,128)(2,1)S(1)} collective-permute-done((bf16[128,192]{1,0:T(8,128)(2,1)S(1)}, bf16[128,192]{1,0:T(8,128)(2,1)S(1)}, u32[]{:S(2)}, u32[]{:S(2)}) %collective-permute-start.29) | collective-permute-done | bytes 49184 | tf_op jit(solution)/shard_map/ppermute | solution.py:42
  129.6 8.4 %shard_map.268 = (bf16[512,192]{1,0:T(8,128)(2,1)S(1)}, bf16[2,512,384]{2,1,0:T(8,128)(2,1)S(1)}) custom-call(s32[2]{0:T(128)S(1)} %pad_add_fusion.place, bf16[128,192]{1,0:T(8,128)(2,1)S(1)} %get-tuple-element.143.refs_0_, bf16[128,192]{1,0:T(8,128)(2,1)S(1)} %collective-permute-done.27.refs_1_, bf16[128,192]{1,0:T(8,128)(2,1)S(1)} %collective-permute-done.28.refs_2_, ...), custom_call_target="tpu_custom_call" | custom-call | flops 1 | bytes 1 | tf_op jit(solution)/shard_map/pallas_call | solution.py:586
  139.8 3.5 %shard_map.269 = (bf16[4,128,768]{2,1,0:T(8,128)(2,1)S(1)}, bf16[768,576]{1,0:T(8,128)(2,1)S(1)}, f32[8,768]{1,0:T(8,128)S(1)}) custom-call(s32[2]{0:T(128)S(1)} %pad_add_fusion.place, bf16[512,192]{1,0:T(8,128)(2,1)S(1)} %get-tuple-element.152.refs_0_, bf16[512,384]{1,0:T(8,128)(2,1)S(1)} %get-tuple-element.240.refs_1_, ...), custom_call_target="tpu_custom_call" | custom-call | flops 1 | bytes 1 | tf_op jit(solution)/shard_map/pallas_call | solution.py:624
  148.0 3.2 %collective-permute-done.41 = bf16[128,768]{1,0:T(8,128)(2,1)S(1)} collective-permute-done((bf16[128,768]{1,0:T(8,128)(2,1)S(1)}, bf16[128,768]{1,0:T(8,128)(2,1)S(1)}, u32[]{:S(2)}, u32[]{:S(2)}) %collective-permute-start.41) | collective-permute-done | bytes 196640 | tf_op jit(solution)/shard_map/ppermute | solution.py:42
  151.2 4.6 %collective-permute-done.42 = bf16[128,768]{1,0:T(8,128)(2,1)} collective-permute-done((bf16[128,768]{1,0:T(8,128)(2,1)S(1)}, bf16[128,768]{1,0:T(8,128)(2,1)}, u32[]{:S(2)}, u32[]{:S(2)}) %collective-permute-start.42) | collective-permute-done | bytes 196640 | tf_op jit(solution)/shard_map/ppermute | solution.py:42
  161.6 7.3 %collective-permute-start.35 = (bf16[130,576]{1,0:T(8,128)(2,1)}, bf16[130,576]{1,0:T(8,128)(2,1)S(1)}, u32[]{:S(2)}, u32[]{:S(2)}) collective-permute-start(bf16[130,576]{1,0:T(8,128)(2,1)} %get-tuple-element.253), channel_id=1, source_target_pairs={{0,1},{1,0},{2,3},{3,2},{4,5},{5,4},{6,7},{7,6},{8,9},{9,8},{10,11... | collective-permute-start | bytes 449288 | tf_op jit(solution)/shard_map/ppermute | solution.py:42
  172.4 4.9 %collective-permute-start.36 = (bf16[130,576]{1,0:T(8,128)(2,1)S(1)}, bf16[130,576]{1,0:T(8,128)(2,1)S(1)}, u32[]{:S(2)}, u32[]{:S(2)}) collective-permute-start(bf16[130,576]{1,0:T(8,128)(2,1)S(1)} %get-tuple-element.252), channel_id=1, source_target_pairs={{0,2},{1,3},{2,0},{3,1},{4,6},{5,7},{6,4},{7,5},{8,10},{9,11},{10,... | collective-permute-start | bytes 449288 | tf_op jit(solution)/shard_map/ppermute | solution.py:42
  178.9 7.9 %collective-permute-done.36 = bf16[130,576]{1,0:T(8,128)(2,1)S(1)} collective-permute-done((bf16[130,576]{1,0:T(8,128)(2,1)S(1)}, bf16[130,576]{1,0:T(8,128)(2,1)S(1)}, u32[]{:S(2)}, u32[]{:S(2)}) %collective-permute-start.36) | collective-permute-done | bytes 149792 | tf_op jit(solution)/shard_map/ppermute | solution.py:42
  193.8 2.0 collective-permute-done.49
  201.9 2.6 %shard_map.271 = f32[192,2304]{1,0:T(8,128)} custom-call(bf16[4,192,576]{2,1,0:T(8,128)(2,1)S(1)} %bitcast.184), custom_call_target="tpu_custom_call" | custom-call | tf_op jit(solution)/shard_map/pallas_call | solution.py:296
  205.9 2.2 fusion.3
  208.5 3.4 %shard_map.272 = (f32[192,3072]{1,0:T(8,128)}, f32[4,192,768]{2,1,0:T(8,128)}) custom-call(bf16[4,192,1536]{2,1,0:T(8,128)(2,1)S(1)} %bitcast.176), custom_call_target="tpu_custom_call" | custom-call | tf_op jit(solution)/shard_map/pallas_call | solution.py:321
  (243 shorter events, 91.1 us)
Async XLA Ops:
  7.2 89.8 %all-gather.2.cloned.1.call-start = ((), (), s32[]{:S(2)}) async-start(), calls=%async_computation.1 | async-start | bytes 2654208 | tf_op jit(solution)/shard_map/all_gather | solution.py:707
  18.2 15.3 %collective-permute-start.3 = (bf16[128,768]{1,0:T(8,128)(2,1)}, bf16[128,768]{1,0:T(8,128)(2,1)S(1)}, u32[]{:S(2)}, u32[]{:S(2)}) collective-permute-start(bf16[128,768]{1,0:T(8,128)(2,1)} %bitcast.179), channel_id=1, source_target_pairs={{0,8},{8,0},{16,24},{24,16},{1,9},{9,1},{17,25},{25,17},{2,10},{10... | collective-permute-start | bytes 589832 | tf_op jit(solution)/shard_map/ppermute | solution.py:42
  19.7 13.8 %collective-permute-start.4 = (bf16[128,768]{1,0:T(8,128)(2,1)}, bf16[128,768]{1,0:T(8,128)(2,1)S(1)}, u32[]{:S(2)}, u32[]{:S(2)}) collective-permute-start(bf16[128,768]{1,0:T(8,128)(2,1)} %bitcast.180), channel_id=1, source_target_pairs={{0,16},{8,24},{16,0},{24,8},{1,17},{9,25},{17,1},{25,9},{2,18},{10... | collective-permute-start | bytes 589832 | tf_op jit(solution)/shard_map/ppermute | solution.py:42
  21.2 12.3 %collective-permute-start.5 = (bf16[128,768]{1,0:T(8,128)(2,1)}, bf16[128,768]{1,0:T(8,128)(2,1)S(1)}, u32[]{:S(2)}, u32[]{:S(2)}) collective-permute-start(bf16[128,768]{1,0:T(8,128)(2,1)} %bitcast.181), channel_id=1, source_target_pairs={{0,24},{8,16},{16,8},{24,0},{1,25},{9,17},{17,9},{25,1},{2,26},{10... | collective-permute-start | bytes 589832 | tf_op jit(solution)/shard_map/ppermute | solution.py:42
  21.7 11.8 %collective-permute-start.1 = (bf16[112,576]{1,0:T(8,128)(2,1)S(1)}, bf16[112,576]{1,0:T(8,128)(2,1)S(1)}, u32[]{:S(2)}, u32[]{:S(2)}) collective-permute-start(bf16[112,576]{1,0:T(8,128)(2,1)S(1)} %shard_map.262.refs_0_), channel_id=1, source_target_pairs={{0,2},{1,3},{2,0},{3,1},{4,6},{5,7},{6,4},{7,5},{8,10},{9,11},{10,... | collective-permute-start | bytes 387080 | tf_op jit(solution)/shard_map/ppermute | solution.py:42
  37.5 131.4 %reduce-scatter.2.cloned.1.call-start = ((), (), s32[]{:S(2)}) async-start(), calls=%async_computation.2 | async-start | bytes 2654208 | tf_op jit(solution)/shard_map/reduce_scatter | solution.py:733
  40.9 19.1 %collective-permute-start.7 = (bf16[96,768]{1,0:T(8,128)(2,1)S(1)}, bf16[96,768]{1,0:T(8,128)(2,1)S(1)}, u32[]{:S(2)}, u32[]{:S(2)}) collective-permute-start(bf16[96,768]{1,0:T(8,128)(2,1)S(1)} %slice.252), channel_id=1, source_target_pairs={{0,2},{1,3},{2,0},{3,1},{4,6},{5,7},{6,4},{7,5},{8,10},{9,11},{10,... | collective-permute-start | bytes 442376 | tf_op jit(solution)/shard_map/ppermute | solution.py:42
  42.0 18.0 %collective-permute-start.8 = (bf16[96,768]{1,0:T(8,128)(2,1)S(1)}, bf16[96,768]{1,0:T(8,128)(2,1)S(1)}, u32[]{:S(2)}, u32[]{:S(2)}) collective-permute-start(bf16[96,768]{1,0:T(8,128)(2,1)S(1)} %slice.252), channel_id=1, source_target_pairs={{0,3},{1,2},{2,1},{3,0},{4,7},{5,6},{6,5},{7,4},{8,11},{9,10},{10,... | collective-permute-start | bytes 442376 | tf_op jit(solution)/shard_map/ppermute | solution.py:42
  43.4 17.1 %collective-permute-start.10 = (bf16[128,768]{1,0:T(8,128)(2,1)}, bf16[128,768]{1,0:T(8,128)(2,1)}, u32[]{:S(2)}, u32[]{:S(2)}) collective-permute-start(bf16[128,768]{1,0:T(8,128)(2,1)} %bitcast.3.refs_4_), channel_id=1, source_target_pairs={{0,16},{8,24},{16,0},{24,8},{1,17},{9,25},{17,1},{25,9},{2,18},{10... | collective-permute-start | bytes 589832 | tf_op jit(solution)/shard_map/ppermute | solution.py:42
  45.0 15.6 %collective-permute-start.11 = (bf16[128,768]{1,0:T(8,128)(2,1)}, bf16[128,768]{1,0:T(8,128)(2,1)}, u32[]{:S(2)}, u32[]{:S(2)}) collective-permute-start(bf16[128,768]{1,0:T(8,128)(2,1)} %bitcast.3.refs_4_), channel_id=1, source_target_pairs={{0,24},{8,16},{16,8},{24,0},{1,25},{9,17},{17,9},{25,1},{2,26},{10... | collective-permute-start | bytes 589832 | tf_op jit(solution)/shard_map/ppermute | solution.py:42
  46.6 15.3 %collective-permute-start.9 = (bf16[128,768]{1,0:T(8,128)(2,1)}, bf16[128,768]{1,0:T(8,128)(2,1)S(1)}, u32[]{:S(2)}, u32[]{:S(2)}) collective-permute-start(bf16[128,768]{1,0:T(8,128)(2,1)} %bitcast.3.refs_4_), channel_id=1, source_target_pairs={{0,8},{8,0},{16,24},{24,16},{1,9},{9,1},{17,25},{25,17},{2,10},{10... | collective-permute-start | bytes 589832 | tf_op jit(solution)/shard_map/ppermute | solution.py:42
  126.0 12.2 %collective-permute-start.31 = (bf16[4,48,768]{2,1,0:T(8,128)(2,1)S(1)}, bf16[4,48,768]{2,1,0:T(8,128)(2,1)S(1)}, u32[]{:S(2)}, u32[]{:S(2)}) collective-permute-start(bf16[4,48,768]{2,1,0:T(8,128)(2,1)S(1)} %get-tuple-element.160), channel_id=1, source_target_pairs={{0,8},{8,0},{16,24},{24,16},{1,9},{9,1},{17,25},{25,17},{2,10},{10... | collective-permute-start | bytes 884744 | tf_op jit(solution)/shard_map/ppermute | solution.py:42
  127.4 10.8 %collective-permute-start.32 = (bf16[4,48,768]{2,1,0:T(8,128)(2,1)S(1)}, bf16[4,48,768]{2,1,0:T(8,128)(2,1)S(1)}, u32[]{:S(2)}, u32[]{:S(2)}) collective-permute-start(bf16[4,48,768]{2,1,0:T(8,128)(2,1)S(1)} %get-tuple-element.161), channel_id=1, source_target_pairs={{0,16},{8,24},{16,0},{24,8},{1,17},{9,25},{17,1},{25,9},{2,18},{10... | collective-permute-start | bytes 884744 | tf_op jit(solution)/shard_map/ppermute | solution.py:42
  144.8 11.0 %collective-permute-start.42 = (bf16[128,768]{1,0:T(8,128)(2,1)S(1)}, bf16[128,768]{1,0:T(8,128)(2,1)}, u32[]{:S(2)}, u32[]{:S(2)}) collective-permute-start(bf16[128,768]{1,0:T(8,128)(2,1)S(1)} %get-tuple-element.236), channel_id=1, source_target_pairs={{0,16},{8,24},{16,0},{24,8},{1,17},{9,25},{17,1},{25,9},{2,18},{10... | collective-permute-start | bytes 589832 | tf_op jit(solution)/shard_map/ppermute | solution.py:42
  145.7 10.1 %collective-permute-start.43 = (bf16[128,768]{1,0:T(8,128)(2,1)S(1)}, bf16[128,768]{1,0:T(8,128)(2,1)}, u32[]{:S(2)}, u32[]{:S(2)}) collective-permute-start(bf16[128,768]{1,0:T(8,128)(2,1)S(1)} %get-tuple-element.235), channel_id=1, source_target_pairs={{0,24},{8,16},{16,8},{24,0},{1,25},{9,17},{17,9},{25,1},{2,26},{10... | collective-permute-start | bytes 589832 | tf_op jit(solution)/shard_map/ppermute | solution.py:42
  147.9 12.7 %collective-permute-start.34 = (bf16[4,130,576]{2,0,1:T(4,128)(2,1)S(1)}, bf16[4,130,576]{2,0,1:T(4,128)(2,1)S(1)}, u32[]{:S(2)}, u32[]{:S(2)}) collective-permute-start(bf16[4,130,576]{2,0,1:T(4,128)(2,1)S(1)} %copy.100), channel_id=1, source_target_pairs={{0,4},{4,0},{1,5},{5,1},{2,6},{6,2},{3,7},{7,3},{8,12},{12,8},{9,1... | collective-permute-start | bytes 1797128 | tf_op jit(solution)/shard_map/ppermute | solution.py:42
  155.8 13.9 %collective-permute-start.44 = (bf16[128,768]{1,0:T(8,128)(2,1)S(1)}, bf16[128,768]{1,0:T(8,128)(2,1)S(1)}, u32[]{:S(2)}, u32[]{:S(2)}) collective-permute-start(bf16[128,768]{1,0:T(8,128)(2,1)S(1)} %get-tuple-element.233), channel_id=1, source_target_pairs={{0,8},{8,0},{16,24},{24,16},{1,9},{9,1},{17,25},{25,17},{2,10},{10... | collective-permute-start | bytes 589832 | tf_op jit(solution)/shard_map/ppermute | solution.py:42
  156.6 14.2 %collective-permute-start.45 = (bf16[128,768]{1,0:T(8,128)(2,1)S(1)}, bf16[128,768]{1,0:T(8,128)(2,1)S(1)}, u32[]{:S(2)}, u32[]{:S(2)}) collective-permute-start(bf16[128,768]{1,0:T(8,128)(2,1)S(1)} %get-tuple-element.232), channel_id=1, source_target_pairs={{0,16},{8,24},{16,0},{24,8},{1,17},{9,25},{17,1},{25,9},{2,18},{10... | collective-permute-start | bytes 589832 | tf_op jit(solution)/shard_map/ppermute | solution.py:42
  157.8 14.6 %collective-permute-start.46 = (bf16[128,768]{1,0:T(8,128)(2,1)S(1)}, bf16[128,768]{1,0:T(8,128)(2,1)S(1)}, u32[]{:S(2)}, u32[]{:S(2)}) collective-permute-start(bf16[128,768]{1,0:T(8,128)(2,1)S(1)} %get-tuple-element.231), channel_id=1, source_target_pairs={{0,24},{8,16},{16,8},{24,0},{1,25},{9,17},{17,9},{25,1},{2,26},{10... | collective-permute-start | bytes 589832 | tf_op jit(solution)/shard_map/ppermute | solution.py:42
  161.6 15.7 %collective-permute-start.35 = (bf16[130,576]{1,0:T(8,128)(2,1)}, bf16[130,576]{1,0:T(8,128)(2,1)S(1)}, u32[]{:S(2)}, u32[]{:S(2)}) collective-permute-start(bf16[130,576]{1,0:T(8,128)(2,1)} %get-tuple-element.253), channel_id=1, source_target_pairs={{0,1},{1,0},{2,3},{3,2},{4,5},{5,4},{6,7},{7,6},{8,9},{9,8},{10,11... | collective-permute-start | bytes 449288 | tf_op jit(solution)/shard_map/ppermute | solution.py:42
  168.9 17.9 %collective-permute-start.38 = (bf16[96,1536]{1,0:T(8,128)(2,1)}, bf16[96,1536]{1,0:T(8,128)(2,1)S(1)}, u32[]{:S(2)}, u32[]{:S(2)}) collective-permute-start(bf16[96,1536]{1,0:T(8,128)(2,1)} %reduce-scatter.2.cloned.1.call-done), channel_id=1, source_target_pairs={{0,8},{8,0},{16,24},{24,16},{1,9},{9,1},{17,25},{25,17},{2,10},{10... | collective-permute-start | bytes 884744 | tf_op jit(solution)/shard_map/ppermute | solution.py:42
  169.7 17.1 %collective-permute-start.39 = (bf16[96,1536]{1,0:T(8,128)(2,1)}, bf16[96,1536]{1,0:T(8,128)(2,1)S(1)}, u32[]{:S(2)}, u32[]{:S(2)}) collective-permute-start(bf16[96,1536]{1,0:T(8,128)(2,1)} %reduce-scatter.2.cloned.1.call-done), channel_id=1, source_target_pairs={{0,16},{8,24},{16,0},{24,8},{1,17},{9,25},{17,1},{25,9},{2,18},{10... | collective-permute-start | bytes 884744 | tf_op jit(solution)/shard_map/ppermute | solution.py:42
  170.8 16.0 %collective-permute-start.40 = (bf16[96,1536]{1,0:T(8,128)(2,1)}, bf16[96,1536]{1,0:T(8,128)(2,1)S(1)}, u32[]{:S(2)}, u32[]{:S(2)}) collective-permute-start(bf16[96,1536]{1,0:T(8,128)(2,1)} %reduce-scatter.2.cloned.1.call-done), channel_id=1, source_target_pairs={{0,24},{8,16},{16,8},{24,0},{1,25},{9,17},{17,9},{25,1},{2,26},{10... | collective-permute-start | bytes 884744 | tf_op jit(solution)/shard_map/ppermute | solution.py:42
  172.4 14.4 %collective-permute-start.36 = (bf16[130,576]{1,0:T(8,128)(2,1)S(1)}, bf16[130,576]{1,0:T(8,128)(2,1)S(1)}, u32[]{:S(2)}, u32[]{:S(2)}) collective-permute-start(bf16[130,576]{1,0:T(8,128)(2,1)S(1)} %get-tuple-element.252), channel_id=1, source_target_pairs={{0,2},{1,3},{2,0},{3,1},{4,6},{5,7},{6,4},{7,5},{8,10},{9,11},{10,... | collective-permute-start | bytes 449288 | tf_op jit(solution)/shard_map/ppermute | solution.py:42
  (55 other events, 298.4 us)
Sparse Core Ops, SparseCore 0:
  37.7 39.2 all-gather.1
  115.1 41.8 reduce-scatter.1

commit v5 on v4

--- a/solution.py
+++ b/solution.py
@@ -16,6 +16,7 @@
 GELU_CUBE = 0.044715
 
 SHORT = pl.CostEstimate(flops=1, bytes_accessed=1, transcendentals=0)
+LONG = pl.CostEstimate(flops=8 * 10**9, bytes_accessed=1, transcendentals=0)
 
 BF = jnp.bfloat16
 F32 = jnp.float32
@@ -119,8 +120,15 @@
 
 
 def cut_first_kernel(place, *refs):
-    source, vectors, cut, held = refs[0], refs[1:-2], refs[-2], refs[-1]
-    rows, wide = source.shape
+    source, other, vectors, cut, held = refs[0], refs[1], refs[2:-2], refs[-2], refs[-1]
+    rows = source.shape[0]
+    third, cols = rows // 3, cut.shape[1]
+    cut[rows + 16 : 2 * rows + 16, :] = other[:, :cols]
+    over = other.shape[1] - cols
+    for part in range(3):
+        cut[2 * rows + 16 :, part * over : (part + 1) * over] = other[
+            part * third : (part + 1) * third, cols:
+        ]
     unit = vectors[0].shape[0]
     per = cut.shape[1] // unit
     held[...] = jnp.zeros_like(held)
@@ -133,7 +141,7 @@
                 :, part * unit : (part + 1) * unit
             ]
             spot += 1
-    cut[rows:, :] = held[...].astype(BF)
+    cut[rows : rows + 16, :] = held[...].astype(BF)
     for i in range(GROUPS):
 
         @pl.when(place[0] == i)
@@ -141,21 +149,62 @@
             cut_columns(source, cut.at[:rows, :], 3, i)
 
 
-def cut_first(weight, vectors, g, k, ks):
+def cut_first(weight, other, vectors, g, k, ks):
     rows, cols = weight.shape[0] // ks, weight.shape[1] // GROUPS
+    tall = 2 * rows + 16 + rows // 3
+    by_k = lambda i, place: (place[1], 0)
     return pl.pallas_call(
         cut_first_kernel,
         grid_spec=pltpu.PrefetchScalarGridSpec(
             num_scalar_prefetch=1,
             grid=(1,),
-            in_specs=[pl.BlockSpec((rows, weight.shape[1]), lambda i, place: (place[1], 0))]
+            in_specs=[
+                pl.BlockSpec((rows, weight.shape[1]), by_k),
+                pl.BlockSpec((rows, other.shape[1]), by_k),
+            ]
             + [pl.BlockSpec(v.shape, lambda i, place: (0,)) for v in vectors],
-            out_specs=pl.BlockSpec((rows + 16, cols), lambda i, place: (0, 0)),
+            out_specs=pl.BlockSpec((tall, cols), lambda i, place: (0, 0)),
             scratch_shapes=[pltpu.VMEM((16, cols), F32)],
         ),
-        out_shape=jax.ShapeDtypeStruct((rows + 16, cols), BF),
+        out_shape=jax.ShapeDtypeStruct((tall, cols), BF),
         compiler_params=pltpu.CompilerParams(vmem_limit_bytes=8 * 2**20),
-    )(jnp.stack([g, k]).astype(jnp.int32), weight, *vectors)
+        cost_estimate=SHORT,
+    )(jnp.stack([g, k]).astype(jnp.int32), *in_hbm(weight, other, *vectors))
+
+
+def both_weights_kernel(rows, place, *refs):
+    pieces, in_w, out_w = refs[:-2], refs[-2], refs[-1]
+    zs, ks = in_w.shape[:2]
+    third, cols = rows // 3, in_w.shape[3]
+    over = out_w.shape[3] - cols
+    low = rows + 16
+    for j in range(ks):
+        for i in range(zs):
+            piece = pieces[j * zs + i]
+            in_w[place[1] ^ i, place[2] ^ j] = piece[:rows, :]
+            spot = (place[1] ^ i ^ place[0], place[2] ^ j)
+            out_w[spot[0], spot[1], :, :cols] = piece[low : low + rows, :]
+            for part in range(3):
+                out_w[spot[0], spot[1], part * third : (part + 1) * third, cols:] = piece[
+                    low + rows :, part * over : (part + 1) * over
+                ]
+
+
+def both_weights(pieces, g, z, k, rows, width):
+    ks, zs = len(pieces), len(pieces[0])
+    cols = pieces[0][0].shape[1]
+    vmem = pl.BlockSpec(memory_space=pltpu.VMEM)
+    shapes = [(zs, ks, rows, cols), (zs, ks, rows, width)]
+    in_w, out_w = pl.pallas_call(
+        functools.partial(both_weights_kernel, rows),
+        grid_spec=pltpu.PrefetchScalarGridSpec(
+            num_scalar_prefetch=1, in_specs=[vmem] * (zs * ks), out_specs=[vmem] * 2
+        ),
+        out_shape=[jax.ShapeDtypeStruct(s, BF) for s in shapes],
+        compiler_params=pltpu.CompilerParams(vmem_limit_bytes=16 * 2**20),
+        cost_estimate=SHORT,
+    )(jnp.stack([g, z, k]).astype(jnp.int32), *[p for group in pieces for p in group])
+    return in_w.reshape(width, cols), out_w.reshape(width, width)
 
 
 def table_kernel(unit, place, *refs):
@@ -184,14 +233,14 @@
             out[2:4, :cols] = out[10:12, i * cols : (i + 1) * cols]
 
 
-def vector_table(pieces, unit, width, g, z):
-    rows, cols = pieces[0].shape
+def vector_table(pieces, below, unit, width, g, z):
+    cols = pieces[0].shape[1]
     return pl.pallas_call(
         functools.partial(table_kernel, unit),
         grid_spec=pltpu.PrefetchScalarGridSpec(
             num_scalar_prefetch=1,
             grid=(1,),
-            in_specs=[pl.BlockSpec((16, cols), lambda i, place: (rows // 16 - 1, 0))] * len(pieces),
+            in_specs=[pl.BlockSpec((16, cols), lambda i, place: (below // 16, 0))] * len(pieces),
             out_specs=pl.BlockSpec((16, width), lambda i, place: (0, 0)),
             scratch_shapes=[pltpu.VMEM((len(pieces), 16, cols), F32)],
         ),
@@ -239,24 +288,21 @@
     )(jnp.stack([g]).astype(jnp.int32), sums, *vectors)
 
 
-def cut_rest_kernel(parts, place, con_ref, exp_ref, out_ref, cut):
+def cut_rest_kernel(parts, place, con_ref, exp_ref, cut):
     width = con_ref.shape[1]
-    wide = exp_ref.shape[1] // GROUPS
     cut[:, :width] = con_ref[...]
-    cut[:, width + wide :] = out_ref[...]
     for i in range(GROUPS):
 
         @pl.when(place[0] == i)
         def _():
-            cut_columns(exp_ref, cut.at[:, width : width + wide], parts, i)
-
-
-def cut_rest(con_w, exp_w, out_w, parts, g, k, ks):
-    width = out_w.shape[1]
-    rows, ff_rows = out_w.shape[0] // ks, con_w.shape[0] // (GROUPS * ks)
+            cut_columns(exp_ref, cut.at[:, width:], parts, i)
+
+
+def cut_rest(con_w, exp_w, parts, g, k, ks):
+    width = con_w.shape[1]
+    rows, ff_rows = exp_w.shape[0] // ks, con_w.shape[0] // (GROUPS * ks)
     wide = exp_w.shape[1] // GROUPS
     if rows % 16 == 0 and rows == ff_rows:
-        by_k = lambda i, place: (place[1], 0)
         return pl.pallas_call(
             functools.partial(cut_rest_kernel, parts),
             grid_spec=pltpu.PrefetchScalarGridSpec(
@@ -264,22 +310,48 @@
                 grid=(1,),
                 in_specs=[
                     pl.BlockSpec((rows, width), lambda i, place: (place[0] * ks + place[1], 0)),
-                    pl.BlockSpec((rows, exp_w.shape[1]), by_k),
-                    pl.BlockSpec((rows, width), by_k),
+                    pl.BlockSpec((rows, exp_w.shape[1]), lambda i, place: (place[1], 0)),
                 ],
-                out_specs=pl.BlockSpec((rows, 2 * width + wide), lambda i, place: (0, 0)),
+                out_specs=pl.BlockSpec((rows, width + wide), lambda i, place: (0, 0)),
             ),
-            out_shape=jax.ShapeDtypeStruct((rows, 2 * width + wide), BF),
+            out_shape=jax.ShapeDtypeStruct((rows, width + wide), BF),
             compiler_params=pltpu.CompilerParams(vmem_limit_bytes=8 * 2**20),
-        )(jnp.stack([g, k]).astype(jnp.int32), con_w, exp_w, out_w)
+        )(jnp.stack([g, k]).astype(jnp.int32), *in_hbm(con_w, exp_w))
     return jnp.concatenate(
         [
             pick(con_w.reshape(GROUPS * ks, ff_rows, width), g * ks + k),
             cut_weight(exp_w, parts, g, k, ks),
-            pick(out_w.reshape(ks, rows, width), k),
         ],
         axis=1,
     )
+
+
+def assemble_kernel(rows, place, *refs):
+    pieces, out = refs[:-1], refs[-1]
+    zs = out.shape[0]
+    for j in range(out.shape[1]):
+        for i in range(zs):
+            out[place[0] ^ i, place[1] ^ j] = pieces[j * zs + i][:rows, :]
+
+
+def assemble(pieces, first, k, rows):
+    ks, zs = len(pieces), len(pieces[0])
+    cols = pieces[0][0].shape[1]
+    shape = (zs, ks, rows, cols)
+    if rows % 16:
+        parts = [in_order([p[:rows] for p in group], first) for group in pieces]
+        return jnp.stack(in_order(parts, k), axis=1).reshape(zs, ks * rows, cols)
+    vmem = pl.BlockSpec(memory_space=pltpu.VMEM)
+    out = pl.pallas_call(
+        functools.partial(assemble_kernel, rows),
+        grid_spec=pltpu.PrefetchScalarGridSpec(
+            num_scalar_prefetch=1, in_specs=[vmem] * (zs * ks), out_specs=vmem
+        ),
+        out_shape=jax.ShapeDtypeStruct(shape, BF),
+        compiler_params=pltpu.CompilerParams(vmem_limit_bytes=8 * 2**20),
+        cost_estimate=SHORT,
+    )(jnp.stack([first, k]).astype(jnp.int32), *[p for group in pieces for p in group])
+    return out.reshape(zs, ks * rows, cols)
 
 
 def weave_kernel(parts, pieces, out):
@@ -303,41 +375,51 @@
     )(pieces)
 
 
-def unfold_kernel(parts, pieces, exp_out, con_out):
-    wide = con_out.shape[2]
+def unfold_kernel(parts, ks, place, *refs):
+    pieces, (exp_out, con_out, held) = refs[:-3], refs[-3:]
+    wide = con_out.shape[3]
     part_wide = wide // parts
-    for i in range(GROUPS):
-        con_out[i] = pieces[i, :, wide:].astype(F32)
-        for part in range(parts):
-            low = (part * GROUPS + i) * part_wide
-            exp_out[:, low : low + part_wide] = pieces[
-                i, :, part * part_wide : (part + 1) * part_wide
-            ].astype(F32)
-
-
-def unfold(pieces, parts):
-    rows, wide = pieces.shape[1], pieces.shape[2] // 2
-    step = 32
-    return pl.pallas_call(
-        functools.partial(unfold_kernel, parts),
-        grid=(rows // step,),
-        in_specs=[pl.BlockSpec((GROUPS, step, 2 * wide), lambda i: (0, i, 0))],
-        out_specs=[
-            pl.BlockSpec((step, GROUPS * wide), lambda i: (i, 0)),
-            pl.BlockSpec((GROUPS, step, wide), lambda i: (0, i, 0)),
-        ],
-        out_shape=[
-            jax.ShapeDtypeStruct((rows, GROUPS * wide), F32),
-            jax.ShapeDtypeStruct((GROUPS, rows, wide), F32),
-        ],
-        compiler_params=pltpu.CompilerParams(vmem_limit_bytes=16 * 2**20),
-    )(pieces)
+    for j in range(ks):
+        for i in range(GROUPS):
+            held[place[0] ^ i] = pieces[j * GROUPS + i][...]
+        spot = place[1] ^ j
+        for i in range(GROUPS):
+            con_out[i, spot] = held[i, :, wide:].astype(F32)
+            for part in range(parts):
+                low = (part * GROUPS + i) * part_wide
+                exp_out[spot, :, low : low + part_wide] = held[
+                    i, :, part * part_wide : (part + 1) * part_wide
+                ].astype(F32)
+
+
+def unfold(pieces, parts, g, k):
+    ks = len(pieces)
+    rows, wide = pieces[0][0].shape[0], pieces[0][0].shape[1] // 2
+    step = rows // 2 if rows % 32 == 0 else rows
+    shapes = [(ks, rows, GROUPS * wide), (GROUPS, ks, rows, wide)]
+    exp, con = pl.pallas_call(
+        functools.partial(unfold_kernel, parts, ks),
+        grid_spec=pltpu.PrefetchScalarGridSpec(
+            num_scalar_prefetch=1,
+            grid=(rows // step,),
+            in_specs=[pl.BlockSpec((step, 2 * wide), lambda i, place: (i, 0))] * (ks * GROUPS),
+            out_specs=[
+                pl.BlockSpec((ks, step, GROUPS * wide), lambda i, place: (0, i, 0)),
+                pl.BlockSpec((GROUPS, ks, step, wide), lambda i, place: (0, 0, i, 0)),
+            ],
+            scratch_shapes=[pltpu.VMEM((GROUPS, step, 2 * wide), BF)],
+        ),
+        out_shape=[jax.ShapeDtypeStruct(s, F32) for s in shapes],
+        compiler_params=pltpu.CompilerParams(vmem_limit_bytes=20 * 2**20),
+        cost_estimate=SHORT,
+    )(jnp.stack([g, k]).astype(jnp.int32), *[p for group in pieces for p in group])
+    return exp.reshape(ks * rows, -1), con.reshape(-1, wide)
 
 
 def join_rows(pieces, joined):
-    tok = pieces[0].shape[0]
+    tok = joined.shape[0] // GROUPS
     for i, piece in enumerate(pieces):
-        joined[i * tok : (i + 1) * tok, :] = piece[...]
+        joined[i * tok : (i + 1) * tok, :] = piece[...].reshape(tok, joined.shape[1])
 
 
 def hidden_kernel(*refs):
@@ -395,7 +477,8 @@
     return pl.pallas_call(
         hidden_kernel,
         grid=(hidden // step,),
-        in_specs=[pl.BlockSpec((tok, width), fixed)] * (2 * GROUPS)
+        in_specs=[pl.BlockSpec((tok, width), fixed)] * GROUPS
+        + [pl.BlockSpec((1, tok, width), lambda i: (1, 0, 0))] * GROUPS
         + [
             pl.BlockSpec((width, step), lambda i: (0, width // step + i)),
             pl.BlockSpec((step, width), lambda i: (i, 0)),
@@ -445,13 +528,13 @@
         hidden_grad_kernel,
         grid=(width // step,),
         in_specs=[pl.BlockSpec((tok, step), cols)] * GROUPS
-        + [pl.BlockSpec((tok, width), fixed)] * GROUPS
+        + [pl.BlockSpec((1, tok, width), lambda i: (1, 0, 0))] * GROUPS
         + [pl.BlockSpec((rows, hidden), fixed), pl.BlockSpec((rows, step), cols)],
         out_specs=pl.BlockSpec((step, hidden + width), lambda i: (i, 0)),
         out_shape=jax.ShapeDtypeStruct((width, hidden + width), BF),
         scratch_shapes=[pltpu.VMEM((rows, step), BF), pltpu.VMEM((rows, width), BF)],
         compiler_params=pltpu.CompilerParams(vmem_limit_bytes=16 * 2**20),
-        cost_estimate=SHORT,
+        cost_estimate=LONG,
     )(*h_rows, *in_hbm(*s_rows), slope_inner, act)
 
 
@@ -473,12 +556,13 @@
     in_w, table = refs[GROUPS * ks : GROUPS * ks + 2]
     slots, q_out, k_out, v_out, att_out, lse_out, h_out, hat_out, h_all = refs[GROUPS * ks + 2 :]
     g, k = place[0], place[1]
-    tok, width = pieces[0].shape
+    tok, width = pieces[-1].shape
     cols = q_out.shape[1]
     gain, shift = table[0:1, :], table[1:2, :]
     for j in range(ks):
         for i in range(GROUPS):
-            hat, _ = norm_stats(pieces[j * GROUPS + i][...].astype(F32))
+            piece = pieces[j * GROUPS + i]
+            hat, _ = norm_stats((piece[...] if j else piece[0]).astype(F32))
             normed = (hat * gain + shift).astype(BF)
             spot = pl.multiple_of(((g ^ i) * ks + (k ^ j)) * tok, tok)
             h_all[pl.ds(spot, tok), :] = normed
@@ -508,8 +592,8 @@
         slots[g ^ i] = att_out[i * tok : (i + 1) * tok, :].astype(BF)
 
 
-def attend(g, k, ks, head, pieces, in_w, table):
-    tok, width = pieces[0].shape
+def attend(g, k, ks, head, both, more, in_w, table):
+    tok, width = both[0].shape[1:]
     cols = in_w.shape[1] // 3
     mine, rows = GROUPS * tok, GROUPS * ks * tok
     vmem = pl.BlockSpec(memory_space=pltpu.VMEM)
@@ -527,14 +611,16 @@
         functools.partial(attend_kernel, ks, head),
         grid_spec=pltpu.PrefetchScalarGridSpec(
             num_scalar_prefetch=1,
-            in_specs=[vmem] * (len(pieces) + 2),
+            in_specs=[pl.BlockSpec((1, tok, width), lambda i, place: (0, 0, 0))] * GROUPS
+            + [vmem] * (len(more) + 2),
+            grid=(1,),
             out_specs=[vmem] * len(shapes),
             scratch_shapes=[pltpu.VMEM((rows, width), BF)],
         ),
         out_shape=[jax.ShapeDtypeStruct(*shapes[0])] + [pltpu.HBM(s, t) for s, t in shapes[1:]],
         compiler_params=pltpu.CompilerParams(vmem_limit_bytes=(16 if ks == 2 else 48) * 2**20),
         cost_estimate=SHORT,
-    )(jnp.stack([g, k]).astype(jnp.int32), *pieces, in_w, table)
+    )(jnp.stack([g, k]).astype(jnp.int32), *both, *more, in_w, table)
 
 
 def attend_back_kernel(ks, head, place, *refs):
@@ -596,7 +682,7 @@
             jax.ShapeDtypeStruct((ks, mine, 2 * cols), BF),
         ],
         compiler_params=pltpu.CompilerParams(vmem_limit_bytes=(16 if ks == 2 else 48) * 2**20),
-        cost_estimate=SHORT,
+        cost_estimate=LONG,
     )(jnp.stack([g, k]).astype(jnp.int32), *slopes, *in_hbm(q, keys, values, att, lse))
 
 
@@ -672,21 +758,30 @@
     x_own = inputs[0]
     slope_own = cotangent[0]
 
-    x_rows = gather_flips(x_own, "grp")
-
     smalls = [first_gain, first_shift, query_bias, value_bias, output_bias]
     smalls += [second_gain, second_shift, contract_bias, expand_bias]
     own = rows_z // ks
-    aligned = own % 16 == 0
+    aligned = own % 48 == 0 and zs == GROUPS
     if aligned:
-        in_pieces = gather_flips(cut_first(input_weight, smalls, g, k, ks), "fsdp")
+        cut = cut_first(input_weight, output_weight, smalls, g, k, ks)
     else:
-        in_pieces = gather_flips(cut_weight(input_weight, 3, g, k, ks), "fsdp")
-    in_pieces, x_rows = lax.optimization_barrier((in_pieces, x_rows))
-    x_more = [[send(b, "core", j) for b in x_rows] for j in range(1, ks)]
+        cut = cut_weight(input_weight, 3, g, k, ks)
+    pieces = gather_flips(cut, "fsdp")
+    rows_both = gather_flips(jnp.concatenate([inputs, cotangent]), "grp")
+    pieces, rows_both, con_raw, exp_raw = lax.optimization_barrier(
+        (pieces, rows_both, contract_weight, expand_weight)
+    )
+    x_more = [send(b[0], "core", j) for j in range(1, ks) for b in rows_both]
+    more = [[send(b, "core", j) for b in pieces] for j in range(1, ks)]
     if aligned:
-        table = vector_table(in_pieces, rows_z, width, g, z)
+        table = vector_table(pieces, own, rows_z, width, g, z)
+        in_w, out_w = both_weights([pieces] + more, g, z, k, own, width)
     else:
+        in_w = assemble([pieces] + more, z, k, own).reshape(width, 3 * cols)
+        out_w = gather_flips(pick(output_weight.reshape(ks, own, width), k), "fsdp")
+        out_more = [[send(b, "core", j) for b in out_w] for j in range(1, ks)]
+        out_w = assemble([out_w] + out_more, z, k, own).reshape(GROUPS, cols, width)
+        out_w = jnp.concatenate([pick(out_w, g ^ i) for i in range(GROUPS)])
         got = in_order(gather_flips(jnp.concatenate(smalls), "fsdp"), z).astype(F32)
         vectors = [got[:, i * rows_z : (i + 1) * rows_z].reshape(width) for i in range(8)]
         for i in (2, 3):
@@ -696,25 +791,11 @@
         table = jnp.pad(jnp.stack(vectors), ((0, 7), (0, 0)))
     o_bias, gain_two, shift_two, c_bias = [table[i : i + 1] for i in range(4, 8)]
 
-    con_raw, exp_raw, out_raw, slope_late, in_pieces = lax.optimization_barrier(
-        (contract_weight, expand_weight, output_weight, slope_own, in_pieces)
-    )
-    in_half = in_order([p[:own] for p in in_pieces], z)
-    in_w = jnp.stack(in_order(gather_flips(in_half, "core"), k), axis=1).reshape(width, 3 * cols)
-    rest = cut_rest(con_raw, exp_raw, out_raw, zs, g, k, ks)
-    split = width + zs * ff_g
-    out_pieces = gather_flips(rest[:, split:], "fsdp")
-    rest = lax.all_gather(rest[:, :split], ("fsdp", "core"), axis=0, tiled=True)
-
-    slope_rows = gather_flips(slope_late, "grp")
-    out_pieces, slope_rows, x_more = lax.optimization_barrier((out_pieces, slope_rows, x_more))
-    half = in_order(out_pieces, z)
-    out_w = jnp.stack(in_order(gather_flips(half, "core"), k), axis=1)
-    out_w = out_w.reshape(GROUPS, cols, width)
-    out_w = jnp.concatenate([pick(out_w, g ^ i) for i in range(GROUPS)])
-    in_w, out_w = lax.optimization_barrier((in_w, out_w))
+    rest = cut_rest(con_raw, exp_raw, zs, g, k, ks)
+    rest = lax.all_gather(rest, ("fsdp", "core"), axis=0, tiled=True)
+
     slots, qs, keys, values, att_full, lse, h1, hat_one = attend(
-        g, k, ks, head, x_rows + [b for bs in x_more for b in bs], in_w, table
+        g, k, ks, head, rows_both, x_more, in_w, table
     )
     att = jnp.concatenate(swap_flips([slots[i] for i in range(GROUPS)], "grp"), axis=1)
     x_f = x_own.astype(F32)
@@ -724,10 +805,10 @@
     h2_rows = gather_flips(h2, "grp")
 
     act, slope_inner, sh2_part, out_part, d_exp_b = hidden_part(
-        h2_rows, slope_rows, rest, table
+        h2_rows, rows_both, rest, table
     )
     sh2 = swap_flips([sh2_part[i] for i in range(GROUPS)], "grp")
-    d_hidden = hidden_grads(h2_rows, slope_rows, slope_inner, act)
+    d_hidden = hidden_grads(h2_rows, rows_both, slope_inner, act)
     sh2, d_hidden = lax.optimization_barrier((sh2, d_hidden))
     sh2 = total(sh2)
     d_hidden = lax.psum_scatter(d_hidden, ("fsdp", "core"), scatter_dimension=0, tiled=True)
@@ -743,18 +824,22 @@
     datt, slope_late = lax.optimization_barrier((datt, slope_branch))
     d_out = mm_lt(att, slope_late).astype(BF).reshape(GROUPS, cols, width)
     d_out = in_order([d_out[i] for i in range(GROUPS)], g)
-    d_out = d_out.reshape(zs, GROUPS, rows_z // GROUPS, width)
-    pieces = [lax.dynamic_index_in_dim(d_out, g ^ i, axis=1, keepdims=False) for i in range(GROUPS)]
+    d_out = d_out.reshape(zs, GROUPS, ks, own // GROUPS, width)
+    pieces = [lax.dynamic_index_in_dim(d_out, k ^ j, axis=2, keepdims=False) for j in range(ks)]
     datt, pieces = lax.optimization_barrier((datt, pieces))
-    d_out = swap_flips(pieces, "grp")
+    d_out = swap_flips(pieces, "core")
 
     dq, dkv = attend_back(g, k, ks, head, datt, qs, keys, values, att_full, lse)
     dkv = swap_flips([dkv[j] for j in range(ks)], "core")
+    dkv, d_out = lax.optimization_barrier((dkv, d_out))
+    d_out = total(d_out).astype(BF)
+    pieces = [lax.dynamic_index_in_dim(d_out, g ^ i, axis=1, keepdims=False) for i in range(GROUPS)]
+    dkv, pieces = lax.optimization_barrier((dkv, pieces))
+    d_out = swap_flips(pieces, "grp")
     sh1_part, d_in, sums = project_back(g, k, dq, dkv, h1, hat_one, in_w)
     sh1 = swap_flips([sh1_part[i] for i in range(GROUPS)], "grp")
-    sh1, out_late = lax.optimization_barrier((sh1, out_part))
+    sh1, d_out = lax.optimization_barrier((sh1, d_out))
     sh1 = total(sh1)
-    out_sum = swap_flips([out_late[i] for i in range(GROUPS)], "grp")
     hat_own, rate_own = norm_stats(x_f)
     delta_inputs = (slope_middle + norm_back(sh1, table[0:1], hat_own, rate_own)).astype(BF)[None]
 
@@ -771,31 +856,31 @@
         jnp.sum(slope_f, axis=0, keepdims=True),
         d_exp_b,
     )
-    d_out = total(d_out).astype(BF).reshape(zs, ks, -1, width)
-    third = d_out.shape[2] // 3
+    d_out = total(d_out).astype(BF)
+    third = d_out.shape[1] // 3
     tail = d_out[..., 3 * cols :]
-    tail = [tail[:, :, i * third : (i + 1) * third] for i in range(3)]
-    d_out = jnp.concatenate([d_out[..., : 3 * cols], jnp.concatenate(tail, axis=3)], axis=2)
+    tail = [tail[:, i * third : (i + 1) * third] for i in range(3)]
+    d_out = jnp.concatenate([d_out[..., : 3 * cols], jnp.concatenate(tail, axis=2)], axis=1)
     d_in = jnp.concatenate(
         [
             d_in.reshape(zs, ks, own, 3 * cols),
             packed.astype(BF).reshape(zs, ks, extra, 3 * cols),
-            d_out,
         ],
         axis=2,
     )
     pieces = [lax.dynamic_index_in_dim(d_in, k ^ j, axis=1, keepdims=False) for j in range(ks)]
     d_in = total(swap_flips(pieces, "core")).astype(BF)
+    d_in = jnp.concatenate([d_in, d_out], axis=1)
     d_in = swap_flips([pick(d_in, z ^ i) for i in range(zs)], "fsdp")
     d_hidden = gather_flips(d_hidden, "grp")
-    d_in, d_hidden, out_sum = lax.optimization_barrier((d_in, d_hidden, out_sum))
-    d_in = in_order(gather_flips(total(d_in).astype(BF), "grp"), g)
-    d_in = in_order(gather_flips(d_in, "core"), k)
+    d_in, d_hidden = lax.optimization_barrier((d_in, d_hidden))
+    d_in = gather_flips(total(d_in).astype(BF), "grp")
+    d_hidden = [d_hidden] + [[send(p, "core", j) for p in d_hidden] for j in range(1, ks)]
+    d_exp_w, d_con_w = unfold(d_hidden, zs, g, k)
+    d_in, d_exp_w, d_con_w, out_part = lax.optimization_barrier((d_in, d_exp_w, d_con_w, out_part))
+    out_sum = swap_flips([out_part[i] for i in range(GROUPS)], "grp")
+    d_in = in_order(gather_flips(in_order(d_in, g), "core"), k)
     outputs = (middle + total(out_sum) + c_bias).astype(BF)[None]
-    d_hidden = in_order(d_hidden, g)
-    d_hidden = jnp.stack(in_order(gather_flips(d_hidden, "core"), k), axis=1)
-    d_exp_w, d_con_w = unfold(d_hidden.reshape(GROUPS, rows_z, -1), zs)
-    d_con_w = d_con_w.reshape(ff_z, width)
     packed = jnp.sum(d_in[:, :, own : own + extra].astype(F32), axis=1).reshape(-1)
     d_out = d_in[:, :, own + extra :].transpose(1, 0, 2, 3)
     tail = d_out[:, :, 3 * third :].reshape(GROUPS, ks, third, 3, width - 3 * cols)

time: 221 us -> 208 us (0.941)
  waiting for transfers between devices: 60.3 us -> 77.4 us
  starting transfers between devices: 66.6 us -> 50.7 us
  local copies, waits for them, and re-layouts: 18.1 us -> 8.96 us
  other arithmetic: 17.2 us -> 9.51 us
  Pallas kernels: 40 us -> 43.3 us
    ppermute x52, starting transfers between devices: 66.5 us -> 50.7 us  [send(): return lax.ppermute(value, axis, [(s, s ^ flip) for s in range(count)])]
    ppermute x52, waiting for transfers between devices: 60.3 us -> 75.6 us  [send(): return lax.ppermute(value, axis, [(s, s ^ flip) for s in range(count)])]
    unnamed x50 -> x57, local copies, waits for them, and re-layouts: 11.1 us -> 3.11 us
    another operation x9 -> x3, other arithmetic: 6.45 us -> 0.94 us  [in_order(): stacked = jnp.stack(pieces)]
    another operation x5 -> x2, other arithmetic: 3.9 us -> 0.31 us  [in_order(): return jnp.stack([pick(stacked, me ^ j) for j in range(len(pieces))])]
  transfers between devices with their start and end apart: 54 -> 54, of which waited for: 19 -> 26; matrix products, arithmetic and copies ran while one was open for 9% -> 4% of each run, Pallas kernels for 13% -> 14%
where the time goes in v5:
time: 208 us; the launch traced here: 206 us
  waiting for transfers between devices  77.4 us (37%)
  starting transfers between devices  50.7 us (24%)
  Pallas kernels  43.3 us (21%)
  between operations  14.9 us (7%)
  other arithmetic  9.51 us (5%)
  local copies, waits for them, and re-layouts  8.96 us (4%)
    ppermute x52, waiting for transfers between devices, send(): return lax.ppermute(value, axis, [(s, s ^ flip) for s in range(count)])  75.6 us
    ppermute x52, starting transfers between devices, send(): return lax.ppermute(value, axis, [(s, s ^ flip) for s in range(count)])  50.7 us
    pallas_call x1, Pallas kernels, attend_back(): pl.pallas_call(functools.partial(attend_back_kernel, ks, head), grid_spec...  8.39 us
    pallas_call x1, Pallas kernels, attend(): pl.pallas_call(functools.partial(attend_kernel, ks, head), grid_spec=pltp...  8.09 us
    pallas_call x1, Pallas kernels, hidden_part(): pl.pallas_call(hidden_kernel, grid=(hidden // step,), in_specs=[pl.BlockS...  7.16 us
    pallas_call x1, Pallas kernels, hidden_grads(): pl.pallas_call(hidden_grad_kernel, grid=(width // step,), in_specs=[pl.Bl...  4.34 us
  transfers between devices with their start and end apart: 54, of which 26 were waited for; matrix products, arithmetic and copies ran while one was open for 4% of the time, Pallas kernels for 14%

profile of v5, /device:TPU:0, one launch (start us, length us, event | category | flops | bytes accessed | tf_op | source)
XLA Modules:
  0.0 206.5 jit_solution(7201644220558173543)
XLA Ops:
  9.2 3.1 %collective-permute-start = (bf16[240,576]{1,0:T(8,128)(2,1)S(1)}, bf16[240,576]{1,0:T(8,128)(2,1)S(1)}, u32[]{:S(2)}, u32[]{:S(2)}) collective-permute-start(bf16[240,576]{1,0:T(8,128)(2,1)S(1)} %shard_map.262.refs_0_), channel_id=1, source_target_pairs={{0,1},{1,0},{2,3},{3,2},{4,5},{5,4},{6,7},{7,6},{8,9},{9,8},{10,11... | collective-permute-start | bytes 829448 | tf_op jit(solution)/shard_map/ppermute | solution.py:43
  15.9 2.6 %collective-permute-start.1 = (bf16[240,576]{1,0:T(8,128)(2,1)S(1)}, bf16[240,576]{1,0:T(8,128)(2,1)S(1)}, u32[]{:S(2)}, u32[]{:S(2)}) collective-permute-start(bf16[240,576]{1,0:T(8,128)(2,1)S(1)} %shard_map.262.refs_0_), channel_id=1, source_target_pairs={{0,2},{1,3},{2,0},{3,1},{4,6},{5,7},{6,4},{7,5},{8,10},{9,11},{10,... | collective-permute-start | bytes 829448 | tf_op jit(solution)/shard_map/ppermute | solution.py:43
  18.5 4.8 %collective-permute-done.refs_1_ = bf16[240,576]{1,0:T(8,128)(2,1)S(1)} collective-permute-done((bf16[240,576]{1,0:T(8,128)(2,1)S(1)}, bf16[240,576]{1,0:T(8,128)(2,1)S(1)}, u32[]{:S(2)}, u32[]{:S(2)}) %collective-permute-start) | collective-permute-done | bytes 276512 | tf_op jit(solution)/shard_map/ppermute | solution.py:43
  23.3 2.6 %collective-permute-start.2 = (bf16[240,576]{1,0:T(8,128)(2,1)S(1)}, bf16[240,576]{1,0:T(8,128)(2,1)S(1)}, u32[]{:S(2)}, u32[]{:S(2)}) collective-permute-start(bf16[240,576]{1,0:T(8,128)(2,1)S(1)} %shard_map.262.refs_0_), channel_id=1, source_target_pairs={{0,3},{1,2},{2,1},{3,0},{4,7},{5,6},{6,5},{7,4},{8,11},{9,10},{10,... | collective-permute-start | bytes 829448 | tf_op jit(solution)/shard_map/ppermute | solution.py:43
  25.9 14.3 %collective-permute-done.1.refs_2_ = bf16[240,576]{1,0:T(8,128)(2,1)S(1)} collective-permute-done((bf16[240,576]{1,0:T(8,128)(2,1)S(1)}, bf16[240,576]{1,0:T(8,128)(2,1)S(1)}, u32[]{:S(2)}, u32[]{:S(2)}) %collective-permute-start.1) | collective-permute-done | bytes 276512 | tf_op jit(solution)/shard_map/ppermute | solution.py:43
  40.3 2.5 %shard_map.266 = bf16[96,1536]{1,0:T(8,128)(2,1)} custom-call(s32[2]{0:T(128)S(1)} %pad_add_fusion.place, bf16[768,768]{1,0:T(8,128)(2,1)} %con_ref, bf16[192,3072]{1,0:T(8,128)(2,1)} %exp_ref), custom_call_target="tpu_custom_call" | custom-call | tf_op jit(solution)/shard_map/pallas_call | solution.py:306
  48.2 8.1 %shard_map.265 = (bf16[4,128,192]{2,1,0:T(8,128)(2,1)S(1)}, bf16[512,192]{1,0:T(8,128)(2,1)}, bf16[1024,192]{1,0:T(8,128)(2,1)}, bf16[1024,192]{1,0:T(8,128)(2,1...) custom-call(s32[2]{0:T(128)S(1)} %pad_add_fusion.place, ...), custom_call_target="tpu_custom_call" | custom-call | flops 1 | bytes 1 | tf_op jit(solution)/shard_map/pallas_call | solution.py:610
  62.2 2.4 %collective-permute-done.16 = bf16[128,192]{1,0:T(8,128)(2,1)S(1)} collective-permute-done((bf16[128,192]{1,0:T(8,128)(2,1)S(1)}, bf16[128,192]{1,0:T(8,128)(2,1)S(1)}, u32[]{:S(2)}, u32[]{:S(2)}) %collective-permute-start.16) | collective-permute-done | bytes 49184 | tf_op jit(solution)/shard_map/ppermute | solution.py:43
  66.6 2.5 %collective-permute-start.19 = (bf16[128,768]{1,0:T(8,128)(2,1)S(1)}, bf16[128,768]{1,0:T(8,128)(2,1)S(1)}, u32[]{:S(2)}, u32[]{:S(2)}) collective-permute-start(bf16[128,768]{1,0:T(8,128)(2,1)S(1)} %add_convert_fusion.1.refs_0_), channel_id=1, source_target_pairs={{0,24},{8,16},{16,8},{24,0},{1,25},{9,17},{17,9},{25,1},{2,26},{10... | collective-permute-start | bytes 589832 | tf_op jit(solution)/shard_map/ppermute | solution.py:43
  69.1 4.4 %collective-permute-done.17.refs_1_ = bf16[128,768]{1,0:T(8,128)(2,1)S(1)} collective-permute-done((bf16[128,768]{1,0:T(8,128)(2,1)S(1)}, bf16[128,768]{1,0:T(8,128)(2,1)S(1)}, u32[]{:S(2)}, u32[]{:S(2)}) %collective-permute-start.17) | collective-permute-done | bytes 196640 | tf_op jit(solution)/shard_map/ppermute | solution.py:43
  73.4 2.4 %collective-permute-done.18.refs_2_ = bf16[128,768]{1,0:T(8,128)(2,1)S(1)} collective-permute-done((bf16[128,768]{1,0:T(8,128)(2,1)S(1)}, bf16[128,768]{1,0:T(8,128)(2,1)S(1)}, u32[]{:S(2)}, u32[]{:S(2)}) %collective-permute-start.18) | collective-permute-done | bytes 196640 | tf_op jit(solution)/shard_map/ppermute | solution.py:43
  77.6 7.2 %shard_map.267 = (bf16[512,768]{1,0:T(8,128)(2,1)S(1)}, bf16[512,768]{1,0:T(8,128)(2,1)S(1)}, bf16[4,128,768]{2,1,0:T(8,128)(2,1)S(1)}, bf16[4,128,768]{2,1,0:T(8,128)(2,1)}, f32[1,768]{1,0:T(1,128)S(1)}) custom-call(bf16[128,768]{1,0:T(8,128)(2,1)S(1)} %add_convert_fusion.1.refs_0_, bf16[128,768]{1,0:T(8,128)(2,1)S(1)} %collective-permute-done.17.refs_1_, ...), custom_call_target="tpu_custom_call" | custom-call | flops 1 | bytes 1 | tf_op jit(solution)/shard_map/pallas_call | solution.py:477
  85.7 1.9 collective-permute-start.20
  89.2 4.3 %shard_map.268 = bf16[768,1536]{1,0:T(8,128)(2,1)} custom-call(bf16[128,768]{1,0:T(8,128)(2,1)S(1)} %add_convert_fusion.1.refs_0_, bf16[128,768]{1,0:T(8,128)(2,1)S(1)} %collective-permute-done.17.refs_1_, bf16[128,768]{1,0:T(8,128)(2,1)S(1)} %collective-permute-done.18.refs_2_, bf16[128,768]{1,0:T(8,128)(2,1)S(1)} %collective-permute-done.19.refs_3_, ...), custom_call_target="tpu_custom_call" | custom-call | flops 8000000000 | bytes 1 | tf_op jit(solution)/shard_map/pallas_call | solution.py:527
  93.6 5.3 %collective-permute-done.21 = bf16[128,768]{1,0:T(8,128)(2,1)} collective-permute-done((bf16[128,768]{1,0:T(8,128)(2,1)}, bf16[128,768]{1,0:T(8,128)(2,1)}, u32[]{:S(2)}, u32[]{:S(2)}) %collective-permute-start.21) | collective-permute-done | bytes 196640 | tf_op jit(solution)/shard_map/ppermute | solution.py:43
  110.9 8.4 %shard_map.269 = (bf16[512,192]{1,0:T(8,128)(2,1)S(1)}, bf16[2,512,384]{2,1,0:T(8,128)(2,1)S(1)}) custom-call(s32[2]{0:T(128)S(1)} %pad_add_fusion.place, bf16[128,192]{1,0:T(8,128)(2,1)S(1)} %get-tuple-element.121.refs_0_, bf16[128,192]{1,0:T(8,128)(2,1)S(1)} %collective-permute-done.23.refs_1_, bf16[128,192]{1,0:T(8,128)(2,1)S(1)} %collective-permute-done.24.refs_2_, ...), custom_call_target="tpu_custom_call" | custom-call | flops 8000000000 | bytes 1 | tf_op jit(solution)/shard_map/pallas_call | solution.py:672
  123.0 3.5 %shard_map.270 = (bf16[4,128,768]{2,1,0:T(8,128)(2,1)S(1)}, bf16[768,576]{1,0:T(8,128)(2,1)S(1)}, f32[8,768]{1,0:T(8,128)S(1)}) custom-call(s32[2]{0:T(128)S(1)} %pad_add_fusion.place, bf16[512,192]{1,0:T(8,128)(2,1)S(1)} %get-tuple-element.130.refs_0_, bf16[512,384]{1,0:T(8,128)(2,1)S(1)} %get-tuple-element.138.refs_1_, ...), custom_call_target="tpu_custom_call" | custom-call | flops 1 | bytes 1 | tf_op jit(solution)/shard_map/pallas_call | solution.py:710
  133.7 11.6 %collective-permute-done.33 = bf16[4,24,768]{2,1,0:T(8,128)(2,1)S(1)} collective-permute-done((bf16[4,24,768]{2,1,0:T(8,128)(2,1)S(1)}, bf16[4,24,768]{2,1,0:T(8,128)(2,1)S(1)}, u32[]{:S(2)}, u32[]{:S(2)}) %collective-permute-start.33) | collective-permute-done | bytes 147488 | tf_op jit(solution)/shard_map/ppermute | solution.py:43
  156.9 9.5 %collective-permute-done.36 = bf16[130,576]{1,0:T(8,128)(2,1)S(1)} collective-permute-done((bf16[130,576]{1,0:T(8,128)(2,1)S(1)}, bf16[130,576]{1,0:T(8,128)(2,1)S(1)}, u32[]{:S(2)}, u32[]{:S(2)}) %collective-permute-start.36) | collective-permute-done | bytes 149792 | tf_op jit(solution)/shard_map/ppermute | solution.py:43
  171.2 3.1 %shard_map.272 = (f32[2,96,3072]{2,1,0:T(8,128)}, f32[4,2,96,768]{3,2,1,0:T(8,128)}) custom-call(s32[2]{0:T(128)S(1)} %pad_add_fusion.place, bf16[96,1536]{1,0:T(8,128)(2,1)S(1)} %copy-done.8, bf16[96,1536]{1,0:T(8,128)(2,1)S(1)} %collective-permute-done.38.refs_1_, bf16[96,1536]{1,0:T(8,128)(2,1)S(1)} %collective-permute-done.39.refs_2_, ...), custom_call_target="tpu_custom_call" | custom-call | flops 1 | bytes 1 | tf_op jit(solution)/shard_map/pallas_call | solution.py:400
  175.0 4.0 %collective-permute-done.42 = bf16[130,576]{1,0:T(8,128)(2,1)S(1)} collective-permute-done((bf16[130,576]{1,0:T(8,128)(2,1)S(1)}, bf16[130,576]{1,0:T(8,128)(2,1)S(1)}, u32[]{:S(2)}, u32[]{:S(2)}) %collective-permute-start.42) | collective-permute-done | bytes 149792 | tf_op jit(solution)/shard_map/ppermute | solution.py:43
  185.0 3.5 %collective-permute-done.48 = bf16[128,768]{1,0:T(8,128)(2,1)S(1)} collective-permute-done((bf16[128,768]{1,0:T(8,128)(2,1)S(1)}, bf16[128,768]{1,0:T(8,128)(2,1)S(1)}, u32[]{:S(2)}, u32[]{:S(2)}) %collective-permute-start.48) | collective-permute-done | bytes 196640 | tf_op jit(solution)/shard_map/ppermute | solution.py:43
  188.9 2.9 %collective-permute-done.50 = bf16[128,768]{1,0:T(8,128)(2,1)S(1)} collective-permute-done((bf16[128,768]{1,0:T(8,128)(2,1)S(1)}, bf16[128,768]{1,0:T(8,128)(2,1)S(1)}, u32[]{:S(2)}, u32[]{:S(2)}) %collective-permute-start.50) | collective-permute-done | bytes 196640 | tf_op jit(solution)/shard_map/ppermute | solution.py:43
  197.0 2.6 %shard_map.273 = f32[192,2304]{1,0:T(8,128)} custom-call(bf16[4,192,576]{2,1,0:T(8,128)(2,1)S(1)} %bitcast.169), custom_call_target="tpu_custom_call" | custom-call | tf_op jit(solution)/shard_map/pallas_call | solution.py:368
  (236 shorter events, 74.1 us)
Async XLA Ops:
  7.2 70.4 %all-gather.2.cloned.1.call-start = ((), (), s32[]{:S(2)}) async-start(), calls=%async_computation.1 | async-start | bytes 2654208 | tf_op jit(solution)/shard_map/all_gather | solution.py:795
  9.2 14.1 %collective-permute-start = (bf16[240,576]{1,0:T(8,128)(2,1)S(1)}, bf16[240,576]{1,0:T(8,128)(2,1)S(1)}, u32[]{:S(2)}, u32[]{:S(2)}) collective-permute-start(bf16[240,576]{1,0:T(8,128)(2,1)S(1)} %shard_map.262.refs_0_), channel_id=1, source_target_pairs={{0,1},{1,0},{2,3},{3,2},{4,5},{5,4},{6,7},{7,6},{8,9},{9,8},{10,11... | collective-permute-start | bytes 829448 | tf_op jit(solution)/shard_map/ppermute | solution.py:43
  12.4 27.8 %collective-permute-start.3 = (bf16[2,128,768]{2,1,0:T(8,128)(2,1)S(1)}, bf16[2,128,768]{2,1,0:T(8,128)(2,1)S(1)}, u32[]{:S(2)}, u32[]{:S(2)}) collective-permute-start(bf16[2,128,768]{2,1,0:T(8,128)(2,1)S(1)} %constant_dynamic-update-slice_fusion.refs_0_.refs_4_), channel_id=1, source_target_pairs={{0,8},{8,0},{16,24},{24,16},{1,9},{9,1},{17,25},{25,17},{2,10},{10... | collective-permute-start | bytes 1179656 | tf_op jit(solution)/shard_map/ppermute | solution.py:43
  14.0 26.3 %collective-permute-start.4 = (bf16[2,128,768]{2,1,0:T(8,128)(2,1)S(1)}, bf16[2,128,768]{2,1,0:T(8,128)(2,1)S(1)}, u32[]{:S(2)}, u32[]{:S(2)}) collective-permute-start(bf16[2,128,768]{2,1,0:T(8,128)(2,1)S(1)} %constant_dynamic-update-slice_fusion.refs_0_.refs_4_), channel_id=1, source_target_pairs={{0,16},{8,24},{16,0},{24,8},{1,17},{9,25},{17,1},{25,9},{2,18},{10... | collective-permute-start | bytes 1179656 | tf_op jit(solution)/shard_map/ppermute | solution.py:43
  15.5 24.8 %collective-permute-start.5 = (bf16[2,128,768]{2,1,0:T(8,128)(2,1)S(1)}, bf16[2,128,768]{2,1,0:T(8,128)(2,1)S(1)}, u32[]{:S(2)}, u32[]{:S(2)}) collective-permute-start(bf16[2,128,768]{2,1,0:T(8,128)(2,1)S(1)} %constant_dynamic-update-slice_fusion.refs_0_.refs_4_), channel_id=1, source_target_pairs={{0,24},{8,16},{16,8},{24,0},{1,25},{9,17},{17,9},{25,1},{2,26},{10... | collective-permute-start | bytes 1179656 | tf_op jit(solution)/shard_map/ppermute | solution.py:43
  15.9 24.3 %collective-permute-start.1 = (bf16[240,576]{1,0:T(8,128)(2,1)S(1)}, bf16[240,576]{1,0:T(8,128)(2,1)S(1)}, u32[]{:S(2)}, u32[]{:S(2)}) collective-permute-start(bf16[240,576]{1,0:T(8,128)(2,1)S(1)} %shard_map.262.refs_0_), channel_id=1, source_target_pairs={{0,2},{1,3},{2,0},{3,1},{4,6},{5,7},{6,4},{7,5},{8,10},{9,11},{10,... | collective-permute-start | bytes 829448 | tf_op jit(solution)/shard_map/ppermute | solution.py:43
  23.3 16.9 %collective-permute-start.2 = (bf16[240,576]{1,0:T(8,128)(2,1)S(1)}, bf16[240,576]{1,0:T(8,128)(2,1)S(1)}, u32[]{:S(2)}, u32[]{:S(2)}) collective-permute-start(bf16[240,576]{1,0:T(8,128)(2,1)S(1)} %shard_map.262.refs_0_), channel_id=1, source_target_pairs={{0,3},{1,2},{2,1},{3,0},{4,7},{5,6},{6,5},{7,4},{8,11},{9,10},{10,... | collective-permute-start | bytes 829448 | tf_op jit(solution)/shard_map/ppermute | solution.py:43
  42.8 105.8 %reduce-scatter.2.cloned.1.call-start = ((), (), s32[]{:S(2)}) async-start(), calls=%async_computation.2 | async-start | bytes 2654208 | tf_op jit(solution)/shard_map/reduce_scatter | solution.py:814
  87.6 11.3 %collective-permute-start.21 = (bf16[128,768]{1,0:T(8,128)(2,1)}, bf16[128,768]{1,0:T(8,128)(2,1)}, u32[]{:S(2)}, u32[]{:S(2)}) collective-permute-start(bf16[128,768]{1,0:T(8,128)(2,1)} %get-tuple-element.215), channel_id=1, source_target_pairs={{0,16},{8,24},{16,0},{24,8},{1,17},{9,25},{17,1},{25,9},{2,18},{10... | collective-permute-start | bytes 589832 | tf_op jit(solution)/shard_map/ppermute | solution.py:43
  89.1 9.8 %collective-permute-start.22 = (bf16[128,768]{1,0:T(8,128)(2,1)}, bf16[128,768]{1,0:T(8,128)(2,1)}, u32[]{:S(2)}, u32[]{:S(2)}) collective-permute-start(bf16[128,768]{1,0:T(8,128)(2,1)} %get-tuple-element.214), channel_id=1, source_target_pairs={{0,24},{8,16},{16,8},{24,0},{1,25},{9,17},{17,9},{25,1},{2,26},{10... | collective-permute-start | bytes 589832 | tf_op jit(solution)/shard_map/ppermute | solution.py:43
  110.8 10.5 %collective-permute-start.27 = (bf16[4,4,24,768]{3,2,1,0:T(8,128)(2,1)S(1)}, bf16[4,4,24,768]{3,2,1,0:T(8,128)(2,1)S(1)}, u32[]{:S(2)}, u32[]{:S(2)}) collective-permute-start(bf16[4,4,24,768]{3,2,1,0:T(8,128)(2,1)S(1)} %get-tuple-element.133), channel_id=1, source_target_pairs={{0,4},{4,0},{1,5},{5,1},{2,6},{6,2},{3,7},{7,3},{8,12},{12,8},{9,1... | collective-permute-start | bytes 1769480 | tf_op jit(solution)/shard_map/ppermute | solution.py:43
  121.5 9.9 %collective-permute-start.32 = (bf16[4,24,768]{2,1,0:T(8,128)(2,1)S(1)}, bf16[4,24,768]{2,1,0:T(8,128)(2,1)S(1)}, u32[]{:S(2)}, u32[]{:S(2)}) collective-permute-start(bf16[4,24,768]{2,1,0:T(8,128)(2,1)S(1)} %get-tuple-element.147), channel_id=1, source_target_pairs={{0,8},{8,0},{16,24},{24,16},{1,9},{9,1},{17,25},{25,17},{2,10},{10... | collective-permute-start | bytes 442376 | tf_op jit(solution)/shard_map/ppermute | solution.py:43
  127.3 17.9 %collective-permute-start.29 = (bf16[128,768]{1,0:T(8,128)(2,1)}, bf16[128,768]{1,0:T(8,128)(2,1)}, u32[]{:S(2)}, u32[]{:S(2)}) collective-permute-start(bf16[128,768]{1,0:T(8,128)(2,1)} %get-tuple-element.210), channel_id=1, source_target_pairs={{0,8},{8,0},{16,24},{24,16},{1,9},{9,1},{17,25},{25,17},{2,10},{10... | collective-permute-start | bytes 589832 | tf_op jit(solution)/shard_map/ppermute | solution.py:43
  127.9 17.4 %collective-permute-start.30 = (bf16[128,768]{1,0:T(8,128)(2,1)}, bf16[128,768]{1,0:T(8,128)(2,1)}, u32[]{:S(2)}, u32[]{:S(2)}) collective-permute-start(bf16[128,768]{1,0:T(8,128)(2,1)} %get-tuple-element.209), channel_id=1, source_target_pairs={{0,16},{8,24},{16,0},{24,8},{1,17},{9,25},{17,1},{25,9},{2,18},{10... | collective-permute-start | bytes 589832 | tf_op jit(solution)/shard_map/ppermute | solution.py:43
  129.1 16.2 %collective-permute-start.31 = (bf16[128,768]{1,0:T(8,128)(2,1)}, bf16[128,768]{1,0:T(8,128)(2,1)}, u32[]{:S(2)}, u32[]{:S(2)}) collective-permute-start(bf16[128,768]{1,0:T(8,128)(2,1)} %get-tuple-element.208), channel_id=1, source_target_pairs={{0,24},{8,16},{16,8},{24,0},{1,25},{9,17},{17,9},{25,1},{2,26},{10... | collective-permute-start | bytes 589832 | tf_op jit(solution)/shard_map/ppermute | solution.py:43
  130.8 14.4 %collective-permute-start.33 = (bf16[4,24,768]{2,1,0:T(8,128)(2,1)S(1)}, bf16[4,24,768]{2,1,0:T(8,128)(2,1)S(1)}, u32[]{:S(2)}, u32[]{:S(2)}) collective-permute-start(bf16[4,24,768]{2,1,0:T(8,128)(2,1)S(1)} %get-tuple-element.148), channel_id=1, source_target_pairs={{0,16},{8,24},{16,0},{24,8},{1,17},{9,25},{17,1},{25,9},{2,18},{10... | collective-permute-start | bytes 442376 | tf_op jit(solution)/shard_map/ppermute | solution.py:43
  131.4 13.9 %collective-permute-start.34 = (bf16[4,24,768]{2,1,0:T(8,128)(2,1)S(1)}, bf16[4,24,768]{2,1,0:T(8,128)(2,1)}, u32[]{:S(2)}, u32[]{:S(2)}) collective-permute-start(bf16[4,24,768]{2,1,0:T(8,128)(2,1)S(1)} %get-tuple-element.149), channel_id=1, source_target_pairs={{0,24},{8,16},{16,8},{24,0},{1,25},{9,17},{17,9},{25,1},{2,26},{10... | collective-permute-start | bytes 442376 | tf_op jit(solution)/shard_map/ppermute | solution.py:43
  148.6 17.8 %collective-permute-start.38 = (bf16[96,1536]{1,0:T(8,128)(2,1)}, bf16[96,1536]{1,0:T(8,128)(2,1)S(1)}, u32[]{:S(2)}, u32[]{:S(2)}) collective-permute-start(bf16[96,1536]{1,0:T(8,128)(2,1)} %reduce-scatter.2.cloned.1.call-done.refs_0_), channel_id=1, source_target_pairs={{0,8},{8,0},{16,24},{24,16},{1,9},{9,1},{17,25},{25,17},{2,10},{10... | collective-permute-start | bytes 884744 | tf_op jit(solution)/shard_map/ppermute | solution.py:43
  150.0 16.3 %collective-permute-start.39 = (bf16[96,1536]{1,0:T(8,128)(2,1)}, bf16[96,1536]{1,0:T(8,128)(2,1)S(1)}, u32[]{:S(2)}, u32[]{:S(2)}) collective-permute-start(bf16[96,1536]{1,0:T(8,128)(2,1)} %reduce-scatter.2.cloned.1.call-done.refs_0_), channel_id=1, source_target_pairs={{0,16},{8,24},{16,0},{24,8},{1,17},{9,25},{17,1},{25,9},{2,18},{10... | collective-permute-start | bytes 884744 | tf_op jit(solution)/shard_map/ppermute | solution.py:43
  150.8 15.6 %collective-permute-start.40 = (bf16[96,1536]{1,0:T(8,128)(2,1)}, bf16[96,1536]{1,0:T(8,128)(2,1)S(1)}, u32[]{:S(2)}, u32[]{:S(2)}) collective-permute-start(bf16[96,1536]{1,0:T(8,128)(2,1)} %reduce-scatter.2.cloned.1.call-done.refs_0_), channel_id=1, source_target_pairs={{0,24},{8,16},{16,8},{24,0},{1,25},{9,17},{17,9},{25,1},{2,26},{10... | collective-permute-start | bytes 884744 | tf_op jit(solution)/shard_map/ppermute | solution.py:43
  152.1 14.3 %collective-permute-start.36 = (bf16[130,576]{1,0:T(8,128)(2,1)S(1)}, bf16[130,576]{1,0:T(8,128)(2,1)S(1)}, u32[]{:S(2)}, u32[]{:S(2)}) collective-permute-start(bf16[130,576]{1,0:T(8,128)(2,1)S(1)} %get-tuple-element.225), channel_id=1, source_target_pairs={{0,2},{1,3},{2,0},{3,1},{4,6},{5,7},{6,4},{7,5},{8,10},{9,11},{10,... | collective-permute-start | bytes 449288 | tf_op jit(solution)/shard_map/ppermute | solution.py:43
  154.0 12.4 %collective-permute-start.37 = (bf16[130,576]{1,0:T(8,128)(2,1)S(1)}, bf16[130,576]{1,0:T(8,128)(2,1)S(1)}, u32[]{:S(2)}, u32[]{:S(2)}) collective-permute-start(bf16[130,576]{1,0:T(8,128)(2,1)S(1)} %get-tuple-element.224), channel_id=1, source_target_pairs={{0,3},{1,2},{2,1},{3,0},{4,7},{5,6},{6,5},{7,4},{8,11},{9,10},{10,... | collective-permute-start | bytes 449288 | tf_op jit(solution)/shard_map/ppermute | solution.py:43
  169.1 9.9 %collective-permute-start.42 = (bf16[130,576]{1,0:T(8,128)(2,1)S(1)}, bf16[130,576]{1,0:T(8,128)(2,1)S(1)}, u32[]{:S(2)}, u32[]{:S(2)}) collective-permute-start(bf16[130,576]{1,0:T(8,128)(2,1)S(1)} %add_convert_fusion.2), channel_id=1, source_target_pairs={{0,16},{8,24},{16,0},{24,8},{1,17},{9,25},{17,1},{25,9},{2,18},{10... | collective-permute-start | bytes 449288 | tf_op jit(solution)/shard_map/ppermute | solution.py:43
  179.7 13.0 %collective-permute-start.51 = (bf16[4,130,576]{2,0,1:T(4,128)(2,1)S(1)}, bf16[4,130,576]{2,0,1:T(4,128)(2,1)S(1)}, u32[]{:S(2)}, u32[]{:S(2)}) collective-permute-start(bf16[4,130,576]{2,0,1:T(4,128)(2,1)S(1)} %copy.78), channel_id=1, source_target_pairs={{0,4},{4,0},{1,5},{5,1},{2,6},{6,2},{3,7},{7,3},{8,12},{12,8},{9,1... | collective-permute-start | bytes 1797128 | tf_op jit(solution)/shard_map/ppermute | solution.py:43
  (59 other events, 370.6 us)
Sparse Core Ops, SparseCore 0:
  42.9 34.7 all-gather.1
  102.4 34.5 reduce-scatter.1

commit v6 on v5

--- a/solution.py
+++ b/solution.py
@@ -424,7 +424,10 @@
 
 def hidden_kernel(*refs):
     h_rows, s_rows = refs[:GROUPS], refs[GROUPS : 2 * GROUPS]
-    (exp_w, con_w, bias, act_ref, inner_ref, back_ref, out_ref, bias_ref) = refs[2 * GROUPS : -4]
+    exp_w, con_w, bias, act_ref, inner_ref = refs[2 * GROUPS : 2 * GROUPS + 5]
+    back_ref = refs[2 * GROUPS + 5 : 3 * GROUPS + 5]
+    out_ref = refs[3 * GROUPS + 5 : 4 * GROUPS + 5]
+    bias_ref = refs[4 * GROUPS + 5]
     h_ref, s_ref, back_sum, out_sum = refs[-4:]
     step = pl.program_id(0)
     tok = h_rows[0].shape[0]
@@ -462,8 +465,8 @@
     @pl.when(step == pl.num_programs(0) - 1)
     def _():
         for i in range(GROUPS):
-            back_ref[i] = back_sum[i * tok : (i + 1) * tok, :].astype(BF)
-            out_ref[i] = out_sum[i * tok : (i + 1) * tok, :].astype(BF)
+            back_ref[i][...] = back_sum[i * tok : (i + 1) * tok, :].astype(BF)
+            out_ref[i][...] = out_sum[i * tok : (i + 1) * tok, :].astype(BF)
 
 
 def hidden_part(h_rows, s_rows, weights, table):
@@ -473,8 +476,8 @@
     step = 256
     fixed = lambda i: (0, 0)
     cols = lambda i: (0, i)
-    slots = pl.BlockSpec((GROUPS, tok, width), lambda i: (0, 0, 0))
-    return pl.pallas_call(
+    slots = [pl.BlockSpec((tok, width), fixed)] * GROUPS
+    got = pl.pallas_call(
         hidden_kernel,
         grid=(hidden // step,),
         in_specs=[pl.BlockSpec((tok, width), fixed)] * GROUPS
@@ -487,21 +490,22 @@
         out_specs=[
             pl.BlockSpec((rows, step), cols),
             pl.BlockSpec((rows, step), cols),
-            slots,
-            slots,
+            *slots,
+            *slots,
             pl.BlockSpec((1, step), cols),
         ],
         out_shape=[
             jax.ShapeDtypeStruct((rows, hidden), BF),
             jax.ShapeDtypeStruct((rows, hidden), BF),
-            jax.ShapeDtypeStruct((GROUPS, tok, width), BF),
-            pltpu.HBM((GROUPS, tok, width), BF),
+            *[jax.ShapeDtypeStruct((tok, width), BF)] * GROUPS,
+            *[pltpu.HBM((tok, width), BF)] * GROUPS,
             jax.ShapeDtypeStruct((1, hidden), F32),
         ],
         scratch_shapes=[pltpu.VMEM((rows, width), BF)] * 2 + [pltpu.VMEM((rows, width), F32)] * 2,
         compiler_params=pltpu.CompilerParams(vmem_limit_bytes=24 * 2**20),
         cost_estimate=SHORT,
     )(*h_rows, *in_hbm(*s_rows, weights, weights), table)
+    return got[0], got[1], got[2 : 2 + GROUPS], got[2 + GROUPS : 2 + 2 * GROUPS], got[-1]
 
 
 def hidden_grad_kernel(*refs):
@@ -554,7 +558,8 @@
 def attend_kernel(ks, head, place, *refs):
     pieces = refs[: GROUPS * ks]
     in_w, table = refs[GROUPS * ks : GROUPS * ks + 2]
-    slots, q_out, k_out, v_out, att_out, lse_out, h_out, hat_out, h_all = refs[GROUPS * ks + 2 :]
+    slots = refs[GROUPS * ks + 2 : GROUPS * ks + 2 + GROUPS]
+    q_out, k_out, v_out, att_out, lse_out, h_out, hat_out, h_all = refs[GROUPS * ks + 2 + GROUPS :]
     g, k = place[0], place[1]
     tok, width = pieces[-1].shape
     cols = q_out.shape[1]
@@ -589,7 +594,7 @@
             att = mm(weights.astype(BF), v_out[:span, low:high]) / mass
             att_out[rows, low:high] = att
     for i in range(GROUPS):
-        slots[g ^ i] = att_out[i * tok : (i + 1) * tok, :].astype(BF)
+        slots[i][...] = att_out[pl.ds(pl.multiple_of((g ^ i) * tok, tok), tok), :].astype(BF)
 
 
 def attend(g, k, ks, head, both, more, in_w, table):
@@ -598,7 +603,7 @@
     mine, rows = GROUPS * tok, GROUPS * ks * tok
     vmem = pl.BlockSpec(memory_space=pltpu.VMEM)
     shapes = [
-        ((GROUPS, tok, cols), BF),
+        *[((tok, cols), BF)] * GROUPS,
         ((mine, cols), BF),
         ((rows, cols), BF),
         ((rows, cols), BF),
@@ -617,46 +622,46 @@
             out_specs=[vmem] * len(shapes),
             scratch_shapes=[pltpu.VMEM((rows, width), BF)],
         ),
-        out_shape=[jax.ShapeDtypeStruct(*shapes[0])] + [pltpu.HBM(s, t) for s, t in shapes[1:]],
+        out_shape=[jax.ShapeDtypeStruct(s, t) for s, t in shapes[:GROUPS]]
+        + [pltpu.HBM(s, t) for s, t in shapes[GROUPS:]],
         compiler_params=pltpu.CompilerParams(vmem_limit_bytes=(16 if ks == 2 else 48) * 2**20),
         cost_estimate=SHORT,
     )(jnp.stack([g, k]).astype(jnp.int32), *both, *more, in_w, table)
 
 
-def attend_back_kernel(ks, head, place, *refs):
+def attend_back_kernel(ks, head, first, place, *refs):
     slopes = refs[:GROUPS]
-    q_ref, k_ref, v_ref, att_ref, lse_ref, dq_out, dkv_out, dk_sum, dv_sum = refs[GROUPS:]
+    q_ref, k_ref, v_ref, att_ref, lse_ref, dq_out, dkv_out = refs[GROUPS : GROUPS + 7]
+    dk_sum, dv_sum, slope_rows = refs[GROUPS + 7 :]
     g, k = place[0], place[1]
-    tok, cols = slopes[0].shape
-    d_rows = dq_out
+    tok = slopes[0].shape[0]
+    heads = dq_out.shape[1] // head
     for i in range(GROUPS):
-        d_rows[pl.ds(pl.multiple_of((g ^ i) * tok, tok), tok), :] = slopes[i][...]
+        slope_rows[pl.ds(pl.multiple_of((g ^ i) * tok, tok), tok), :] = slopes[i][...]
     seen = visible(k, tok, ks * tok)
     for i in reversed(range(GROUPS)):
         rows = slice(i * tok, (i + 1) * tok)
         span = (i + 1) * ks * tok
-        slope_all = d_rows[rows, :]
-        parts = []
-        for h in range(cols // head):
-            low, high = h * head, (h + 1) * head
+        for h in range(heads):
+            low, high = (first + h) * head, (first + h + 1) * head
+            to = slice(h * head, (h + 1) * head)
             query = (q_ref[rows, low:high].astype(F32) * head**-0.5).astype(BF)
             keys = k_ref[:span, low:high]
-            slope = slope_all[:, low:high]
+            slope = slope_rows[rows, low:high]
             scores = masked_scores(query, keys, seen)
-            chances = jnp.exp(scores - lse_ref[rows, h : h + 1])
+            chances = jnp.exp(scores - lse_ref[rows, first + h : first + h + 1])
             diag = jnp.sum(slope.astype(F32) * att_ref[rows, low:high], axis=-1, keepdims=True)
             slope_chances = mm_rt(slope, v_ref[:span, low:high])
             slope_scores = (chances * (slope_chances - diag)).astype(BF)
-            parts.append(mm(slope_scores, keys) * head**-0.5)
+            dq_out[rows, to] = (mm(slope_scores, keys) * head**-0.5).astype(BF)
             dk = mm_lt(slope_scores, query)
             dv = mm_lt(chances.astype(BF), slope)
             if i == GROUPS - 1:
-                dk_sum[:, low:high] = dk
-                dv_sum[:, low:high] = dv
+                dk_sum[:, to] = dk
+                dv_sum[:, to] = dv
             else:
-                dk_sum[:span, low:high] += dk
-                dv_sum[:span, low:high] += dv
-        dq_out[rows, :] = jnp.concatenate(parts, axis=1).astype(BF)
+                dk_sum[:span, to] += dk
+                dv_sum[:span, to] += dv
     for i in range(GROUPS):
         for j in range(ks):
             spot = slice((i * ks + j) * tok, (i * ks + j + 1) * tok)
@@ -665,64 +670,81 @@
             ).astype(BF)
 
 
-def attend_back(g, k, ks, head, slopes, q, keys, values, att, lse):
+def attend_back(g, k, ks, head, first, heads, slopes, q, keys, values, att, lse):
     tok, cols = slopes[0].shape
     mine, rows = GROUPS * tok, GROUPS * ks * tok
+    wide = heads * head
     vmem = pl.BlockSpec(memory_space=pltpu.VMEM)
     return pl.pallas_call(
-        functools.partial(attend_back_kernel, ks, head),
+        functools.partial(attend_back_kernel, ks, head, first),
         grid_spec=pltpu.PrefetchScalarGridSpec(
             num_scalar_prefetch=1,
             in_specs=[vmem] * (len(slopes) + 5),
             out_specs=[vmem] * 2,
-            scratch_shapes=[pltpu.VMEM((rows, cols), F32)] * 2,
+            scratch_shapes=[pltpu.VMEM((rows, wide), F32)] * 2 + [pltpu.VMEM((mine, cols), BF)],
         ),
         out_shape=[
-            jax.ShapeDtypeStruct((mine, cols), BF),
-            jax.ShapeDtypeStruct((ks, mine, 2 * cols), BF),
+            jax.ShapeDtypeStruct((mine, wide), BF),
+            jax.ShapeDtypeStruct((ks, mine, 2 * wide), BF),
         ],
         compiler_params=pltpu.CompilerParams(vmem_limit_bytes=(16 if ks == 2 else 48) * 2**20),
         cost_estimate=LONG,
     )(jnp.stack([g, k]).astype(jnp.int32), *slopes, *in_hbm(q, keys, values, att, lse))
 
 
-def project_back_kernel(ks, place, *refs):
-    dq, dkv = refs[0], refs[1 : 1 + ks]
-    h_ref, hat_ref, in_w, slots, d_in, sums, project = refs[1 + ks :]
+def project_back_kernel(ks, parts, place, *refs):
+    count = len(parts)
+    dq, dkv = refs[:count], refs[count : count + count * ks]
+    h_ref, hat_ref, in_w = refs[count * (ks + 1) : count * (ks + 1) + 3]
+    slots, (d_in, sums, project, back) = refs[-GROUPS - 4 : -4], refs[-4:]
     g = place[0]
-    tok = slots.shape[1]
-    cols = dq.shape[1]
-    project[:, :cols] = dq[...]
-    project[:, cols:] = total([part[...] for part in dkv]).astype(BF)
-    back = mm_rt(project[...], in_w[...])
+    tok = slots[0].shape[0]
+    cols = sum(parts)
+    low = 0
+    for n, wide in enumerate(parts):
+        project[:, low : low + wide] = dq[n][...]
+        both = total([dkv[n * ks + j][...] for j in range(ks)]).astype(BF)
+        project[:, cols + low : cols + low + wide] = both[:, :wide]
+        project[:, 2 * cols + low : 2 * cols + low + wide] = both[:, wide:]
+        low += wide
+    back[...] = mm_rt(project[...], in_w[...])
     for i in range(GROUPS):
-        slots[g ^ i] = back[i * tok : (i + 1) * tok, :].astype(BF)
-    sums[0:1, :] = jnp.sum(back * hat_ref[...].astype(F32), axis=0, keepdims=True)
-    sums[1:2, :] = jnp.sum(back, axis=0, keepdims=True)
+        slots[i][...] = back[pl.ds(pl.multiple_of((g ^ i) * tok, tok), tok), :].astype(BF)
+    sums[0:1, :] = jnp.sum(back[...] * hat_ref[...].astype(F32), axis=0, keepdims=True)
+    sums[1:2, :] = jnp.sum(back[...], axis=0, keepdims=True)
     sums[2:3, : 3 * cols] = jnp.sum(project[...].astype(F32), axis=0, keepdims=True)
     d_in[...] = mm_lt(h_ref[...], project[...]).astype(BF)
 
 
-def project_back(g, k, dq, dkv, h, hat, in_w):
+def project_back(g, dq, dkv, h, hat, in_w):
     mine, width = h.shape
-    cols = dq.shape[1]
+    parts = [part.shape[1] for part in dq]
+    cols = sum(parts)
+    ks = len(dkv[0])
     vmem = pl.BlockSpec(memory_space=pltpu.VMEM)
-    return pl.pallas_call(
-        functools.partial(project_back_kernel, len(dkv)),
+    got = pl.pallas_call(
+        functools.partial(project_back_kernel, ks, parts),
         grid_spec=pltpu.PrefetchScalarGridSpec(
             num_scalar_prefetch=1,
-            in_specs=[vmem] * (len(dkv) + 4),
-            out_specs=[vmem] * 3,
-            scratch_shapes=[pltpu.VMEM((mine, 3 * cols), BF)],
+            in_specs=[vmem] * (len(dq) * (ks + 1) + 3),
+            out_specs=[vmem] * (GROUPS + 2),
+            scratch_shapes=[pltpu.VMEM((mine, 3 * cols), BF), pltpu.VMEM((mine, width), F32)],
         ),
-        out_shape=[
-            jax.ShapeDtypeStruct((GROUPS, mine // GROUPS, width), BF),
+        out_shape=[jax.ShapeDtypeStruct((mine // GROUPS, width), BF)] * GROUPS
+        + [
             jax.ShapeDtypeStruct((width, 3 * cols), BF),
             jax.ShapeDtypeStruct((8, width), F32),
         ],
         compiler_params=pltpu.CompilerParams(vmem_limit_bytes=16 * 2**20),
         cost_estimate=SHORT,
-    )(jnp.stack([g, k]).astype(jnp.int32), dq, *dkv, *in_hbm(h, hat), in_w)
+    )(
+        jnp.stack([g]).astype(jnp.int32),
+        *dq,
+        *[p for pieces in dkv for p in pieces],
+        *in_hbm(h, hat),
+        in_w,
+    )
+    return got[:GROUPS], got[GROUPS], got[GROUPS + 1]
 
 
 def shards(
@@ -794,10 +816,10 @@
     rest = cut_rest(con_raw, exp_raw, zs, g, k, ks)
     rest = lax.all_gather(rest, ("fsdp", "core"), axis=0, tiled=True)
 
-    slots, qs, keys, values, att_full, lse, h1, hat_one = attend(
+    *slots, qs, keys, values, att_full, lse, h1, hat_one = attend(
         g, k, ks, head, rows_both, x_more, in_w, table
     )
-    att = jnp.concatenate(swap_flips([slots[i] for i in range(GROUPS)], "grp"), axis=1)
+    att = jnp.concatenate(swap_flips(slots, "grp"), axis=1)
     x_f = x_own.astype(F32)
     middle = x_f + mm(att, out_w) + o_bias
     hat_two, rate_two = norm_stats(middle)
@@ -807,7 +829,7 @@
     act, slope_inner, sh2_part, out_part, d_exp_b = hidden_part(
         h2_rows, rows_both, rest, table
     )
-    sh2 = swap_flips([sh2_part[i] for i in range(GROUPS)], "grp")
+    sh2 = swap_flips(sh2_part, "grp")
     d_hidden = hidden_grads(h2_rows, rows_both, slope_inner, act)
     sh2, d_hidden = lax.optimization_barrier((sh2, d_hidden))
     sh2 = total(sh2)
@@ -821,7 +843,8 @@
     slope_att = mm_rt(slope_branch, out_w).astype(BF)
     datt = swap_flips([slope_att[:, i * cols : (i + 1) * cols] for i in range(GROUPS)], "grp")
 
-    datt, slope_late = lax.optimization_barrier((datt, slope_branch))
+    datt, slope_late, out_part = lax.optimization_barrier((datt, slope_branch, out_part))
+    out_sum = swap_flips(out_part, "grp")
     d_out = mm_lt(att, slope_late).astype(BF).reshape(GROUPS, cols, width)
     d_out = in_order([d_out[i] for i in range(GROUPS)], g)
     d_out = d_out.reshape(zs, GROUPS, ks, own // GROUPS, width)
@@ -829,17 +852,20 @@
     datt, pieces = lax.optimization_barrier((datt, pieces))
     d_out = swap_flips(pieces, "core")
 
-    dq, dkv = attend_back(g, k, ks, head, datt, qs, keys, values, att_full, lse)
-    dkv = swap_flips([dkv[j] for j in range(ks)], "core")
-    dkv, d_out = lax.optimization_barrier((dkv, d_out))
+    kept = (qs, keys, values, att_full, lse)
+    split = (heads_here + 1) // 2
+    dq, dkv = attend_back(g, k, ks, head, 0, split, datt, *kept)
+    dq, dkv = [dq], [swap_flips([dkv[j] for j in range(ks)], "core")]
+    datt, d_out, out_sum = lax.optimization_barrier((datt, d_out, out_sum))
     d_out = total(d_out).astype(BF)
     pieces = [lax.dynamic_index_in_dim(d_out, g ^ i, axis=1, keepdims=False) for i in range(GROUPS)]
-    dkv, pieces = lax.optimization_barrier((dkv, pieces))
+    datt, pieces = lax.optimization_barrier((datt, pieces))
     d_out = swap_flips(pieces, "grp")
-    sh1_part, d_in, sums = project_back(g, k, dq, dkv, h1, hat_one, in_w)
-    sh1 = swap_flips([sh1_part[i] for i in range(GROUPS)], "grp")
-    sh1, d_out = lax.optimization_barrier((sh1, d_out))
-    sh1 = total(sh1)
+    more = attend_back(g, k, ks, head, split, heads_here - split, datt, *kept)
+    dq.append(more[0])
+    dkv.append(swap_flips([more[1][j] for j in range(ks)], "core"))
+    sh1_part, d_in, sums = project_back(g, dq, dkv, h1, hat_one, in_w)
+    sh1 = total(swap_flips(sh1_part, "grp"))
     hat_own, rate_own = norm_stats(x_f)
     delta_inputs = (slope_middle + norm_back(sh1, table[0:1], hat_own, rate_own)).astype(BF)[None]
 
@@ -871,14 +897,14 @@
     pieces = [lax.dynamic_index_in_dim(d_in, k ^ j, axis=1, keepdims=False) for j in range(ks)]
     d_in = total(swap_flips(pieces, "core")).astype(BF)
     d_in = jnp.concatenate([d_in, d_out], axis=1)
-    d_in = swap_flips([pick(d_in, z ^ i) for i in range(zs)], "fsdp")
+    pieces = lax.optimization_barrier([pick(d_in, z ^ i) for i in range(zs)])
+    d_in = swap_flips(pieces, "fsdp")
     d_hidden = gather_flips(d_hidden, "grp")
     d_in, d_hidden = lax.optimization_barrier((d_in, d_hidden))
     d_in = gather_flips(total(d_in).astype(BF), "grp")
     d_hidden = [d_hidden] + [[send(p, "core", j) for p in d_hidden] for j in range(1, ks)]
     d_exp_w, d_con_w = unfold(d_hidden, zs, g, k)
-    d_in, d_exp_w, d_con_w, out_part = lax.optimization_barrier((d_in, d_exp_w, d_con_w, out_part))
-    out_sum = swap_flips([out_part[i] for i in range(GROUPS)], "grp")
+    d_in, d_exp_w, d_con_w = lax.optimization_barrier((d_in, d_exp_w, d_con_w))
     d_in = in_order(gather_flips(in_order(d_in, g), "core"), k)
     outputs = (middle + total(out_sum) + c_bias).astype(BF)[None]
     packed = jnp.sum(d_in[:, :, own : own + extra].astype(F32), axis=1).reshape(-1)

time: 208 us -> 204 us (0.981)
  waiting for transfers between devices: 77.4 us -> 62.2 us
  local copies, waits for them, and re-layouts: 8.96 us -> 17.1 us
    ppermute x52 -> x53, waiting for transfers between devices: 75.6 us -> 62.2 us  [send(): return lax.ppermute(value, axis, [(s, s ^ flip) for s in range(count)])]
    unnamed x57 -> x115, local copies, waits for them, and re-layouts: 3.11 us -> 11 us
    pallas_call x2 -> x3, Pallas kernels: 11.9 us -> 13.3 us  [the longest x2 10.3 us: attend_back(): pl.pallas_call(functools.partial(attend_back_kernel, ks, head, first), gr...]
    ppermute x52 -> x53, starting transfers between devices: 50.7 us -> 50.5 us  [send(): return lax.ppermute(value, axis, [(s, s ^ flip) for s in range(count)])]
  transfers between devices with their start and end apart: 54 -> 55, of which waited for: 26 -> 23; matrix products, arithmetic and copies ran while one was open for 4% -> 5% of each run, Pallas kernels for 14% -> 15%
where the time goes in v6:
time: 204 us; the launch traced here: 201 us
  waiting for transfers between devices  62.2 us (30%)
  starting transfers between devices  50.6 us (25%)
  Pallas kernels  45.1 us (22%)
  local copies, waits for them, and re-layouts  17.1 us (8%)
  between operations  15.2 us (7%)
  other arithmetic  9.64 us (5%)
    ppermute x53, waiting for transfers between devices, send(): return lax.ppermute(value, axis, [(s, s ^ flip) for s in range(count)])  62.2 us
    ppermute x53, starting transfers between devices, send(): return lax.ppermute(value, axis, [(s, s ^ flip) for s in range(count)])  50.5 us
    unnamed x115, local copies, waits for them, and re-layouts  11 us
    pallas_call x2, Pallas kernels, attend_back(): pl.pallas_call(functools.partial(attend_back_kernel, ks, head, first), gr...  10.3 us
    pallas_call x1, Pallas kernels, attend(): pl.pallas_call(functools.partial(attend_kernel, ks, head), grid_spec=pltp...  8.47 us
    pallas_call x1, Pallas kernels, hidden_part(): pl.pallas_call(hidden_kernel, grid=(hidden // step,), in_specs=[pl.BlockS...  7.17 us
    pallas_call x1, Pallas kernels, hidden_grads(): pl.pallas_call(hidden_grad_kernel, grid=(width // step,), in_specs=[pl.Bl...  4.31 us
  transfers between devices with their start and end apart: 55, of which 23 were waited for; matrix products, arithmetic and copies ran while one was open for 5% of the time, Pallas kernels for 15%

profile of v6, /device:TPU:0, one launch (start us, length us, event | category | flops | bytes accessed | tf_op | source)
XLA Modules:
  0.0 201.4 jit_solution(11886051858845511384)
XLA Ops:
  7.3 1.9 shard_map.262.refs_0_
  9.2 3.1 %collective-permute-start = (bf16[240,576]{1,0:T(8,128)(2,1)S(1)}, bf16[240,576]{1,0:T(8,128)(2,1)S(1)}, u32[]{:S(2)}, u32[]{:S(2)}) collective-permute-start(bf16[240,576]{1,0:T(8,128)(2,1)S(1)} %shard_map.262.refs_0_), channel_id=1, source_target_pairs={{0,1},{1,0},{2,3},{3,2},{4,5},{5,4},{6,7},{7,6},{8,9},{9,8},{10,11... | collective-permute-start | bytes 829448 | tf_op jit(solution)/shard_map/ppermute | solution.py:43
  15.9 2.6 %collective-permute-start.1 = (bf16[240,576]{1,0:T(8,128)(2,1)S(1)}, bf16[240,576]{1,0:T(8,128)(2,1)S(1)}, u32[]{:S(2)}, u32[]{:S(2)}) collective-permute-start(bf16[240,576]{1,0:T(8,128)(2,1)S(1)} %shard_map.262.refs_0_), channel_id=1, source_target_pairs={{0,2},{1,3},{2,0},{3,1},{4,6},{5,7},{6,4},{7,5},{8,10},{9,11},{10,... | collective-permute-start | bytes 829448 | tf_op jit(solution)/shard_map/ppermute | solution.py:43
  18.5 4.8 %collective-permute-done.refs_1_ = bf16[240,576]{1,0:T(8,128)(2,1)S(1)} collective-permute-done((bf16[240,576]{1,0:T(8,128)(2,1)S(1)}, bf16[240,576]{1,0:T(8,128)(2,1)S(1)}, u32[]{:S(2)}, u32[]{:S(2)}) %collective-permute-start) | collective-permute-done | bytes 276512 | tf_op jit(solution)/shard_map/ppermute | solution.py:43
  23.3 2.6 %collective-permute-start.2 = (bf16[240,576]{1,0:T(8,128)(2,1)S(1)}, bf16[240,576]{1,0:T(8,128)(2,1)S(1)}, u32[]{:S(2)}, u32[]{:S(2)}) collective-permute-start(bf16[240,576]{1,0:T(8,128)(2,1)S(1)} %shard_map.262.refs_0_), channel_id=1, source_target_pairs={{0,3},{1,2},{2,1},{3,0},{4,7},{5,6},{6,5},{7,4},{8,11},{9,10},{10,... | collective-permute-start | bytes 829448 | tf_op jit(solution)/shard_map/ppermute | solution.py:43
  25.9 14.3 %collective-permute-done.1.refs_2_ = bf16[240,576]{1,0:T(8,128)(2,1)S(1)} collective-permute-done((bf16[240,576]{1,0:T(8,128)(2,1)S(1)}, bf16[240,576]{1,0:T(8,128)(2,1)S(1)}, u32[]{:S(2)}, u32[]{:S(2)}) %collective-permute-start.1) | collective-permute-done | bytes 276512 | tf_op jit(solution)/shard_map/ppermute | solution.py:43
  40.3 2.5 %shard_map.266 = bf16[96,1536]{1,0:T(8,128)(2,1)} custom-call(s32[2]{0:T(128)S(1)} %pad_add_fusion.place, bf16[768,768]{1,0:T(8,128)(2,1)} %con_ref, bf16[192,3072]{1,0:T(8,128)(2,1)} %exp_ref), custom_call_target="tpu_custom_call" | custom-call | tf_op jit(solution)/shard_map/pallas_call | solution.py:306
  48.2 8.5 %shard_map.265 = (bf16[128,192]{1,0:T(8,128)(2,1)S(1)}, bf16[128,192]{1,0:T(8,128)(2,1)S(1)}, bf16[128,192]{1,0:T(8,128)(2,1)S(1)}, bf16[128,192]{1,0:T(8,128)(2...) custom-call(s32[2]{0:T(128)S(1)} %pad_add_fusion.place, ...), custom_call_target="tpu_custom_call" | custom-call | flops 1 | bytes 1 | tf_op jit(solution)/shard_map/pallas_call | solution.py:615
  62.5 2.4 %collective-permute-done.16 = bf16[128,192]{1,0:T(8,128)(2,1)S(1)} collective-permute-done((bf16[128,192]{1,0:T(8,128)(2,1)S(1)}, bf16[128,192]{1,0:T(8,128)(2,1)S(1)}, u32[]{:S(2)}, u32[]{:S(2)}) %collective-permute-start.16) | collective-permute-done | bytes 49184 | tf_op jit(solution)/shard_map/ppermute | solution.py:43
  66.9 2.5 %collective-permute-start.19 = (bf16[128,768]{1,0:T(8,128)(2,1)S(1)}, bf16[128,768]{1,0:T(8,128)(2,1)S(1)}, u32[]{:S(2)}, u32[]{:S(2)}) collective-permute-start(bf16[128,768]{1,0:T(8,128)(2,1)S(1)} %add_convert_fusion.2.refs_0_), channel_id=1, source_target_pairs={{0,24},{8,16},{16,8},{24,0},{1,25},{9,17},{17,9},{25,1},{2,26},{10... | collective-permute-start | bytes 589832 | tf_op jit(solution)/shard_map/ppermute | solution.py:43
  69.4 4.3 %collective-permute-done.17.refs_1_ = bf16[128,768]{1,0:T(8,128)(2,1)S(1)} collective-permute-done((bf16[128,768]{1,0:T(8,128)(2,1)S(1)}, bf16[128,768]{1,0:T(8,128)(2,1)S(1)}, u32[]{:S(2)}, u32[]{:S(2)}) %collective-permute-start.17) | collective-permute-done | bytes 196640 | tf_op jit(solution)/shard_map/ppermute | solution.py:43
  80.4 7.2 %shard_map.267 = (bf16[512,768]{1,0:T(8,128)(2,1)S(1)}, bf16[512,768]{1,0:T(8,128)(2,1)S(1)}, bf16[128,768]{1,0:T(8,128)(2,1)S(1)}, bf16[128,768]{1,0:T(8,128)(2...) custom-call(bf16[128,768]{1,0:T(8,128)(2,1)S(1)} %add_convert_fusion, ...), custom_call_target="tpu_custom_call" | custom-call | flops 1 | bytes 1 | tf_op jit(solution)/shard_map/pallas_call | solution.py:480
  88.3 1.9 collective-permute-start.20
  91.8 4.3 %shard_map.268 = bf16[768,1536]{1,0:T(8,128)(2,1)} custom-call(bf16[128,768]{1,0:T(8,128)(2,1)S(1)} %add_convert_fusion.2.refs_0_, bf16[128,768]{1,0:T(8,128)(2,1)S(1)} %copy-done.10, bf16[128,768]{1,0:T(8,128)(2,1)S(1)} %copy-done.12, bf16[128,768]{1,0:T(8,128)(2,1)S(1)} %copy-done.14, bf16[2,128,768]{2,1,0:T(8,128)(2,1)} %copy-done, ...), custom_call_target="tpu_custom_call" | custom-call | flops 8000000000 | bytes 1 | tf_op jit(solution)/shard_map/pallas_call | solution.py:531
  96.1 5.2 %collective-permute-done.21 = bf16[128,768]{1,0:T(8,128)(2,1)} collective-permute-done((bf16[128,768]{1,0:T(8,128)(2,1)S(1)}, bf16[128,768]{1,0:T(8,128)(2,1)}, u32[]{:S(2)}, u32[]{:S(2)}) %collective-permute-start.21) | collective-permute-done | bytes 196640 | tf_op jit(solution)/shard_map/ppermute | solution.py:43
  117.7 6.6 %shard_map.269 = (bf16[512,128]{1,0:T(8,128)(2,1)S(1)}, bf16[2,512,256]{2,1,0:T(8,128)(2,1)S(1)}) custom-call(s32[2]{0:T(128)S(1)} %pad_add_fusion.place, bf16[128,192]{1,0:T(8,128)(2,1)S(1)} %get-tuple-element.178.refs_0_, bf16[128,192]{1,0:T(8,128)(2,1)S(1)} %collective-permute-done.23.refs_1_, bf16[128,192]{1,0:T(8,128)(2,1)S(1)} %collective-permute-done.24.refs_2_, ...), custom_call_target="tpu_custom_call" | custom-call | flops 8000000000 | bytes 1 | tf_op jit(solution)/shard_map/pallas_call | solution.py:678
  127.2 3.7 %shard_map.270 = (bf16[512,64]{1,0:T(8,128)(2,1)S(1)}, bf16[2,512,128]{2,1,0:T(8,128)(2,1)S(1)}) custom-call(s32[2]{0:T(128)S(1)} %pad_add_fusion.place, bf16[128,192]{1,0:T(8,128)(2,1)S(1)} %get-tuple-element.178.refs_0_, bf16[128,192]{1,0:T(8,128)(2,1)S(1)} %collective-permute-done.23.refs_1_, bf16[128,192]{1,0:T(8,128)(2,1)S(1)} %collective-permute-done.24.refs_2_, ...), custom_call_target="tpu_custom_call" | custom-call | flops 8000000000 | bytes 1 | tf_op jit(solution)/shard_map/pallas_call | solution.py:678
  134.9 2.9 %shard_map.271 = (bf16[128,768]{1,0:T(8,128)(2,1)S(1)}, bf16[128,768]{1,0:T(8,128)(2,1)S(1)}, bf16[128,768]{1,0:T(8,128)(2,1)S(1)}, bf16[128,768]{1,0:T(8,128)(2...) custom-call(s32[1]{0:T(128)} %bitcast.1.place, bf16[512,128]{1,0:T(8,128)(2,1)S(1)} %get-tuple-element.171.refs_0_, ...), custom_call_target="tpu_custom_call" | custom-call | flops 1 | bytes 1 | tf_op jit(solution)/shard_map/pallas_call | solution.py:725
  150.4 1.8 collective-permute-start.41
  152.2 11.0 %collective-permute-done.40 = bf16[130,576]{1,0:T(8,128)(2,1)S(1)} collective-permute-done((bf16[130,576]{1,0:T(8,128)(2,1)}, bf16[130,576]{1,0:T(8,128)(2,1)S(1)}, u32[]{:S(2)}, u32[]{:S(2)}) %collective-permute-start.40) | collective-permute-done | bytes 149792 | tf_op jit(solution)/shard_map/ppermute | solution.py:43
  170.9 3.3 %collective-permute-done.34 = bf16[128,768]{1,0:T(8,128)(2,1)S(1)} collective-permute-done((bf16[128,768]{1,0:T(8,128)(2,1)S(1)}, bf16[128,768]{1,0:T(8,128)(2,1)S(1)}, u32[]{:S(2)}, u32[]{:S(2)}) %collective-permute-start.34) | collective-permute-done | bytes 196640 | tf_op jit(solution)/shard_map/ppermute | solution.py:43
  178.0 3.1 %shard_map.273 = (f32[2,96,3072]{2,1,0:T(8,128)}, f32[4,2,96,768]{3,2,1,0:T(8,128)}) custom-call(s32[2]{0:T(128)S(1)} %pad_add_fusion.place, bf16[96,1536]{1,0:T(8,128)(2,1)S(1)} %copy-done.8, bf16[96,1536]{1,0:T(8,128)(2,1)S(1)} %collective-permute-done.42.refs_1_, bf16[96,1536]{1,0:T(8,128)(2,1)S(1)} %collective-permute-done.43.refs_2_, ...), custom_call_target="tpu_custom_call" | custom-call | flops 1 | bytes 1 | tf_op jit(solution)/shard_map/pallas_call | solution.py:400
  181.1 3.7 %collective-permute-done.46 = bf16[130,576]{1,0:T(8,128)(2,1)S(1)} collective-permute-done((bf16[130,576]{1,0:T(8,128)(2,1)S(1)}, bf16[130,576]{1,0:T(8,128)(2,1)S(1)}, u32[]{:S(2)}, u32[]{:S(2)}) %collective-permute-start.46) | collective-permute-done | bytes 149792 | tf_op jit(solution)/shard_map/ppermute | solution.py:43
  192.0 2.6 %shard_map.274 = f32[192,2304]{1,0:T(8,128)} custom-call(bf16[4,192,576]{2,1,0:T(8,128)(2,1)S(1)} %bitcast.140), custom_call_target="tpu_custom_call" | custom-call | tf_op jit(solution)/shard_map/pallas_call | solution.py:368
  (294 shorter events, 79.4 us)
Async XLA Ops:
  7.2 70.4 %all-gather.2.cloned.1.call-start = ((), (), s32[]{:S(2)}) async-start(), calls=%async_computation.1 | async-start | bytes 2654208 | tf_op jit(solution)/shard_map/all_gather | solution.py:817
  9.2 14.1 %collective-permute-start = (bf16[240,576]{1,0:T(8,128)(2,1)S(1)}, bf16[240,576]{1,0:T(8,128)(2,1)S(1)}, u32[]{:S(2)}, u32[]{:S(2)}) collective-permute-start(bf16[240,576]{1,0:T(8,128)(2,1)S(1)} %shard_map.262.refs_0_), channel_id=1, source_target_pairs={{0,1},{1,0},{2,3},{3,2},{4,5},{5,4},{6,7},{7,6},{8,9},{9,8},{10,11... | collective-permute-start | bytes 829448 | tf_op jit(solution)/shard_map/ppermute | solution.py:43
  12.4 27.8 %collective-permute-start.3 = (bf16[2,128,768]{2,1,0:T(8,128)(2,1)S(1)}, bf16[2,128,768]{2,1,0:T(8,128)(2,1)S(1)}, u32[]{:S(2)}, u32[]{:S(2)}) collective-permute-start(bf16[2,128,768]{2,1,0:T(8,128)(2,1)S(1)} %constant_dynamic-update-slice_fusion.refs_0_.refs_4_), channel_id=1, source_target_pairs={{0,8},{8,0},{16,24},{24,16},{1,9},{9,1},{17,25},{25,17},{2,10},{10... | collective-permute-start | bytes 1179656 | tf_op jit(solution)/shard_map/ppermute | solution.py:43
  14.0 26.3 %collective-permute-start.4 = (bf16[2,128,768]{2,1,0:T(8,128)(2,1)S(1)}, bf16[2,128,768]{2,1,0:T(8,128)(2,1)S(1)}, u32[]{:S(2)}, u32[]{:S(2)}) collective-permute-start(bf16[2,128,768]{2,1,0:T(8,128)(2,1)S(1)} %constant_dynamic-update-slice_fusion.refs_0_.refs_4_), channel_id=1, source_target_pairs={{0,16},{8,24},{16,0},{24,8},{1,17},{9,25},{17,1},{25,9},{2,18},{10... | collective-permute-start | bytes 1179656 | tf_op jit(solution)/shard_map/ppermute | solution.py:43
  15.5 24.8 %collective-permute-start.5 = (bf16[2,128,768]{2,1,0:T(8,128)(2,1)S(1)}, bf16[2,128,768]{2,1,0:T(8,128)(2,1)S(1)}, u32[]{:S(2)}, u32[]{:S(2)}) collective-permute-start(bf16[2,128,768]{2,1,0:T(8,128)(2,1)S(1)} %constant_dynamic-update-slice_fusion.refs_0_.refs_4_), channel_id=1, source_target_pairs={{0,24},{8,16},{16,8},{24,0},{1,25},{9,17},{17,9},{25,1},{2,26},{10... | collective-permute-start | bytes 1179656 | tf_op jit(solution)/shard_map/ppermute | solution.py:43
  15.9 24.3 %collective-permute-start.1 = (bf16[240,576]{1,0:T(8,128)(2,1)S(1)}, bf16[240,576]{1,0:T(8,128)(2,1)S(1)}, u32[]{:S(2)}, u32[]{:S(2)}) collective-permute-start(bf16[240,576]{1,0:T(8,128)(2,1)S(1)} %shard_map.262.refs_0_), channel_id=1, source_target_pairs={{0,2},{1,3},{2,0},{3,1},{4,6},{5,7},{6,4},{7,5},{8,10},{9,11},{10,... | collective-permute-start | bytes 829448 | tf_op jit(solution)/shard_map/ppermute | solution.py:43
  23.3 16.9 %collective-permute-start.2 = (bf16[240,576]{1,0:T(8,128)(2,1)S(1)}, bf16[240,576]{1,0:T(8,128)(2,1)S(1)}, u32[]{:S(2)}, u32[]{:S(2)}) collective-permute-start(bf16[240,576]{1,0:T(8,128)(2,1)S(1)} %shard_map.262.refs_0_), channel_id=1, source_target_pairs={{0,3},{1,2},{2,1},{3,0},{4,7},{5,6},{6,5},{7,4},{8,11},{9,10},{10,... | collective-permute-start | bytes 829448 | tf_op jit(solution)/shard_map/ppermute | solution.py:43
  42.8 102.4 %reduce-scatter.2.cloned.1.call-start = ((), (), s32[]{:S(2)}) async-start(), calls=%async_computation.2 | async-start | bytes 2654208 | tf_op jit(solution)/shard_map/reduce_scatter | solution.py:836
  66.4 9.8 %collective-permute-start.18 = (bf16[128,768]{1,0:T(8,128)(2,1)S(1)}, bf16[128,768]{1,0:T(8,128)(2,1)S(1)}, u32[]{:S(2)}, u32[]{:S(2)}) collective-permute-start(bf16[128,768]{1,0:T(8,128)(2,1)S(1)} %add_convert_fusion.2.refs_0_), channel_id=1, source_target_pairs={{0,16},{8,24},{16,0},{24,8},{1,17},{9,25},{17,1},{25,9},{2,18},{10... | collective-permute-start | bytes 589832 | tf_op jit(solution)/shard_map/ppermute | solution.py:43
  66.9 10.0 %collective-permute-start.19 = (bf16[128,768]{1,0:T(8,128)(2,1)S(1)}, bf16[128,768]{1,0:T(8,128)(2,1)S(1)}, u32[]{:S(2)}, u32[]{:S(2)}) collective-permute-start(bf16[128,768]{1,0:T(8,128)(2,1)S(1)} %add_convert_fusion.2.refs_0_), channel_id=1, source_target_pairs={{0,24},{8,16},{16,8},{24,0},{1,25},{9,17},{17,9},{25,1},{2,26},{10... | collective-permute-start | bytes 589832 | tf_op jit(solution)/shard_map/ppermute | solution.py:43
  90.2 11.1 %collective-permute-start.21 = (bf16[128,768]{1,0:T(8,128)(2,1)S(1)}, bf16[128,768]{1,0:T(8,128)(2,1)}, u32[]{:S(2)}, u32[]{:S(2)}) collective-permute-start(bf16[128,768]{1,0:T(8,128)(2,1)S(1)} %get-tuple-element.135), channel_id=1, source_target_pairs={{0,16},{8,24},{16,0},{24,8},{1,17},{9,25},{17,1},{25,9},{2,18},{10... | collective-permute-start | bytes 589832 | tf_op jit(solution)/shard_map/ppermute | solution.py:43
  91.7 9.6 %collective-permute-start.22 = (bf16[128,768]{1,0:T(8,128)(2,1)S(1)}, bf16[128,768]{1,0:T(8,128)(2,1)}, u32[]{:S(2)}, u32[]{:S(2)}) collective-permute-start(bf16[128,768]{1,0:T(8,128)(2,1)S(1)} %get-tuple-element.136), channel_id=1, source_target_pairs={{0,24},{8,16},{16,8},{24,0},{1,25},{9,17},{17,9},{25,1},{2,26},{10... | collective-permute-start | bytes 589832 | tf_op jit(solution)/shard_map/ppermute | solution.py:43
  113.4 12.8 %collective-permute-start.26 = (bf16[4,4,24,768]{3,2,1,0:T(8,128)(2,1)S(1)}, bf16[4,4,24,768]{3,2,1,0:T(8,128)(2,1)S(1)}, u32[]{:S(2)}, u32[]{:S(2)}) collective-permute-start(bf16[4,4,24,768]{3,2,1,0:T(8,128)(2,1)S(1)} %get-tuple-element.157), channel_id=1, source_target_pairs={{0,4},{4,0},{1,5},{5,1},{2,6},{6,2},{3,7},{7,3},{8,12},{12,8},{9,1... | collective-permute-start | bytes 1769480 | tf_op jit(solution)/shard_map/ppermute | solution.py:43
  114.2 10.2 %collective-permute-start.27 = (bf16[128,768]{1,0:T(8,128)(2,1)S(1)}, bf16[128,768]{1,0:T(8,128)(2,1)S(1)}, u32[]{:S(2)}, u32[]{:S(2)}) collective-permute-start(bf16[128,768]{1,0:T(8,128)(2,1)S(1)} %copy-done.56), channel_id=1, source_target_pairs={{0,8},{8,0},{16,24},{24,16},{1,9},{9,1},{17,25},{25,17},{2,10},{10... | collective-permute-start | bytes 589832 | tf_op jit(solution)/shard_map/ppermute | solution.py:43
  115.7 10.5 %collective-permute-start.28 = (bf16[128,768]{1,0:T(8,128)(2,1)S(1)}, bf16[128,768]{1,0:T(8,128)(2,1)S(1)}, u32[]{:S(2)}, u32[]{:S(2)}) collective-permute-start(bf16[128,768]{1,0:T(8,128)(2,1)S(1)} %copy-done.55), channel_id=1, source_target_pairs={{0,16},{8,24},{16,0},{24,8},{1,17},{9,25},{17,1},{25,9},{2,18},{10... | collective-permute-start | bytes 589832 | tf_op jit(solution)/shard_map/ppermute | solution.py:43
  116.3 9.9 %collective-permute-start.29 = (bf16[128,768]{1,0:T(8,128)(2,1)S(1)}, bf16[128,768]{1,0:T(8,128)(2,1)S(1)}, u32[]{:S(2)}, u32[]{:S(2)}) collective-permute-start(bf16[128,768]{1,0:T(8,128)(2,1)S(1)} %copy-done.54), channel_id=1, source_target_pairs={{0,24},{8,16},{16,8},{24,0},{1,25},{9,17},{17,9},{25,1},{2,26},{10... | collective-permute-start | bytes 589832 | tf_op jit(solution)/shard_map/ppermute | solution.py:43
  124.4 10.5 %collective-permute-start.30 = (bf16[512,256]{1,0:T(8,128)(2,1)S(1)}, bf16[512,256]{1,0:T(8,128)(2,1)S(1)}, u32[]{:S(2)}, u32[]{:S(2)}) collective-permute-start(bf16[512,256]{1,0:T(8,128)(2,1)S(1)} %get-tuple-element.261), channel_id=1, source_target_pairs={{0,4},{4,0},{1,5},{5,1},{2,6},{6,2},{3,7},{7,3},{8,12},{12,8},{9,1... | collective-permute-start | bytes 786440 | tf_op jit(solution)/shard_map/ppermute | solution.py:43
  145.2 19.8 %collective-permute-start.42 = (bf16[96,1536]{1,0:T(8,128)(2,1)}, bf16[96,1536]{1,0:T(8,128)(2,1)S(1)}, u32[]{:S(2)}, u32[]{:S(2)}) collective-permute-start(bf16[96,1536]{1,0:T(8,128)(2,1)} %reduce-scatter.2.cloned.1.call-done.refs_0_), channel_id=1, source_target_pairs={{0,8},{8,0},{16,24},{24,16},{1,9},{9,1},{17,25},{25,17},{2,10},{10... | collective-permute-start | bytes 884744 | tf_op jit(solution)/shard_map/ppermute | solution.py:43
  146.2 18.8 %collective-permute-start.43 = (bf16[96,1536]{1,0:T(8,128)(2,1)}, bf16[96,1536]{1,0:T(8,128)(2,1)S(1)}, u32[]{:S(2)}, u32[]{:S(2)}) collective-permute-start(bf16[96,1536]{1,0:T(8,128)(2,1)} %reduce-scatter.2.cloned.1.call-done.refs_0_), channel_id=1, source_target_pairs={{0,16},{8,24},{16,0},{24,8},{1,17},{9,25},{17,1},{25,9},{2,18},{10... | collective-permute-start | bytes 884744 | tf_op jit(solution)/shard_map/ppermute | solution.py:43
  147.5 17.5 %collective-permute-start.44 = (bf16[96,1536]{1,0:T(8,128)(2,1)}, bf16[96,1536]{1,0:T(8,128)(2,1)S(1)}, u32[]{:S(2)}, u32[]{:S(2)}) collective-permute-start(bf16[96,1536]{1,0:T(8,128)(2,1)} %reduce-scatter.2.cloned.1.call-done.refs_0_), channel_id=1, source_target_pairs={{0,24},{8,16},{16,8},{24,0},{1,25},{9,17},{17,9},{25,1},{2,26},{10... | collective-permute-start | bytes 884744 | tf_op jit(solution)/shard_map/ppermute | solution.py:43
  148.9 14.3 %collective-permute-start.40 = (bf16[130,576]{1,0:T(8,128)(2,1)}, bf16[130,576]{1,0:T(8,128)(2,1)S(1)}, u32[]{:S(2)}, u32[]{:S(2)}) collective-permute-start(bf16[130,576]{1,0:T(8,128)(2,1)} %get-tuple-element.200), channel_id=1, source_target_pairs={{0,2},{1,3},{2,0},{3,1},{4,6},{5,7},{6,4},{7,5},{8,10},{9,11},{10,... | collective-permute-start | bytes 449288 | tf_op jit(solution)/shard_map/ppermute | solution.py:43
  150.4 13.8 %collective-permute-start.41 = (bf16[130,576]{1,0:T(8,128)(2,1)}, bf16[130,576]{1,0:T(8,128)(2,1)S(1)}, u32[]{:S(2)}, u32[]{:S(2)}) collective-permute-start(bf16[130,576]{1,0:T(8,128)(2,1)} %get-tuple-element.201), channel_id=1, source_target_pairs={{0,3},{1,2},{2,1},{3,0},{4,7},{5,6},{6,5},{7,4},{8,11},{9,10},{10,... | collective-permute-start | bytes 449288 | tf_op jit(solution)/shard_map/ppermute | solution.py:43
  165.0 10.8 %collective-permute-start.48 = (bf16[96,1536]{1,0:T(8,128)(2,1)}, bf16[96,1536]{1,0:T(8,128)(2,1)S(1)}, u32[]{:S(2)}, u32[]{:S(2)}) collective-permute-start(bf16[96,1536]{1,0:T(8,128)(2,1)} %reduce-scatter.2.cloned.1.call-done.refs_0_), channel_id=1, source_target_pairs={{0,4},{4,0},{1,5},{5,1},{2,6},{6,2},{3,7},{7,3},{8,12},{12,8},{9,1... | collective-permute-start | bytes 884744 | tf_op jit(solution)/shard_map/ppermute | solution.py:43
  165.1 11.4 %collective-permute-start.49 = (bf16[96,1536]{1,0:T(8,128)(2,1)S(1)}, bf16[96,1536]{1,0:T(8,128)(2,1)S(1)}, u32[]{:S(2)}, u32[]{:S(2)}) collective-permute-start(bf16[96,1536]{1,0:T(8,128)(2,1)S(1)} %collective-permute-done.42.refs_1_), channel_id=1, source_target_pairs={{0,4},{4,0},{1,5},{5,1},{2,6},{6,2},{3,7},{7,3},{8,12},{12,8},{9,1... | collective-permute-start | bytes 884744 | tf_op jit(solution)/shard_map/ppermute | solution.py:43
  (89 other events, 649.7 us)
Sparse Core Ops, SparseCore 0:
  42.9 34.6 all-gather.1
  108.7 35.3 reduce-scatter.1

commit v7 on v6

--- a/solution.py
+++ b/solution.py
@@ -352,27 +352,6 @@
         cost_estimate=SHORT,
     )(jnp.stack([first, k]).astype(jnp.int32), *[p for group in pieces for p in group])
     return out.reshape(zs, ks * rows, cols)
-
-
-def weave_kernel(parts, pieces, out):
-    wide = pieces.shape[2] // parts
-    for i in range(GROUPS):
-        for part in range(parts):
-            low = (part * GROUPS + i) * wide
-            out[:, low : low + wide] = pieces[i, :, part * wide : (part + 1) * wide].astype(F32)
-
-
-def weave(pieces, parts):
-    rows, cols = pieces.shape[1], pieces.shape[2]
-    step = 32
-    return pl.pallas_call(
-        functools.partial(weave_kernel, parts),
-        grid=(rows // step,),
-        in_specs=[pl.BlockSpec((GROUPS, step, cols), lambda i: (0, i, 0))],
-        out_specs=pl.BlockSpec((step, GROUPS * cols), lambda i: (i, 0)),
-        out_shape=jax.ShapeDtypeStruct((rows, GROUPS * cols), F32),
-        compiler_params=pltpu.CompilerParams(vmem_limit_bytes=16 * 2**20),
-    )(pieces)
 
 
 def unfold_kernel(parts, ks, place, *refs):
@@ -504,7 +483,7 @@
         scratch_shapes=[pltpu.VMEM((rows, width), BF)] * 2 + [pltpu.VMEM((rows, width), F32)] * 2,
         compiler_params=pltpu.CompilerParams(vmem_limit_bytes=24 * 2**20),
         cost_estimate=SHORT,
-    )(*h_rows, *in_hbm(*s_rows, weights, weights), table)
+    )(*in_hbm(*h_rows, *s_rows, weights, weights), table)
     return got[0], got[1], got[2 : 2 + GROUPS], got[2 + GROUPS : 2 + 2 * GROUPS], got[-1]
 
 
@@ -539,7 +518,7 @@
         scratch_shapes=[pltpu.VMEM((rows, step), BF), pltpu.VMEM((rows, width), BF)],
         compiler_params=pltpu.CompilerParams(vmem_limit_bytes=16 * 2**20),
         cost_estimate=LONG,
-    )(*h_rows, *in_hbm(*s_rows), slope_inner, act)
+    )(*in_hbm(*h_rows, *s_rows), slope_inner, act)
 
 
 def visible(k, tok, keys):
@@ -747,6 +726,48 @@
     return got[:GROUPS], got[GROUPS], got[GROUPS + 1]
 
 
+def finish_kernel(ks, extra, place, *refs):
+    pieces, (in_out, out_out, vec_out, held) = refs[:-4], refs[-4:]
+    own, cols = in_out.shape[1], held.shape[2]
+    part, low = cols // 3, own + extra
+    share = own // GROUPS
+    third = share // 3
+    over = out_out.shape[3] - cols
+    for j in range(ks):
+        for i in range(GROUPS):
+            held[place[0] ^ i] = pieces[j * GROUPS + i][...].astype(F32)
+        spot = place[1] ^ j
+        for i in range(GROUPS):
+            for n in range(3):
+                to = (n * GROUPS + i) * part
+                in_out[spot, :, to : to + part] = held[i, :own, n * part : (n + 1) * part]
+                out_out[i, spot, n * third : (n + 1) * third, cols:] = held[
+                    i, low + share :, n * over : (n + 1) * over
+                ]
+            out_out[i, spot, :, :cols] = held[i, low : low + share, :]
+        vec_out[spot] = total([held[i, own:low, :] for i in range(GROUPS)])
+
+
+def finish(pieces, own, extra, width, g, k):
+    ks = len(pieces)
+    tall, cols = pieces[0][0].shape
+    vmem = pl.BlockSpec(memory_space=pltpu.VMEM)
+    shapes = [(ks, own, GROUPS * cols), (GROUPS, ks, own // GROUPS, width), (ks, extra, cols)]
+    in_w, out_w, vectors = pl.pallas_call(
+        functools.partial(finish_kernel, ks, extra),
+        grid_spec=pltpu.PrefetchScalarGridSpec(
+            num_scalar_prefetch=1,
+            in_specs=[vmem] * (ks * GROUPS),
+            out_specs=[vmem] * 3,
+            scratch_shapes=[pltpu.VMEM((GROUPS, tall, cols), F32)],
+        ),
+        out_shape=[jax.ShapeDtypeStruct(s, F32) for s in shapes],
+        compiler_params=pltpu.CompilerParams(vmem_limit_bytes=16 * 2**20),
+        cost_estimate=SHORT,
+    )(jnp.stack([g, k]).astype(jnp.int32), *[p for group in pieces for p in group])
+    return in_w.reshape(ks * own, -1), out_w.reshape(ks * own, width), vectors.reshape(-1)
+
+
 def shards(
     inputs,
     cotangent,
@@ -790,9 +811,8 @@
         cut = cut_weight(input_weight, 3, g, k, ks)
     pieces = gather_flips(cut, "fsdp")
     rows_both = gather_flips(jnp.concatenate([inputs, cotangent]), "grp")
-    pieces, rows_both, con_raw, exp_raw = lax.optimization_barrier(
-        (pieces, rows_both, contract_weight, expand_weight)
-    )
+    rest = cut_rest(contract_weight, expand_weight, zs, g, k, ks)
+    pieces, rows_both, rest = lax.optimization_barrier((pieces, rows_both, rest))
     x_more = [send(b[0], "core", j) for j in range(1, ks) for b in rows_both]
     more = [[send(b, "core", j) for b in pieces] for j in range(1, ks)]
     if aligned:
@@ -813,7 +833,6 @@
         table = jnp.pad(jnp.stack(vectors), ((0, 7), (0, 0)))
     o_bias, gain_two, shift_two, c_bias = [table[i : i + 1] for i in range(4, 8)]
 
-    rest = cut_rest(con_raw, exp_raw, zs, g, k, ks)
     rest = lax.all_gather(rest, ("fsdp", "core"), axis=0, tiled=True)
 
     *slots, qs, keys, values, att_full, lse, h1, hat_one = attend(
@@ -865,7 +884,8 @@
     dq.append(more[0])
     dkv.append(swap_flips([more[1][j] for j in range(ks)], "core"))
     sh1_part, d_in, sums = project_back(g, dq, dkv, h1, hat_one, in_w)
-    sh1 = total(swap_flips(sh1_part, "grp"))
+    sh1, d_hidden = lax.optimization_barrier((swap_flips(sh1_part, "grp"), d_hidden))
+    sh1 = total(sh1)
     hat_own, rate_own = norm_stats(x_f)
     delta_inputs = (slope_middle + norm_back(sh1, table[0:1], hat_own, rate_own)).astype(BF)[None]
 
@@ -900,30 +920,13 @@
     pieces = lax.optimization_barrier([pick(d_in, z ^ i) for i in range(zs)])
     d_in = swap_flips(pieces, "fsdp")
     d_hidden = gather_flips(d_hidden, "grp")
-    d_in, d_hidden = lax.optimization_barrier((d_in, d_hidden))
     d_in = gather_flips(total(d_in).astype(BF), "grp")
     d_hidden = [d_hidden] + [[send(p, "core", j) for p in d_hidden] for j in range(1, ks)]
     d_exp_w, d_con_w = unfold(d_hidden, zs, g, k)
     d_in, d_exp_w, d_con_w = lax.optimization_barrier((d_in, d_exp_w, d_con_w))
-    d_in = in_order(gather_flips(in_order(d_in, g), "core"), k)
     outputs = (middle + total(out_sum) + c_bias).astype(BF)[None]
-    packed = jnp.sum(d_in[:, :, own : own + extra].astype(F32), axis=1).reshape(-1)
-    d_out = d_in[:, :, own + extra :].transpose(1, 0, 2, 3)
-    tail = d_out[:, :, 3 * third :].reshape(GROUPS, ks, third, 3, width - 3 * cols)
-    d_out_w = (
-        jnp.concatenate(
-            [
-                d_out[:, :, : 3 * third],
-                jnp.concatenate([tail[:, :, :, i] for i in range(3)], axis=2),
-            ],
-            axis=3,
-        )
-        .reshape(rows_z, width)
-        .astype(F32)
-    )
-    d_in_w = weave(
-        d_in[:, :, :own].transpose(1, 0, 2, 3).reshape(GROUPS, rows_z, 3 * cols), 3
-    )
+    d_in = [d_in] + [[send(p, "core", j) for p in d_in] for j in range(1, ks)]
+    d_in_w, d_out_w, packed = finish(d_in, own, extra, width, g, k)
 
     def vec(i):
         return packed[i * rows_z : (i + 1) * rows_z]

time: 204 us -> 183 us (0.90)
  local copies, waits for them, and re-layouts: 17.1 us -> 6.16 us
  waiting for transfers between devices: 62.2 us -> 54.8 us
  other arithmetic: 9.64 us -> 7.22 us
    ppermute x53 -> x56, waiting for transfers between devices: 62.2 us -> 52.8 us  [send(): return lax.ppermute(value, axis, [(s, s ^ flip) for s in range(count)])]
    unnamed x115 -> x75, local copies, waits for them, and re-layouts: 11 us -> 2.29 us
    ppermute x53 -> x56, starting transfers between devices: 50.5 us -> 51.4 us  [send(): return lax.ppermute(value, axis, [(s, s ^ flip) for s in range(count)])]
  transfers between devices with their start and end apart: 55 -> 58, of which waited for: 23 -> 23; matrix products, arithmetic and copies ran while one was open for 5% -> 5% of each run, Pallas kernels for 15% -> 19%
where the time goes in v7:
time: 183 us; the launch traced here: 182 us
  waiting for transfers between devices  54.8 us (30%)
  starting transfers between devices  51.5 us (28%)
  Pallas kernels  46.2 us (25%)
  between operations  14.9 us (8%)
  other arithmetic  7.22 us (4%)
  local copies, waits for them, and re-layouts  6.16 us (3%)
    ppermute x56, waiting for transfers between devices, send(): return lax.ppermute(value, axis, [(s, s ^ flip) for s in range(count)])  52.8 us
    ppermute x56, starting transfers between devices, send(): return lax.ppermute(value, axis, [(s, s ^ flip) for s in range(count)])  51.4 us
    pallas_call x2, Pallas kernels, attend_back(): pl.pallas_call(functools.partial(attend_back_kernel, ks, head, first), gr...  10.3 us
    pallas_call x1, Pallas kernels, attend(): pl.pallas_call(functools.partial(attend_kernel, ks, head), grid_spec=pltp...  8.43 us
    pallas_call x1, Pallas kernels, hidden_part(): pl.pallas_call(hidden_kernel, grid=(hidden // step,), in_specs=[pl.BlockS...  7.5 us
    pallas_call x1, Pallas kernels, hidden_grads(): pl.pallas_call(hidden_grad_kernel, grid=(width // step,), in_specs=[pl.Bl...  4.71 us
  transfers between devices with their start and end apart: 58, of which 23 were waited for; matrix products, arithmetic and copies ran while one was open for 5% of the time, Pallas kernels for 19%

profile of v7, /device:TPU:0, one launch (start us, length us, event | category | flops | bytes accessed | tf_op | source)
XLA Modules:
  0.0 182.2 jit_solution(15087144213898957027)
XLA Ops:
  9.2 3.1 %collective-permute-start = (bf16[240,576]{1,0:T(8,128)(2,1)S(1)}, bf16[240,576]{1,0:T(8,128)(2,1)S(1)}, u32[]{:S(2)}, u32[]{:S(2)}) collective-permute-start(bf16[240,576]{1,0:T(8,128)(2,1)S(1)} %shard_map.262.refs_0_), channel_id=1, source_target_pairs={{0,1},{1,0},{2,3},{3,2},{4,5},{5,4},{6,7},{7,6},{8,9},{9,8},{10,11... | collective-permute-start | bytes 829448 | tf_op jit(solution)/shard_map/ppermute | solution.py:43
  15.9 2.6 %collective-permute-start.1 = (bf16[240,576]{1,0:T(8,128)(2,1)S(1)}, bf16[240,576]{1,0:T(8,128)(2,1)S(1)}, u32[]{:S(2)}, u32[]{:S(2)}) collective-permute-start(bf16[240,576]{1,0:T(8,128)(2,1)S(1)} %shard_map.262.refs_0_), channel_id=1, source_target_pairs={{0,2},{1,3},{2,0},{3,1},{4,6},{5,7},{6,4},{7,5},{8,10},{9,11},{10,... | collective-permute-start | bytes 829448 | tf_op jit(solution)/shard_map/ppermute | solution.py:43
  18.5 4.8 %collective-permute-done.refs_1_ = bf16[240,576]{1,0:T(8,128)(2,1)S(1)} collective-permute-done((bf16[240,576]{1,0:T(8,128)(2,1)S(1)}, bf16[240,576]{1,0:T(8,128)(2,1)S(1)}, u32[]{:S(2)}, u32[]{:S(2)}) %collective-permute-start) | collective-permute-done | bytes 276512 | tf_op jit(solution)/shard_map/ppermute | solution.py:43
  23.3 2.6 %collective-permute-start.2 = (bf16[240,576]{1,0:T(8,128)(2,1)S(1)}, bf16[240,576]{1,0:T(8,128)(2,1)S(1)}, u32[]{:S(2)}, u32[]{:S(2)}) collective-permute-start(bf16[240,576]{1,0:T(8,128)(2,1)S(1)} %shard_map.262.refs_0_), channel_id=1, source_target_pairs={{0,3},{1,2},{2,1},{3,0},{4,7},{5,6},{6,5},{7,4},{8,11},{9,10},{10,... | collective-permute-start | bytes 829448 | tf_op jit(solution)/shard_map/ppermute | solution.py:43
  25.9 2.5 %shard_map.263 = bf16[96,1536]{1,0:T(8,128)(2,1)} custom-call(s32[2]{0:T(128)S(1)} %pad_add_fusion.place, bf16[768,768]{1,0:T(8,128)(2,1)} %con_ref.1, bf16[192,3072]{1,0:T(8,128)(2,1)} %exp_ref.1), custom_call_target="tpu_custom_call" | custom-call | tf_op jit(solution)/shard_map/pallas_call | solution.py:306
  28.4 11.8 %collective-permute-done.1.refs_2_ = bf16[240,576]{1,0:T(8,128)(2,1)S(1)} collective-permute-done((bf16[240,576]{1,0:T(8,128)(2,1)S(1)}, bf16[240,576]{1,0:T(8,128)(2,1)S(1)}, u32[]{:S(2)}, u32[]{:S(2)}) %collective-permute-start.1) | collective-permute-done | bytes 276512 | tf_op jit(solution)/shard_map/ppermute | solution.py:43
  45.8 8.4 %shard_map.266 = (bf16[128,192]{1,0:T(8,128)(2,1)S(1)}, bf16[128,192]{1,0:T(8,128)(2,1)S(1)}, bf16[128,192]{1,0:T(8,128)(2,1)S(1)}, bf16[128,192]{1,0:T(8,128)(2...) custom-call(s32[2]{0:T(128)S(1)} %pad_add_fusion.place, ...), custom_call_target="tpu_custom_call" | custom-call | flops 1 | bytes 1 | tf_op jit(solution)/shard_map/pallas_call | solution.py:594
  60.0 2.4 %collective-permute-done.16 = bf16[128,192]{1,0:T(8,128)(2,1)S(1)} collective-permute-done((bf16[128,192]{1,0:T(8,128)(2,1)S(1)}, bf16[128,192]{1,0:T(8,128)(2,1)S(1)}, u32[]{:S(2)}, u32[]{:S(2)}) %collective-permute-start.16) | collective-permute-done | bytes 49184 | tf_op jit(solution)/shard_map/ppermute | solution.py:43
  64.4 2.5 %collective-permute-start.19 = (bf16[128,768]{1,0:T(8,128)(2,1)S(1)}, bf16[128,768]{1,0:T(8,128)(2,1)S(1)}, u32[]{:S(2)}, u32[]{:S(2)}) collective-permute-start(bf16[128,768]{1,0:T(8,128)(2,1)S(1)} %add_convert_fusion.2.refs_0_), channel_id=1, source_target_pairs={{0,24},{8,16},{16,8},{24,0},{1,25},{9,17},{17,9},{25,1},{2,26},{10... | collective-permute-start | bytes 589832 | tf_op jit(solution)/shard_map/ppermute | solution.py:43
  66.9 4.3 %collective-permute-done.17.refs_1_ = bf16[128,768]{1,0:T(8,128)(2,1)S(1)} collective-permute-done((bf16[128,768]{1,0:T(8,128)(2,1)S(1)}, bf16[128,768]{1,0:T(8,128)(2,1)S(1)}, u32[]{:S(2)}, u32[]{:S(2)}) %collective-permute-start.17) | collective-permute-done | bytes 196640 | tf_op jit(solution)/shard_map/ppermute | solution.py:43
  71.3 2.5 %collective-permute-done.18.refs_2_ = bf16[128,768]{1,0:T(8,128)(2,1)S(1)} collective-permute-done((bf16[128,768]{1,0:T(8,128)(2,1)S(1)}, bf16[128,768]{1,0:T(8,128)(2,1)S(1)}, u32[]{:S(2)}, u32[]{:S(2)}) %collective-permute-start.18) | collective-permute-done | bytes 196640 | tf_op jit(solution)/shard_map/ppermute | solution.py:43
  73.7 1.9 %all-gather.2.cloned.1.call-done.refs_8_.refs_9_ = bf16[768,1536]{1,0:T(8,128)(2,1)} async-done(((bf16[96,1536]{1,0:T(8,128)(2,1)}), bf16[768,1536]{1,0:T(8,128)(2,1)}) %all-gather.2.cloned.1.call-update) | async-done | bytes 2359312 | tf_op jit(solution)/shard_map/all_gather | solution.py:836
  75.6 7.5 %shard_map.267 = (bf16[512,768]{1,0:T(8,128)(2,1)S(1)}, bf16[512,768]{1,0:T(8,128)(2,1)S(1)}, bf16[128,768]{1,0:T(8,128)(2,1)S(1)}, bf16[128,768]{1,0:T(8,128)(2...) custom-call(bf16[128,768]{1,0:T(8,128)(2,1)} %copy-done.18, ...), custom_call_target="tpu_custom_call" | custom-call | flops 1 | bytes 1 | tf_op jit(solution)/shard_map/pallas_call | solution.py:459
  86.6 4.7 %shard_map.268 = bf16[768,1536]{1,0:T(8,128)(2,1)} custom-call(bf16[128,768]{1,0:T(8,128)(2,1)} %copy-done.18, bf16[128,768]{1,0:T(8,128)(2,1)} %copy-done.20, bf16[128,768]{1,0:T(8,128)(2,1)} %copy-done.21, bf16[128,768]{1,0:T(8,128)(2,1)} %copy-done.22, bf16[2,128,768]{2,1,0:T(8,128)(2,1)} %copy-done, bf16[2,128,768]{2,1,0:T(8,128)(2,1)} %copy-done.1, ...), custom_call_target="tpu_custom_call" | custom-call | flops 8000000000 | bytes 1 | tf_op jit(solution)/shard_map/pallas_call | solution.py:510
  91.3 4.2 %collective-permute-done.21 = bf16[128,768]{1,0:T(8,128)(2,1)S(1)} collective-permute-done((bf16[128,768]{1,0:T(8,128)(2,1)S(1)}, bf16[128,768]{1,0:T(8,128)(2,1)S(1)}, u32[]{:S(2)}, u32[]{:S(2)}) %collective-permute-start.21) | collective-permute-done | bytes 196640 | tf_op jit(solution)/shard_map/ppermute | solution.py:43
  110.7 6.6 %shard_map.269 = (bf16[512,128]{1,0:T(8,128)(2,1)S(1)}, bf16[2,512,256]{2,1,0:T(8,128)(2,1)S(1)}) custom-call(s32[2]{0:T(128)S(1)} %pad_add_fusion.place, bf16[128,192]{1,0:T(8,128)(2,1)S(1)} %get-tuple-element.176.refs_0_, bf16[128,192]{1,0:T(8,128)(2,1)S(1)} %collective-permute-done.23.refs_1_, bf16[128,192]{1,0:T(8,128)(2,1)S(1)} %collective-permute-done.24.refs_2_, ...), custom_call_target="tpu_custom_call" | custom-call | flops 8000000000 | bytes 1 | tf_op jit(solution)/shard_map/pallas_call | solution.py:657
  120.2 3.7 %shard_map.270 = (bf16[512,64]{1,0:T(8,128)(2,1)S(1)}, bf16[2,512,128]{2,1,0:T(8,128)(2,1)S(1)}) custom-call(s32[2]{0:T(128)S(1)} %pad_add_fusion.place, bf16[128,192]{1,0:T(8,128)(2,1)S(1)} %get-tuple-element.176.refs_0_, bf16[128,192]{1,0:T(8,128)(2,1)S(1)} %collective-permute-done.23.refs_1_, bf16[128,192]{1,0:T(8,128)(2,1)S(1)} %collective-permute-done.24.refs_2_, ...), custom_call_target="tpu_custom_call" | custom-call | flops 8000000000 | bytes 1 | tf_op jit(solution)/shard_map/pallas_call | solution.py:657
  127.7 3.3 %shard_map.271 = (bf16[128,768]{1,0:T(8,128)(2,1)S(1)}, bf16[128,768]{1,0:T(8,128)(2,1)}, bf16[128,768]{1,0:T(8,128)(2,1)}, bf16[128,768]{1,0:T(8,128)(2,1)S(1)}...) custom-call(s32[1]{0:T(128)} %bitcast.1.place, bf16[512,128]{1,0:T(8,128)(2,1)S(1)} %get-tuple-element.169.refs_0_, ...), custom_call_target="tpu_custom_call" | custom-call | flops 1 | bytes 1 | tf_op jit(solution)/shard_map/pallas_call | solution.py:704
  140.4 2.3 %collective-permute-start.41 = (bf16[130,576]{1,0:T(8,128)(2,1)}, bf16[130,576]{1,0:T(8,128)(2,1)S(1)}, u32[]{:S(2)}, u32[]{:S(2)}) collective-permute-start(bf16[130,576]{1,0:T(8,128)(2,1)} %get-tuple-element.204), channel_id=1, source_target_pairs={{0,3},{1,2},{2,1},{3,0},{4,7},{5,6},{6,5},{7,4},{8,11},{9,10},{10,... | collective-permute-start | bytes 449288 | tf_op jit(solution)/shard_map/ppermute | solution.py:43
  145.5 2.3 %collective-permute-done.39 = bf16[130,576]{1,0:T(8,128)(2,1)S(1)} collective-permute-done((bf16[130,576]{1,0:T(8,128)(2,1)}, bf16[130,576]{1,0:T(8,128)(2,1)S(1)}, u32[]{:S(2)}, u32[]{:S(2)}) %collective-permute-start.39) | collective-permute-done | bytes 149792 | tf_op jit(solution)/shard_map/ppermute | solution.py:43
  148.9 6.4 %collective-permute-done.40 = bf16[130,576]{1,0:T(8,128)(2,1)S(1)} collective-permute-done((bf16[130,576]{1,0:T(8,128)(2,1)}, bf16[130,576]{1,0:T(8,128)(2,1)S(1)}, u32[]{:S(2)}, u32[]{:S(2)}) %collective-permute-start.40) | collective-permute-done | bytes 149792 | tf_op jit(solution)/shard_map/ppermute | solution.py:43
  161.8 3.1 %shard_map.273 = (f32[2,96,3072]{2,1,0:T(8,128)}, f32[4,2,96,768]{3,2,1,0:T(8,128)}) custom-call(s32[2]{0:T(128)S(1)} %pad_add_fusion.place, bf16[96,1536]{1,0:T(8,128)(2,1)S(1)} %copy-done.8, bf16[96,1536]{1,0:T(8,128)(2,1)S(1)} %collective-permute-done.45.refs_1_, bf16[96,1536]{1,0:T(8,128)(2,1)S(1)} %collective-permute-done.46.refs_2_, ...), custom_call_target="tpu_custom_call" | custom-call | flops 1 | bytes 1 | tf_op jit(solution)/shard_map/pallas_call | solution.py:379
  164.9 4.3 %collective-permute-done.43.refs_2_ = bf16[130,576]{1,0:T(8,128)(2,1)S(1)} collective-permute-done((bf16[130,576]{1,0:T(8,128)(2,1)S(1)}, bf16[130,576]{1,0:T(8,128)(2,1)S(1)}, u32[]{:S(2)}, u32[]{:S(2)}) %collective-permute-start.43) | collective-permute-done | bytes 149792 | tf_op jit(solution)/shard_map/ppermute | solution.py:43
  171.4 2.7 %shard_map.274 = (f32[2,96,2304]{2,1,0:T(8,128)}, f32[4,2,24,768]{3,2,1,0:T(8,128)}, f32[2,2,576]{2,1,0:T(2,128)S(1)}) custom-call(s32[2]{0:T(128)S(1)} %pad_add_fusion.place, bf16[130,576]{1,0:T(8,128)(2,1)S(1)} %add_convert_fusion.3.refs_0_, bf16[130,576]{1,0:T(8,128)(2,1)S(1)} %collective-permute-done.42.refs_1_, ...), custom_call_target="tpu_custom_call" | custom-call | flops 1 | bytes 1 | tf_op jit(solution)/shard_map/pallas_call | solution.py:756
  (239 shorter events, 66.9 us)
Async XLA Ops:
  7.2 68.4 %all-gather.2.cloned.1.call-start = ((), (), s32[]{:S(2)}) async-start(), calls=%async_computation.1 | async-start | bytes 2654208 | tf_op jit(solution)/shard_map/all_gather | solution.py:836
  9.2 14.1 %collective-permute-start = (bf16[240,576]{1,0:T(8,128)(2,1)S(1)}, bf16[240,576]{1,0:T(8,128)(2,1)S(1)}, u32[]{:S(2)}, u32[]{:S(2)}) collective-permute-start(bf16[240,576]{1,0:T(8,128)(2,1)S(1)} %shard_map.262.refs_0_), channel_id=1, source_target_pairs={{0,1},{1,0},{2,3},{3,2},{4,5},{5,4},{6,7},{7,6},{8,9},{9,8},{10,11... | collective-permute-start | bytes 829448 | tf_op jit(solution)/shard_map/ppermute | solution.py:43
  12.4 27.8 %collective-permute-start.3 = (bf16[2,128,768]{2,1,0:T(8,128)(2,1)S(1)}, bf16[2,128,768]{2,1,0:T(8,128)(2,1)S(1)}, u32[]{:S(2)}, u32[]{:S(2)}) collective-permute-start(bf16[2,128,768]{2,1,0:T(8,128)(2,1)S(1)} %constant_dynamic-update-slice_fusion.refs_0_.refs_4_), channel_id=1, source_target_pairs={{0,8},{8,0},{16,24},{24,16},{1,9},{9,1},{17,25},{25,17},{2,10},{10... | collective-permute-start | bytes 1179656 | tf_op jit(solution)/shard_map/ppermute | solution.py:43
  14.0 26.3 %collective-permute-start.4 = (bf16[2,128,768]{2,1,0:T(8,128)(2,1)S(1)}, bf16[2,128,768]{2,1,0:T(8,128)(2,1)S(1)}, u32[]{:S(2)}, u32[]{:S(2)}) collective-permute-start(bf16[2,128,768]{2,1,0:T(8,128)(2,1)S(1)} %constant_dynamic-update-slice_fusion.refs_0_.refs_4_), channel_id=1, source_target_pairs={{0,16},{8,24},{16,0},{24,8},{1,17},{9,25},{17,1},{25,9},{2,18},{10... | collective-permute-start | bytes 1179656 | tf_op jit(solution)/shard_map/ppermute | solution.py:43
  15.5 24.8 %collective-permute-start.5 = (bf16[2,128,768]{2,1,0:T(8,128)(2,1)S(1)}, bf16[2,128,768]{2,1,0:T(8,128)(2,1)S(1)}, u32[]{:S(2)}, u32[]{:S(2)}) collective-permute-start(bf16[2,128,768]{2,1,0:T(8,128)(2,1)S(1)} %constant_dynamic-update-slice_fusion.refs_0_.refs_4_), channel_id=1, source_target_pairs={{0,24},{8,16},{16,8},{24,0},{1,25},{9,17},{17,9},{25,1},{2,26},{10... | collective-permute-start | bytes 1179656 | tf_op jit(solution)/shard_map/ppermute | solution.py:43
  15.9 24.3 %collective-permute-start.1 = (bf16[240,576]{1,0:T(8,128)(2,1)S(1)}, bf16[240,576]{1,0:T(8,128)(2,1)S(1)}, u32[]{:S(2)}, u32[]{:S(2)}) collective-permute-start(bf16[240,576]{1,0:T(8,128)(2,1)S(1)} %shard_map.262.refs_0_), channel_id=1, source_target_pairs={{0,2},{1,3},{2,0},{3,1},{4,6},{5,7},{6,4},{7,5},{8,10},{9,11},{10,... | collective-permute-start | bytes 829448 | tf_op jit(solution)/shard_map/ppermute | solution.py:43
  23.3 16.9 %collective-permute-start.2 = (bf16[240,576]{1,0:T(8,128)(2,1)S(1)}, bf16[240,576]{1,0:T(8,128)(2,1)S(1)}, u32[]{:S(2)}, u32[]{:S(2)}) collective-permute-start(bf16[240,576]{1,0:T(8,128)(2,1)S(1)} %shard_map.262.refs_0_), channel_id=1, source_target_pairs={{0,3},{1,2},{2,1},{3,0},{4,7},{5,6},{6,5},{7,4},{8,11},{9,10},{10,... | collective-permute-start | bytes 829448 | tf_op jit(solution)/shard_map/ppermute | solution.py:43
  40.3 102.3 %reduce-scatter.2.cloned.1.call-start = ((), (), s32[]{:S(2)}) async-start(), calls=%async_computation.2 | async-start | bytes 2654208 | tf_op jit(solution)/shard_map/reduce_scatter | solution.py:855
  63.9 9.8 %collective-permute-start.18 = (bf16[128,768]{1,0:T(8,128)(2,1)S(1)}, bf16[128,768]{1,0:T(8,128)(2,1)S(1)}, u32[]{:S(2)}, u32[]{:S(2)}) collective-permute-start(bf16[128,768]{1,0:T(8,128)(2,1)S(1)} %add_convert_fusion.2.refs_0_), channel_id=1, source_target_pairs={{0,16},{8,24},{16,0},{24,8},{1,17},{9,25},{17,1},{25,9},{2,18},{10... | collective-permute-start | bytes 589832 | tf_op jit(solution)/shard_map/ppermute | solution.py:43
  84.6 11.0 %collective-permute-start.21 = (bf16[128,768]{1,0:T(8,128)(2,1)S(1)}, bf16[128,768]{1,0:T(8,128)(2,1)S(1)}, u32[]{:S(2)}, u32[]{:S(2)}) collective-permute-start(bf16[128,768]{1,0:T(8,128)(2,1)S(1)} %get-tuple-element.133), channel_id=1, source_target_pairs={{0,16},{8,24},{16,0},{24,8},{1,17},{9,25},{17,1},{25,9},{2,18},{10... | collective-permute-start | bytes 589832 | tf_op jit(solution)/shard_map/ppermute | solution.py:43
  86.0 9.6 %collective-permute-start.22 = (bf16[128,768]{1,0:T(8,128)(2,1)S(1)}, bf16[128,768]{1,0:T(8,128)(2,1)S(1)}, u32[]{:S(2)}, u32[]{:S(2)}) collective-permute-start(bf16[128,768]{1,0:T(8,128)(2,1)S(1)} %get-tuple-element.134), channel_id=1, source_target_pairs={{0,24},{8,16},{16,8},{24,0},{1,25},{9,17},{17,9},{25,1},{2,26},{10... | collective-permute-start | bytes 589832 | tf_op jit(solution)/shard_map/ppermute | solution.py:43
  106.4 12.7 %collective-permute-start.26 = (bf16[4,4,24,768]{3,2,1,0:T(8,128)(2,1)S(1)}, bf16[4,4,24,768]{3,2,1,0:T(8,128)(2,1)S(1)}, u32[]{:S(2)}, u32[]{:S(2)}) collective-permute-start(bf16[4,4,24,768]{3,2,1,0:T(8,128)(2,1)S(1)} %get-tuple-element.155), channel_id=1, source_target_pairs={{0,4},{4,0},{1,5},{5,1},{2,6},{6,2},{3,7},{7,3},{8,12},{12,8},{9,1... | collective-permute-start | bytes 1769480 | tf_op jit(solution)/shard_map/ppermute | solution.py:43
  107.2 10.2 %collective-permute-start.27 = (bf16[128,768]{1,0:T(8,128)(2,1)S(1)}, bf16[128,768]{1,0:T(8,128)(2,1)S(1)}, u32[]{:S(2)}, u32[]{:S(2)}) collective-permute-start(bf16[128,768]{1,0:T(8,128)(2,1)S(1)} %copy-done.36), channel_id=1, source_target_pairs={{0,8},{8,0},{16,24},{24,16},{1,9},{9,1},{17,25},{25,17},{2,10},{10... | collective-permute-start | bytes 589832 | tf_op jit(solution)/shard_map/ppermute | solution.py:43
  108.6 10.5 %collective-permute-start.28 = (bf16[128,768]{1,0:T(8,128)(2,1)S(1)}, bf16[128,768]{1,0:T(8,128)(2,1)S(1)}, u32[]{:S(2)}, u32[]{:S(2)}) collective-permute-start(bf16[128,768]{1,0:T(8,128)(2,1)S(1)} %copy-done.35), channel_id=1, source_target_pairs={{0,16},{8,24},{16,0},{24,8},{1,17},{9,25},{17,1},{25,9},{2,18},{10... | collective-permute-start | bytes 589832 | tf_op jit(solution)/shard_map/ppermute | solution.py:43
  109.2 9.9 %collective-permute-start.29 = (bf16[128,768]{1,0:T(8,128)(2,1)S(1)}, bf16[128,768]{1,0:T(8,128)(2,1)S(1)}, u32[]{:S(2)}, u32[]{:S(2)}) collective-permute-start(bf16[128,768]{1,0:T(8,128)(2,1)S(1)} %copy-done.34), channel_id=1, source_target_pairs={{0,24},{8,16},{16,8},{24,0},{1,25},{9,17},{17,9},{25,1},{2,26},{10... | collective-permute-start | bytes 589832 | tf_op jit(solution)/shard_map/ppermute | solution.py:43
  117.4 10.3 %collective-permute-start.30 = (bf16[512,256]{1,0:T(8,128)(2,1)S(1)}, bf16[512,256]{1,0:T(8,128)(2,1)S(1)}, u32[]{:S(2)}, u32[]{:S(2)}) collective-permute-start(bf16[512,256]{1,0:T(8,128)(2,1)S(1)} %get-tuple-element.251), channel_id=1, source_target_pairs={{0,4},{4,0},{1,5},{5,1},{2,6},{6,2},{3,7},{7,3},{8,12},{12,8},{9,1... | collective-permute-start | bytes 786440 | tf_op jit(solution)/shard_map/ppermute | solution.py:43
  124.7 10.5 %collective-permute-start.37 = (bf16[4,24,768]{2,1,0:T(8,128)(2,1)}, bf16[4,24,768]{2,1,0:T(8,128)(2,1)}, u32[]{:S(2)}, u32[]{:S(2)}) collective-permute-start(bf16[4,24,768]{2,1,0:T(8,128)(2,1)} %get-tuple-element.199), channel_id=1, source_target_pairs={{0,16},{8,24},{16,0},{24,8},{1,17},{9,25},{17,1},{25,9},{2,18},{10... | collective-permute-start | bytes 442376 | tf_op jit(solution)/shard_map/ppermute | solution.py:43
  131.6 11.0 %collective-permute-start.33 = (bf16[128,768]{1,0:T(8,128)(2,1)}, bf16[128,768]{1,0:T(8,128)(2,1)}, u32[]{:S(2)}, u32[]{:S(2)}) collective-permute-start(bf16[128,768]{1,0:T(8,128)(2,1)} %get-tuple-element.187), channel_id=1, source_target_pairs={{0,16},{8,24},{16,0},{24,8},{1,17},{9,25},{17,1},{25,9},{2,18},{10... | collective-permute-start | bytes 589832 | tf_op jit(solution)/shard_map/ppermute | solution.py:43
  139.4 15.9 %collective-permute-start.40 = (bf16[130,576]{1,0:T(8,128)(2,1)}, bf16[130,576]{1,0:T(8,128)(2,1)S(1)}, u32[]{:S(2)}, u32[]{:S(2)}) collective-permute-start(bf16[130,576]{1,0:T(8,128)(2,1)} %get-tuple-element.203), channel_id=1, source_target_pairs={{0,2},{1,3},{2,0},{3,1},{4,6},{5,7},{6,4},{7,5},{8,10},{9,11},{10,... | collective-permute-start | bytes 449288 | tf_op jit(solution)/shard_map/ppermute | solution.py:43
  140.4 14.9 %collective-permute-start.41 = (bf16[130,576]{1,0:T(8,128)(2,1)}, bf16[130,576]{1,0:T(8,128)(2,1)S(1)}, u32[]{:S(2)}, u32[]{:S(2)}) collective-permute-start(bf16[130,576]{1,0:T(8,128)(2,1)} %get-tuple-element.204), channel_id=1, source_target_pairs={{0,3},{1,2},{2,1},{3,0},{4,7},{5,6},{6,5},{7,4},{8,11},{9,10},{10,... | collective-permute-start | bytes 449288 | tf_op jit(solution)/shard_map/ppermute | solution.py:43
  142.6 13.5 %collective-permute-start.45 = (bf16[96,1536]{1,0:T(8,128)(2,1)}, bf16[96,1536]{1,0:T(8,128)(2,1)S(1)}, u32[]{:S(2)}, u32[]{:S(2)}) collective-permute-start(bf16[96,1536]{1,0:T(8,128)(2,1)} %reduce-scatter.2.cloned.1.call-done.refs_0_), channel_id=1, source_target_pairs={{0,8},{8,0},{16,24},{24,16},{1,9},{9,1},{17,25},{25,17},{2,10},{10... | collective-permute-start | bytes 884744 | tf_op jit(solution)/shard_map/ppermute | solution.py:43
  144.9 13.4 %collective-permute-start.46 = (bf16[96,1536]{1,0:T(8,128)(2,1)S(1)}, bf16[96,1536]{1,0:T(8,128)(2,1)S(1)}, u32[]{:S(2)}, u32[]{:S(2)}) collective-permute-start(bf16[96,1536]{1,0:T(8,128)(2,1)S(1)} %copy-done.8), channel_id=1, source_target_pairs={{0,16},{8,24},{16,0},{24,8},{1,17},{9,25},{17,1},{25,9},{2,18},{10... | collective-permute-start | bytes 884744 | tf_op jit(solution)/shard_map/ppermute | solution.py:43
  147.7 10.9 %collective-permute-start.47 = (bf16[96,1536]{1,0:T(8,128)(2,1)S(1)}, bf16[96,1536]{1,0:T(8,128)(2,1)S(1)}, u32[]{:S(2)}, u32[]{:S(2)}) collective-permute-start(bf16[96,1536]{1,0:T(8,128)(2,1)S(1)} %copy-done.8), channel_id=1, source_target_pairs={{0,24},{8,16},{16,8},{24,0},{1,25},{9,17},{17,9},{25,1},{2,26},{10... | collective-permute-start | bytes 884744 | tf_op jit(solution)/shard_map/ppermute | solution.py:43
  158.7 10.5 %collective-permute-start.43 = (bf16[130,576]{1,0:T(8,128)(2,1)S(1)}, bf16[130,576]{1,0:T(8,128)(2,1)S(1)}, u32[]{:S(2)}, u32[]{:S(2)}) collective-permute-start(bf16[130,576]{1,0:T(8,128)(2,1)S(1)} %add_convert_fusion.3.refs_0_), channel_id=1, source_target_pairs={{0,16},{8,24},{16,0},{24,8},{1,17},{9,25},{17,1},{25,9},{2,18},{10... | collective-permute-start | bytes 449288 | tf_op jit(solution)/shard_map/ppermute | solution.py:43
  (71 other events, 416.7 us)
Sparse Core Ops, SparseCore 0:
  40.4 35.1 all-gather.1
  101.9 35.1 reduce-scatter.1

commit v8 on v7

--- a/solution.py
+++ b/solution.py
@@ -44,7 +44,7 @@
 
 
 def gather_flips(value, axis):
-    return [value] + [send(value, axis, i) for i in range(1, lax.axis_size(axis))]
+    return swap_flips([value] * lax.axis_size(axis), axis)
 
 
 def swap_flips(pieces, axis):
@@ -355,12 +355,12 @@
 
 
 def unfold_kernel(parts, ks, place, *refs):
-    pieces, (exp_out, con_out, held) = refs[:-3], refs[-3:]
+    pieces, (exp_out, con_out, held) = refs[: GROUPS + ks - 1], refs[-3:]
     wide = con_out.shape[3]
     part_wide = wide // parts
     for j in range(ks):
         for i in range(GROUPS):
-            held[place[0] ^ i] = pieces[j * GROUPS + i][...]
+            held[place[0] ^ i] = pieces[GROUPS + j - 1][i] if j else pieces[i][...]
         spot = place[1] ^ j
         for i in range(GROUPS):
             con_out[i, spot] = held[i, :, wide:].astype(F32)
@@ -371,9 +371,9 @@
                 ].astype(F32)
 
 
-def unfold(pieces, parts, g, k):
-    ks = len(pieces)
-    rows, wide = pieces[0][0].shape[0], pieces[0][0].shape[1] // 2
+def unfold(pieces, more, parts, g, k):
+    ks = len(more) + 1
+    rows, wide = pieces[0].shape[0], pieces[0].shape[1] // 2
     step = rows // 2 if rows % 32 == 0 else rows
     shapes = [(ks, rows, GROUPS * wide), (GROUPS, ks, rows, wide)]
     exp, con = pl.pallas_call(
@@ -381,7 +381,8 @@
         grid_spec=pltpu.PrefetchScalarGridSpec(
             num_scalar_prefetch=1,
             grid=(rows // step,),
-            in_specs=[pl.BlockSpec((step, 2 * wide), lambda i, place: (i, 0))] * (ks * GROUPS),
+            in_specs=[pl.BlockSpec((step, 2 * wide), lambda i, place: (i, 0))] * GROUPS
+            + [pl.BlockSpec((GROUPS, step, 2 * wide), lambda i, place: (0, i, 0))] * (ks - 1),
             out_specs=[
                 pl.BlockSpec((ks, step, GROUPS * wide), lambda i, place: (0, i, 0)),
                 pl.BlockSpec((GROUPS, ks, step, wide), lambda i, place: (0, 0, i, 0)),
@@ -391,7 +392,7 @@
         out_shape=[jax.ShapeDtypeStruct(s, F32) for s in shapes],
         compiler_params=pltpu.CompilerParams(vmem_limit_bytes=20 * 2**20),
         cost_estimate=SHORT,
-    )(jnp.stack([g, k]).astype(jnp.int32), *[p for group in pieces for p in group])
+    )(jnp.stack([g, k]).astype(jnp.int32), *pieces, *more)
     return exp.reshape(ks * rows, -1), con.reshape(-1, wide)
 
 
@@ -812,7 +813,9 @@
     pieces = gather_flips(cut, "fsdp")
     rows_both = gather_flips(jnp.concatenate([inputs, cotangent]), "grp")
     rest = cut_rest(contract_weight, expand_weight, zs, g, k, ks)
+    pieces.append(pieces.pop(1))
     pieces, rows_both, rest = lax.optimization_barrier((pieces, rows_both, rest))
+    pieces.insert(1, pieces.pop())
     x_more = [send(b[0], "core", j) for j in range(1, ks) for b in rows_both]
     more = [[send(b, "core", j) for b in pieces] for j in range(1, ks)]
     if aligned:
@@ -920,12 +923,14 @@
     pieces = lax.optimization_barrier([pick(d_in, z ^ i) for i in range(zs)])
     d_in = swap_flips(pieces, "fsdp")
     d_hidden = gather_flips(d_hidden, "grp")
+    d_in.append(d_in.pop(1))
     d_in = gather_flips(total(d_in).astype(BF), "grp")
-    d_hidden = [d_hidden] + [[send(p, "core", j) for p in d_hidden] for j in range(1, ks)]
-    d_exp_w, d_con_w = unfold(d_hidden, zs, g, k)
-    d_in, d_exp_w, d_con_w = lax.optimization_barrier((d_in, d_exp_w, d_con_w))
+    more = jnp.stack(d_hidden)
+    more = [send(more, "core", j) for j in range(1, ks)]
+    d_exp_w, d_con_w = unfold(d_hidden, more, zs, g, k)
     outputs = (middle + total(out_sum) + c_bias).astype(BF)[None]
     d_in = [d_in] + [[send(p, "core", j) for p in d_in] for j in range(1, ks)]
+    d_in, d_exp_w, d_con_w = lax.optimization_barrier((d_in, d_exp_w, d_con_w))
     d_in_w, d_out_w, packed = finish(d_in, own, extra, width, g, k)
 
     def vec(i):

time: 183 us -> 187 us (1.022)
  waiting for transfers between devices: 54.8 us -> 63.2 us
  starting transfers between devices: 51.5 us -> 46.6 us
    ppermute x56 -> x53, waiting for transfers between devices: 52.8 us -> 62.5 us  [send(): return lax.ppermute(value, axis, [(s, s ^ flip) for s in range(count)])]
    ppermute x56 -> x53, starting transfers between devices: 51.4 us -> 46.5 us  [send(): return lax.ppermute(value, axis, [(s, s ^ flip) for s in range(count)])]
  transfers between devices with their start and end apart: 58 -> 55, of which waited for: 23 -> 22; matrix products, arithmetic and copies ran while one was open for 5% -> 5% of each run, Pallas kernels for 19% -> 18%
where the time goes in v8:
time: 187 us; the launch traced here: 186 us
  waiting for transfers between devices  63.2 us (34%)
  starting transfers between devices  46.6 us (25%)
  Pallas kernels  46.2 us (25%)
  between operations  14.9 us (8%)
  other arithmetic  8.37 us (4%)
  local copies, waits for them, and re-layouts  5.58 us (3%)
    ppermute x53, waiting for transfers between devices, send(): return lax.ppermute(value, axis, [(s, s ^ flip) for s in range(count)])  62.5 us
    ppermute x53, starting transfers between devices, send(): return lax.ppermute(value, axis, [(s, s ^ flip) for s in range(count)])  46.5 us
    pallas_call x2, Pallas kernels, attend_back(): pl.pallas_call(functools.partial(attend_back_kernel, ks, head, first), gr...  10.3 us
    pallas_call x1, Pallas kernels, attend(): pl.pallas_call(functools.partial(attend_kernel, ks, head), grid_spec=pltp...  8.42 us
    pallas_call x1, Pallas kernels, hidden_part(): pl.pallas_call(hidden_kernel, grid=(hidden // step,), in_specs=[pl.BlockS...  7.48 us
    pallas_call x1, Pallas kernels, hidden_grads(): pl.pallas_call(hidden_grad_kernel, grid=(width // step,), in_specs=[pl.Bl...  4.7 us
  transfers between devices with their start and end apart: 55, of which 22 were waited for; matrix products, arithmetic and copies ran while one was open for 5% of the time, Pallas kernels for 18%

profile of v8, /device:TPU:0, one launch (start us, length us, event | category | flops | bytes accessed | tf_op | source)
XLA Modules:
  0.0 186.4 jit_solution(12124405799476312372)
XLA Ops:
  7.3 1.9 %shard_map.262.refs_0_ = bf16[240,576]{1,0:T(8,128)(2,1)S(1)} custom-call(s32[2]{0:T(128)S(1)} %pad_add_fusion.place, bf16[192,2304]{1,0:T(8,128)(2,1)} %refs_0_.1, bf16[192,768]{1,0:T(8,128)(2,1)} %refs_1_.1, bf16[192]{0:T(256)(128)(2,1)} %refs_2_.1, bf16[192]{0:T(256)(128)(2,1)} %refs_3_.1, bf16[192]{0:T(256)(128)(2,1)} %refs_4_.1, bf16[192]{0:T(256)(128)(2,1)} %refs_5_.1, ...), custom_call_target="tpu_custom_call" | custom-call | flops 1 | bytes 1 | tf_op jit(solution)/shard_map/pallas_call | solution.py:156
  9.2 4.1 %collective-permute-start = (bf16[240,576]{1,0:T(8,128)(2,1)S(1)}, bf16[240,576]{1,0:T(8,128)(2,1)S(1)}, u32[]{:S(2)}, u32[]{:S(2)}) collective-permute-start(bf16[240,576]{1,0:T(8,128)(2,1)S(1)} %shard_map.262.refs_0_), channel_id=1, source_target_pairs={{0,2},{1,3},{2,0},{3,1},{4,6},{5,7},{6,4},{7,5},{8,10},{9,11},{10,... | collective-permute-start | bytes 829448 | tf_op jit(solution)/shard_map/ppermute | solution.py:43
  18.3 16.3 %collective-permute-done.refs_2_ = bf16[240,576]{1,0:T(8,128)(2,1)S(1)} collective-permute-done((bf16[240,576]{1,0:T(8,128)(2,1)S(1)}, bf16[240,576]{1,0:T(8,128)(2,1)S(1)}, u32[]{:S(2)}, u32[]{:S(2)}) %collective-permute-start) | collective-permute-done | bytes 276512 | tf_op jit(solution)/shard_map/ppermute | solution.py:43
  34.6 2.5 %shard_map.263 = bf16[96,1536]{1,0:T(8,128)(2,1)} custom-call(s32[2]{0:T(128)S(1)} %pad_add_fusion.place, bf16[768,768]{1,0:T(8,128)(2,1)} %con_ref.1, bf16[192,3072]{1,0:T(8,128)(2,1)} %exp_ref.1), custom_call_target="tpu_custom_call" | custom-call | tf_op jit(solution)/shard_map/pallas_call | solution.py:306
  37.1 5.2 %collective-permute-done.2.refs_1_ = bf16[240,576]{1,0:T(8,128)(2,1)S(1)} collective-permute-done((bf16[240,576]{1,0:T(8,128)(2,1)S(1)}, bf16[240,576]{1,0:T(8,128)(2,1)S(1)}, u32[]{:S(2)}, u32[]{:S(2)}) %collective-permute-start.2) | collective-permute-done | bytes 276512 | tf_op jit(solution)/shard_map/ppermute | solution.py:43
  47.7 8.4 %shard_map.266 = (bf16[128,192]{1,0:T(8,128)(2,1)S(1)}, bf16[128,192]{1,0:T(8,128)(2,1)S(1)}, bf16[128,192]{1,0:T(8,128)(2,1)S(1)}, bf16[128,192]{1,0:T(8,128)(2...) custom-call(s32[2]{0:T(128)S(1)} %pad_add_fusion.place, ...), custom_call_target="tpu_custom_call" | custom-call | flops 1 | bytes 1 | tf_op jit(solution)/shard_map/pallas_call | solution.py:595
  61.7 2.4 %collective-permute-done.16 = bf16[128,192]{1,0:T(8,128)(2,1)S(1)} collective-permute-done((bf16[128,192]{1,0:T(8,128)(2,1)S(1)}, bf16[128,192]{1,0:T(8,128)(2,1)S(1)}, u32[]{:S(2)}, u32[]{:S(2)}) %collective-permute-start.16) | collective-permute-done | bytes 49184 | tf_op jit(solution)/shard_map/ppermute | solution.py:43
  66.3 2.3 %collective-permute-start.19 = (bf16[128,768]{1,0:T(8,128)(2,1)S(1)}, bf16[128,768]{1,0:T(8,128)(2,1)S(1)}, u32[]{:S(2)}, u32[]{:S(2)}) collective-permute-start(bf16[128,768]{1,0:T(8,128)(2,1)S(1)} %add_convert_fusion.2.refs_0_), channel_id=1, source_target_pairs={{0,24},{8,16},{16,8},{24,0},{1,25},{9,17},{17,9},{25,1},{2,26},{10... | collective-permute-start | bytes 589832 | tf_op jit(solution)/shard_map/ppermute | solution.py:43
  68.6 4.4 %collective-permute-done.17.refs_1_ = bf16[128,768]{1,0:T(8,128)(2,1)S(1)} collective-permute-done((bf16[128,768]{1,0:T(8,128)(2,1)S(1)}, bf16[128,768]{1,0:T(8,128)(2,1)S(1)}, u32[]{:S(2)}, u32[]{:S(2)}) %collective-permute-start.17) | collective-permute-done | bytes 196640 | tf_op jit(solution)/shard_map/ppermute | solution.py:43
  72.9 2.5 %collective-permute-done.18.refs_2_ = bf16[128,768]{1,0:T(8,128)(2,1)S(1)} collective-permute-done((bf16[128,768]{1,0:T(8,128)(2,1)S(1)}, bf16[128,768]{1,0:T(8,128)(2,1)S(1)}, u32[]{:S(2)}, u32[]{:S(2)}) %collective-permute-start.18) | collective-permute-done | bytes 196640 | tf_op jit(solution)/shard_map/ppermute | solution.py:43
  76.2 7.5 %shard_map.267 = (bf16[512,768]{1,0:T(8,128)(2,1)S(1)}, bf16[512,768]{1,0:T(8,128)(2,1)S(1)}, bf16[128,768]{1,0:T(8,128)(2,1)S(1)}, bf16[128,768]{1,0:T(8,128)(2...) custom-call(bf16[128,768]{1,0:T(8,128)(2,1)} %copy-done.18, ...), custom_call_target="tpu_custom_call" | custom-call | flops 1 | bytes 1 | tf_op jit(solution)/shard_map/pallas_call | solution.py:460
  87.1 4.7 %shard_map.268 = bf16[768,1536]{1,0:T(8,128)(2,1)} custom-call(bf16[128,768]{1,0:T(8,128)(2,1)} %copy-done.18, bf16[128,768]{1,0:T(8,128)(2,1)} %copy-done.20, bf16[128,768]{1,0:T(8,128)(2,1)} %copy-done.21, bf16[128,768]{1,0:T(8,128)(2,1)} %copy-done.22, bf16[2,128,768]{2,1,0:T(8,128)(2,1)} %copy-done, bf16[2,128,768]{2,1,0:T(8,128)(2,1)} %copy-done.1, ...), custom_call_target="tpu_custom_call" | custom-call | flops 8000000000 | bytes 1 | tf_op jit(solution)/shard_map/pallas_call | solution.py:511
  91.9 4.1 %collective-permute-done.21 = bf16[128,768]{1,0:T(8,128)(2,1)S(1)} collective-permute-done((bf16[128,768]{1,0:T(8,128)(2,1)S(1)}, bf16[128,768]{1,0:T(8,128)(2,1)S(1)}, u32[]{:S(2)}, u32[]{:S(2)}) %collective-permute-start.21) | collective-permute-done | bytes 196640 | tf_op jit(solution)/shard_map/ppermute | solution.py:43
  111.2 6.6 %shard_map.269 = (bf16[512,128]{1,0:T(8,128)(2,1)S(1)}, bf16[2,512,256]{2,1,0:T(8,128)(2,1)S(1)}) custom-call(s32[2]{0:T(128)S(1)} %pad_add_fusion.place, bf16[128,192]{1,0:T(8,128)(2,1)S(1)} %get-tuple-element.180.refs_0_, bf16[128,192]{1,0:T(8,128)(2,1)S(1)} %collective-permute-done.23.refs_1_, bf16[128,192]{1,0:T(8,128)(2,1)S(1)} %collective-permute-done.24.refs_2_, ...), custom_call_target="tpu_custom_call" | custom-call | flops 8000000000 | bytes 1 | tf_op jit(solution)/shard_map/pallas_call | solution.py:658
  120.7 3.7 %shard_map.270 = (bf16[512,64]{1,0:T(8,128)(2,1)S(1)}, bf16[2,512,128]{2,1,0:T(8,128)(2,1)S(1)}) custom-call(s32[2]{0:T(128)S(1)} %pad_add_fusion.place, bf16[128,192]{1,0:T(8,128)(2,1)S(1)} %get-tuple-element.180.refs_0_, bf16[128,192]{1,0:T(8,128)(2,1)S(1)} %collective-permute-done.23.refs_1_, bf16[128,192]{1,0:T(8,128)(2,1)S(1)} %collective-permute-done.24.refs_2_, ...), custom_call_target="tpu_custom_call" | custom-call | flops 8000000000 | bytes 1 | tf_op jit(solution)/shard_map/pallas_call | solution.py:658
  126.4 1.7 collective-permute-start.38
  128.3 3.3 %shard_map.271 = (bf16[128,768]{1,0:T(8,128)(2,1)S(1)}, bf16[128,768]{1,0:T(8,128)(2,1)}, bf16[128,768]{1,0:T(8,128)(2,1)}, bf16[128,768]{1,0:T(8,128)(2,1)S(1)}...) custom-call(s32[1]{0:T(128)} %bitcast.1.place, bf16[512,128]{1,0:T(8,128)(2,1)S(1)} %get-tuple-element.173.refs_0_, ...), custom_call_target="tpu_custom_call" | custom-call | flops 1 | bytes 1 | tf_op jit(solution)/shard_map/pallas_call | solution.py:705
  134.0 1.8 collective-permute-start.34
  139.8 2.0 %collective-permute-start.40 = (bf16[130,576]{1,0:T(8,128)(2,1)S(1)}, bf16[130,576]{1,0:T(8,128)(2,1)S(1)}, u32[]{:S(2)}, u32[]{:S(2)}) collective-permute-start(bf16[130,576]{1,0:T(8,128)(2,1)S(1)} %get-tuple-element.207), channel_id=1, source_target_pairs={{0,3},{1,2},{2,1},{3,0},{4,7},{5,6},{6,5},{7,4},{8,11},{9,10},{10,... | collective-permute-start | bytes 449288 | tf_op jit(solution)/shard_map/ppermute | solution.py:43
  145.1 8.5 %collective-permute-done.39 = bf16[130,576]{1,0:T(8,128)(2,1)S(1)} collective-permute-done((bf16[130,576]{1,0:T(8,128)(2,1)S(1)}, bf16[130,576]{1,0:T(8,128)(2,1)S(1)}, u32[]{:S(2)}, u32[]{:S(2)}) %collective-permute-start.39) | collective-permute-done | bytes 149792 | tf_op jit(solution)/shard_map/ppermute | solution.py:43
  158.4 6.3 %collective-permute-done.51.refs_3_ = bf16[96,1536]{1,0:T(8,128)(2,1)S(1)} collective-permute-done((bf16[96,1536]{1,0:T(8,128)(2,1)}, bf16[96,1536]{1,0:T(8,128)(2,1)S(1)}, u32[]{:S(2)}, u32[]{:S(2)}) %collective-permute-start.51) | collective-permute-done | bytes 294944 | tf_op jit(solution)/shard_map/ppermute | solution.py:43
  168.2 1.9 %collective-permute-done.44.refs_3_ = bf16[130,576]{1,0:T(8,128)(2,1)S(1)} collective-permute-done((bf16[130,576]{1,0:T(8,128)(2,1)S(1)}, bf16[130,576]{1,0:T(8,128)(2,1)S(1)}, u32[]{:S(2)}, u32[]{:S(2)}) %collective-permute-start.44) | collective-permute-done | bytes 149792 | tf_op jit(solution)/shard_map/ppermute | solution.py:43
  172.3 3.2 %shard_map.273 = (f32[2,96,3072]{2,1,0:T(8,128)}, f32[4,2,96,768]{3,2,1,0:T(8,128)}) custom-call(s32[2]{0:T(128)S(1)} %pad_add_fusion.place, bf16[96,1536]{1,0:T(8,128)(2,1)S(1)} %copy-done.6, bf16[96,1536]{1,0:T(8,128)(2,1)S(1)} %collective-permute-done.49.refs_1_, bf16[96,1536]{1,0:T(8,128)(2,1)S(1)} %collective-permute-done.50.refs_2_, ...), custom_call_target="tpu_custom_call" | custom-call | flops 1 | bytes 1 | tf_op jit(solution)/shard_map/pallas_call | solution.py:379
  175.5 2.7 %shard_map.274 = (f32[2,96,2304]{2,1,0:T(8,128)}, f32[4,2,24,768]{3,2,1,0:T(8,128)}, f32[2,2,576]{2,1,0:T(2,128)S(1)}) custom-call(s32[2]{0:T(128)S(1)} %pad_add_fusion.place, bf16[130,576]{1,0:T(8,128)(2,1)S(1)} %add_convert_fusion.3.refs_0_, bf16[130,576]{1,0:T(8,128)(2,1)S(1)} %collective-permute-done.42.refs_1_, ...), custom_call_target="tpu_custom_call" | custom-call | flops 1 | bytes 1 | tf_op jit(solution)/shard_map/pallas_call | solution.py:757
  (234 shorter events, 63.8 us)
Async XLA Ops:
  7.2 68.8 %all-gather.2.cloned.1.call-start = ((), (), s32[]{:S(2)}) async-start(), calls=%async_computation.1 | async-start | bytes 2654208 | tf_op jit(solution)/shard_map/all_gather | solution.py:839
  9.2 25.4 %collective-permute-start = (bf16[240,576]{1,0:T(8,128)(2,1)S(1)}, bf16[240,576]{1,0:T(8,128)(2,1)S(1)}, u32[]{:S(2)}, u32[]{:S(2)}) collective-permute-start(bf16[240,576]{1,0:T(8,128)(2,1)S(1)} %shard_map.262.refs_0_), channel_id=1, source_target_pairs={{0,2},{1,3},{2,0},{3,1},{4,6},{5,7},{6,4},{7,5},{8,10},{9,11},{10,... | collective-permute-start | bytes 829448 | tf_op jit(solution)/shard_map/ppermute | solution.py:43
  13.4 28.8 %collective-permute-start.3 = (bf16[2,128,768]{2,1,0:T(8,128)(2,1)S(1)}, bf16[2,128,768]{2,1,0:T(8,128)(2,1)S(1)}, u32[]{:S(2)}, u32[]{:S(2)}) collective-permute-start(bf16[2,128,768]{2,1,0:T(8,128)(2,1)S(1)} %constant_dynamic-update-slice_fusion.refs_0_.refs_4_), channel_id=1, source_target_pairs={{0,8},{8,0},{16,24},{24,16},{1,9},{9,1},{17,25},{25,17},{2,10},{10... | collective-permute-start | bytes 1179656 | tf_op jit(solution)/shard_map/ppermute | solution.py:43
  15.0 27.3 %collective-permute-start.4 = (bf16[2,128,768]{2,1,0:T(8,128)(2,1)S(1)}, bf16[2,128,768]{2,1,0:T(8,128)(2,1)S(1)}, u32[]{:S(2)}, u32[]{:S(2)}) collective-permute-start(bf16[2,128,768]{2,1,0:T(8,128)(2,1)S(1)} %constant_dynamic-update-slice_fusion.refs_0_.refs_4_), channel_id=1, source_target_pairs={{0,16},{8,24},{16,0},{24,8},{1,17},{9,25},{17,1},{25,9},{2,18},{10... | collective-permute-start | bytes 1179656 | tf_op jit(solution)/shard_map/ppermute | solution.py:43
  16.5 25.8 %collective-permute-start.5 = (bf16[2,128,768]{2,1,0:T(8,128)(2,1)S(1)}, bf16[2,128,768]{2,1,0:T(8,128)(2,1)S(1)}, u32[]{:S(2)}, u32[]{:S(2)}) collective-permute-start(bf16[2,128,768]{2,1,0:T(8,128)(2,1)S(1)} %constant_dynamic-update-slice_fusion.refs_0_.refs_4_), channel_id=1, source_target_pairs={{0,24},{8,16},{16,8},{24,0},{1,25},{9,17},{17,9},{25,1},{2,26},{10... | collective-permute-start | bytes 1179656 | tf_op jit(solution)/shard_map/ppermute | solution.py:43
  16.9 20.1 %collective-permute-start.1 = (bf16[240,576]{1,0:T(8,128)(2,1)S(1)}, bf16[240,576]{1,0:T(8,128)(2,1)S(1)}, u32[]{:S(2)}, u32[]{:S(2)}) collective-permute-start(bf16[240,576]{1,0:T(8,128)(2,1)S(1)} %shard_map.262.refs_0_), channel_id=1, source_target_pairs={{0,3},{1,2},{2,1},{3,0},{4,7},{5,6},{6,5},{7,4},{8,11},{9,10},{10,... | collective-permute-start | bytes 829448 | tf_op jit(solution)/shard_map/ppermute | solution.py:43
  42.3 100.8 %reduce-scatter.2.cloned.1.call-start = ((), (), s32[]{:S(2)}) async-start(), calls=%async_computation.2 | async-start | bytes 2654208 | tf_op jit(solution)/shard_map/reduce_scatter | solution.py:858
  85.2 10.8 %collective-permute-start.21 = (bf16[128,768]{1,0:T(8,128)(2,1)S(1)}, bf16[128,768]{1,0:T(8,128)(2,1)S(1)}, u32[]{:S(2)}, u32[]{:S(2)}) collective-permute-start(bf16[128,768]{1,0:T(8,128)(2,1)S(1)} %get-tuple-element.137), channel_id=1, source_target_pairs={{0,16},{8,24},{16,0},{24,8},{1,17},{9,25},{17,1},{25,9},{2,18},{10... | collective-permute-start | bytes 589832 | tf_op jit(solution)/shard_map/ppermute | solution.py:43
  106.9 12.8 %collective-permute-start.26 = (bf16[4,4,24,768]{3,2,1,0:T(8,128)(2,1)S(1)}, bf16[4,4,24,768]{3,2,1,0:T(8,128)(2,1)S(1)}, u32[]{:S(2)}, u32[]{:S(2)}) collective-permute-start(bf16[4,4,24,768]{3,2,1,0:T(8,128)(2,1)S(1)} %get-tuple-element.159), channel_id=1, source_target_pairs={{0,4},{4,0},{1,5},{5,1},{2,6},{6,2},{3,7},{7,3},{8,12},{12,8},{9,1... | collective-permute-start | bytes 1769480 | tf_op jit(solution)/shard_map/ppermute | solution.py:43
  107.7 10.2 %collective-permute-start.27 = (bf16[128,768]{1,0:T(8,128)(2,1)S(1)}, bf16[128,768]{1,0:T(8,128)(2,1)S(1)}, u32[]{:S(2)}, u32[]{:S(2)}) collective-permute-start(bf16[128,768]{1,0:T(8,128)(2,1)S(1)} %copy-done.36), channel_id=1, source_target_pairs={{0,8},{8,0},{16,24},{24,16},{1,9},{9,1},{17,25},{25,17},{2,10},{10... | collective-permute-start | bytes 589832 | tf_op jit(solution)/shard_map/ppermute | solution.py:43
  109.1 10.5 %collective-permute-start.28 = (bf16[128,768]{1,0:T(8,128)(2,1)S(1)}, bf16[128,768]{1,0:T(8,128)(2,1)S(1)}, u32[]{:S(2)}, u32[]{:S(2)}) collective-permute-start(bf16[128,768]{1,0:T(8,128)(2,1)S(1)} %copy-done.35), channel_id=1, source_target_pairs={{0,16},{8,24},{16,0},{24,8},{1,17},{9,25},{17,1},{25,9},{2,18},{10... | collective-permute-start | bytes 589832 | tf_op jit(solution)/shard_map/ppermute | solution.py:43
  117.8 10.5 %collective-permute-start.30 = (bf16[512,256]{1,0:T(8,128)(2,1)S(1)}, bf16[512,256]{1,0:T(8,128)(2,1)S(1)}, u32[]{:S(2)}, u32[]{:S(2)}) collective-permute-start(bf16[512,256]{1,0:T(8,128)(2,1)S(1)} %get-tuple-element.259), channel_id=1, source_target_pairs={{0,4},{4,0},{1,5},{5,1},{2,6},{6,2},{3,7},{7,3},{8,12},{12,8},{9,1... | collective-permute-start | bytes 786440 | tf_op jit(solution)/shard_map/ppermute | solution.py:43
  125.2 10.6 %collective-permute-start.37 = (bf16[4,24,768]{2,1,0:T(8,128)(2,1)}, bf16[4,24,768]{2,1,0:T(8,128)(2,1)}, u32[]{:S(2)}, u32[]{:S(2)}) collective-permute-start(bf16[4,24,768]{2,1,0:T(8,128)(2,1)} %get-tuple-element.203), channel_id=1, source_target_pairs={{0,16},{8,24},{16,0},{24,8},{1,17},{9,25},{17,1},{25,9},{2,18},{10... | collective-permute-start | bytes 442376 | tf_op jit(solution)/shard_map/ppermute | solution.py:43
  131.6 10.2 %collective-permute-start.32 = (bf16[128,768]{1,0:T(8,128)(2,1)}, bf16[128,768]{1,0:T(8,128)(2,1)S(1)}, u32[]{:S(2)}, u32[]{:S(2)}) collective-permute-start(bf16[128,768]{1,0:T(8,128)(2,1)} %get-tuple-element.190), channel_id=1, source_target_pairs={{0,8},{8,0},{16,24},{24,16},{1,9},{9,1},{17,25},{25,17},{2,10},{10... | collective-permute-start | bytes 589832 | tf_op jit(solution)/shard_map/ppermute | solution.py:43
  132.2 10.9 %collective-permute-start.33 = (bf16[128,768]{1,0:T(8,128)(2,1)}, bf16[128,768]{1,0:T(8,128)(2,1)}, u32[]{:S(2)}, u32[]{:S(2)}) collective-permute-start(bf16[128,768]{1,0:T(8,128)(2,1)} %get-tuple-element.191), channel_id=1, source_target_pairs={{0,16},{8,24},{16,0},{24,8},{1,17},{9,25},{17,1},{25,9},{2,18},{10... | collective-permute-start | bytes 589832 | tf_op jit(solution)/shard_map/ppermute | solution.py:43
  138.1 15.5 %collective-permute-start.39 = (bf16[130,576]{1,0:T(8,128)(2,1)S(1)}, bf16[130,576]{1,0:T(8,128)(2,1)S(1)}, u32[]{:S(2)}, u32[]{:S(2)}) collective-permute-start(bf16[130,576]{1,0:T(8,128)(2,1)S(1)} %get-tuple-element.206), channel_id=1, source_target_pairs={{0,2},{1,3},{2,0},{3,1},{4,6},{5,7},{6,4},{7,5},{8,10},{9,11},{10,... | collective-permute-start | bytes 449288 | tf_op jit(solution)/shard_map/ppermute | solution.py:43
  139.8 14.9 %collective-permute-start.40 = (bf16[130,576]{1,0:T(8,128)(2,1)S(1)}, bf16[130,576]{1,0:T(8,128)(2,1)S(1)}, u32[]{:S(2)}, u32[]{:S(2)}) collective-permute-start(bf16[130,576]{1,0:T(8,128)(2,1)S(1)} %get-tuple-element.207), channel_id=1, source_target_pairs={{0,3},{1,2},{2,1},{3,0},{4,7},{5,6},{6,5},{7,4},{8,11},{9,10},{10,... | collective-permute-start | bytes 449288 | tf_op jit(solution)/shard_map/ppermute | solution.py:43
  141.8 12.9 %collective-permute-start.41 = (bf16[130,576]{1,0:T(8,128)(2,1)S(1)}, bf16[130,576]{1,0:T(8,128)(2,1)S(1)}, u32[]{:S(2)}, u32[]{:S(2)}) collective-permute-start(bf16[130,576]{1,0:T(8,128)(2,1)S(1)} %get-tuple-element.208), channel_id=1, source_target_pairs={{0,1},{1,0},{2,3},{3,2},{4,5},{5,4},{6,7},{7,6},{8,9},{9,8},{10,11... | collective-permute-start | bytes 449288 | tf_op jit(solution)/shard_map/ppermute | solution.py:43
  143.1 14.1 %collective-permute-start.49 = (bf16[96,1536]{1,0:T(8,128)(2,1)}, bf16[96,1536]{1,0:T(8,128)(2,1)S(1)}, u32[]{:S(2)}, u32[]{:S(2)}) collective-permute-start(bf16[96,1536]{1,0:T(8,128)(2,1)} %reduce-scatter.2.cloned.1.call-done.refs_0_), channel_id=1, source_target_pairs={{0,8},{8,0},{16,24},{24,16},{1,9},{9,1},{17,25},{25,17},{2,10},{10... | collective-permute-start | bytes 884744 | tf_op jit(solution)/shard_map/ppermute | solution.py:43
  144.5 13.9 %collective-permute-start.50 = (bf16[96,1536]{1,0:T(8,128)(2,1)}, bf16[96,1536]{1,0:T(8,128)(2,1)S(1)}, u32[]{:S(2)}, u32[]{:S(2)}) collective-permute-start(bf16[96,1536]{1,0:T(8,128)(2,1)} %reduce-scatter.2.cloned.1.call-done.refs_0_), channel_id=1, source_target_pairs={{0,16},{8,24},{16,0},{24,8},{1,17},{9,25},{17,1},{25,9},{2,18},{10... | collective-permute-start | bytes 884744 | tf_op jit(solution)/shard_map/ppermute | solution.py:43
  153.5 11.1 %collective-permute-start.51 = (bf16[96,1536]{1,0:T(8,128)(2,1)}, bf16[96,1536]{1,0:T(8,128)(2,1)S(1)}, u32[]{:S(2)}, u32[]{:S(2)}) collective-permute-start(bf16[96,1536]{1,0:T(8,128)(2,1)} %reduce-scatter.2.cloned.1.call-done.refs_0_), channel_id=1, source_target_pairs={{0,24},{8,16},{16,8},{24,0},{1,25},{9,17},{17,9},{25,1},{2,26},{10... | collective-permute-start | bytes 884744 | tf_op jit(solution)/shard_map/ppermute | solution.py:43
  154.8 12.5 %collective-permute-start.42 = (bf16[130,576]{1,0:T(8,128)(2,1)S(1)}, bf16[130,576]{1,0:T(8,128)(2,1)S(1)}, u32[]{:S(2)}, u32[]{:S(2)}) collective-permute-start(bf16[130,576]{1,0:T(8,128)(2,1)S(1)} %add_convert_fusion.3.refs_0_), channel_id=1, source_target_pairs={{0,8},{8,0},{16,24},{24,16},{1,9},{9,1},{17,25},{25,17},{2,10},{10... | collective-permute-start | bytes 449288 | tf_op jit(solution)/shard_map/ppermute | solution.py:43
  155.7 12.4 %collective-permute-start.43 = (bf16[130,576]{1,0:T(8,128)(2,1)S(1)}, bf16[130,576]{1,0:T(8,128)(2,1)S(1)}, u32[]{:S(2)}, u32[]{:S(2)}) collective-permute-start(bf16[130,576]{1,0:T(8,128)(2,1)S(1)} %add_convert_fusion.3.refs_0_), channel_id=1, source_target_pairs={{0,16},{8,24},{16,0},{24,8},{1,17},{9,25},{17,1},{25,9},{2,18},{10... | collective-permute-start | bytes 449288 | tf_op jit(solution)/shard_map/ppermute | solution.py:43
  157.2 12.9 %collective-permute-start.44 = (bf16[130,576]{1,0:T(8,128)(2,1)S(1)}, bf16[130,576]{1,0:T(8,128)(2,1)S(1)}, u32[]{:S(2)}, u32[]{:S(2)}) collective-permute-start(bf16[130,576]{1,0:T(8,128)(2,1)S(1)} %add_convert_fusion.3.refs_0_), channel_id=1, source_target_pairs={{0,24},{8,16},{16,8},{24,0},{1,25},{9,17},{17,9},{25,1},{2,26},{10... | collective-permute-start | bytes 449288 | tf_op jit(solution)/shard_map/ppermute | solution.py:43
  (68 other events, 384.4 us)
Sparse Core Ops, SparseCore 0:
  42.4 33.5 all-gather.1
  102.1 35.1 reduce-scatter.1

commit v9 on v7

--- a/solution.py
+++ b/solution.py
@@ -727,7 +727,8 @@
 
 
 def finish_kernel(ks, extra, place, *refs):
-    pieces, (in_out, out_out, vec_out, held) = refs[:-4], refs[-4:]
+    pieces, (in_out, out_out) = refs[: ks * GROUPS], refs[ks * GROUPS : ks * GROUPS + 2]
+    vectors, (held, sums) = refs[ks * GROUPS + 2 : -2], refs[-2:]
     own, cols = in_out.shape[1], held.shape[2]
     part, low = cols // 3, own + extra
     share = own // GROUPS
@@ -745,27 +746,42 @@
                     i, low + share :, n * over : (n + 1) * over
                 ]
             out_out[i, spot, :, :cols] = held[i, low : low + share, :]
-        vec_out[spot] = total([held[i, own:low, :] for i in range(GROUPS)])
+        sums[spot] = total([held[i, own:low, :] for i in range(GROUPS)])
+    unit = vectors[0].shape[0]
+    per = cols // unit
+
+    def slot(n):
+        row, col = n // per, n % per * unit
+        return sums[row // extra, row % extra : row % extra + 1, col : col + unit]
+
+    for n in range(8):
+        vectors[n][...] = slot(n).reshape(unit)
+    last = jnp.concatenate([slot(8 + n) for n in range(GROUPS)], axis=1)
+    vectors[8][...] = last.reshape(GROUPS * unit)
 
 
 def finish(pieces, own, extra, width, g, k):
     ks = len(pieces)
     tall, cols = pieces[0][0].shape
     vmem = pl.BlockSpec(memory_space=pltpu.VMEM)
-    shapes = [(ks, own, GROUPS * cols), (GROUPS, ks, own // GROUPS, width), (ks, extra, cols)]
-    in_w, out_w, vectors = pl.pallas_call(
+    shapes = [(ks, own, GROUPS * cols), (GROUPS, ks, own // GROUPS, width)]
+    shapes += [(ks * own,)] * 8 + [(GROUPS * ks * own,)]
+    in_w, out_w, *vectors = pl.pallas_call(
         functools.partial(finish_kernel, ks, extra),
         grid_spec=pltpu.PrefetchScalarGridSpec(
             num_scalar_prefetch=1,
             in_specs=[vmem] * (ks * GROUPS),
-            out_specs=[vmem] * 3,
-            scratch_shapes=[pltpu.VMEM((GROUPS, tall, cols), F32)],
+            out_specs=[vmem] * len(shapes),
+            scratch_shapes=[
+                pltpu.VMEM((GROUPS, tall, cols), F32),
+                pltpu.VMEM((ks, extra, cols), F32),
+            ],
         ),
         out_shape=[jax.ShapeDtypeStruct(s, F32) for s in shapes],
         compiler_params=pltpu.CompilerParams(vmem_limit_bytes=16 * 2**20),
         cost_estimate=SHORT,
     )(jnp.stack([g, k]).astype(jnp.int32), *[p for group in pieces for p in group])
-    return in_w.reshape(ks * own, -1), out_w.reshape(ks * own, width), vectors.reshape(-1)
+    return in_w.reshape(ks * own, -1), out_w.reshape(ks * own, width), vectors
 
 
 def shards(
@@ -862,9 +878,9 @@
     slope_att = mm_rt(slope_branch, out_w).astype(BF)
     datt = swap_flips([slope_att[:, i * cols : (i + 1) * cols] for i in range(GROUPS)], "grp")
 
-    datt, slope_late, out_part = lax.optimization_barrier((datt, slope_branch, out_part))
+    datt, out_part = lax.optimization_barrier((datt, out_part))
     out_sum = swap_flips(out_part, "grp")
-    d_out = mm_lt(att, slope_late).astype(BF).reshape(GROUPS, cols, width)
+    d_out = mm_lt(att, slope_branch).astype(BF).reshape(GROUPS, cols, width)
     d_out = in_order([d_out[i] for i in range(GROUPS)], g)
     d_out = d_out.reshape(zs, GROUPS, ks, own // GROUPS, width)
     pieces = [lax.dynamic_index_in_dim(d_out, k ^ j, axis=2, keepdims=False) for j in range(ks)]
@@ -928,25 +944,22 @@
     d_in = [d_in] + [[send(p, "core", j) for p in d_in] for j in range(1, ks)]
     d_in_w, d_out_w, packed = finish(d_in, own, extra, width, g, k)
 
-    def vec(i):
-        return packed[i * rows_z : (i + 1) * rows_z]
-
     return (
         outputs,
         delta_inputs,
-        vec(0),
-        vec(1),
+        packed[0],
+        packed[1],
         d_in_w,
-        vec(2),
-        vec(3),
+        packed[2],
+        packed[3],
         d_out_w,
-        vec(4),
-        vec(5),
-        vec(6),
+        packed[4],
+        packed[5],
+        packed[6],
         d_exp_w,
-        packed[8 * rows_z : 8 * rows_z + ff_z],
+        packed[8],
         d_con_w,
-        vec(7),
+        packed[7],
     )
 
 

time: 183 us -> 182 us (level)
  waiting for transfers between devices: 54.8 us -> 57 us
    ppermute x56, waiting for transfers between devices: 52.8 us -> 55.1 us  [send(): return lax.ppermute(value, axis, [(s, s ^ flip) for s in range(count)])]
  transfers between devices with their start and end apart: 58 -> 58, of which waited for: 23 -> 22; matrix products, arithmetic and copies ran while one was open for 5% -> 5% of each run, Pallas kernels for 19% -> 19%
where the time goes in v9:
time: 182 us; the launch traced here: 181 us
  waiting for transfers between devices  57 us (31%)
  starting transfers between devices  49.8 us (27%)
  Pallas kernels  46 us (25%)
  between operations  14.9 us (8%)
  other arithmetic  6.46 us (4%)
  local copies, waits for them, and re-layouts  5.68 us (3%)
    ppermute x56, waiting for transfers between devices, send(): return lax.ppermute(value, axis, [(s, s ^ flip) for s in range(count)])  55.1 us
    ppermute x56, starting transfers between devices, send(): return lax.ppermute(value, axis, [(s, s ^ flip) for s in range(count)])  49.7 us
    pallas_call x2, Pallas kernels, attend_back(): pl.pallas_call(functools.partial(attend_back_kernel, ks, head, first), gr...  10.3 us
    pallas_call x1, Pallas kernels, attend(): pl.pallas_call(functools.partial(attend_kernel, ks, head), grid_spec=pltp...  8.43 us
    pallas_call x1, Pallas kernels, hidden_part(): pl.pallas_call(hidden_kernel, grid=(hidden // step,), in_specs=[pl.BlockS...  7.51 us
    pallas_call x1, Pallas kernels, hidden_grads(): pl.pallas_call(hidden_grad_kernel, grid=(width // step,), in_specs=[pl.Bl...  4.71 us
  transfers between devices with their start and end apart: 58, of which 22 were waited for; matrix products, arithmetic and copies ran while one was open for 5% of the time, Pallas kernels for 19%

profile of v9, /device:TPU:0, one launch (start us, length us, event | category | flops | bytes accessed | tf_op | source)
XLA Modules:
  0.0 181.5 jit_solution(12145456229781106069)
XLA Ops:
  9.2 3.1 %collective-permute-start = (bf16[240,576]{1,0:T(8,128)(2,1)S(1)}, bf16[240,576]{1,0:T(8,128)(2,1)S(1)}, u32[]{:S(2)}, u32[]{:S(2)}) collective-permute-start(bf16[240,576]{1,0:T(8,128)(2,1)S(1)} %shard_map.262.refs_0_), channel_id=1, source_target_pairs={{0,1},{1,0},{2,3},{3,2},{4,5},{5,4},{6,7},{7,6},{8,9},{9,8},{10,11... | collective-permute-start | bytes 829448 | tf_op jit(solution)/shard_map/ppermute | solution.py:43
  15.9 2.6 %collective-permute-start.1 = (bf16[240,576]{1,0:T(8,128)(2,1)S(1)}, bf16[240,576]{1,0:T(8,128)(2,1)S(1)}, u32[]{:S(2)}, u32[]{:S(2)}) collective-permute-start(bf16[240,576]{1,0:T(8,128)(2,1)S(1)} %shard_map.262.refs_0_), channel_id=1, source_target_pairs={{0,2},{1,3},{2,0},{3,1},{4,6},{5,7},{6,4},{7,5},{8,10},{9,11},{10,... | collective-permute-start | bytes 829448 | tf_op jit(solution)/shard_map/ppermute | solution.py:43
  18.5 4.8 %collective-permute-done.refs_1_ = bf16[240,576]{1,0:T(8,128)(2,1)S(1)} collective-permute-done((bf16[240,576]{1,0:T(8,128)(2,1)S(1)}, bf16[240,576]{1,0:T(8,128)(2,1)S(1)}, u32[]{:S(2)}, u32[]{:S(2)}) %collective-permute-start) | collective-permute-done | bytes 276512 | tf_op jit(solution)/shard_map/ppermute | solution.py:43
  23.3 2.6 %collective-permute-start.2 = (bf16[240,576]{1,0:T(8,128)(2,1)S(1)}, bf16[240,576]{1,0:T(8,128)(2,1)S(1)}, u32[]{:S(2)}, u32[]{:S(2)}) collective-permute-start(bf16[240,576]{1,0:T(8,128)(2,1)S(1)} %shard_map.262.refs_0_), channel_id=1, source_target_pairs={{0,3},{1,2},{2,1},{3,0},{4,7},{5,6},{6,5},{7,4},{8,11},{9,10},{10,... | collective-permute-start | bytes 829448 | tf_op jit(solution)/shard_map/ppermute | solution.py:43
  25.9 2.5 %shard_map.263 = bf16[96,1536]{1,0:T(8,128)(2,1)} custom-call(s32[2]{0:T(128)S(1)} %pad_add_fusion.place, bf16[768,768]{1,0:T(8,128)(2,1)} %con_ref.1, bf16[192,3072]{1,0:T(8,128)(2,1)} %exp_ref.1), custom_call_target="tpu_custom_call" | custom-call | tf_op jit(solution)/shard_map/pallas_call | solution.py:306
  28.4 11.8 %collective-permute-done.1.refs_2_ = bf16[240,576]{1,0:T(8,128)(2,1)S(1)} collective-permute-done((bf16[240,576]{1,0:T(8,128)(2,1)S(1)}, bf16[240,576]{1,0:T(8,128)(2,1)S(1)}, u32[]{:S(2)}, u32[]{:S(2)}) %collective-permute-start.1) | collective-permute-done | bytes 276512 | tf_op jit(solution)/shard_map/ppermute | solution.py:43
  45.8 8.4 %shard_map.266 = (bf16[128,192]{1,0:T(8,128)(2,1)S(1)}, bf16[128,192]{1,0:T(8,128)(2,1)S(1)}, bf16[128,192]{1,0:T(8,128)(2,1)S(1)}, bf16[128,192]{1,0:T(8,128)(2...) custom-call(s32[2]{0:T(128)S(1)} %pad_add_fusion.place, ...), custom_call_target="tpu_custom_call" | custom-call | flops 1 | bytes 1 | tf_op jit(solution)/shard_map/pallas_call | solution.py:594
  60.0 2.4 %collective-permute-done.16 = bf16[128,192]{1,0:T(8,128)(2,1)S(1)} collective-permute-done((bf16[128,192]{1,0:T(8,128)(2,1)S(1)}, bf16[128,192]{1,0:T(8,128)(2,1)S(1)}, u32[]{:S(2)}, u32[]{:S(2)}) %collective-permute-start.16) | collective-permute-done | bytes 49184 | tf_op jit(solution)/shard_map/ppermute | solution.py:43
  64.4 2.5 %collective-permute-start.19 = (bf16[128,768]{1,0:T(8,128)(2,1)S(1)}, bf16[128,768]{1,0:T(8,128)(2,1)S(1)}, u32[]{:S(2)}, u32[]{:S(2)}) collective-permute-start(bf16[128,768]{1,0:T(8,128)(2,1)S(1)} %add_convert_fusion.2.refs_0_), channel_id=1, source_target_pairs={{0,24},{8,16},{16,8},{24,0},{1,25},{9,17},{17,9},{25,1},{2,26},{10... | collective-permute-start | bytes 589832 | tf_op jit(solution)/shard_map/ppermute | solution.py:43
  67.1 4.2 %collective-permute-done.17.refs_1_ = bf16[128,768]{1,0:T(8,128)(2,1)S(1)} collective-permute-done((bf16[128,768]{1,0:T(8,128)(2,1)S(1)}, bf16[128,768]{1,0:T(8,128)(2,1)S(1)}, u32[]{:S(2)}, u32[]{:S(2)}) %collective-permute-start.17) | collective-permute-done | bytes 196640 | tf_op jit(solution)/shard_map/ppermute | solution.py:43
  71.3 2.5 %collective-permute-done.18.refs_2_ = bf16[128,768]{1,0:T(8,128)(2,1)S(1)} collective-permute-done((bf16[128,768]{1,0:T(8,128)(2,1)S(1)}, bf16[128,768]{1,0:T(8,128)(2,1)S(1)}, u32[]{:S(2)}, u32[]{:S(2)}) %collective-permute-start.18) | collective-permute-done | bytes 196640 | tf_op jit(solution)/shard_map/ppermute | solution.py:43
  75.6 7.5 %shard_map.267 = (bf16[512,768]{1,0:T(8,128)(2,1)S(1)}, bf16[512,768]{1,0:T(8,128)(2,1)S(1)}, bf16[128,768]{1,0:T(8,128)(2,1)S(1)}, bf16[128,768]{1,0:T(8,128)(2...) custom-call(bf16[128,768]{1,0:T(8,128)(2,1)} %copy-done.19, ...), custom_call_target="tpu_custom_call" | custom-call | flops 1 | bytes 1 | tf_op jit(solution)/shard_map/pallas_call | solution.py:459
  86.6 4.7 %shard_map.268 = bf16[768,1536]{1,0:T(8,128)(2,1)} custom-call(bf16[128,768]{1,0:T(8,128)(2,1)} %copy-done.19, bf16[128,768]{1,0:T(8,128)(2,1)} %copy-done.21, bf16[128,768]{1,0:T(8,128)(2,1)} %copy-done.22, bf16[128,768]{1,0:T(8,128)(2,1)} %copy-done.23, bf16[2,128,768]{2,1,0:T(8,128)(2,1)} %copy-done, bf16[2,128,768]{2,1,0:T(8,128)(2,1)} %copy-done.1, ...), custom_call_target="tpu_custom_call" | custom-call | flops 8000000000 | bytes 1 | tf_op jit(solution)/shard_map/pallas_call | solution.py:510
  91.3 4.2 %collective-permute-done.21 = bf16[128,768]{1,0:T(8,128)(2,1)S(1)} collective-permute-done((bf16[128,768]{1,0:T(8,128)(2,1)S(1)}, bf16[128,768]{1,0:T(8,128)(2,1)S(1)}, u32[]{:S(2)}, u32[]{:S(2)}) %collective-permute-start.21) | collective-permute-done | bytes 196640 | tf_op jit(solution)/shard_map/ppermute | solution.py:43
  109.1 6.6 %shard_map.269 = (bf16[512,128]{1,0:T(8,128)(2,1)S(1)}, bf16[2,512,256]{2,1,0:T(8,128)(2,1)S(1)}) custom-call(s32[2]{0:T(128)S(1)} %pad_add_fusion.place, bf16[128,192]{1,0:T(8,128)(2,1)S(1)} %get-tuple-element.182.refs_0_, bf16[128,192]{1,0:T(8,128)(2,1)S(1)} %collective-permute-done.23.refs_1_, bf16[128,192]{1,0:T(8,128)(2,1)S(1)} %collective-permute-done.24.refs_2_, ...), custom_call_target="tpu_custom_call" | custom-call | flops 8000000000 | bytes 1 | tf_op jit(solution)/shard_map/pallas_call | solution.py:657
  115.8 2.5 %collective-permute-done.28 = bf16[128,768]{1,0:T(8,128)(2,1)S(1)} collective-permute-done((bf16[128,768]{1,0:T(8,128)(2,1)S(1)}, bf16[128,768]{1,0:T(8,128)(2,1)S(1)}, u32[]{:S(2)}, u32[]{:S(2)}) %collective-permute-start.28) | collective-permute-done | bytes 196640 | tf_op jit(solution)/shard_map/ppermute | solution.py:43
  120.6 3.7 %shard_map.270 = (bf16[512,64]{1,0:T(8,128)(2,1)S(1)}, bf16[2,512,128]{2,1,0:T(8,128)(2,1)S(1)}) custom-call(s32[2]{0:T(128)S(1)} %pad_add_fusion.place, bf16[128,192]{1,0:T(8,128)(2,1)S(1)} %get-tuple-element.182.refs_0_, bf16[128,192]{1,0:T(8,128)(2,1)S(1)} %collective-permute-done.23.refs_1_, bf16[128,192]{1,0:T(8,128)(2,1)S(1)} %collective-permute-done.24.refs_2_, ...), custom_call_target="tpu_custom_call" | custom-call | flops 8000000000 | bytes 1 | tf_op jit(solution)/shard_map/pallas_call | solution.py:657
  125.6 2.4 %collective-permute-start.38 = (bf16[4,24,768]{2,1,0:T(8,128)(2,1)}, bf16[4,24,768]{2,1,0:T(8,128)(2,1)}, u32[]{:S(2)}, u32[]{:S(2)}) collective-permute-start(bf16[4,24,768]{2,1,0:T(8,128)(2,1)} %get-tuple-element.206), channel_id=1, source_target_pairs={{0,24},{8,16},{16,8},{24,0},{1,25},{9,17},{17,9},{25,1},{2,26},{10... | collective-permute-start | bytes 442376 | tf_op jit(solution)/shard_map/ppermute | solution.py:43
  128.1 3.3 %shard_map.271 = (bf16[128,768]{1,0:T(8,128)(2,1)S(1)}, bf16[128,768]{1,0:T(8,128)(2,1)}, bf16[128,768]{1,0:T(8,128)(2,1)}, bf16[128,768]{1,0:T(8,128)(2,1)S(1)}...) custom-call(s32[1]{0:T(128)} %bitcast.1.place, bf16[512,128]{1,0:T(8,128)(2,1)S(1)} %get-tuple-element.175.refs_0_, ...), custom_call_target="tpu_custom_call" | custom-call | flops 1 | bytes 1 | tf_op jit(solution)/shard_map/pallas_call | solution.py:704
  133.1 2.5 %collective-permute-start.34 = (bf16[128,768]{1,0:T(8,128)(2,1)S(1)}, bf16[128,768]{1,0:T(8,128)(2,1)}, u32[]{:S(2)}, u32[]{:S(2)}) collective-permute-start(bf16[128,768]{1,0:T(8,128)(2,1)S(1)} %get-tuple-element.194), channel_id=1, source_target_pairs={{0,24},{8,16},{16,8},{24,0},{1,25},{9,17},{17,9},{25,1},{2,26},{10... | collective-permute-start | bytes 589832 | tf_op jit(solution)/shard_map/ppermute | solution.py:43
  148.2 6.6 %collective-permute-done.40 = bf16[130,576]{1,0:T(8,128)(2,1)S(1)} collective-permute-done((bf16[130,576]{1,0:T(8,128)(2,1)S(1)}, bf16[130,576]{1,0:T(8,128)(2,1)S(1)}, u32[]{:S(2)}, u32[]{:S(2)}) %collective-permute-start.40) | collective-permute-done | bytes 149792 | tf_op jit(solution)/shard_map/ppermute | solution.py:43
  161.4 3.1 %shard_map.273 = (f32[2,96,3072]{2,1,0:T(8,128)}, f32[4,2,96,768]{3,2,1,0:T(8,128)}) custom-call(s32[2]{0:T(128)S(1)} %pad_add_fusion.place, bf16[96,1536]{1,0:T(8,128)(2,1)S(1)} %copy-done.8, bf16[96,1536]{1,0:T(8,128)(2,1)S(1)} %collective-permute-done.45.refs_1_, bf16[96,1536]{1,0:T(8,128)(2,1)S(1)} %collective-permute-done.46.refs_2_, ...), custom_call_target="tpu_custom_call" | custom-call | flops 1 | bytes 1 | tf_op jit(solution)/shard_map/pallas_call | solution.py:379
  164.5 5.4 %collective-permute-done.43.refs_2_ = bf16[130,576]{1,0:T(8,128)(2,1)S(1)} collective-permute-done((bf16[130,576]{1,0:T(8,128)(2,1)S(1)}, bf16[130,576]{1,0:T(8,128)(2,1)S(1)}, u32[]{:S(2)}, u32[]{:S(2)}) %collective-permute-start.43) | collective-permute-done | bytes 149792 | tf_op jit(solution)/shard_map/ppermute | solution.py:43
  172.1 2.6 %shard_map.274 = (f32[2,96,2304]{2,1,0:T(8,128)}, f32[4,2,24,768]{3,2,1,0:T(8,128)}, f32[192]{0:T(256)}, f32[192]{0:T(256)}, f32[192]{0:T(256)}, /*index=5*/f32[...) custom-call(s32[2]{0:T(128)S(1)} %pad_add_fusion.place, ...), custom_call_target="tpu_custom_call" | custom-call | flops 1 | bytes 1 | tf_op jit(solution)/shard_map/pallas_call | solution.py:769
  (242 shorter events, 64.2 us)
Async XLA Ops:
  7.2 68.4 %all-gather.2.cloned.1.call-start = ((), (), s32[]{:S(2)}) async-start(), calls=%async_computation.1 | async-start | bytes 2654208 | tf_op jit(solution)/shard_map/all_gather | solution.py:852
  9.2 14.1 %collective-permute-start = (bf16[240,576]{1,0:T(8,128)(2,1)S(1)}, bf16[240,576]{1,0:T(8,128)(2,1)S(1)}, u32[]{:S(2)}, u32[]{:S(2)}) collective-permute-start(bf16[240,576]{1,0:T(8,128)(2,1)S(1)} %shard_map.262.refs_0_), channel_id=1, source_target_pairs={{0,1},{1,0},{2,3},{3,2},{4,5},{5,4},{6,7},{7,6},{8,9},{9,8},{10,11... | collective-permute-start | bytes 829448 | tf_op jit(solution)/shard_map/ppermute | solution.py:43
  12.4 27.8 %collective-permute-start.3 = (bf16[2,128,768]{2,1,0:T(8,128)(2,1)S(1)}, bf16[2,128,768]{2,1,0:T(8,128)(2,1)S(1)}, u32[]{:S(2)}, u32[]{:S(2)}) collective-permute-start(bf16[2,128,768]{2,1,0:T(8,128)(2,1)S(1)} %constant_dynamic-update-slice_fusion.refs_0_.refs_4_), channel_id=1, source_target_pairs={{0,8},{8,0},{16,24},{24,16},{1,9},{9,1},{17,25},{25,17},{2,10},{10... | collective-permute-start | bytes 1179656 | tf_op jit(solution)/shard_map/ppermute | solution.py:43
  14.0 26.3 %collective-permute-start.4 = (bf16[2,128,768]{2,1,0:T(8,128)(2,1)S(1)}, bf16[2,128,768]{2,1,0:T(8,128)(2,1)S(1)}, u32[]{:S(2)}, u32[]{:S(2)}) collective-permute-start(bf16[2,128,768]{2,1,0:T(8,128)(2,1)S(1)} %constant_dynamic-update-slice_fusion.refs_0_.refs_4_), channel_id=1, source_target_pairs={{0,16},{8,24},{16,0},{24,8},{1,17},{9,25},{17,1},{25,9},{2,18},{10... | collective-permute-start | bytes 1179656 | tf_op jit(solution)/shard_map/ppermute | solution.py:43
  15.5 24.8 %collective-permute-start.5 = (bf16[2,128,768]{2,1,0:T(8,128)(2,1)S(1)}, bf16[2,128,768]{2,1,0:T(8,128)(2,1)S(1)}, u32[]{:S(2)}, u32[]{:S(2)}) collective-permute-start(bf16[2,128,768]{2,1,0:T(8,128)(2,1)S(1)} %constant_dynamic-update-slice_fusion.refs_0_.refs_4_), channel_id=1, source_target_pairs={{0,24},{8,16},{16,8},{24,0},{1,25},{9,17},{17,9},{25,1},{2,26},{10... | collective-permute-start | bytes 1179656 | tf_op jit(solution)/shard_map/ppermute | solution.py:43
  15.9 24.3 %collective-permute-start.1 = (bf16[240,576]{1,0:T(8,128)(2,1)S(1)}, bf16[240,576]{1,0:T(8,128)(2,1)S(1)}, u32[]{:S(2)}, u32[]{:S(2)}) collective-permute-start(bf16[240,576]{1,0:T(8,128)(2,1)S(1)} %shard_map.262.refs_0_), channel_id=1, source_target_pairs={{0,2},{1,3},{2,0},{3,1},{4,6},{5,7},{6,4},{7,5},{8,10},{9,11},{10,... | collective-permute-start | bytes 829448 | tf_op jit(solution)/shard_map/ppermute | solution.py:43
  23.3 16.9 %collective-permute-start.2 = (bf16[240,576]{1,0:T(8,128)(2,1)S(1)}, bf16[240,576]{1,0:T(8,128)(2,1)S(1)}, u32[]{:S(2)}, u32[]{:S(2)}) collective-permute-start(bf16[240,576]{1,0:T(8,128)(2,1)S(1)} %shard_map.262.refs_0_), channel_id=1, source_target_pairs={{0,3},{1,2},{2,1},{3,0},{4,7},{5,6},{6,5},{7,4},{8,11},{9,10},{10,... | collective-permute-start | bytes 829448 | tf_op jit(solution)/shard_map/ppermute | solution.py:43
  40.3 102.6 %reduce-scatter.2.cloned.1.call-start = ((), (), s32[]{:S(2)}) async-start(), calls=%async_computation.2 | async-start | bytes 2654208 | tf_op jit(solution)/shard_map/reduce_scatter | solution.py:871
  63.9 9.8 %collective-permute-start.18 = (bf16[128,768]{1,0:T(8,128)(2,1)S(1)}, bf16[128,768]{1,0:T(8,128)(2,1)S(1)}, u32[]{:S(2)}, u32[]{:S(2)}) collective-permute-start(bf16[128,768]{1,0:T(8,128)(2,1)S(1)} %add_convert_fusion.2.refs_0_), channel_id=1, source_target_pairs={{0,16},{8,24},{16,0},{24,8},{1,17},{9,25},{17,1},{25,9},{2,18},{10... | collective-permute-start | bytes 589832 | tf_op jit(solution)/shard_map/ppermute | solution.py:43
  84.6 11.0 %collective-permute-start.21 = (bf16[128,768]{1,0:T(8,128)(2,1)S(1)}, bf16[128,768]{1,0:T(8,128)(2,1)S(1)}, u32[]{:S(2)}, u32[]{:S(2)}) collective-permute-start(bf16[128,768]{1,0:T(8,128)(2,1)S(1)} %get-tuple-element.140), channel_id=1, source_target_pairs={{0,16},{8,24},{16,0},{24,8},{1,17},{9,25},{17,1},{25,9},{2,18},{10... | collective-permute-start | bytes 589832 | tf_op jit(solution)/shard_map/ppermute | solution.py:43
  105.6 14.0 %collective-permute-start.26 = (bf16[4,4,24,768]{3,2,1,0:T(8,128)(2,1)S(1)}, bf16[4,4,24,768]{3,2,1,0:T(8,128)(2,1)S(1)}, u32[]{:S(2)}, u32[]{:S(2)}) collective-permute-start(bf16[4,4,24,768]{3,2,1,0:T(8,128)(2,1)S(1)} %get-tuple-element.161), channel_id=1, source_target_pairs={{0,4},{4,0},{1,5},{5,1},{2,6},{6,2},{3,7},{7,3},{8,12},{12,8},{9,1... | collective-permute-start | bytes 1769480 | tf_op jit(solution)/shard_map/ppermute | solution.py:43
  105.6 10.2 %collective-permute-start.27 = (bf16[128,768]{1,0:T(8,128)(2,1)S(1)}, bf16[128,768]{1,0:T(8,128)(2,1)S(1)}, u32[]{:S(2)}, u32[]{:S(2)}) collective-permute-start(bf16[128,768]{1,0:T(8,128)(2,1)S(1)} %copy-done.39), channel_id=1, source_target_pairs={{0,8},{8,0},{16,24},{24,16},{1,9},{9,1},{17,25},{25,17},{2,10},{10... | collective-permute-start | bytes 589832 | tf_op jit(solution)/shard_map/ppermute | solution.py:43
  107.0 11.2 %collective-permute-start.28 = (bf16[128,768]{1,0:T(8,128)(2,1)S(1)}, bf16[128,768]{1,0:T(8,128)(2,1)S(1)}, u32[]{:S(2)}, u32[]{:S(2)}) collective-permute-start(bf16[128,768]{1,0:T(8,128)(2,1)S(1)} %copy-done.38), channel_id=1, source_target_pairs={{0,16},{8,24},{16,0},{24,8},{1,17},{9,25},{17,1},{25,9},{2,18},{10... | collective-permute-start | bytes 589832 | tf_op jit(solution)/shard_map/ppermute | solution.py:43
  107.6 10.6 %collective-permute-start.29 = (bf16[128,768]{1,0:T(8,128)(2,1)S(1)}, bf16[128,768]{1,0:T(8,128)(2,1)S(1)}, u32[]{:S(2)}, u32[]{:S(2)}) collective-permute-start(bf16[128,768]{1,0:T(8,128)(2,1)S(1)} %copy-done.37), channel_id=1, source_target_pairs={{0,24},{8,16},{16,8},{24,0},{1,25},{9,17},{17,9},{25,1},{2,26},{10... | collective-permute-start | bytes 589832 | tf_op jit(solution)/shard_map/ppermute | solution.py:43
  115.7 12.4 %collective-permute-start.30 = (bf16[512,256]{1,0:T(8,128)(2,1)S(1)}, bf16[512,256]{1,0:T(8,128)(2,1)S(1)}, u32[]{:S(2)}, u32[]{:S(2)}) collective-permute-start(bf16[512,256]{1,0:T(8,128)(2,1)S(1)} %get-tuple-element.264), channel_id=1, source_target_pairs={{0,4},{4,0},{1,5},{5,1},{2,6},{6,2},{3,7},{7,3},{8,12},{12,8},{9,1... | collective-permute-start | bytes 786440 | tf_op jit(solution)/shard_map/ppermute | solution.py:43
  125.1 10.5 %collective-permute-start.37 = (bf16[4,24,768]{2,1,0:T(8,128)(2,1)}, bf16[4,24,768]{2,1,0:T(8,128)(2,1)}, u32[]{:S(2)}, u32[]{:S(2)}) collective-permute-start(bf16[4,24,768]{2,1,0:T(8,128)(2,1)} %get-tuple-element.205), channel_id=1, source_target_pairs={{0,16},{8,24},{16,0},{24,8},{1,17},{9,25},{17,1},{25,9},{2,18},{10... | collective-permute-start | bytes 442376 | tf_op jit(solution)/shard_map/ppermute | solution.py:43
  125.6 10.1 %collective-permute-start.38 = (bf16[4,24,768]{2,1,0:T(8,128)(2,1)}, bf16[4,24,768]{2,1,0:T(8,128)(2,1)}, u32[]{:S(2)}, u32[]{:S(2)}) collective-permute-start(bf16[4,24,768]{2,1,0:T(8,128)(2,1)} %get-tuple-element.206), channel_id=1, source_target_pairs={{0,24},{8,16},{16,8},{24,0},{1,25},{9,17},{17,9},{25,1},{2,26},{10... | collective-permute-start | bytes 442376 | tf_op jit(solution)/shard_map/ppermute | solution.py:43
  132.0 10.9 %collective-permute-start.33 = (bf16[128,768]{1,0:T(8,128)(2,1)}, bf16[128,768]{1,0:T(8,128)(2,1)}, u32[]{:S(2)}, u32[]{:S(2)}) collective-permute-start(bf16[128,768]{1,0:T(8,128)(2,1)} %get-tuple-element.193), channel_id=1, source_target_pairs={{0,16},{8,24},{16,0},{24,8},{1,17},{9,25},{17,1},{25,9},{2,18},{10... | collective-permute-start | bytes 589832 | tf_op jit(solution)/shard_map/ppermute | solution.py:43
  139.2 15.7 %collective-permute-start.40 = (bf16[130,576]{1,0:T(8,128)(2,1)S(1)}, bf16[130,576]{1,0:T(8,128)(2,1)S(1)}, u32[]{:S(2)}, u32[]{:S(2)}) collective-permute-start(bf16[130,576]{1,0:T(8,128)(2,1)S(1)} %get-tuple-element.209), channel_id=1, source_target_pairs={{0,2},{1,3},{2,0},{3,1},{4,6},{5,7},{6,4},{7,5},{8,10},{9,11},{10,... | collective-permute-start | bytes 449288 | tf_op jit(solution)/shard_map/ppermute | solution.py:43
  140.1 14.7 %collective-permute-start.41 = (bf16[130,576]{1,0:T(8,128)(2,1)S(1)}, bf16[130,576]{1,0:T(8,128)(2,1)S(1)}, u32[]{:S(2)}, u32[]{:S(2)}) collective-permute-start(bf16[130,576]{1,0:T(8,128)(2,1)S(1)} %get-tuple-element.210), channel_id=1, source_target_pairs={{0,3},{1,2},{2,1},{3,0},{4,7},{5,6},{6,5},{7,4},{8,11},{9,10},{10,... | collective-permute-start | bytes 449288 | tf_op jit(solution)/shard_map/ppermute | solution.py:43
  142.9 12.4 %collective-permute-start.45 = (bf16[96,1536]{1,0:T(8,128)(2,1)}, bf16[96,1536]{1,0:T(8,128)(2,1)S(1)}, u32[]{:S(2)}, u32[]{:S(2)}) collective-permute-start(bf16[96,1536]{1,0:T(8,128)(2,1)} %reduce-scatter.2.cloned.1.call-done.refs_0_), channel_id=1, source_target_pairs={{0,8},{8,0},{16,24},{24,16},{1,9},{9,1},{17,25},{25,17},{2,10},{10... | collective-permute-start | bytes 884744 | tf_op jit(solution)/shard_map/ppermute | solution.py:43
  145.3 12.0 %collective-permute-start.46 = (bf16[96,1536]{1,0:T(8,128)(2,1)S(1)}, bf16[96,1536]{1,0:T(8,128)(2,1)S(1)}, u32[]{:S(2)}, u32[]{:S(2)}) collective-permute-start(bf16[96,1536]{1,0:T(8,128)(2,1)S(1)} %copy-done.8), channel_id=1, source_target_pairs={{0,16},{8,24},{16,0},{24,8},{1,17},{9,25},{17,1},{25,9},{2,18},{10... | collective-permute-start | bytes 884744 | tf_op jit(solution)/shard_map/ppermute | solution.py:43
  147.3 12.0 %collective-permute-start.47 = (bf16[96,1536]{1,0:T(8,128)(2,1)S(1)}, bf16[96,1536]{1,0:T(8,128)(2,1)S(1)}, u32[]{:S(2)}, u32[]{:S(2)}) collective-permute-start(bf16[96,1536]{1,0:T(8,128)(2,1)S(1)} %copy-done.8), channel_id=1, source_target_pairs={{0,24},{8,16},{16,8},{24,0},{1,25},{9,17},{17,9},{25,1},{2,26},{10... | collective-permute-start | bytes 884744 | tf_op jit(solution)/shard_map/ppermute | solution.py:43
  159.3 10.6 %collective-permute-start.43 = (bf16[130,576]{1,0:T(8,128)(2,1)S(1)}, bf16[130,576]{1,0:T(8,128)(2,1)S(1)}, u32[]{:S(2)}, u32[]{:S(2)}) collective-permute-start(bf16[130,576]{1,0:T(8,128)(2,1)S(1)} %add_convert_fusion.3.refs_0_), channel_id=1, source_target_pairs={{0,16},{8,24},{16,0},{24,8},{1,17},{9,25},{17,1},{25,9},{2,18},{10... | collective-permute-start | bytes 449288 | tf_op jit(solution)/shard_map/ppermute | solution.py:43
  (74 other events, 437.4 us)
Sparse Core Ops, SparseCore 0:
  40.4 35.1 all-gather.1
  101.8 35.3 reduce-scatter.1

commit v10 on v9

--- a/solution.py
+++ b/solution.py
@@ -892,6 +892,8 @@
     dq, dkv = attend_back(g, k, ks, head, 0, split, datt, *kept)
     dq, dkv = [dq], [swap_flips([dkv[j] for j in range(ks)], "core")]
     datt, d_out, out_sum = lax.optimization_barrier((datt, d_out, out_sum))
+    outputs = (middle + total(out_sum) + c_bias).astype(BF)[None]
+    datt, outputs = lax.optimization_barrier((datt, outputs))
     d_out = total(d_out).astype(BF)
     pieces = [lax.dynamic_index_in_dim(d_out, g ^ i, axis=1, keepdims=False) for i in range(GROUPS)]
     datt, pieces = lax.optimization_barrier((datt, pieces))
@@ -940,7 +942,6 @@
     d_hidden = [d_hidden] + [[send(p, "core", j) for p in d_hidden] for j in range(1, ks)]
     d_exp_w, d_con_w = unfold(d_hidden, zs, g, k)
     d_in, d_exp_w, d_con_w = lax.optimization_barrier((d_in, d_exp_w, d_con_w))
-    outputs = (middle + total(out_sum) + c_bias).astype(BF)[None]
     d_in = [d_in] + [[send(p, "core", j) for p in d_in] for j in range(1, ks)]
     d_in_w, d_out_w, packed = finish(d_in, own, extra, width, g, k)
 

time: 182 us -> 181 us (level)
  transfers between devices with their start and end apart: 58 -> 58, of which waited for: 22 -> 24; matrix products, arithmetic and copies ran while one was open for 5% -> 4% of each run, Pallas kernels for 19% -> 19%
where the time goes in v10:
time: 181 us
  waiting for transfers between devices  58 us (32%)
  starting transfers between devices  50.6 us (28%)
  Pallas kernels  46 us (25%)
  between operations  14.9 us (8%)
  other arithmetic  5.35 us (3%)
  local copies, waits for them, and re-layouts  4.27 us (2%)
    ppermute x56, waiting for transfers between devices, send(): return lax.ppermute(value, axis, [(s, s ^ flip) for s in range(count)])  56.2 us
    ppermute x56, starting transfers between devices, send(): return lax.ppermute(value, axis, [(s, s ^ flip) for s in range(count)])  50.5 us
    pallas_call x2, Pallas kernels, attend_back(): pl.pallas_call(functools.partial(attend_back_kernel, ks, head, first), gr...  10.3 us
    pallas_call x1, Pallas kernels, attend(): pl.pallas_call(functools.partial(attend_kernel, ks, head), grid_spec=pltp...  8.44 us
    pallas_call x1, Pallas kernels, hidden_part(): pl.pallas_call(hidden_kernel, grid=(hidden // step,), in_specs=[pl.BlockS...  7.47 us
    pallas_call x1, Pallas kernels, hidden_grads(): pl.pallas_call(hidden_grad_kernel, grid=(width // step,), in_specs=[pl.Bl...  4.71 us
  transfers between devices with their start and end apart: 58, of which 24 were waited for; matrix products, arithmetic and copies ran while one was open for 4% of the time, Pallas kernels for 19%

profile of v10, /device:TPU:0, one launch (start us, length us, event | category | flops | bytes accessed | tf_op | source)
XLA Modules:
  0.0 180.7 jit_solution(1009687833233030658)
XLA Ops:
  9.2 3.1 %collective-permute-start = (bf16[240,576]{1,0:T(8,128)(2,1)S(1)}, bf16[240,576]{1,0:T(8,128)(2,1)S(1)}, u32[]{:S(2)}, u32[]{:S(2)}) collective-permute-start(bf16[240,576]{1,0:T(8,128)(2,1)S(1)} %shard_map.262.refs_0_), channel_id=1, source_target_pairs={{0,1},{1,0},{2,3},{3,2},{4,5},{5,4},{6,7},{7,6},{8,9},{9,8},{10,11... | collective-permute-start | bytes 829448 | tf_op jit(solution)/shard_map/ppermute | solution.py:43
  15.9 2.6 %collective-permute-start.1 = (bf16[240,576]{1,0:T(8,128)(2,1)S(1)}, bf16[240,576]{1,0:T(8,128)(2,1)S(1)}, u32[]{:S(2)}, u32[]{:S(2)}) collective-permute-start(bf16[240,576]{1,0:T(8,128)(2,1)S(1)} %shard_map.262.refs_0_), channel_id=1, source_target_pairs={{0,2},{1,3},{2,0},{3,1},{4,6},{5,7},{6,4},{7,5},{8,10},{9,11},{10,... | collective-permute-start | bytes 829448 | tf_op jit(solution)/shard_map/ppermute | solution.py:43
  18.5 4.8 %collective-permute-done.refs_1_ = bf16[240,576]{1,0:T(8,128)(2,1)S(1)} collective-permute-done((bf16[240,576]{1,0:T(8,128)(2,1)S(1)}, bf16[240,576]{1,0:T(8,128)(2,1)S(1)}, u32[]{:S(2)}, u32[]{:S(2)}) %collective-permute-start) | collective-permute-done | bytes 276512 | tf_op jit(solution)/shard_map/ppermute | solution.py:43
  23.3 2.6 %collective-permute-start.2 = (bf16[240,576]{1,0:T(8,128)(2,1)S(1)}, bf16[240,576]{1,0:T(8,128)(2,1)S(1)}, u32[]{:S(2)}, u32[]{:S(2)}) collective-permute-start(bf16[240,576]{1,0:T(8,128)(2,1)S(1)} %shard_map.262.refs_0_), channel_id=1, source_target_pairs={{0,3},{1,2},{2,1},{3,0},{4,7},{5,6},{6,5},{7,4},{8,11},{9,10},{10,... | collective-permute-start | bytes 829448 | tf_op jit(solution)/shard_map/ppermute | solution.py:43
  25.9 2.5 %shard_map.263 = bf16[96,1536]{1,0:T(8,128)(2,1)} custom-call(s32[2]{0:T(128)S(1)} %pad_add_fusion.place, bf16[768,768]{1,0:T(8,128)(2,1)} %con_ref.1, bf16[192,3072]{1,0:T(8,128)(2,1)} %exp_ref.1), custom_call_target="tpu_custom_call" | custom-call | tf_op jit(solution)/shard_map/pallas_call | solution.py:306
  28.4 11.8 %collective-permute-done.1.refs_2_ = bf16[240,576]{1,0:T(8,128)(2,1)S(1)} collective-permute-done((bf16[240,576]{1,0:T(8,128)(2,1)S(1)}, bf16[240,576]{1,0:T(8,128)(2,1)S(1)}, u32[]{:S(2)}, u32[]{:S(2)}) %collective-permute-start.1) | collective-permute-done | bytes 276512 | tf_op jit(solution)/shard_map/ppermute | solution.py:43
  45.8 8.4 %shard_map.266 = (bf16[128,192]{1,0:T(8,128)(2,1)S(1)}, bf16[128,192]{1,0:T(8,128)(2,1)S(1)}, bf16[128,192]{1,0:T(8,128)(2,1)S(1)}, bf16[128,192]{1,0:T(8,128)(2...) custom-call(s32[2]{0:T(128)S(1)} %pad_add_fusion.place, ...), custom_call_target="tpu_custom_call" | custom-call | flops 1 | bytes 1 | tf_op jit(solution)/shard_map/pallas_call | solution.py:594
  60.1 2.4 %collective-permute-done.16 = bf16[128,192]{1,0:T(8,128)(2,1)S(1)} collective-permute-done((bf16[128,192]{1,0:T(8,128)(2,1)S(1)}, bf16[128,192]{1,0:T(8,128)(2,1)S(1)}, u32[]{:S(2)}, u32[]{:S(2)}) %collective-permute-start.16) | collective-permute-done | bytes 49184 | tf_op jit(solution)/shard_map/ppermute | solution.py:43
  64.5 2.5 %collective-permute-start.19 = (bf16[128,768]{1,0:T(8,128)(2,1)S(1)}, bf16[128,768]{1,0:T(8,128)(2,1)S(1)}, u32[]{:S(2)}, u32[]{:S(2)}) collective-permute-start(bf16[128,768]{1,0:T(8,128)(2,1)S(1)} %add_convert_fusion.2.refs_0_), channel_id=1, source_target_pairs={{0,24},{8,16},{16,8},{24,0},{1,25},{9,17},{17,9},{25,1},{2,26},{10... | collective-permute-start | bytes 589832 | tf_op jit(solution)/shard_map/ppermute | solution.py:43
  67.0 4.3 %collective-permute-done.17.refs_1_ = bf16[128,768]{1,0:T(8,128)(2,1)S(1)} collective-permute-done((bf16[128,768]{1,0:T(8,128)(2,1)S(1)}, bf16[128,768]{1,0:T(8,128)(2,1)S(1)}, u32[]{:S(2)}, u32[]{:S(2)}) %collective-permute-start.17) | collective-permute-done | bytes 196640 | tf_op jit(solution)/shard_map/ppermute | solution.py:43
  71.3 2.5 %collective-permute-done.18.refs_2_ = bf16[128,768]{1,0:T(8,128)(2,1)S(1)} collective-permute-done((bf16[128,768]{1,0:T(8,128)(2,1)S(1)}, bf16[128,768]{1,0:T(8,128)(2,1)S(1)}, u32[]{:S(2)}, u32[]{:S(2)}) %collective-permute-start.18) | collective-permute-done | bytes 196640 | tf_op jit(solution)/shard_map/ppermute | solution.py:43
  75.6 7.5 %shard_map.267 = (bf16[512,768]{1,0:T(8,128)(2,1)S(1)}, bf16[512,768]{1,0:T(8,128)(2,1)S(1)}, bf16[128,768]{1,0:T(8,128)(2,1)S(1)}, bf16[128,768]{1,0:T(8,128)(2...) custom-call(bf16[128,768]{1,0:T(8,128)(2,1)} %copy-done.17, ...), custom_call_target="tpu_custom_call" | custom-call | flops 1 | bytes 1 | tf_op jit(solution)/shard_map/pallas_call | solution.py:459
  86.6 4.7 %shard_map.268 = bf16[768,1536]{1,0:T(8,128)(2,1)} custom-call(bf16[128,768]{1,0:T(8,128)(2,1)} %copy-done.17, bf16[128,768]{1,0:T(8,128)(2,1)} %copy-done.19, bf16[128,768]{1,0:T(8,128)(2,1)} %copy-done.20, bf16[128,768]{1,0:T(8,128)(2,1)} %copy-done.21, bf16[2,128,768]{2,1,0:T(8,128)(2,1)} %copy-done, bf16[2,128,768]{2,1,0:T(8,128)(2,1)} %copy-done.1, ...), custom_call_target="tpu_custom_call" | custom-call | flops 8000000000 | bytes 1 | tf_op jit(solution)/shard_map/pallas_call | solution.py:510
  91.3 4.2 %collective-permute-done.21 = bf16[128,768]{1,0:T(8,128)(2,1)S(1)} collective-permute-done((bf16[128,768]{1,0:T(8,128)(2,1)S(1)}, bf16[128,768]{1,0:T(8,128)(2,1)S(1)}, u32[]{:S(2)}, u32[]{:S(2)}) %collective-permute-start.21) | collective-permute-done | bytes 196640 | tf_op jit(solution)/shard_map/ppermute | solution.py:43
  108.7 6.6 %shard_map.269 = (bf16[512,128]{1,0:T(8,128)(2,1)S(1)}, bf16[2,512,256]{2,1,0:T(8,128)(2,1)S(1)}) custom-call(s32[2]{0:T(128)S(1)} %pad_add_fusion.place, bf16[128,192]{1,0:T(8,128)(2,1)S(1)} %get-tuple-element.192.refs_0_, bf16[128,192]{1,0:T(8,128)(2,1)S(1)} %collective-permute-done.23.refs_1_, bf16[128,192]{1,0:T(8,128)(2,1)S(1)} %collective-permute-done.24.refs_2_, ...), custom_call_target="tpu_custom_call" | custom-call | flops 8000000000 | bytes 1 | tf_op jit(solution)/shard_map/pallas_call | solution.py:657
  115.5 2.6 %collective-permute-done.28 = bf16[128,768]{1,0:T(8,128)(2,1)S(1)} collective-permute-done((bf16[128,768]{1,0:T(8,128)(2,1)S(1)}, bf16[128,768]{1,0:T(8,128)(2,1)S(1)}, u32[]{:S(2)}, u32[]{:S(2)}) %collective-permute-start.28) | collective-permute-done | bytes 196640 | tf_op jit(solution)/shard_map/ppermute | solution.py:43
  119.8 3.7 %shard_map.270 = (bf16[512,64]{1,0:T(8,128)(2,1)S(1)}, bf16[2,512,128]{2,1,0:T(8,128)(2,1)S(1)}) custom-call(s32[2]{0:T(128)S(1)} %pad_add_fusion.place, bf16[128,192]{1,0:T(8,128)(2,1)S(1)} %get-tuple-element.192.refs_0_, bf16[128,192]{1,0:T(8,128)(2,1)S(1)} %collective-permute-done.23.refs_1_, bf16[128,192]{1,0:T(8,128)(2,1)S(1)} %collective-permute-done.24.refs_2_, ...), custom_call_target="tpu_custom_call" | custom-call | flops 8000000000 | bytes 1 | tf_op jit(solution)/shard_map/pallas_call | solution.py:657
  127.6 3.3 %shard_map.271 = (bf16[128,768]{1,0:T(8,128)(2,1)S(1)}, bf16[128,768]{1,0:T(8,128)(2,1)}, bf16[128,768]{1,0:T(8,128)(2,1)}, bf16[128,768]{1,0:T(8,128)(2,1)S(1)}...) custom-call(s32[1]{0:T(128)} %bitcast.2.place, bf16[512,128]{1,0:T(8,128)(2,1)S(1)} %get-tuple-element.185.refs_0_, ...), custom_call_target="tpu_custom_call" | custom-call | flops 1 | bytes 1 | tf_op jit(solution)/shard_map/pallas_call | solution.py:704
  139.4 2.3 %collective-permute-start.41 = (bf16[130,576]{1,0:T(8,128)(2,1)S(1)}, bf16[130,576]{1,0:T(8,128)(2,1)S(1)}, u32[]{:S(2)}, u32[]{:S(2)}) collective-permute-start(bf16[130,576]{1,0:T(8,128)(2,1)S(1)} %get-tuple-element.220), channel_id=1, source_target_pairs={{0,3},{1,2},{2,1},{3,0},{4,7},{5,6},{6,5},{7,4},{8,11},{9,10},{10,... | collective-permute-start | bytes 449288 | tf_op jit(solution)/shard_map/ppermute | solution.py:43
  144.3 2.4 %collective-permute-done.39 = bf16[130,576]{1,0:T(8,128)(2,1)S(1)} collective-permute-done((bf16[130,576]{1,0:T(8,128)(2,1)S(1)}, bf16[130,576]{1,0:T(8,128)(2,1)S(1)}, u32[]{:S(2)}, u32[]{:S(2)}) %collective-permute-start.39) | collective-permute-done | bytes 149792 | tf_op jit(solution)/shard_map/ppermute | solution.py:43
  148.0 6.1 %collective-permute-done.40 = bf16[130,576]{1,0:T(8,128)(2,1)S(1)} collective-permute-done((bf16[130,576]{1,0:T(8,128)(2,1)S(1)}, bf16[130,576]{1,0:T(8,128)(2,1)S(1)}, u32[]{:S(2)}, u32[]{:S(2)}) %collective-permute-start.40) | collective-permute-done | bytes 149792 | tf_op jit(solution)/shard_map/ppermute | solution.py:43
  160.8 3.1 %shard_map.273 = (f32[2,96,3072]{2,1,0:T(8,128)}, f32[4,2,96,768]{3,2,1,0:T(8,128)}) custom-call(s32[2]{0:T(128)S(1)} %pad_add_fusion.place, bf16[96,1536]{1,0:T(8,128)(2,1)S(1)} %copy-done.8, bf16[96,1536]{1,0:T(8,128)(2,1)S(1)} %collective-permute-done.45.refs_1_, bf16[96,1536]{1,0:T(8,128)(2,1)S(1)} %collective-permute-done.46.refs_2_, ...), custom_call_target="tpu_custom_call" | custom-call | flops 1 | bytes 1 | tf_op jit(solution)/shard_map/pallas_call | solution.py:379
  163.9 5.3 %collective-permute-done.43.refs_2_ = bf16[130,576]{1,0:T(8,128)(2,1)S(1)} collective-permute-done((bf16[130,576]{1,0:T(8,128)(2,1)S(1)}, bf16[130,576]{1,0:T(8,128)(2,1)S(1)}, u32[]{:S(2)}, u32[]{:S(2)}) %collective-permute-start.43) | collective-permute-done | bytes 149792 | tf_op jit(solution)/shard_map/ppermute | solution.py:43
  171.3 2.6 %shard_map.274 = (f32[2,96,2304]{2,1,0:T(8,128)}, f32[4,2,24,768]{3,2,1,0:T(8,128)}, f32[192]{0:T(256)}, f32[192]{0:T(256)}, f32[192]{0:T(256)}, /*index=5*/f32[...) custom-call(s32[2]{0:T(128)S(1)} %pad_add_fusion.place, ...), custom_call_target="tpu_custom_call" | custom-call | flops 1 | bytes 1 | tf_op jit(solution)/shard_map/pallas_call | solution.py:769
  (226 shorter events, 64.0 us)
Async XLA Ops:
  7.2 68.4 %all-gather.2.cloned.1.call-start = ((), (), s32[]{:S(2)}) async-start(), calls=%async_computation.1 | async-start | bytes 2654208 | tf_op jit(solution)/shard_map/all_gather | solution.py:852
  9.2 14.1 %collective-permute-start = (bf16[240,576]{1,0:T(8,128)(2,1)S(1)}, bf16[240,576]{1,0:T(8,128)(2,1)S(1)}, u32[]{:S(2)}, u32[]{:S(2)}) collective-permute-start(bf16[240,576]{1,0:T(8,128)(2,1)S(1)} %shard_map.262.refs_0_), channel_id=1, source_target_pairs={{0,1},{1,0},{2,3},{3,2},{4,5},{5,4},{6,7},{7,6},{8,9},{9,8},{10,11... | collective-permute-start | bytes 829448 | tf_op jit(solution)/shard_map/ppermute | solution.py:43
  12.4 27.8 %collective-permute-start.3 = (bf16[2,128,768]{2,1,0:T(8,128)(2,1)S(1)}, bf16[2,128,768]{2,1,0:T(8,128)(2,1)S(1)}, u32[]{:S(2)}, u32[]{:S(2)}) collective-permute-start(bf16[2,128,768]{2,1,0:T(8,128)(2,1)S(1)} %constant_dynamic-update-slice_fusion.refs_0_.refs_4_), channel_id=1, source_target_pairs={{0,8},{8,0},{16,24},{24,16},{1,9},{9,1},{17,25},{25,17},{2,10},{10... | collective-permute-start | bytes 1179656 | tf_op jit(solution)/shard_map/ppermute | solution.py:43
  14.0 26.3 %collective-permute-start.4 = (bf16[2,128,768]{2,1,0:T(8,128)(2,1)S(1)}, bf16[2,128,768]{2,1,0:T(8,128)(2,1)S(1)}, u32[]{:S(2)}, u32[]{:S(2)}) collective-permute-start(bf16[2,128,768]{2,1,0:T(8,128)(2,1)S(1)} %constant_dynamic-update-slice_fusion.refs_0_.refs_4_), channel_id=1, source_target_pairs={{0,16},{8,24},{16,0},{24,8},{1,17},{9,25},{17,1},{25,9},{2,18},{10... | collective-permute-start | bytes 1179656 | tf_op jit(solution)/shard_map/ppermute | solution.py:43
  15.5 24.8 %collective-permute-start.5 = (bf16[2,128,768]{2,1,0:T(8,128)(2,1)S(1)}, bf16[2,128,768]{2,1,0:T(8,128)(2,1)S(1)}, u32[]{:S(2)}, u32[]{:S(2)}) collective-permute-start(bf16[2,128,768]{2,1,0:T(8,128)(2,1)S(1)} %constant_dynamic-update-slice_fusion.refs_0_.refs_4_), channel_id=1, source_target_pairs={{0,24},{8,16},{16,8},{24,0},{1,25},{9,17},{17,9},{25,1},{2,26},{10... | collective-permute-start | bytes 1179656 | tf_op jit(solution)/shard_map/ppermute | solution.py:43
  15.9 24.3 %collective-permute-start.1 = (bf16[240,576]{1,0:T(8,128)(2,1)S(1)}, bf16[240,576]{1,0:T(8,128)(2,1)S(1)}, u32[]{:S(2)}, u32[]{:S(2)}) collective-permute-start(bf16[240,576]{1,0:T(8,128)(2,1)S(1)} %shard_map.262.refs_0_), channel_id=1, source_target_pairs={{0,2},{1,3},{2,0},{3,1},{4,6},{5,7},{6,4},{7,5},{8,10},{9,11},{10,... | collective-permute-start | bytes 829448 | tf_op jit(solution)/shard_map/ppermute | solution.py:43
  23.3 16.9 %collective-permute-start.2 = (bf16[240,576]{1,0:T(8,128)(2,1)S(1)}, bf16[240,576]{1,0:T(8,128)(2,1)S(1)}, u32[]{:S(2)}, u32[]{:S(2)}) collective-permute-start(bf16[240,576]{1,0:T(8,128)(2,1)S(1)} %shard_map.262.refs_0_), channel_id=1, source_target_pairs={{0,3},{1,2},{2,1},{3,0},{4,7},{5,6},{6,5},{7,4},{8,11},{9,10},{10,... | collective-permute-start | bytes 829448 | tf_op jit(solution)/shard_map/ppermute | solution.py:43
  40.3 101.9 %reduce-scatter.2.cloned.1.call-start = ((), (), s32[]{:S(2)}) async-start(), calls=%async_computation.2 | async-start | bytes 2654208 | tf_op jit(solution)/shard_map/reduce_scatter | solution.py:871
  64.0 9.8 %collective-permute-start.18 = (bf16[128,768]{1,0:T(8,128)(2,1)S(1)}, bf16[128,768]{1,0:T(8,128)(2,1)S(1)}, u32[]{:S(2)}, u32[]{:S(2)}) collective-permute-start(bf16[128,768]{1,0:T(8,128)(2,1)S(1)} %add_convert_fusion.2.refs_0_), channel_id=1, source_target_pairs={{0,16},{8,24},{16,0},{24,8},{1,17},{9,25},{17,1},{25,9},{2,18},{10... | collective-permute-start | bytes 589832 | tf_op jit(solution)/shard_map/ppermute | solution.py:43
  84.5 11.0 %collective-permute-start.21 = (bf16[128,768]{1,0:T(8,128)(2,1)S(1)}, bf16[128,768]{1,0:T(8,128)(2,1)S(1)}, u32[]{:S(2)}, u32[]{:S(2)}) collective-permute-start(bf16[128,768]{1,0:T(8,128)(2,1)S(1)} %get-tuple-element.145), channel_id=1, source_target_pairs={{0,16},{8,24},{16,0},{24,8},{1,17},{9,25},{17,1},{25,9},{2,18},{10... | collective-permute-start | bytes 589832 | tf_op jit(solution)/shard_map/ppermute | solution.py:43
  105.2 12.8 %collective-permute-start.26 = (bf16[4,4,24,768]{3,2,1,0:T(8,128)(2,1)S(1)}, bf16[4,4,24,768]{3,2,1,0:T(8,128)(2,1)S(1)}, u32[]{:S(2)}, u32[]{:S(2)}) collective-permute-start(bf16[4,4,24,768]{3,2,1,0:T(8,128)(2,1)S(1)} %get-tuple-element.166), channel_id=1, source_target_pairs={{0,4},{4,0},{1,5},{5,1},{2,6},{6,2},{3,7},{7,3},{8,12},{12,8},{9,1... | collective-permute-start | bytes 1769480 | tf_op jit(solution)/shard_map/ppermute | solution.py:43
  105.2 10.2 %collective-permute-start.27 = (bf16[128,768]{1,0:T(8,128)(2,1)S(1)}, bf16[128,768]{1,0:T(8,128)(2,1)S(1)}, u32[]{:S(2)}, u32[]{:S(2)}) collective-permute-start(bf16[128,768]{1,0:T(8,128)(2,1)S(1)} %copy-done.31), channel_id=1, source_target_pairs={{0,8},{8,0},{16,24},{24,16},{1,9},{9,1},{17,25},{25,17},{2,10},{10... | collective-permute-start | bytes 589832 | tf_op jit(solution)/shard_map/ppermute | solution.py:43
  106.8 11.2 %collective-permute-start.28 = (bf16[128,768]{1,0:T(8,128)(2,1)S(1)}, bf16[128,768]{1,0:T(8,128)(2,1)S(1)}, u32[]{:S(2)}, u32[]{:S(2)}) collective-permute-start(bf16[128,768]{1,0:T(8,128)(2,1)S(1)} %copy-done.30), channel_id=1, source_target_pairs={{0,16},{8,24},{16,0},{24,8},{1,17},{9,25},{17,1},{25,9},{2,18},{10... | collective-permute-start | bytes 589832 | tf_op jit(solution)/shard_map/ppermute | solution.py:43
  107.3 10.7 %collective-permute-start.29 = (bf16[128,768]{1,0:T(8,128)(2,1)S(1)}, bf16[128,768]{1,0:T(8,128)(2,1)S(1)}, u32[]{:S(2)}, u32[]{:S(2)}) collective-permute-start(bf16[128,768]{1,0:T(8,128)(2,1)S(1)} %copy-done.29), channel_id=1, source_target_pairs={{0,24},{8,16},{16,8},{24,0},{1,25},{9,17},{17,9},{25,1},{2,26},{10... | collective-permute-start | bytes 589832 | tf_op jit(solution)/shard_map/ppermute | solution.py:43
  115.4 12.2 %collective-permute-start.30 = (bf16[512,256]{1,0:T(8,128)(2,1)S(1)}, bf16[512,256]{1,0:T(8,128)(2,1)S(1)}, u32[]{:S(2)}, u32[]{:S(2)}) collective-permute-start(bf16[512,256]{1,0:T(8,128)(2,1)S(1)} %get-tuple-element.274), channel_id=1, source_target_pairs={{0,4},{4,0},{1,5},{5,1},{2,6},{6,2},{3,7},{7,3},{8,12},{12,8},{9,1... | collective-permute-start | bytes 786440 | tf_op jit(solution)/shard_map/ppermute | solution.py:43
  124.5 10.6 %collective-permute-start.37 = (bf16[4,24,768]{2,1,0:T(8,128)(2,1)}, bf16[4,24,768]{2,1,0:T(8,128)(2,1)}, u32[]{:S(2)}, u32[]{:S(2)}) collective-permute-start(bf16[4,24,768]{2,1,0:T(8,128)(2,1)} %get-tuple-element.215), channel_id=1, source_target_pairs={{0,16},{8,24},{16,0},{24,8},{1,17},{9,25},{17,1},{25,9},{2,18},{10... | collective-permute-start | bytes 442376 | tf_op jit(solution)/shard_map/ppermute | solution.py:43
  131.4 10.8 %collective-permute-start.33 = (bf16[128,768]{1,0:T(8,128)(2,1)}, bf16[128,768]{1,0:T(8,128)(2,1)S(1)}, u32[]{:S(2)}, u32[]{:S(2)}) collective-permute-start(bf16[128,768]{1,0:T(8,128)(2,1)} %get-tuple-element.203), channel_id=1, source_target_pairs={{0,16},{8,24},{16,0},{24,8},{1,17},{9,25},{17,1},{25,9},{2,18},{10... | collective-permute-start | bytes 589832 | tf_op jit(solution)/shard_map/ppermute | solution.py:43
  138.4 15.7 %collective-permute-start.40 = (bf16[130,576]{1,0:T(8,128)(2,1)S(1)}, bf16[130,576]{1,0:T(8,128)(2,1)S(1)}, u32[]{:S(2)}, u32[]{:S(2)}) collective-permute-start(bf16[130,576]{1,0:T(8,128)(2,1)S(1)} %get-tuple-element.219), channel_id=1, source_target_pairs={{0,2},{1,3},{2,0},{3,1},{4,6},{5,7},{6,4},{7,5},{8,10},{9,11},{10,... | collective-permute-start | bytes 449288 | tf_op jit(solution)/shard_map/ppermute | solution.py:43
  139.4 14.6 %collective-permute-start.41 = (bf16[130,576]{1,0:T(8,128)(2,1)S(1)}, bf16[130,576]{1,0:T(8,128)(2,1)S(1)}, u32[]{:S(2)}, u32[]{:S(2)}) collective-permute-start(bf16[130,576]{1,0:T(8,128)(2,1)S(1)} %get-tuple-element.220), channel_id=1, source_target_pairs={{0,3},{1,2},{2,1},{3,0},{4,7},{5,6},{6,5},{7,4},{8,11},{9,10},{10,... | collective-permute-start | bytes 449288 | tf_op jit(solution)/shard_map/ppermute | solution.py:43
  142.2 12.8 %collective-permute-start.45 = (bf16[96,1536]{1,0:T(8,128)(2,1)}, bf16[96,1536]{1,0:T(8,128)(2,1)S(1)}, u32[]{:S(2)}, u32[]{:S(2)}) collective-permute-start(bf16[96,1536]{1,0:T(8,128)(2,1)} %reduce-scatter.2.cloned.1.call-done.refs_0_), channel_id=1, source_target_pairs={{0,8},{8,0},{16,24},{24,16},{1,9},{9,1},{17,25},{25,17},{2,10},{10... | collective-permute-start | bytes 884744 | tf_op jit(solution)/shard_map/ppermute | solution.py:43
  143.8 12.6 %collective-permute-start.46 = (bf16[96,1536]{1,0:T(8,128)(2,1)}, bf16[96,1536]{1,0:T(8,128)(2,1)S(1)}, u32[]{:S(2)}, u32[]{:S(2)}) collective-permute-start(bf16[96,1536]{1,0:T(8,128)(2,1)} %reduce-scatter.2.cloned.1.call-done.refs_0_), channel_id=1, source_target_pairs={{0,16},{8,24},{16,0},{24,8},{1,17},{9,25},{17,1},{25,9},{2,18},{10... | collective-permute-start | bytes 884744 | tf_op jit(solution)/shard_map/ppermute | solution.py:43
  146.7 11.8 %collective-permute-start.47 = (bf16[96,1536]{1,0:T(8,128)(2,1)}, bf16[96,1536]{1,0:T(8,128)(2,1)S(1)}, u32[]{:S(2)}, u32[]{:S(2)}) collective-permute-start(bf16[96,1536]{1,0:T(8,128)(2,1)} %reduce-scatter.2.cloned.1.call-done.refs_0_), channel_id=1, source_target_pairs={{0,24},{8,16},{16,8},{24,0},{1,25},{9,17},{17,9},{25,1},{2,26},{10... | collective-permute-start | bytes 884744 | tf_op jit(solution)/shard_map/ppermute | solution.py:43
  154.2 9.7 %collective-permute-start.42 = (bf16[130,576]{1,0:T(8,128)(2,1)S(1)}, bf16[130,576]{1,0:T(8,128)(2,1)S(1)}, u32[]{:S(2)}, u32[]{:S(2)}) collective-permute-start(bf16[130,576]{1,0:T(8,128)(2,1)S(1)} %add_convert_fusion.3.refs_0_), channel_id=1, source_target_pairs={{0,8},{8,0},{16,24},{24,16},{1,9},{9,1},{17,25},{25,17},{2,10},{10... | collective-permute-start | bytes 449288 | tf_op jit(solution)/shard_map/ppermute | solution.py:43
  158.6 10.6 %collective-permute-start.43 = (bf16[130,576]{1,0:T(8,128)(2,1)S(1)}, bf16[130,576]{1,0:T(8,128)(2,1)S(1)}, u32[]{:S(2)}, u32[]{:S(2)}) collective-permute-start(bf16[130,576]{1,0:T(8,128)(2,1)S(1)} %add_convert_fusion.3.refs_0_), channel_id=1, source_target_pairs={{0,16},{8,24},{16,0},{24,8},{1,17},{9,25},{17,1},{25,9},{2,18},{10... | collective-permute-start | bytes 449288 | tf_op jit(solution)/shard_map/ppermute | solution.py:43
  (66 other events, 377.6 us)
Sparse Core Ops, SparseCore 0:
  40.4 35.1 all-gather.1
  101.7 35.3 reduce-scatter.1
